TPU v7x, 32 devices: a whole 2x2x4 slice. The times are simulated.
32 devices in a mesh: dp: 8 (over y, x, core), fsdp: 4 (over z).
Axes of the slice: x: 2, y: 2, z: 4, core: 2. Of those that a mesh axis runs over, the one named last changes fastest.
Arguments:
- hidden_in: bfloat16 [32, 128, 960], P(('dp', 'fsdp')), may hold values from -6 to 6
- segment_ids: int32 [32, 128], P(('dp', 'fsdp')), may hold values from 0 to 3, as said below
- positions: int32 [32, 128], P(('dp', 'fsdp')), may hold values from 0 to 2047, as said below
- query_weight: bfloat16 [960, 960], P('fsdp', 'dp'), may hold values from -0.1875 to 0.1875
- key_weight: bfloat16 [960, 320], P('fsdp', 'dp'), may hold values from -0.1875 to 0.1875
- value_weight: bfloat16 [960, 320], P('fsdp', 'dp'), may hold values from -0.1875 to 0.1875
- output_weight: bfloat16 [960, 960], P('fsdp', 'dp'), may hold values from -0.75 to 0.75
- attention_gain: bfloat16 [960], P('dp'), may hold values from 0.099609375 to 1.8984375
- gate_weight: bfloat16 [960, 2560], P('fsdp', 'dp'), may hold values from -0.1875 to 0.1875
- up_weight: bfloat16 [960, 2560], P('fsdp', 'dp'), may hold values from -0.1875 to 0.1875
- down_weight: bfloat16 [2560, 960], P('fsdp', 'dp'), may hold values from -0.125 to 0.125
- feedforward_gain: bfloat16 [960], P('dp'), may hold values from 0.099609375 to 1.8984375
- output_cotangent: bfloat16 [32, 128, 960], P(('dp', 'fsdp')), may hold values from -6 to 6
Outputs:
- block_output: bfloat16 [32, 128, 960], P(('dp', 'fsdp'))
- input_grad: float32 [32, 128, 960], P(('dp', 'fsdp'))
- query_grad: float32 [960, 960], P('fsdp', 'dp')
- key_grad: float32 [960, 320], P('fsdp', 'dp')
- value_grad: float32 [960, 320], P('fsdp', 'dp')
- output_grad: float32 [960, 960], P('fsdp', 'dp')
- attention_gain_grad: float32 [960], P('dp')
- gate_grad: float32 [960, 2560], P('fsdp', 'dp')
- up_grad: float32 [960, 2560], P('fsdp', 'dp')
- down_grad: float32 [2560, 960], P('fsdp', 'dp')
- feedforward_gain_grad: float32 [960], P('dp')
Inputs may be any that keep to these rules, and one draw needn't show every extreme that they name: `segment_ids`: each row of 128 tokens holds exactly 4 documents of consecutive tokens, numbered in order from 0. Within a document positions rise by one from token to token; the first document of every row starts at position 0.
All inputs are finite; a program needn't handle non-finite values.
Results may differ from a plain program's by a relative error of at most 0.013.
Values may be sent and summed in bfloat16 or wider, within the bound.
No kernel may reach another device: no remote copies, remote signals or barrier semaphores. Data moves between devices by JAX's collectives and lax.ppermute only.
A program may use at most 192 MiB of HBM per device.

v0:
```python
import jax
import jax.numpy as jnp
from jax import lax
from jax.sharding import PartitionSpec as P

HEADS = 15
KV_HEADS = 5
HD = 64


EPS = 1e-05
THETA = 100000.0
NEGATIVE = -1e30


def rotary_tables(position, head_dim):
    inverse = THETA ** (-jnp.arange(0, head_dim, 2).astype(jnp.float32) / head_dim)
    angles = position.astype(jnp.float32)[:, None] * inverse[None, :]
    cosines = jnp.cos(angles)
    sine_values = jnp.sin(angles)
    return (
        jnp.concatenate([cosines, cosines], -1),
        jnp.concatenate([sine_values, sine_values], -1),
    )


def rotate(values, cosines, sine_values):
    half_dim = values.shape[-1] // 2
    turned = jnp.concatenate([-values[..., half_dim:], values[..., :half_dim]], -1)
    return values * cosines[:, None, :] + turned * sine_values[:, None, :]


def rotate_back(gradient, cosines, sine_values):
    half_dim = gradient.shape[-1] // 2
    sine_scaled = gradient * sine_values[:, None, :]
    turned = jnp.concatenate([-sine_scaled[..., half_dim:], sine_scaled[..., :half_dim]], -1)
    return gradient * cosines[:, None, :] - turned


def norm_forward(values, gain):
    row_scale = lax.rsqrt(jnp.mean(values * values, -1, keepdims=True) + EPS)
    return (row_scale, (values * row_scale * gain.astype(jnp.float32)).astype(jnp.bfloat16))


def norm_backward(values, row_scale, gain, upstream):
    unit_rows = values * row_scale
    scaled = upstream * gain.astype(jnp.float32)
    gain_grad = jnp.sum(upstream * unit_rows, 0)
    result = row_scale * (scaled - unit_rows * jnp.mean(scaled * unit_rows, -1, keepdims=True))
    return (result, gain_grad)


def contract_first(left, right):
    return lax.dot_general(
        left, right, (((0,), (0,)), ((), ())), preferred_element_type=jnp.float32
    )


def contract_last(left, right):
    return lax.dot_general(
        left, right, (((1,), (1,)), ((), ())), preferred_element_type=jnp.float32
    )


def owner_blocks(gradient, dp_count, fsdp_count):
    row_count, column_count = gradient.shape
    shaped = gradient.reshape(
        fsdp_count, row_count // fsdp_count, dp_count, column_count // dp_count
    )
    return shaped.transpose(2, 0, 1, 3).reshape(
        dp_count * fsdp_count, row_count // fsdp_count * (column_count // dp_count)
    )


def gain_blocks(gain_grad, dp_count, fsdp_count):
    feature_count = gain_grad.shape[0]
    spread = jnp.broadcast_to(
        gain_grad.reshape(dp_count, 1, feature_count // dp_count),
        (dp_count, fsdp_count, feature_count // dp_count),
    )
    return spread.reshape(dp_count * fsdp_count, feature_count // dp_count)


def block_scores(query_block, key_turned, segment, start, block_rows):
    length = key_turned.shape[0]
    head_dim = key_turned.shape[2]
    scores = jnp.einsum(
        "qkgd,tkd->kgqt", query_block, key_turned, preferred_element_type=jnp.float32
    ) * head_dim ** (-0.5)
    key_index = jnp.arange(length)
    query_index = start + jnp.arange(block_rows)
    allowed = (segment[:, None] == segment[None, :]) & (query_index[:, None] >= key_index[None, :])
    return jnp.where(allowed, scores, NEGATIVE)


def attend_forward(query_turned, key_turned, value_rounded, segment, group):
    length, head_count, head_dim = query_turned.shape
    kv_heads = key_turned.shape[1]
    block_rows = min(length, 512)
    block_count = length // block_rows
    grouped = query_turned.reshape(block_count, block_rows, kv_heads, group, head_dim)
    starts = jnp.arange(block_count) * block_rows

    def one_block(inputs):
        query_block, start = inputs
        scores = block_scores(query_block, key_turned, segment, start, block_rows)
        row_max = jnp.max(scores, -1, keepdims=True)
        exponentials = jnp.exp(scores - row_max)
        totals = jnp.sum(exponentials, -1, keepdims=True)
        probs_rounded = (exponentials / totals).astype(jnp.bfloat16)
        attended = jnp.einsum(
            "kgqt,tkd->qkgd", probs_rounded, value_rounded, preferred_element_type=jnp.float32
        )
        return (
            attended.reshape(block_rows, head_count * head_dim).astype(jnp.bfloat16),
            row_max + jnp.log(totals),
        )

    attended, log_totals = lax.map(one_block, (grouped, starts))
    return (attended.reshape(length, head_count * head_dim), log_totals)


def attend_backward(
    query_turned, key_turned, value_rounded, segment, group, log_totals, attended_grad
):
    length, head_count, head_dim = query_turned.shape
    kv_heads = key_turned.shape[1]
    block_rows = min(length, 512)
    block_count = length // block_rows
    grouped = query_turned.reshape(block_count, block_rows, kv_heads, group, head_dim)
    grad_grouped = attended_grad.reshape(block_count, block_rows, kv_heads, group, head_dim)
    starts = jnp.arange(block_count) * block_rows

    def one_block(running, inputs):
        key_sum, value_sum = running
        query_block, grad_block, log_block, start = inputs
        scores = block_scores(query_block, key_turned, segment, start, block_rows)
        probs_again = jnp.exp(scores - log_block)
        probs_rounded = probs_again.astype(jnp.bfloat16)
        value_sum = value_sum + jnp.einsum(
            "kgqt,qkgd->tkd", probs_rounded, grad_block, preferred_element_type=jnp.float32
        )
        prob_grad = jnp.einsum(
            "qkgd,tkd->kgqt", grad_block, value_rounded, preferred_element_type=jnp.float32
        )
        inner_rows = jnp.sum(probs_again * prob_grad, -1, keepdims=True)
        score_grad = (probs_again * (prob_grad - inner_rows) * head_dim ** (-0.5)).astype(
            jnp.bfloat16
        )
        query_part = jnp.einsum(
            "kgqt,tkd->qkgd", score_grad, key_turned, preferred_element_type=jnp.float32
        )
        key_sum = key_sum + jnp.einsum(
            "kgqt,qkgd->tkd", score_grad, query_block, preferred_element_type=jnp.float32
        )
        return ((key_sum, value_sum), query_part)

    zero_sums = jnp.zeros((length, kv_heads, head_dim), jnp.float32)
    (key_sum, value_sum), query_parts = lax.scan(
        one_block, (zero_sums, zero_sums), (grouped, grad_grouped, log_totals, starts)
    )
    return (query_parts.reshape(length, head_count, head_dim), key_sum, value_sum)


def local(
    hidden_in,
    segment_ids,
    positions,
    query_weight,
    key_weight,
    value_weight,
    output_weight,
    attention_gain,
    gate_weight,
    up_weight,
    down_weight,
    feedforward_gain,
    output_cotangent,
):
    hidden_rows = hidden_in[0].astype(jnp.float32)
    segment = segment_ids[0]
    position = positions[0]
    cotangent = output_cotangent[0]
    length = hidden_rows.shape[0]
    group = HEADS // KV_HEADS
    width = HEADS * HD
    dp_count = lax.axis_size("dp")
    fsdp_count = lax.axis_size("fsdp")
    attention_rows = (
        lax.all_gather(query_weight, "fsdp", axis=0, tiled=True),
        lax.all_gather(key_weight, "fsdp", axis=0, tiled=True),
        lax.all_gather(value_weight, "fsdp", axis=0, tiled=True),
        lax.all_gather(output_weight, "fsdp", axis=0, tiled=True),
    )
    attention_full = (
        lax.all_gather(attention_rows[0], "dp", axis=1, tiled=True),
        lax.all_gather(attention_rows[1], "dp", axis=1, tiled=True),
        lax.all_gather(attention_rows[2], "dp", axis=1, tiled=True),
        lax.all_gather(attention_rows[3], "dp", axis=1, tiled=True),
        lax.all_gather(attention_gain, "dp", axis=0, tiled=True),
    )
    query_full, key_full, value_full, output_full, attention_gain_full = attention_full
    scale_one, normed_one = norm_forward(hidden_rows, attention_gain_full)
    cosines, sine_values = rotary_tables(position, HD)
    query_proj = jnp.dot(normed_one, query_full, preferred_element_type=jnp.float32).reshape(
        length, HEADS, HD
    )
    key_proj = jnp.dot(normed_one, key_full, preferred_element_type=jnp.float32).reshape(
        length, KV_HEADS, HD
    )
    value_proj = jnp.dot(normed_one, value_full, preferred_element_type=jnp.float32).reshape(
        length, KV_HEADS, HD
    )
    query_turned = rotate(query_proj, cosines, sine_values).astype(jnp.bfloat16)
    key_turned = rotate(key_proj, cosines, sine_values).astype(jnp.bfloat16)
    value_rounded = value_proj.astype(jnp.bfloat16)
    attended, log_totals = attend_forward(query_turned, key_turned, value_rounded, segment, group)
    residual = hidden_rows + jnp.dot(attended, output_full, preferred_element_type=jnp.float32)
    feed_rows = (
        lax.all_gather(gate_weight, "fsdp", axis=0, tiled=True),
        lax.all_gather(up_weight, "fsdp", axis=0, tiled=True),
        lax.all_gather(down_weight, "fsdp", axis=0, tiled=True),
    )
    feed_full = (
        lax.all_gather(feed_rows[0], "dp", axis=1, tiled=True),
        lax.all_gather(feed_rows[1], "dp", axis=1, tiled=True),
        lax.all_gather(feed_rows[2], "dp", axis=1, tiled=True),
        lax.all_gather(feedforward_gain, "dp", axis=0, tiled=True),
    )
    gate_full, up_full, down_full, feed_gain_full = feed_full
    scale_two, normed_two = norm_forward(residual, feed_gain_full)
    gate_proj = jnp.dot(normed_two, gate_full, preferred_element_type=jnp.float32)
    up_proj = jnp.dot(normed_two, up_full, preferred_element_type=jnp.float32)
    sigmoid_gate = jax.nn.sigmoid(gate_proj)
    silu_gate = gate_proj * sigmoid_gate
    mixed = (silu_gate * up_proj).astype(jnp.bfloat16)
    block_output = (
        residual + jnp.dot(mixed, down_full, preferred_element_type=jnp.float32)
    ).astype(jnp.bfloat16)
    gate_back, up_back, down_back, feed_gain_back = feed_full
    down_grad = contract_first(mixed, cotangent)
    mixed_grad = contract_last(cotangent, down_back)
    gate_delta = (
        mixed_grad * up_proj * sigmoid_gate * (1.0 + gate_proj * (1.0 - sigmoid_gate))
    ).astype(jnp.bfloat16)
    up_delta = (mixed_grad * silu_gate).astype(jnp.bfloat16)
    gate_grad = contract_first(normed_two, gate_delta)
    up_grad = contract_first(normed_two, up_delta)
    normed_two_grad = contract_last(gate_delta, gate_back) + contract_last(up_delta, up_back)
    residual_part, feed_gain_grad = norm_backward(
        residual, scale_two, feed_gain_back, normed_two_grad
    )
    residual_grad = cotangent.astype(jnp.float32) + residual_part
    gate_blocks = owner_blocks(gate_grad, dp_count, fsdp_count)
    up_blocks = owner_blocks(up_grad, dp_count, fsdp_count)
    down_blocks = owner_blocks(down_grad, dp_count, fsdp_count)
    feed_gain_blocks = gain_blocks(feed_gain_grad, dp_count, fsdp_count)
    feed_done = (
        lax.psum_scatter(gate_blocks, ("dp", "fsdp"), scatter_dimension=0, tiled=True),
        lax.psum_scatter(up_blocks, ("dp", "fsdp"), scatter_dimension=0, tiled=True),
        lax.psum_scatter(down_blocks, ("dp", "fsdp"), scatter_dimension=0, tiled=True),
        lax.psum_scatter(feed_gain_blocks, ("dp", "fsdp"), scatter_dimension=0, tiled=True),
    )
    query_back, key_back, value_back, output_back, attention_gain_back = attention_full
    residual_rounded = residual_grad.astype(jnp.bfloat16)
    output_grad = contract_first(attended, residual_rounded)
    attended_grad = contract_last(residual_rounded, output_back).astype(jnp.bfloat16)
    query_raw, key_raw, value_raw = attend_backward(
        query_turned, key_turned, value_rounded, segment, group, log_totals, attended_grad
    )
    query_delta = (
        rotate_back(query_raw, cosines, sine_values).reshape(length, width).astype(jnp.bfloat16)
    )
    key_delta = (
        rotate_back(key_raw, cosines, sine_values)
        .reshape(length, KV_HEADS * HD)
        .astype(jnp.bfloat16)
    )
    value_delta = value_raw.reshape(length, KV_HEADS * HD).astype(jnp.bfloat16)
    query_grad = contract_first(normed_one, query_delta)
    key_grad = contract_first(normed_one, key_delta)
    value_grad = contract_first(normed_one, value_delta)
    normed_one_grad = (
        contract_last(query_delta, query_back)
        + contract_last(key_delta, key_back)
        + contract_last(value_delta, value_back)
    )
    input_part, attention_gain_grad = norm_backward(
        hidden_rows, scale_one, attention_gain_back, normed_one_grad
    )
    input_grad = residual_grad + input_part
    query_blocks = owner_blocks(query_grad, dp_count, fsdp_count)
    key_blocks = owner_blocks(key_grad, dp_count, fsdp_count)
    value_blocks = owner_blocks(value_grad, dp_count, fsdp_count)
    output_blocks = owner_blocks(output_grad, dp_count, fsdp_count)
    attention_gain_blocks = gain_blocks(attention_gain_grad, dp_count, fsdp_count)
    attention_done = (
        lax.psum_scatter(query_blocks, ("dp", "fsdp"), scatter_dimension=0, tiled=True),
        lax.psum_scatter(key_blocks, ("dp", "fsdp"), scatter_dimension=0, tiled=True),
        lax.psum_scatter(value_blocks, ("dp", "fsdp"), scatter_dimension=0, tiled=True),
        lax.psum_scatter(output_blocks, ("dp", "fsdp"), scatter_dimension=0, tiled=True),
        lax.psum_scatter(attention_gain_blocks, ("dp", "fsdp"), scatter_dimension=0, tiled=True),
    )
    query_out = attention_done[0].reshape(query_weight.shape)
    key_out = attention_done[1].reshape(key_weight.shape)
    value_out = attention_done[2].reshape(value_weight.shape)
    output_out = attention_done[3].reshape(output_weight.shape)
    attention_gain_out = attention_done[4].reshape(attention_gain.shape)
    gate_out = feed_done[0].reshape(gate_weight.shape)
    up_out = feed_done[1].reshape(up_weight.shape)
    down_out = feed_done[2].reshape(down_weight.shape)
    feed_gain_out = feed_done[3].reshape(feedforward_gain.shape)
    return (
        block_output[None],
        input_grad[None],
        query_out,
        key_out,
        value_out,
        output_out,
        attention_gain_out,
        gate_out,
        up_out,
        down_out,
        feed_gain_out,
    )


def solution(mesh):
    in_specs = (
        P(("dp", "fsdp"), None, None),
        P(("dp", "fsdp"), None),
        P(("dp", "fsdp"), None),
        P("fsdp", "dp"),
        P("fsdp", "dp"),
        P("fsdp", "dp"),
        P("fsdp", "dp"),
        P("dp"),
        P("fsdp", "dp"),
        P("fsdp", "dp"),
        P("fsdp", "dp"),
        P("dp"),
        P(("dp", "fsdp"), None, None),
    )
    out_specs = (
        P(("dp", "fsdp"), None, None),
        P(("dp", "fsdp"), None, None),
        P("fsdp", "dp"),
        P("fsdp", "dp"),
        P("fsdp", "dp"),
        P("fsdp", "dp"),
        P("dp"),
        P("fsdp", "dp"),
        P("fsdp", "dp"),
        P("fsdp", "dp"),
        P("dp"),
    )
    return jax.shard_map(local, mesh=mesh, in_specs=in_specs, out_specs=out_specs, check_vma=False)
```

profile of v0, /device:TPU:8, one launch (start us, length us, event | category | flops | bytes accessed | tf_op | source)
XLA Modules:
  0.0 993.7 jit_solution(7710728416811595128)
XLA Ops:
  7.2 14.9 %all_gather.53 = bf16[960,120]{1,0:T(8,128)(2,1)S(1)} all-gather(bf16[240,120]{1,0:T(8,128)(2,1)} %param.16), channel_id=1, replica_groups=mesh['dp'=8,'fsdp'=4] {'fsdp'}, dimensions={0}, use_global_device_ids=true | all-gather | bytes 288000 | tf_op jit(solution)/shard_map/all_gather | solution.py:190
  22.1 0.8 copy.81
  23.0 14.0 %all_gather.55 = bf16[960,120]{1,0:T(8,128)(2,1)S(1)} all-gather(bf16[240,120]{1,0:T(8,128)(2,1)} %param.19), channel_id=1, replica_groups=mesh['dp'=8,'fsdp'=4] {'fsdp'}, dimensions={0}, use_global_device_ids=true | all-gather | bytes 288000 | tf_op jit(solution)/shard_map/all_gather | solution.py:193
  37.0 0.8 copy.83
  38.0 17.2 %all-gather.2 = bf16[4,240,320]{1,2,0:T(8,128)(2,1)S(1)} all-gather(bf16[1,240,320]{1,2,0:T(8,128)(2,1)S(1)} %bitcast.295), channel_id=1, replica_groups=mesh['dp'=8,'fsdp'=4] {'fsdp'}, dimensions={0}, use_global_device_ids=true | all-gather | bytes 768000 | tf_op jit(solution)/shard_map/all_gather | solution.py:220
  55.7 1.4 reshape.264
  57.2 17.4 %all-gather.3 = bf16[4,240,320]{1,2,0:T(8,128)(2,1)S(1)} all-gather(bf16[1,240,320]{1,2,0:T(8,128)(2,1)S(1)} %bitcast.296), channel_id=1, replica_groups=mesh['dp'=8,'fsdp'=4] {'fsdp'}, dimensions={0}, use_global_device_ids=true | all-gather | bytes 768000 | tf_op jit(solution)/shard_map/all_gather | solution.py:221
  75.2 1.4 reshape.266
  76.7 16.0 %all_gather.62 = bf16[2560,120]{0,1:T(8,128)(2,1)} all-gather(bf16[640,120]{0,1:T(8,128)(2,1)S(1)} %copy-done.24), channel_id=1, replica_groups=mesh['dp'=8,'fsdp'=4] {'fsdp'}, dimensions={0}, use_global_device_ids=true | all-gather | bytes 768000 | tf_op jit(solution)/shard_map/all_gather | solution.py:222
  94.6 12.0 %all-reduce.13 = (bf16[960]{0:T(1024)(128)(2,1)S(1)}, bf16[960]{0:T(1024)(128)(2,1)S(1)}) all-reduce(bf16[960]{0:T(1024)(128)(2,1)S(1)} %dynamic-update-slice, bf16[960]{0:T(1024)(128)(2,1)S(1)} %dynamic-update-slice.1), channel_id=1, replica_groups=mesh['dp'=8,'fsdp'=4] {'dp'}, use_global_device_ids=true, to_apply=%add | all-reduce | flops 1920 | bytes 7680
  106.6 13.4 %all-gather.1 = bf16[4,240,40]{1,2,0:T(8,128)(2,1)S(1)} all-gather(bf16[1,240,40]{1,2,0:T(8,128)(2,1)S(1)} %bitcast.299), channel_id=1, replica_groups=mesh['dp'=8,'fsdp'=4] {'fsdp'}, dimensions={0}, use_global_device_ids=true | all-gather | bytes 96000 | tf_op jit(solution)/shard_map/all_gather | solution.py:191
  120.1 13.2 %all-gather = bf16[4,240,40]{1,2,0:T(8,128)(2,1)S(1)} all-gather(bf16[1,240,40]{1,2,0:T(8,128)(2,1)S(1)} %bitcast.300), channel_id=1, replica_groups=mesh['dp'=8,'fsdp'=4] {'fsdp'}, dimensions={0}, use_global_device_ids=true | all-gather | bytes 96000 | tf_op jit(solution)/shard_map/all_gather | solution.py:192
  133.9 12.8 %all_gather.50 = bf16[960,320]{0,1:T(8,128)(2,1)S(1)} all-gather(bf16[960,40]{0,1:T(8,128)(2,1)S(1)} %reshape.260), channel_id=1, replica_groups=mesh['dp'=8,'fsdp'=4] {'dp'}, dimensions={1}, use_global_device_ids=true | all-gather | bytes 691200 | tf_op jit(solution)/shard_map/all_gather | solution.py:198
  146.6 11.3 %all_gather.52 = bf16[960,320]{0,1:T(8,128)(2,1)S(1)} all-gather(bf16[960,40]{0,1:T(8,128)(2,1)S(1)} %reshape.262), channel_id=1, replica_groups=mesh['dp'=8,'fsdp'=4] {'dp'}, dimensions={1}, use_global_device_ids=true | all-gather | bytes 691200 | tf_op jit(solution)/shard_map/all_gather | solution.py:197
  159.1 2.4 fusion.69
  163.2 2.3 multiply_reduce_fusion.3
  166.4 5.5 fusion.78
  171.9 6.2 fusion.6
  178.1 34.2 %all-gather.18.cloned.1.call-done = bf16[2560,960]{0,1:T(8,128)(2,1)} async-done(((bf16[2560,120]{0,1:T(8,128)(2,1)}), bf16[2560,960]{0,1:T(8,128)(2,1)}) %all-gather.18.cloned.1.call-update) | async-done | bytes 4915216 | tf_op jit(solution)/shard_map/all_gather | solution.py:227
  212.4 4.7 multiply_convert_fusion
  217.1 2.1 fusion.79
  220.0 1.9 multiply_reduce_fusion.1
  222.2 1.5 convolution_convert_fusion
  223.7 1.3 convolution_bitcast_fusion.5
  225.4 2.9 broadcast_multiply_fusion
  228.2 2.8 fusion.21
  231.0 6.7 fusion.83
  237.7 5.5 fusion.82
  243.2 2.2 copy.117
  245.4 1.5 fusion.81
  247.0 0.9 slice_negate_fusion.2
  247.9 0.9 fusion.59
  249.5 1.3 copy-done.1
  250.9 1.0 fusion.37
  251.9 1.1 fusion.36
  253.4 1.4 convolution_bitcast_fusion.4
  254.8 3.8 copy.90
  258.6 4.5 reshape.234
  263.0 2.6 copy.91
  265.7 4.5 reshape.236
  270.8 2.2 copy.89
  273.1 5.3 reshape.232
  279.1 2.2 copy.92
  281.3 5.3 reshape.238
  286.6 5.2 convolution_bitcast_fusion
  291.7 11.0 %copy.98 = f32[8,4,640,120]{3,2,1,0:T(8,128)} copy(f32[8,4,640,120]{2,3,0,1:T(8,128)} %convolution_bitcast_fusion) | data formatting | bytes 19660800 | tf_op jit(solution)/shard_map/transpose | solution.py:70
  302.8 12.0 %reshape.248 = f32[32,76800]{1,0:T(8,128)} reshape(f32[8,4,640,120]{3,2,1,0:T(8,128)} %copy.98) | data formatting | bytes 19660800 | tf_op jit(solution)/shard_map/reshape | solution.py:70
  314.8 14.3 %reshape.245 = f32[4,240,8,320]{1,0,3,2:T(4,128)} reshape(f32[960,2560]{0,1:T(8,128)} %fusion.83) | data formatting | bytes 19660800 | tf_op jit(solution)/shard_map/reshape | solution.py:67
  329.1 12.9 %copy.96 = f32[8,4,240,320]{3,2,1,0:T(8,128)} copy(f32[8,4,240,320]{2,1,3,0:T(4,128)} %bitcast.271) | data formatting | bytes 19660800 | tf_op jit(solution)/shard_map/transpose | solution.py:70
  342.0 10.3 %reshape.246 = f32[32,76800]{1,0:T(8,128)} reshape(f32[8,4,240,320]{3,2,1,0:T(8,128)} %copy.96) | data formatting | bytes 19660800 | tf_op jit(solution)/shard_map/reshape | solution.py:70
  352.3 14.3 %reshape.242 = f32[4,240,8,320]{1,0,3,2:T(4,128)} reshape(f32[960,2560]{0,1:T(8,128)} %fusion.82) | data formatting | bytes 19660800 | tf_op jit(solution)/shard_map/reshape | solution.py:67
  366.7 12.9 %copy.94 = f32[8,4,240,320]{3,2,1,0:T(8,128)} copy(f32[8,4,240,320]{2,1,3,0:T(4,128)} %bitcast.272) | data formatting | bytes 19660800 | tf_op jit(solution)/shard_map/transpose | solution.py:70
  379.6 10.2 %reshape.243 = f32[32,76800]{1,0:T(8,128)} reshape(f32[8,4,240,320]{3,2,1,0:T(8,128)} %copy.94) | data formatting | bytes 19660800 | tf_op jit(solution)/shard_map/reshape | solution.py:70
  390.0 41.5 %all-reduce.11 = (f32[32,120]{1,0:T(8,128)S(1)}, f32[32,120]{1,0:T(8,128)S(1)}) all-reduce(f32[32,120]{1,0:T(8,128)S(1)} %bitcast.298, f32[32,120]{1,0:T(8,128)S(1)} %bitcast.297), channel_id=6, replica_groups=mesh['dp'=8,'fsdp'=4] {'dp','fsdp'}, use_global_device_ids=true, to_apply=%region_12.13.clone | all-reduce | flops 7680 | bytes 61440
  432.0 5.1 fusion.14
  437.0 533.0 %all-reduce.16.cloned.1.call-done = (f32[32,28800]{1,0:T(8,128)}, f32[32,9600]{1,0:T(8,128)}, f32[32,9600]{1,0:T(8,128)}, f32[32,28800]{1,0:T(8,128)}, f32[32,76...) async-done(((f32[32,28800]{1,0:T(8,128)}, f32[32,9600]{1,0:T(8,128)}, f32[32,9600]{1,0:T(8,128)}, f32[32,28800]{1,0:T(8,128)}, f32[32,76800]{1,0:T(8,128)}, ...) | async-done | bytes 39321616
  970.1 2.1 dynamic-slice_reduce_fusion.3
  972.1 0.8 reshape.239
  972.9 1.3 dynamic-slice_reduce_fusion.5
  976.7 2.5 dynamic-slice_reduce_fusion.2
  979.2 4.1 dynamic-slice_reduce_fusion
  983.7 0.9 copy.103
  984.7 0.9 copy.101
  985.7 0.9 copy.102
  (148 shorter events, 14.2 us)
Async XLA Ops:
  7.2 30.8 %copy-start.22 = (bf16[240,320]{0,1:T(8,128)(2,1)S(1)}, bf16[240,320]{0,1:T(8,128)(2,1)}, u32[]{:S(2)}) copy-start(bf16[240,320]{0,1:T(8,128)(2,1)} %param.21) | copy-start | bytes 460804
  7.2 151.9 %all-gather.10.cloned.1.call-start = ((), (), s32[]{:S(2)}) async-start(), calls=%async_computation | async-start | bytes 2211840 | tf_op jit(solution)/shard_map/all_gather | solution.py:196
  22.9 140.2 %all-gather.12.cloned.1.call-start = ((), (), s32[]{:S(2)}) async-start(), calls=%async_computation.1 | async-start | bytes 2211840 | tf_op jit(solution)/shard_map/all_gather | solution.py:199
  37.9 128.5 %all-gather.14.cloned.1.call-start = ((), (), s32[]{:S(2)}) async-start(), calls=%async_computation.2 | async-start | bytes 5898240 | tf_op jit(solution)/shard_map/all_gather | solution.py:225
  37.9 19.3 %copy-start.23 = (bf16[240,320]{0,1:T(8,128)(2,1)S(1)}, bf16[240,320]{0,1:T(8,128)(2,1)}, u32[]{:S(2)}) copy-start(bf16[240,320]{0,1:T(8,128)(2,1)} %param.22) | copy-start | bytes 460804
  57.1 114.7 %all-gather.16.cloned.1.call-start = ((), (), s32[]{:S(2)}) async-start(), calls=%async_computation.3 | async-start | bytes 5898240 | tf_op jit(solution)/shard_map/all_gather | solution.py:226
  57.2 19.5 %copy-start.24 = (bf16[640,120]{0,1:T(8,128)(2,1)S(1)}, bf16[640,120]{0,1:T(8,128)(2,1)}, u32[]{:S(2)}) copy-start(bf16[640,120]{0,1:T(8,128)(2,1)} %param.23) | copy-start | bytes 460804
  75.1 17.7 %copy-start.34 = (u32[32]{0:T(128)S(1)}, u32[32]{0:T(128)}, u32[]{:S(2)}) copy-start(u32[32]{0:T(128)} %constant.72) | copy-start | bytes 388
  75.1 19.0 %copy-start.31 = (bf16[120]{0:T(256)(128)(2,1)S(1)}, bf16[120]{0:T(256)(128)(2,1)}, u32[]{:S(2)}) copy-start(bf16[120]{0:T(256)(128)(2,1)} %param.20) | copy-start | bytes 724
  75.2 19.2 %copy-start.32 = (bf16[120]{0:T(256)(128)(2,1)S(1)}, bf16[120]{0:T(256)(128)(2,1)}, u32[]{:S(2)}) copy-start(bf16[120]{0:T(256)(128)(2,1)} %param.24) | copy-start | bytes 724
  75.2 31.4 %copy-start.28 = (bf16[240,40]{0,1:T(8,128)(2,1)S(1)}, bf16[240,40]{0,1:T(8,128)(2,1)}, u32[]{:S(2)}) copy-start(bf16[240,40]{0,1:T(8,128)(2,1)} %param.17) | copy-start | bytes 57604
  75.2 44.9 %copy-start.29 = (bf16[240,40]{0,1:T(8,128)(2,1)S(1)}, bf16[240,40]{0,1:T(8,128)(2,1)}, u32[]{:S(2)}) copy-start(bf16[240,40]{0,1:T(8,128)(2,1)} %param.18) | copy-start | bytes 57604
  75.2 58.3 %copy-start.33 = (s32[1,128]{1,0:T(1,128)S(1)}, s32[1,128]{1,0:T(1,128)}, u32[]{:S(2)}) copy-start(s32[1,128]{1,0:T(1,128)} %param.15) | copy-start | bytes 1540
  75.2 58.5 %copy-start = (bf16[1,128,960]{1,2,0:T(8,128)(2,1)S(1)}, bf16[1,128,960]{1,2,0:T(8,128)(2,1)}, u32[]{:S(2)}) copy-start(bf16[1,128,960]{1,2,0:T(8,128)(2,1)} %param.13) | copy-start | bytes 737284
  76.7 135.7 %all-gather.18.cloned.1.call-start = ((), (), s32[]{:S(2)}) async-start(), calls=%async_computation.4 | async-start | bytes 5529600 | tf_op jit(solution)/shard_map/all_gather | solution.py:227
  92.8 65.7 %copy-start.30 = (s32[1,128]{1,0:T(1,128)S(1)}, s32[1,128]{1,0:T(1,128)}, u32[]{:S(2)}) copy-start(s32[1,128]{1,0:T(1,128)} %param.14) | copy-start | bytes 1540
  92.8 877.3 %all-reduce.16.cloned.1.call-start = ((), (), s32[]{:S(2)}) async-start(), calls=%async_computation.5 | async-start | bytes 78643200
  133.7 27.8 %copy-start.19 = (f32[128,64]{0,1:T(8,128)}, f32[128,64]{0,1:T(8,128)S(1)}, u32[]{:S(2)}) copy-start(f32[128,64]{0,1:T(8,128)S(1)} %pad_maximum_fusion.2) | copy-start | bytes 98308
  146.6 11.4 %copy-start.10 = (bf16[960,320]{0,1:T(8,128)(2,1)}, bf16[960,320]{0,1:T(8,128)(2,1)S(1)}, u32[]{:S(2)}) copy-start(bf16[960,320]{0,1:T(8,128)(2,1)S(1)} %all_gather.50) | copy-start | bytes 1843204
  158.4 4.4 copy-start.25
  159.1 2.6 copy-start.21
  161.6 0.7 copy-start.16
  163.1 3.0 copy-start.17
  166.3 5.6 copy-start.4
  171.9 45.2 %slice-start = ((s8[5242880]{0:T(1024)(128)(4,1)}), s8[1048576]{0:T(1024)(128)(4,1)S(1)}, s32[]{:S(2)}) async-start(s8[5242880]{0:T(1024)(128)(4,1)} %bitcast.273), calls=%async_computation.6 | async-start | bytes 2097152
  212.4 4.7 slice-start.1
  217.0 2.2 copy-start.7
  217.0 2.2 copy-start.9
  217.1 2.9 copy-start.3
  220.0 1.9 copy-start.11
  220.0 2.2 copy-start.2
  222.0 1.7 copy-start.26
  222.2 2.8 copy-start.12
  222.2 2.8 copy-start.27
  222.2 3.1 copy-start.20
  225.4 5.6 copy-start.5
  231.0 6.7 copy-start.8
  243.2 6.1 copy-start.14
  249.3 1.5 copy-start.1
  273.1 5.3 copy-start.13
  273.1 5.3 copy-start.18
  281.3 5.3 copy-start.6
  389.8 42.2 %copy-start.15 = (f32[128,2560]{1,0:T(8,128)S(1)}, f32[128,2560]{1,0:T(8,128)}, u32[]{:S(2)}) copy-start(f32[128,2560]{1,0:T(8,128)} %fusion.78) | copy-start | bytes 3932164
Sparse Core Ops, SparseCore 0:
  23.1 28.3 all-gather.9
  53.9 27.3 all-gather.11
  83.2 41.1 all-gather.13
  126.1 44.7 all-gather.15
  172.6 39.6 all-gather.17
  389.9 580.1 all-reduce.15
where the time goes:
time: 1000 us; the launch traced here: 994 us
  waiting for transfers between devices  567 us (57%)
  blocking collectives  184 us (18%)
  local copies, waits for them, and re-layouts  158 us (16%)
  matrix products  64 us (6%)
  between operations  15.8 us (2%)
    unnamed x7, waiting for transfers between devices  533 us
    unnamed x2, blocking collectives  53.4 us
    reshape x7, local copies, waits for them, and re-layouts, owner_blocks(): shaped.transpose(2, 0, 1, 3)  51.9 us
    transpose x7, local copies, waits for them, and re-layouts, owner_blocks(): shaped.transpose(2, 0, 1, 3)  47.8 us
    all_gather x1, waiting for transfers between devices, local(): lax.all_gather(feed_rows[2], 'dp', axis=1, tiled=True)  34.2 us
    reshape x2, local copies, waits for them, and re-layouts, owner_blocks(): gradient.reshape(fsdp_count, row_count // fsdp_count, dp_count, column_co...  28.7 us
    unnamed x92, local copies, waits for them, and re-layouts  21.1 us
    dot_general x7, matrix products, contract_first(): lax.dot_general(left, right, (((0,), (0,)), ((), ())), preferred_element_...  20.5 us
  transfers between devices with their start and end apart: 6, of which 2 were waited for; matrix products, arithmetic and copies ran while one was open for 3% of the time, Pallas kernels for 0%

commit v1 on v0

v1 whole, which is shorter than its diff:
```python
import jax
import jax.numpy as jnp
from jax import lax
from jax.sharding import PartitionSpec as P

HEADS = 15
KV_HEADS = 5
HD = 64
GROUP = HEADS // KV_HEADS


EPS = 1e-05
THETA = 100000.0
NEGATIVE = -1e30
F32 = jnp.float32
BF16 = jnp.bfloat16


def rotary_tables(position, head_dim):
    inverse = THETA ** (-jnp.arange(0, head_dim, 2).astype(F32) / head_dim)
    angles = position.astype(F32)[:, None] * inverse[None, :]
    cosines = jnp.cos(angles)
    sine_values = jnp.sin(angles)
    return (
        jnp.concatenate([cosines, cosines], -1),
        jnp.concatenate([sine_values, sine_values], -1),
    )


def rotate(values, cosines, sine_values):
    half_dim = values.shape[-1] // 2
    turned = jnp.concatenate([-values[..., half_dim:], values[..., :half_dim]], -1)
    return values * cosines[:, None, :] + turned * sine_values[:, None, :]


def rotate_back(gradient, cosines, sine_values):
    half_dim = gradient.shape[-1] // 2
    sine_scaled = gradient * sine_values[:, None, :]
    turned = jnp.concatenate([-sine_scaled[..., half_dim:], sine_scaled[..., :half_dim]], -1)
    return gradient * cosines[:, None, :] - turned


def row_scale_of(values):
    return lax.rsqrt(jnp.mean(values * values, -1, keepdims=True) + EPS)


def norm_backward(values, row_scale, gain, upstream):
    unit_rows = values * row_scale
    scaled = upstream * gain
    gain_grad = jnp.sum(upstream * unit_rows, 0)
    result = row_scale * (scaled - unit_rows * jnp.mean(scaled * unit_rows, -1, keepdims=True))
    return (result, gain_grad)


def dot(left, right):
    return jnp.dot(left, right, preferred_element_type=F32)


def contract_first(left, right):
    return lax.dot_general(left, right, (((0,), (0,)), ((), ())), preferred_element_type=F32)


def contract_last(left, right):
    return lax.dot_general(left, right, (((1,), (1,)), ((), ())), preferred_element_type=F32)


def send(values, axis, distance):
    count = lax.axis_size(axis)
    return lax.ppermute(values, axis, [(i, i ^ distance) for i in range(count)])


def pick(blocks, index):
    return lax.dynamic_index_in_dim(blocks, index, 0, keepdims=False)


def reorder(blocks, me):
    return jnp.stack([pick(blocks, me ^ s) for s in range(blocks.shape[0])])


def plane_gather(values):
    count = lax.axis_size("dp")
    if count != 8:
        return reorder(lax.all_gather(values, "dp"), lax.axis_index("dp"))
    slots = [values, send(values, "dp", 1)] + [None] * 6
    for s in (2, 4, 6):
        slots[s] = send(values, "dp", s)
        slots[s + 1] = send(slots[s], "dp", 1)
    return jnp.stack(slots)


def plane_exchange(blocks):
    count = lax.axis_size("dp")
    if count != 8:
        me = lax.axis_index("dp")
        return reorder(lax.all_to_all(reorder(blocks, me), "dp", 0, 0), me)
    return jnp.stack([blocks[0]] + [send(blocks[s], "dp", s) for s in range(1, 8)])


def plane_sum(blocks):
    count = lax.axis_size("dp")
    if count != 8:
        return jnp.sum(plane_exchange(blocks.astype(BF16)).astype(F32), 0)
    odd = send(jnp.stack([blocks[s] for s in (1, 3, 5, 7)]).astype(BF16), "dp", 1)
    pair = [blocks[2 * i] + odd[i].astype(F32) for i in range(4)]
    total = pair[0]
    for i in range(1, 4):
        total = total + send(pair[i].astype(BF16), "dp", 2 * i).astype(F32)
    return total


def line_gather(values):
    me = lax.axis_index("fsdp")
    count = lax.axis_size("fsdp")
    out = jnp.zeros((count,) + values.shape, values.dtype)
    out = lax.dynamic_update_index_in_dim(out, values, me, 0)
    for s in range(1, count):
        out = lax.dynamic_update_index_in_dim(out, send(values, "fsdp", s), me ^ s, 0)
    return out


def line_sum(blocks):
    me = lax.axis_index("fsdp")
    total = pick(blocks, me)
    for s in range(1, lax.axis_size("fsdp")):
        total = total + send(pick(blocks, me ^ s).astype(BF16), "fsdp", s).astype(F32)
    return total


def down_routes(dp_count, fsdp_count):
    ratio = dp_count // fsdp_count
    routes = []
    for m in range(ratio):
        pairs = []
        for d in range(dp_count):
            for f in range(fsdp_count):
                target = (ratio * f + (m + d) % ratio) * fsdp_count + d // ratio
                pairs.append((d * fsdp_count + f, target))
        routes.append(pairs)
    return routes


def down_pieces(down_turned, dp_count, fsdp_count):
    ratio = dp_count // fsdp_count
    d = lax.axis_index("dp")
    width = down_turned.shape[1] // ratio
    halves = jnp.stack([down_turned[:, h * width : (h + 1) * width] for h in range(ratio)])
    got = [
        lax.ppermute(pick(halves, (m + d) % ratio), ("dp", "fsdp"), pairs)
        for m, pairs in enumerate(down_routes(dp_count, fsdp_count))
    ]
    stacked = jnp.stack(got)
    ordered = [pick(stacked, (d - j) % ratio) for j in range(ratio)]
    return jnp.concatenate(ordered, 0)


def down_return(grad_turned, dp_count, fsdp_count):
    ratio = dp_count // fsdp_count
    d = lax.axis_index("dp")
    height = grad_turned.shape[0] // ratio
    pieces = grad_turned.reshape(ratio, height, grad_turned.shape[1])
    got = []
    for m, pairs in enumerate(down_routes(dp_count, fsdp_count)):
        back = [(target, source) for source, target in pairs]
        got.append(lax.ppermute(pick(pieces, (d - m) % ratio), ("dp", "fsdp"), back))
    stacked = jnp.stack(got)
    return jnp.concatenate([pick(stacked, (h - d) % ratio) for h in range(ratio)], 1)


def masked_scores(query_turned, key_turned, segment):
    length = query_turned.shape[0]
    grouped = query_turned.reshape(length, KV_HEADS, GROUP, HD)
    scores = jnp.einsum("qkgd,tkd->kgqt", grouped, key_turned, preferred_element_type=F32)
    index = jnp.arange(length)
    allowed = (segment[:, None] == segment[None, :]) & (index[:, None] >= index[None, :])
    return jnp.where(allowed, scores * HD ** (-0.5), NEGATIVE)


def attend_forward(query_turned, key_turned, value_rounded, segment):
    length = query_turned.shape[0]
    scores = masked_scores(query_turned, key_turned, segment)
    row_max = jnp.max(scores, -1, keepdims=True)
    exponentials = jnp.exp(scores - row_max)
    totals = jnp.sum(exponentials, -1, keepdims=True)
    probs_rounded = (exponentials / totals).astype(BF16)
    attended = jnp.einsum("kgqt,tkd->qkgd", probs_rounded, value_rounded, preferred_element_type=F32)
    return (attended.reshape(length, HEADS * HD).astype(BF16), row_max + jnp.log(totals))


def attend_backward(query_turned, key_turned, value_rounded, segment, log_totals, attended_grad):
    length = query_turned.shape[0]
    grouped = query_turned.reshape(length, KV_HEADS, GROUP, HD)
    grad_grouped = attended_grad.reshape(length, KV_HEADS, GROUP, HD)
    scores = masked_scores(query_turned, key_turned, segment)
    probs_again = jnp.exp(scores - log_totals)
    value_sum = jnp.einsum(
        "kgqt,qkgd->tkd", probs_again.astype(BF16), grad_grouped, preferred_element_type=F32
    )
    prob_grad = jnp.einsum(
        "qkgd,tkd->kgqt", grad_grouped, value_rounded, preferred_element_type=F32
    )
    inner_rows = jnp.sum(probs_again * prob_grad, -1, keepdims=True)
    score_grad = (probs_again * (prob_grad - inner_rows) * HD ** (-0.5)).astype(BF16)
    query_part = jnp.einsum("kgqt,tkd->qkgd", score_grad, key_turned, preferred_element_type=F32)
    key_sum = jnp.einsum("kgqt,qkgd->tkd", score_grad, grouped, preferred_element_type=F32)
    return (query_part.reshape(length, HEADS, HD), key_sum, value_sum)


def local(
    hidden_in,
    segment_ids,
    positions,
    query_weight,
    key_weight,
    value_weight,
    output_weight,
    attention_gain,
    gate_weight,
    up_weight,
    down_weight,
    feedforward_gain,
    output_cotangent,
):
    hidden = hidden_in[0]
    hidden_rows = hidden.astype(F32)
    segment = segment_ids[0]
    cotangent = output_cotangent[0]
    length, features = hidden.shape
    width = HEADS * HD
    kv_width = KV_HEADS * HD
    dp_count = lax.axis_size("dp")
    fsdp_count = lax.axis_size("fsdp")
    d = lax.axis_index("dp")
    f = lax.axis_index("fsdp")
    q_cols = width // dp_count
    kv_cols = kv_width // dp_count
    x_cols = features // dp_count
    own_rows = features // fsdp_count
    qkv_cols = q_cols + 2 * kv_cols
    all_cols = qkv_cols + x_cols
    hidden_units = gate_weight.shape[1]

    attention_block = jnp.concatenate(
        [query_weight, key_weight, value_weight, output_weight], 1
    )
    attention_rows = line_gather(attention_block).reshape(features, all_cols)
    gains = jnp.concatenate(
        [attention_gain, feedforward_gain, jnp.zeros((all_cols - 2 * x_cols,), BF16)]
    )
    gains = jnp.concatenate([gains[None], jnp.zeros((15, all_cols), BF16)])
    slots = plane_gather(jnp.concatenate([attention_rows, gains], 0))
    gains_ordered = reorder(slots[:, features, :], d)
    attention_gain_full = gains_ordered[:, :x_cols].reshape(features).astype(F32)
    feed_gain_full = gains_ordered[:, x_cols : 2 * x_cols].reshape(features).astype(F32)
    qkv_slots = slots[:, :features, :qkv_cols]
    output_slots = slots[:, :features, qkv_cols:]

    down_block = down_pieces(down_weight.T, dp_count, fsdp_count)
    feed_block = jnp.concatenate([gate_weight, up_weight, down_block], 1)
    feed = line_gather(feed_block).reshape(features, 3 * hidden_units)

    tokens = plane_gather(jnp.stack([hidden, cotangent]))
    hidden_all = tokens[:, 0].reshape(dp_count * length, features)
    cotangent_all = tokens[:, 1].reshape(dp_count * length, features)

    scale_one = row_scale_of(hidden_rows)
    normed_one = (hidden_rows * scale_one * attention_gain_full).astype(BF16)
    cosines, sine_values = rotary_tables(positions[0], HD)
    qkv = reorder(jnp.einsum("td,sdc->stc", normed_one, qkv_slots, preferred_element_type=F32), d)

    def columns(start, count):
        part = qkv[:, :, start : start + count]
        return part.transpose(1, 0, 2).reshape(length, dp_count * count)

    query_proj = columns(0, q_cols).reshape(length, HEADS, HD)
    key_proj = columns(q_cols, kv_cols).reshape(length, KV_HEADS, HD)
    value_proj = columns(q_cols + kv_cols, kv_cols).reshape(length, KV_HEADS, HD)
    query_turned = rotate(query_proj, cosines, sine_values).astype(BF16)
    key_turned = rotate(key_proj, cosines, sine_values).astype(BF16)
    value_rounded = value_proj.astype(BF16)
    attended, log_totals = attend_forward(query_turned, key_turned, value_rounded, segment)
    added = reorder(jnp.einsum("td,sdc->stc", attended, output_slots, preferred_element_type=F32), d)
    residual = hidden_rows + added.transpose(1, 0, 2).reshape(length, features)

    scale_two = row_scale_of(residual)
    normed_two = (residual * scale_two * feed_gain_full).astype(BF16)
    normed_two_all = plane_gather(normed_two).reshape(dp_count * length, features)
    gate_up = feed[:, : 2 * hidden_units]
    down_turned = feed[:, 2 * hidden_units :]
    both = dot(normed_two_all, gate_up)
    gate_proj = both[:, :hidden_units]
    up_proj = both[:, hidden_units:]
    mixed_grad = dot(cotangent_all, down_turned)
    sigmoid_gate = jax.nn.sigmoid(gate_proj)
    silu_gate = gate_proj * sigmoid_gate
    mixed = (silu_gate * up_proj).astype(BF16)
    gate_delta = (
        mixed_grad * up_proj * sigmoid_gate * (1.0 + gate_proj * (1.0 - sigmoid_gate))
    ).astype(BF16)
    up_delta = (mixed_grad * silu_gate).astype(BF16)
    deltas = jnp.concatenate([gate_delta, up_delta], 1)
    normed_two_grad = plane_sum(
        contract_last(deltas, gate_up).reshape(dp_count, length, features)
    )
    gate_up_grad = contract_first(normed_two_all, deltas)
    down_grad = contract_first(cotangent_all, mixed)
    feed_grad = jnp.concatenate([gate_up_grad, down_grad], 1).reshape(
        fsdp_count, own_rows, 3 * hidden_units
    )
    fed = plane_sum(contract_last(mixed, down_turned).reshape(dp_count, length, features))
    block_output = (residual + fed).astype(BF16)
    attended_all = plane_gather(attended).reshape(dp_count * length, width)

    residual_part, feed_gain_grad = norm_backward(
        residual, scale_two, feed_gain_full, normed_two_grad
    )
    residual_grad = cotangent.astype(F32) + residual_part
    feed_sum = line_sum(feed_grad)

    residual_rounded = residual_grad.astype(BF16)
    residual_blocks = residual_rounded.reshape(length, dp_count, x_cols).transpose(1, 0, 2)
    residual_slots = reorder(residual_blocks, d)
    attended_grad = jnp.einsum(
        "stc,sdc->td", residual_slots, output_slots, preferred_element_type=F32
    ).astype(BF16)
    query_raw, key_raw, value_raw = attend_backward(
        query_turned, key_turned, value_rounded, segment, log_totals, attended_grad
    )
    query_delta = rotate_back(query_raw, cosines, sine_values).astype(BF16)
    key_delta = rotate_back(key_raw, cosines, sine_values).astype(BF16)
    value_delta = value_raw.astype(BF16)
    qkv_delta = jnp.concatenate(
        [
            part.reshape(length, dp_count, -1).transpose(1, 0, 2)
            for part in (query_delta, key_delta, value_delta)
        ],
        2,
    )
    delta_slots = reorder(qkv_delta, d)
    normed_one_grad = jnp.einsum(
        "stc,sdc->td", delta_slots, qkv_slots, preferred_element_type=F32
    )
    input_part, attention_gain_grad = norm_backward(
        hidden_rows, scale_one, attention_gain_full, normed_one_grad
    )
    input_grad = residual_grad + input_part

    gain_rows = jnp.concatenate(
        [
            feed_gain_grad.reshape(dp_count, 1, x_cols),
            attention_gain_grad.reshape(dp_count, 1, x_cols),
            jnp.zeros((dp_count, 1, all_cols - 2 * x_cols), F32),
        ],
        2,
    ).astype(BF16)
    gain_rows = jnp.pad(reorder(gain_rows, d), ((0, 0), (0, 15), (0, 0)))
    outgoing = jnp.concatenate(
        [jnp.concatenate([delta_slots, residual_slots], 2), gain_rows], 1
    )
    arrived = plane_exchange(outgoing)
    deltas_all = arrived[:, :length].reshape(dp_count * length, all_cols)
    gain_sums = jnp.sum(arrived[:, length].astype(F32), 0)
    hidden_all_rows = hidden_all.astype(F32)
    normed_one_all = (
        hidden_all_rows * row_scale_of(hidden_all_rows) * attention_gain_full
    ).astype(BF16)
    qkv_grad = contract_first(normed_one_all, deltas_all[:, :qkv_cols])
    output_grad = contract_first(attended_all, deltas_all[:, qkv_cols:])
    attention_grad = jnp.concatenate([qkv_grad, output_grad], 1).reshape(
        fsdp_count, own_rows, all_cols
    )
    gain_block = jnp.broadcast_to(
        jnp.pad(gain_sums[None], ((0, 15), (0, 0)))[None], (fsdp_count, 16, all_cols)
    )
    attention_sum = line_sum(jnp.concatenate([attention_grad, gain_block], 1))
    down_out = down_return(feed_sum[:, 2 * hidden_units :], dp_count, fsdp_count).T

    ends = (q_cols, q_cols + kv_cols, qkv_cols)
    return (
        block_output[None],
        input_grad[None],
        attention_sum[:own_rows, : ends[0]],
        attention_sum[:own_rows, ends[0] : ends[1]],
        attention_sum[:own_rows, ends[1] : ends[2]],
        attention_sum[:own_rows, ends[2] :],
        attention_sum[own_rows, x_cols : 2 * x_cols],
        feed_sum[:, :hidden_units],
        feed_sum[:, hidden_units : 2 * hidden_units],
        down_out,
        attention_sum[own_rows, :x_cols],
    )


def solution(mesh):
    in_specs = (
        P(("dp", "fsdp"), None, None),
        P(("dp", "fsdp"), None),
        P(("dp", "fsdp"), None),
        P("fsdp", "dp"),
        P("fsdp", "dp"),
        P("fsdp", "dp"),
        P("fsdp", "dp"),
        P("dp"),
        P("fsdp", "dp"),
        P("fsdp", "dp"),
        P("fsdp", "dp"),
        P("dp"),
        P(("dp", "fsdp"), None, None),
    )
    out_specs = (
        P(("dp", "fsdp"), None, None),
        P(("dp", "fsdp"), None, None),
        P("fsdp", "dp"),
        P("fsdp", "dp"),
        P("fsdp", "dp"),
        P("fsdp", "dp"),
        P("dp"),
        P("fsdp", "dp"),
        P("fsdp", "dp"),
        P("fsdp", "dp"),
        P("dp"),
    )
    return jax.shard_map(local, mesh=mesh, in_specs=in_specs, out_specs=out_specs, check_vma=False)
```

time: 1000 us -> 388 us (0.39)
  waiting for transfers between devices: 567 us -> 172 us
  blocking collectives: 184 us -> 0 us
  local copies, waits for them, and re-layouts: 158 us -> 83.4 us
  starting transfers between devices: 0.25 us -> 59.3 us
  matrix products: 64 us -> 34.4 us
  other arithmetic: 4.93 us -> 29 us
  between operations: 15.8 us -> 2.88 us
    unnamed x7 -> x0, waiting for transfers between devices: 533 us -> none
    ppermute x0 -> x59, waiting for transfers between devices: none -> 172 us  [the longest x55 160 us: send(): return lax.ppermute(values, axis, [(i, i ^ distance) for i in range(count)])]
    all_gather x9 -> x0, blocking collectives: 130 us -> none  [the longest x1 17.4 us: local(): lax.all_gather(up_weight, 'fsdp', axis=0, tiled=True)]
    reshape x17 -> x4, local copies, waits for them, and re-layouts: 83.5 us -> 2.86 us  [the longest x1 2.08 us: local(): attention_rows = line_gather(attention_block).reshape(features, all_cols)]
    ppermute x0 -> x59, starting transfers between devices: none -> 59.3 us  [the longest x55 52.8 us: send(): return lax.ppermute(values, axis, [(i, i ^ distance) for i in range(count)])]
    unnamed x2 -> x0, blocking collectives: 53.4 us -> none
    transpose x7 -> x0, local copies, waits for them, and re-layouts: 47.8 us -> none  [owner_blocks(): shaped.transpose(2, 0, 1, 3)]
    all_gather x5 -> x0, waiting for transfers between devices: 34.3 us -> none  [the longest x1 34.2 us: local(): lax.all_gather(feed_rows[2], 'dp', axis=1, tiled=True)]
  transfers between devices with their start and end apart: 6 -> 59, of which waited for: 2 -> 24; matrix products, arithmetic and copies ran while one was open for 3% -> 27% of each run, Pallas kernels for 0% -> 0%
where the time goes in v1:
time: 388 us; the launch traced here: 381 us
  waiting for transfers between devices  172 us (44%)
  local copies, waits for them, and re-layouts  83.4 us (21%)
  starting transfers between devices  59.3 us (15%)
  matrix products  34.4 us (9%)
  other arithmetic  29 us (7%)
    ppermute x55, waiting for transfers between devices, send(): return lax.ppermute(values, axis, [(i, i ^ distance) for i in range(count)])  160 us
    ppermute x55, starting transfers between devices, send(): return lax.ppermute(values, axis, [(i, i ^ distance) for i in range(count)])  52.8 us
    dynamic_update_slice x6, local copies, waits for them, and re-layouts, line_gather(): lax.dynamic_update_index_in_dim(out, send(values, 'fsdp', s), me ^ s, 0)  24.8 us
    unnamed x161, local copies, waits for them, and re-layouts  24.2 us
    ppermute x2, waiting for transfers between devices, down_return(): lax.ppermute(pick(pieces, (d - m) % ratio), ('dp', 'fsdp'), back)  11.8 us
    dot_general x2, matrix products, contract_last(): lax.dot_general(left, right, (((1,), (1,)), ((), ())), preferred_element_...  8.04 us
  transfers between devices with their start and end apart: 59, of which 24 were waited for; matrix products, arithmetic and copies ran while one was open for 27% of the time, Pallas kernels for 0%

profile of v1, /device:TPU:8, one launch (start us, length us, event | category | flops | bytes accessed | tf_op | source)
XLA Modules:
  0.0 380.7 jit_solution(8319949623221418451)
XLA Ops:
  3.6 3.0 collective-permute-start.1
  8.2 4.2 %collective-permute-start.17 = (bf16[120,320]{1,0:T(8,128)(2,1)S(1)}, bf16[120,320]{1,0:T(8,128)(2,1)S(1)}, u32[]{:S(2)}, u32[]{:S(2)}) collective-permute-start(bf16[120,320]{1,0:T(8,128)(2,1)S(1)} %get-tuple-element.131), channel_id=1, source_target_pairs={{0,0},{1,8},{2,16},{3,24},{4,4},{5,12},{6,20},{7,28},{8,1},{9,9},{... | collective-permute-start | bytes 230408 | tf_op jit(solution)/shard_map/ppermute | solution.py:148
  17.5 7.6 %dynamic_update_slice.26 = bf16[4,240,320]{1,0,2:T(4,128)(2,1)} dynamic-update-slice(bf16[4,240,320]{1,0,2:T(4,128)(2,1)} %broadcast_in_dim.96, bf16[1,240,320]{1,0,2:T(2,128)(2,1)S(1)} %copy.117, s32[]{:T(128)S(6)} %select_n.152, s32[]{:T(128)} %constant.250.clone.1, s32[]{:T(128)} %constant.250.clone.1) | dynamic-update-slice | bytes 307204 | tf_op jit(solution)/shard_map/jit(dynamic_update_index_in_dim)/dynamic_update_slice | solution.py:115
  26.5 6.8 %collective-permute-start.20 = (bf16[240,960]{1,0:T(8,128)(2,1)}, bf16[240,960]{1,0:T(8,128)(2,1)}, u32[]{:S(2)}, u32[]{:S(2)}) collective-permute-start(bf16[240,960]{1,0:T(8,128)(2,1)} %get-tuple-element.69), channel_id=1, source_target_pairs={{0,2},{1,3},{2,0},{3,1},{4,6},{5,7},{6,4},{7,5},{8,10},{9,11},{10,... | collective-permute-start | bytes 1382408 | tf_op jit(solution)/shard_map/ppermute | solution.py:69
  37.5 7.6 %dynamic_update_slice.27 = bf16[4,240,320]{1,0,2:T(4,128)(2,1)} dynamic-update-slice(bf16[4,240,320]{1,0,2:T(4,128)(2,1)} %dynamic_update_slice.26, bf16[1,240,320]{1,0,2:T(2,128)(2,1)S(1)} %copy.118, s32[]{:T(128)S(6)} %select_n.153, s32[]{:T(128)} %constant.250.clone.1, s32[]{:T(128)} %constant.250.clone.1) | dynamic-update-slice | bytes 307204 | tf_op jit(solution)/shard_map/jit(dynamic_update_index_in_dim)/dynamic_update_slice | solution.py:117
  45.0 7.6 %dynamic_update_slice.28 = bf16[4,240,320]{1,0,2:T(4,128)(2,1)} dynamic-update-slice(bf16[4,240,320]{1,0,2:T(4,128)(2,1)} %dynamic_update_slice.27, bf16[1,240,320]{1,0,2:T(2,128)(2,1)S(1)} %copy.119, s32[]{:T(128)S(6)} %select_n.154, s32[]{:T(128)} %constant.250.clone.1, s32[]{:T(128)} %constant.250.clone.1) | dynamic-update-slice | bytes 307204 | tf_op jit(solution)/shard_map/jit(dynamic_update_index_in_dim)/dynamic_update_slice | solution.py:117
  52.6 7.6 %dynamic_update_slice.29 = bf16[4,240,320]{1,0,2:T(4,128)(2,1)} dynamic-update-slice(bf16[4,240,320]{1,0,2:T(4,128)(2,1)} %dynamic_update_slice.28, bf16[1,240,320]{1,0,2:T(2,128)(2,1)S(1)} %copy.120, s32[]{:T(128)S(6)} %select_n.155, s32[]{:T(128)} %constant.250.clone.1, s32[]{:T(128)} %constant.250.clone.1) | dynamic-update-slice | bytes 307204 | tf_op jit(solution)/shard_map/jit(dynamic_update_index_in_dim)/dynamic_update_slice | solution.py:117
  60.1 2.1 reshape.324
  63.6 3.4 collective-permute-start.4
  71.2 11.4 %collective-permute-done.4 = bf16[976,320]{0,1:T(8,128)(2,1)S(1)} collective-permute-done((bf16[976,320]{0,1:T(8,128)(2,1)}, bf16[976,320]{0,1:T(8,128)(2,1)S(1)}, u32[]{:S(2)}, u32[]{:S(2)}) %collective-permute-start.4) | collective-permute-done | bytes 624672 | tf_op jit(solution)/shard_map/ppermute | solution.py:69
  82.7 8.2 %collective-permute-done.21 = bf16[240,960]{1,0:T(8,128)(2,1)S(1)} collective-permute-done((bf16[240,960]{1,0:T(8,128)(2,1)}, bf16[240,960]{1,0:T(8,128)(2,1)S(1)}, u32[]{:S(2)}, u32[]{:S(2)}) %collective-permute-start.21) | collective-permute-done | bytes 460832 | tf_op jit(solution)/shard_map/ppermute | solution.py:69
  90.9 7.7 %collective-permute-done.6 = bf16[976,320]{0,1:T(8,128)(2,1)S(1)} collective-permute-done((bf16[976,320]{0,1:T(8,128)(2,1)}, bf16[976,320]{0,1:T(8,128)(2,1)S(1)}, u32[]{:S(2)}, u32[]{:S(2)}) %collective-permute-start.6) | collective-permute-done | bytes 624672 | tf_op jit(solution)/shard_map/ppermute | solution.py:69
  107.3 3.1 fusion.5
  112.2 2.3 fusion.29
  119.3 1.5 collective-permute-start.11
  122.0 14.2 %collective-permute-done.11 = bf16[128,960]{0,1:T(8,128)(2,1)S(1)} collective-permute-done((bf16[128,960]{0,1:T(8,128)(2,1)S(1)}, bf16[128,960]{0,1:T(8,128)(2,1)S(1)}, u32[]{:S(2)}, u32[]{:S(2)}) %collective-permute-start.11) | collective-permute-done | bytes 245792 | tf_op jit(solution)/shard_map/ppermute | solution.py:69
  136.9 6.8 %collective-permute-done.45 = bf16[128,960]{0,1:T(8,128)(2,1)S(1)} collective-permute-done((bf16[128,960]{0,1:T(8,128)(2,1)S(1)}, bf16[128,960]{0,1:T(8,128)(2,1)S(1)}, u32[]{:S(2)}, u32[]{:S(2)}) %collective-permute-start.45) | collective-permute-done | bytes 245792 | tf_op jit(solution)/shard_map/ppermute | solution.py:69
  146.0 9.6 %collective-permute-done.47 = bf16[128,960]{0,1:T(8,128)(2,1)S(1)} collective-permute-done((bf16[128,960]{0,1:T(8,128)(2,1)S(1)}, bf16[128,960]{0,1:T(8,128)(2,1)S(1)}, u32[]{:S(2)}, u32[]{:S(2)}) %collective-permute-start.47) | collective-permute-done | bytes 245792 | tf_op jit(solution)/shard_map/ppermute | solution.py:69
  159.2 2.0 collective-permute-start.49
  161.3 16.2 %collective-permute-done.49 = bf16[128,960]{0,1:T(8,128)(2,1)S(1)} collective-permute-done((bf16[128,960]{0,1:T(8,128)(2,1)S(1)}, bf16[128,960]{0,1:T(8,128)(2,1)S(1)}, u32[]{:S(2)}, u32[]{:S(2)}) %collective-permute-start.49) | collective-permute-done | bytes 245792 | tf_op jit(solution)/shard_map/ppermute | solution.py:69
  178.2 8.0 %collective-permute-done.29 = bf16[2,128,960]{1,2,0:T(8,128)(2,1)S(1)} collective-permute-done((bf16[2,128,960]{1,2,0:T(8,128)(2,1)S(1)}, bf16[2,128,960]{1,2,0:T(8,128)(2,1)S(1)}, u32[]{:S(2)}, u32[]{:S(2)}) %collective-permute-start.29) | collective-permute-done | bytes 491552 | tf_op jit(solution)/shard_map/ppermute | solution.py:69
  188.2 1.6 fusion.19
  190.3 2.6 slice_convert_fusion
  194.6 1.6 multiply_convert_fusion.1
  197.4 1.7 fusion.17
  201.9 4.2 %fusion.159 = (bf16[1024,960]{0,1:T(8,128)(2,1)}, f32[1024,960]{0,1:T(8,128)}) fusion(bf16[1024,320]{0,1:T(8,128)(2,1)S(1)} %get-tuple-element.86, bf16[1024,320]{0,1:T(8,128)(2,1)S(1)} %get-tuple-element.85, bf16[960,960]{1,0:T(8,128)(2,1)S(1)} %bitcast.481), kind=kOutput, calls=%fused_computation.369 | convolution fusion | flops 1261895680 | bytes 8437760 | tf_op jit(solution)/shard_map/dot_general | solution.py:64
  206.2 3.8 fusion.162
  210.0 2.0 copy.156
  212.0 1.5 collective-permute-start.54
  213.5 2.2 copy.157
  215.7 2.3 collective-permute-start.55
  218.0 2.0 copy.158
  220.6 2.5 copy.137
  226.2 4.2 %copy.131 = f32[8,1,128,960]{2,0,3,1:T(8,128)} copy(f32[8,1,128,960]{2,3,1,0:T(8,128)S(1)} %copy-done.1) | data formatting | bytes 7864320 | tf_op jit(solution)/shard_map/convert_element_type | solution.py:362
  232.6 18.4 %collective-permute-done.55 = bf16[240,960]{0,1:T(8,128)(2,1)} collective-permute-done((bf16[240,960]{0,1:T(8,128)(2,1)}, bf16[240,960]{0,1:T(8,128)(2,1)}, u32[]{:S(2)}, u32[]{:S(2)}) %collective-permute-start.55) | collective-permute-done | bytes 460832 | tf_op jit(solution)/shard_map/ppermute | solution.py:69
  251.0 19.2 %collective-permute-done.56 = bf16[240,960]{0,1:T(8,128)(2,1)} collective-permute-done((bf16[240,960]{0,1:T(8,128)(2,1)}, bf16[240,960]{0,1:T(8,128)(2,1)}, u32[]{:S(2)}, u32[]{:S(2)}) %collective-permute-start.56) | collective-permute-done | bytes 460832 | tf_op jit(solution)/shard_map/ppermute | solution.py:69
  270.2 1.5 fusion.53
  273.2 2.2 collective-permute-start.57
  275.6 11.8 %collective-permute-done.57 = f32[120,320]{1,0:T(8,128)S(1)} collective-permute-done((f32[120,320]{1,0:T(8,128)S(1)}, f32[120,320]{1,0:T(8,128)S(1)}, u32[]{:S(2)}, u32[]{:S(2)}) %collective-permute-start.57) | collective-permute-done | bytes 153632 | tf_op jit(solution)/shard_map/ppermute | solution.py:164
  288.3 1.8 fusion.68
  290.2 3.8 %collective-permute-start.35 = (bf16[128,960]{0,1:T(8,128)(2,1)S(1)}, bf16[128,960]{0,1:T(8,128)(2,1)S(1)}, u32[]{:S(2)}, u32[]{:S(2)}) collective-permute-start(bf16[128,960]{0,1:T(8,128)(2,1)S(1)} %get-tuple-element.76), channel_id=1, source_target_pairs={{0,16},{4,20},{8,24},{12,28},{16,0},{20,4},{24,8},{28,12},{1,17},{... | collective-permute-start | bytes 737288 | tf_op jit(solution)/shard_map/ppermute | solution.py:69
  295.4 2.5 fusion.74
  298.5 1.5 collective-permute-start.24
  300.0 2.1 collective-permute-start.25
  302.1 3.5 collective-permute-done.35
  305.6 1.9 collective-permute-done.36
  307.5 1.5 multiply_reduce_fusion.2
  309.5 2.5 fusion.45
  313.3 2.0 fusion.58
  315.3 2.0 broadcast_multiply_fusion
  318.9 4.1 %fusion.98 = (bf16[960]{0:T(1024)(128)(2,1)S(1)}, f32[128]{0:T(128)S(1)}, f32[128,960]{0,1:T(8,128)}) fusion(bf16[1,128,960]{1,2,0:T(8,128)(2,1)S(1)} %copy-done.6, f32[128]{0:T(128)S(1)} %copy-done.42, f32[960]{0:T(1024)S(1)} %reshape.341, bf16[8,128,200]{1,2,0:T(8,128)(2,1)S(1)} %constant_dynamic-update-slice_fusion.26, ...), kind=kOutput, calls=%fused_computation.159 | convolution fusion | flops 394075072 | bytes 4430464 | tf_op jit(solution)/shard_map/stc,sdc->td/dot_general | solution.py:339
  326.6 4.7 %collective-permute-done.38 = bf16[144,320]{0,1:T(8,128)(2,1)S(1)} collective-permute-done((bf16[144,320]{0,1:T(8,128)(2,1)S(1)}, bf16[144,320]{0,1:T(8,128)(2,1)S(1)}, u32[]{:S(2)}, u32[]{:S(2)}) %collective-permute-start.38) | collective-permute-done | bytes 92192 | tf_op jit(solution)/shard_map/ppermute | solution.py:69
  331.9 1.9 collective-permute-done.39
  334.6 2.0 collective-permute-done.40
  336.6 2.0 collective-permute-start.42
  338.6 4.9 %collective-permute-done.41 = bf16[144,320]{0,1:T(8,128)(2,1)S(1)} collective-permute-done((bf16[144,320]{0,1:T(8,128)(2,1)S(1)}, bf16[144,320]{0,1:T(8,128)(2,1)S(1)}, u32[]{:S(2)}, u32[]{:S(2)}) %collective-permute-start.41) | collective-permute-done | bytes 92192 | tf_op jit(solution)/shard_map/ppermute | solution.py:69
  343.5 1.8 collective-permute-start.43
  345.4 5.2 %collective-permute-done.43 = bf16[144,320]{0,1:T(8,128)(2,1)S(1)} collective-permute-done((bf16[144,320]{0,1:T(8,128)(2,1)S(1)}, bf16[144,320]{0,1:T(8,128)(2,1)S(1)}, u32[]{:S(2)}, u32[]{:S(2)}) %collective-permute-start.43) | collective-permute-done | bytes 92192 | tf_op jit(solution)/shard_map/ppermute | solution.py:69
  351.7 1.5 copy-done
  357.1 2.9 collective-permute-start.53
  360.1 2.7 fusion.97
  362.8 1.5 collective-permute-done.51
  364.3 2.8 collective-permute-done.52
  367.0 10.2 %collective-permute-done.53 = bf16[256,320]{1,0:T(8,128)(2,1)S(1)} collective-permute-done((bf16[256,320]{1,0:T(8,128)(2,1)S(1)}, bf16[256,320]{1,0:T(8,128)(2,1)S(1)}, u32[]{:S(2)}, u32[]{:S(2)}) %collective-permute-start.53) | collective-permute-done | bytes 163872 | tf_op jit(solution)/shard_map/ppermute | solution.py:69
  (359 shorter events, 78.5 us)
Async XLA Ops:
  3.5 29.8 %collective-permute-start = (bf16[240,320]{1,0:T(8,128)(2,1)S(1)}, bf16[240,320]{1,0:T(8,128)(2,1)}, u32[]{:S(2)}, u32[]{:S(2)}) collective-permute-start(bf16[240,320]{1,0:T(8,128)(2,1)S(1)} %pad_maximum_fusion.9), channel_id=1, source_target_pairs={{0,1},{1,0},{2,3},{3,2},{4,5},{5,4},{6,7},{7,6},{8,9},{9,8},{10,11... | collective-permute-start | bytes 460808 | tf_op jit(solution)/shard_map/ppermute | solution.py:69
  3.6 30.9 %collective-permute-start.1 = (bf16[240,320]{1,0:T(8,128)(2,1)S(1)}, bf16[240,320]{1,0:T(8,128)(2,1)S(1)}, u32[]{:S(2)}, u32[]{:S(2)}) collective-permute-start(bf16[240,320]{1,0:T(8,128)(2,1)S(1)} %pad_maximum_fusion.9), channel_id=1, source_target_pairs={{0,2},{1,3},{2,0},{3,1},{4,6},{5,7},{6,4},{7,5},{8,10},{9,11},{10,... | collective-permute-start | bytes 460808 | tf_op jit(solution)/shard_map/ppermute | solution.py:69
  6.6 29.7 %collective-permute-start.2 = (bf16[240,320]{1,0:T(8,128)(2,1)S(1)}, bf16[240,320]{1,0:T(8,128)(2,1)}, u32[]{:S(2)}, u32[]{:S(2)}) collective-permute-start(bf16[240,320]{1,0:T(8,128)(2,1)S(1)} %pad_maximum_fusion.9), channel_id=1, source_target_pairs={{0,3},{1,2},{2,1},{3,0},{4,7},{5,6},{6,5},{7,4},{8,11},{9,10},{10,... | collective-permute-start | bytes 460808 | tf_op jit(solution)/shard_map/ppermute | solution.py:69
  7.0 18.0 %copy-start.5 = (bf16[1,128,960]{1,2,0:T(8,128)(2,1)S(1)}, bf16[1,128,960]{1,2,0:T(8,128)(2,1)}, u32[]{:S(2)}) copy-start(bf16[1,128,960]{1,2,0:T(8,128)(2,1)} %param.13) | copy-start | bytes 737284
  8.2 16.9 %collective-permute-start.17 = (bf16[120,320]{1,0:T(8,128)(2,1)S(1)}, bf16[120,320]{1,0:T(8,128)(2,1)S(1)}, u32[]{:S(2)}, u32[]{:S(2)}) collective-permute-start(bf16[120,320]{1,0:T(8,128)(2,1)S(1)} %get-tuple-element.131), channel_id=1, source_target_pairs={{0,0},{1,8},{2,16},{3,24},{4,4},{5,12},{6,20},{7,28},{8,1},{9,9},{... | collective-permute-start | bytes 230408 | tf_op jit(solution)/shard_map/ppermute | solution.py:148
  12.4 12.8 %collective-permute-start.18 = (bf16[120,320]{1,0:T(8,128)(2,1)S(1)}, bf16[120,320]{1,0:T(8,128)(2,1)S(1)}, u32[]{:S(2)}, u32[]{:S(2)}) collective-permute-start(bf16[120,320]{1,0:T(8,128)(2,1)S(1)} %get-tuple-element.130), channel_id=1, source_target_pairs={{0,4},{1,12},{2,20},{3,28},{4,0},{5,8},{6,16},{7,24},{8,5},{9,13},... | collective-permute-start | bytes 230408 | tf_op jit(solution)/shard_map/ppermute | solution.py:148
  26.5 40.7 %collective-permute-start.19 = (bf16[240,960]{1,0:T(8,128)(2,1)}, bf16[240,960]{1,0:T(8,128)(2,1)}, u32[]{:S(2)}, u32[]{:S(2)}) collective-permute-start(bf16[240,960]{1,0:T(8,128)(2,1)} %get-tuple-element.69), channel_id=1, source_target_pairs={{0,1},{1,0},{2,3},{3,2},{4,5},{5,4},{6,7},{7,6},{8,9},{9,8},{10,11... | collective-permute-start | bytes 1382408 | tf_op jit(solution)/shard_map/ppermute | solution.py:69
  26.5 42.8 %collective-permute-start.20 = (bf16[240,960]{1,0:T(8,128)(2,1)}, bf16[240,960]{1,0:T(8,128)(2,1)}, u32[]{:S(2)}, u32[]{:S(2)}) collective-permute-start(bf16[240,960]{1,0:T(8,128)(2,1)} %get-tuple-element.69), channel_id=1, source_target_pairs={{0,2},{1,3},{2,0},{3,1},{4,6},{5,7},{6,4},{7,5},{8,10},{9,11},{10,... | collective-permute-start | bytes 1382408 | tf_op jit(solution)/shard_map/ppermute | solution.py:69
  36.3 25.9 %copy-start.34 = (bf16[976]{0:T(1024)(128)(2,1)S(1)}, bf16[976]{0:T(1024)(128)(2,1)}, u32[]{:S(2)}) copy-start(bf16[976]{0:T(1024)(128)(2,1)} %pad.61.clone) | copy-start | bytes 5860
  63.6 19.1 %collective-permute-start.4 = (bf16[976,320]{0,1:T(8,128)(2,1)}, bf16[976,320]{0,1:T(8,128)(2,1)S(1)}, u32[]{:S(2)}, u32[]{:S(2)}) collective-permute-start(bf16[976,320]{0,1:T(8,128)(2,1)} %get-tuple-element.73), channel_id=1, source_target_pairs={{0,8},{4,12},{8,0},{12,4},{16,24},{20,28},{24,16},{28,20},{1,9},{5... | collective-permute-start | bytes 1873928 | tf_op jit(solution)/shard_map/ppermute | solution.py:69
  67.0 40.4 %copy-start.41 = (f32[128]{0:T(128)}, f32[128]{0:T(128)S(1)}, u32[]{:S(2)}) copy-start(f32[128]{0:T(128)S(1)} %add_rsqrt_fusion.1) | copy-start | bytes 1540
  67.0 23.9 %collective-permute-start.21 = (bf16[240,960]{1,0:T(8,128)(2,1)}, bf16[240,960]{1,0:T(8,128)(2,1)S(1)}, u32[]{:S(2)}, u32[]{:S(2)}) collective-permute-start(bf16[240,960]{1,0:T(8,128)(2,1)} %get-tuple-element.69), channel_id=1, source_target_pairs={{0,3},{1,2},{2,1},{3,0},{4,7},{5,6},{6,5},{7,4},{8,11},{9,10},{10,... | collective-permute-start | bytes 1382408 | tf_op jit(solution)/shard_map/ppermute | solution.py:69
  67.2 31.4 %collective-permute-start.3 = (bf16[976,320]{0,1:T(8,128)(2,1)}, bf16[976,320]{0,1:T(8,128)(2,1)S(1)}, u32[]{:S(2)}, u32[]{:S(2)}) collective-permute-start(bf16[976,320]{0,1:T(8,128)(2,1)} %get-tuple-element.73), channel_id=1, source_target_pairs={{0,4},{4,0},{8,12},{12,8},{16,20},{20,16},{24,28},{28,24},{1,5},{5... | collective-permute-start | bytes 1873928 | tf_op jit(solution)/shard_map/ppermute | solution.py:69
  67.2 31.4 %collective-permute-start.6 = (bf16[976,320]{0,1:T(8,128)(2,1)}, bf16[976,320]{0,1:T(8,128)(2,1)S(1)}, u32[]{:S(2)}, u32[]{:S(2)}) collective-permute-start(bf16[976,320]{0,1:T(8,128)(2,1)} %get-tuple-element.73), channel_id=1, source_target_pairs={{0,16},{4,20},{8,24},{12,28},{16,0},{20,4},{24,8},{28,12},{1,17},{... | collective-permute-start | bytes 1873928 | tf_op jit(solution)/shard_map/ppermute | solution.py:69
  69.3 31.1 %collective-permute-start.8 = (bf16[976,320]{0,1:T(8,128)(2,1)}, bf16[976,320]{0,1:T(8,128)(2,1)S(1)}, u32[]{:S(2)}, u32[]{:S(2)}) collective-permute-start(bf16[976,320]{0,1:T(8,128)(2,1)} %get-tuple-element.73), channel_id=1, source_target_pairs={{0,24},{4,28},{8,16},{12,20},{16,8},{20,12},{24,0},{28,4},{1,25},{... | collective-permute-start | bytes 1873928 | tf_op jit(solution)/shard_map/ppermute | solution.py:69
  82.7 18.2 %collective-permute-start.5 = (bf16[976,320]{0,1:T(8,128)(2,1)S(1)}, bf16[976,320]{0,1:T(8,128)(2,1)S(1)}, u32[]{:S(2)}, u32[]{:S(2)}) collective-permute-start(bf16[976,320]{0,1:T(8,128)(2,1)S(1)} %collective-permute-done.4), channel_id=1, source_target_pairs={{0,4},{4,0},{8,12},{12,8},{16,20},{20,16},{24,28},{28,24},{1,5},{5... | collective-permute-start | bytes 1873928 | tf_op jit(solution)/shard_map/ppermute | solution.py:69
  98.6 4.0 %collective-permute-start.7 = (bf16[976,320]{0,1:T(8,128)(2,1)S(1)}, bf16[976,320]{0,1:T(8,128)(2,1)S(1)}, u32[]{:S(2)}, u32[]{:S(2)}) collective-permute-start(bf16[976,320]{0,1:T(8,128)(2,1)S(1)} %collective-permute-done.6), channel_id=1, source_target_pairs={{0,4},{4,0},{8,12},{12,8},{16,20},{20,16},{24,28},{28,24},{1,5},{5... | collective-permute-start | bytes 1873928 | tf_op jit(solution)/shard_map/ppermute | solution.py:69
  100.4 4.1 %collective-permute-start.9 = (bf16[976,320]{0,1:T(8,128)(2,1)S(1)}, bf16[976,320]{0,1:T(8,128)(2,1)S(1)}, u32[]{:S(2)}, u32[]{:S(2)}) collective-permute-start(bf16[976,320]{0,1:T(8,128)(2,1)S(1)} %collective-permute-done.8), channel_id=1, source_target_pairs={{0,4},{4,0},{8,12},{12,8},{16,20},{20,16},{24,28},{28,24},{1,5},{5... | collective-permute-start | bytes 1873928 | tf_op jit(solution)/shard_map/ppermute | solution.py:69
  117.2 60.3 %collective-permute-start.26 = (bf16[2,128,960]{1,2,0:T(8,128)(2,1)S(1)}, bf16[2,128,960]{1,2,0:T(8,128)(2,1)S(1)}, u32[]{:S(2)}, u32[]{:S(2)}) collective-permute-start(bf16[2,128,960]{1,2,0:T(8,128)(2,1)S(1)} %constant_dynamic-update-slice_fusion.16), channel_id=1, source_target_pairs={{0,4},{4,0},{8,12},{12,8},{16,20},{20,16},{24,28},{28,24},{1,5},{5... | collective-permute-start | bytes 1474568 | tf_op jit(solution)/shard_map/ppermute | solution.py:69
  117.3 60.9 %collective-permute-start.27 = (bf16[2,128,960]{1,2,0:T(8,128)(2,1)S(1)}, bf16[2,128,960]{1,2,0:T(8,128)(2,1)S(1)}, u32[]{:S(2)}, u32[]{:S(2)}) collective-permute-start(bf16[2,128,960]{1,2,0:T(8,128)(2,1)S(1)} %constant_dynamic-update-slice_fusion.16), channel_id=1, source_target_pairs={{0,8},{4,12},{8,0},{12,4},{16,24},{20,28},{24,16},{28,20},{1,9},{5... | collective-permute-start | bytes 1474568 | tf_op jit(solution)/shard_map/ppermute | solution.py:69
  119.1 2.8 collective-permute-start.10
  119.3 16.9 %collective-permute-start.11 = (bf16[128,960]{0,1:T(8,128)(2,1)S(1)}, bf16[128,960]{0,1:T(8,128)(2,1)S(1)}, u32[]{:S(2)}, u32[]{:S(2)}) collective-permute-start(bf16[128,960]{0,1:T(8,128)(2,1)S(1)} %get-tuple-element.70), channel_id=1, source_target_pairs={{0,8},{4,12},{8,0},{12,4},{16,24},{20,28},{24,16},{28,20},{1,9},{5... | collective-permute-start | bytes 737288 | tf_op jit(solution)/shard_map/ppermute | solution.py:69
  120.8 24.1 %collective-permute-start.13 = (bf16[128,960]{0,1:T(8,128)(2,1)S(1)}, bf16[128,960]{0,1:T(8,128)(2,1)S(1)}, u32[]{:S(2)}, u32[]{:S(2)}) collective-permute-start(bf16[128,960]{0,1:T(8,128)(2,1)S(1)} %get-tuple-element.70), channel_id=1, source_target_pairs={{0,16},{4,20},{8,24},{12,28},{16,0},{20,4},{24,8},{28,12},{1,17},{... | collective-permute-start | bytes 737288 | tf_op jit(solution)/shard_map/ppermute | solution.py:69
  121.9 14.9 %collective-permute-start.44 = (bf16[128,960]{0,1:T(8,128)(2,1)S(1)}, bf16[128,960]{0,1:T(8,128)(2,1)S(1)}, u32[]{:S(2)}, u32[]{:S(2)}) collective-permute-start(bf16[128,960]{0,1:T(8,128)(2,1)S(1)} %bitcast.514), channel_id=1, source_target_pairs={{0,4},{4,0},{8,12},{12,8},{16,20},{20,16},{24,28},{28,24},{1,5},{5... | collective-permute-start | bytes 737288 | tf_op jit(solution)/shard_map/ppermute | solution.py:69
  136.2 7.5 %collective-permute-start.45 = (bf16[128,960]{0,1:T(8,128)(2,1)S(1)}, bf16[128,960]{0,1:T(8,128)(2,1)S(1)}, u32[]{:S(2)}, u32[]{:S(2)}) collective-permute-start(bf16[128,960]{0,1:T(8,128)(2,1)S(1)} %bitcast.515), channel_id=1, source_target_pairs={{0,8},{4,12},{8,0},{12,4},{16,24},{20,28},{24,16},{28,20},{1,9},{5... | collective-permute-start | bytes 737288 | tf_op jit(solution)/shard_map/ppermute | solution.py:69
  136.8 8.0 %collective-permute-start.12 = (bf16[128,960]{0,1:T(8,128)(2,1)S(1)}, bf16[128,960]{0,1:T(8,128)(2,1)S(1)}, u32[]{:S(2)}, u32[]{:S(2)}) collective-permute-start(bf16[128,960]{0,1:T(8,128)(2,1)S(1)} %collective-permute-done.11), channel_id=1, source_target_pairs={{0,4},{4,0},{8,12},{12,8},{16,20},{20,16},{24,28},{28,24},{1,5},{5... | collective-permute-start | bytes 737288 | tf_op jit(solution)/shard_map/ppermute | solution.py:69
  143.7 11.9 %collective-permute-start.47 = (bf16[128,960]{0,1:T(8,128)(2,1)S(1)}, bf16[128,960]{0,1:T(8,128)(2,1)S(1)}, u32[]{:S(2)}, u32[]{:S(2)}) collective-permute-start(bf16[128,960]{0,1:T(8,128)(2,1)S(1)} %bitcast.516), channel_id=1, source_target_pairs={{0,16},{4,20},{8,24},{12,28},{16,0},{20,4},{24,8},{28,12},{1,17},{... | collective-permute-start | bytes 737288 | tf_op jit(solution)/shard_map/ppermute | solution.py:69
  144.8 10.8 %collective-permute-start.46 = (bf16[128,960]{0,1:T(8,128)(2,1)S(1)}, bf16[128,960]{0,1:T(8,128)(2,1)S(1)}, u32[]{:S(2)}, u32[]{:S(2)}) collective-permute-start(bf16[128,960]{0,1:T(8,128)(2,1)S(1)} %collective-permute-done.45), channel_id=1, source_target_pairs={{0,4},{4,0},{8,12},{12,8},{16,20},{20,16},{24,28},{28,24},{1,5},{5... | collective-permute-start | bytes 737288 | tf_op jit(solution)/shard_map/ppermute | solution.py:69
  144.9 13.3 %collective-permute-start.15 = (bf16[128,960]{0,1:T(8,128)(2,1)S(1)}, bf16[128,960]{0,1:T(8,128)(2,1)S(1)}, u32[]{:S(2)}, u32[]{:S(2)}) collective-permute-start(bf16[128,960]{0,1:T(8,128)(2,1)S(1)} %get-tuple-element.70), channel_id=1, source_target_pairs={{0,24},{4,28},{8,16},{12,20},{16,8},{20,12},{24,0},{28,4},{1,25},{... | collective-permute-start | bytes 737288 | tf_op jit(solution)/shard_map/ppermute | solution.py:69
  155.6 1.5 collective-permute-start.14
  155.6 3.6 collective-permute-start.48
  157.1 29.1 %collective-permute-start.29 = (bf16[2,128,960]{1,2,0:T(8,128)(2,1)S(1)}, bf16[2,128,960]{1,2,0:T(8,128)(2,1)S(1)}, u32[]{:S(2)}, u32[]{:S(2)}) collective-permute-start(bf16[2,128,960]{1,2,0:T(8,128)(2,1)S(1)} %constant_dynamic-update-slice_fusion.16), channel_id=1, source_target_pairs={{0,16},{4,20},{8,24},{12,28},{16,0},{20,4},{24,8},{28,12},{1,17},{... | collective-permute-start | bytes 1474568 | tf_op jit(solution)/shard_map/ppermute | solution.py:69
  158.2 28.0 %collective-permute-start.31 = (bf16[2,128,960]{1,2,0:T(8,128)(2,1)S(1)}, bf16[2,128,960]{1,2,0:T(8,128)(2,1)S(1)}, u32[]{:S(2)}, u32[]{:S(2)}) collective-permute-start(bf16[2,128,960]{1,2,0:T(8,128)(2,1)S(1)} %constant_dynamic-update-slice_fusion.16), channel_id=1, source_target_pairs={{0,24},{4,28},{8,16},{12,20},{16,8},{20,12},{24,0},{28,4},{1,25},{... | collective-permute-start | bytes 1474568 | tf_op jit(solution)/shard_map/ppermute | solution.py:69
  159.2 18.3 %collective-permute-start.49 = (bf16[128,960]{0,1:T(8,128)(2,1)S(1)}, bf16[128,960]{0,1:T(8,128)(2,1)S(1)}, u32[]{:S(2)}, u32[]{:S(2)}) collective-permute-start(bf16[128,960]{0,1:T(8,128)(2,1)S(1)} %bitcast.517), channel_id=1, source_target_pairs={{0,24},{4,28},{8,16},{12,20},{16,8},{20,12},{24,0},{28,4},{1,25},{... | collective-permute-start | bytes 737288 | tf_op jit(solution)/shard_map/ppermute | solution.py:69
  177.5 9.3 %collective-permute-start.16 = (bf16[128,960]{0,1:T(8,128)(2,1)S(1)}, bf16[128,960]{0,1:T(8,128)(2,1)S(1)}, u32[]{:S(2)}, u32[]{:S(2)}) collective-permute-start(bf16[128,960]{0,1:T(8,128)(2,1)S(1)} %collective-permute-done.15), channel_id=1, source_target_pairs={{0,4},{4,0},{8,12},{12,8},{16,20},{20,16},{24,28},{28,24},{1,5},{5... | collective-permute-start | bytes 737288 | tf_op jit(solution)/shard_map/ppermute | solution.py:69
  177.6 9.3 %collective-permute-start.50 = (bf16[128,960]{0,1:T(8,128)(2,1)S(1)}, bf16[128,960]{0,1:T(8,128)(2,1)S(1)}, u32[]{:S(2)}, u32[]{:S(2)}) collective-permute-start(bf16[128,960]{0,1:T(8,128)(2,1)S(1)} %collective-permute-done.49), channel_id=1, source_target_pairs={{0,4},{4,0},{8,12},{12,8},{16,20},{20,16},{24,28},{28,24},{1,5},{5... | collective-permute-start | bytes 737288 | tf_op jit(solution)/shard_map/ppermute | solution.py:69
  178.1 11.7 %collective-permute-start.28 = (bf16[2,128,960]{1,2,0:T(8,128)(2,1)S(1)}, bf16[2,128,960]{1,2,0:T(8,128)(2,1)S(1)}, u32[]{:S(2)}, u32[]{:S(2)}) collective-permute-start(bf16[2,128,960]{1,2,0:T(8,128)(2,1)S(1)} %collective-permute-done.27), channel_id=1, source_target_pairs={{0,4},{4,0},{8,12},{12,8},{16,20},{20,16},{24,28},{28,24},{1,5},{5... | collective-permute-start | bytes 1474568 | tf_op jit(solution)/shard_map/ppermute | solution.py:69
  186.2 3.8 %collective-permute-start.30 = (bf16[2,128,960]{1,2,0:T(8,128)(2,1)S(1)}, bf16[2,128,960]{1,2,0:T(8,128)(2,1)S(1)}, u32[]{:S(2)}, u32[]{:S(2)}) collective-permute-start(bf16[2,128,960]{1,2,0:T(8,128)(2,1)S(1)} %collective-permute-done.29), channel_id=1, source_target_pairs={{0,4},{4,0},{8,12},{12,8},{16,20},{20,16},{24,28},{28,24},{1,5},{5... | collective-permute-start | bytes 1474568 | tf_op jit(solution)/shard_map/ppermute | solution.py:69
  186.2 4.0 %collective-permute-start.32 = (bf16[2,128,960]{1,2,0:T(8,128)(2,1)S(1)}, bf16[2,128,960]{1,2,0:T(8,128)(2,1)S(1)}, u32[]{:S(2)}, u32[]{:S(2)}) collective-permute-start(bf16[2,128,960]{1,2,0:T(8,128)(2,1)S(1)} %collective-permute-done.31), channel_id=1, source_target_pairs={{0,4},{4,0},{8,12},{12,8},{16,20},{20,16},{24,28},{28,24},{1,5},{5... | collective-permute-start | bytes 1474568 | tf_op jit(solution)/shard_map/ppermute | solution.py:69
  212.0 20.6 %collective-permute-start.54 = (bf16[240,960]{0,1:T(8,128)(2,1)}, bf16[240,960]{0,1:T(8,128)(2,1)}, u32[]{:S(2)}, u32[]{:S(2)}) collective-permute-start(bf16[240,960]{0,1:T(8,128)(2,1)} %bitcast.444), channel_id=1, source_target_pairs={{0,1},{1,0},{2,3},{3,2},{4,5},{5,4},{6,7},{7,6},{8,9},{9,8},{10,11... | collective-permute-start | bytes 1382408 | tf_op jit(solution)/shard_map/ppermute | solution.py:69
  215.7 35.3 %collective-permute-start.55 = (bf16[240,960]{0,1:T(8,128)(2,1)}, bf16[240,960]{0,1:T(8,128)(2,1)}, u32[]{:S(2)}, u32[]{:S(2)}) collective-permute-start(bf16[240,960]{0,1:T(8,128)(2,1)} %bitcast.506), channel_id=1, source_target_pairs={{0,2},{1,3},{2,0},{3,1},{4,6},{5,7},{6,4},{7,5},{8,10},{9,11},{10,... | collective-permute-start | bytes 1382408 | tf_op jit(solution)/shard_map/ppermute | solution.py:69
  220.0 50.2 %collective-permute-start.56 = (bf16[240,960]{0,1:T(8,128)(2,1)}, bf16[240,960]{0,1:T(8,128)(2,1)}, u32[]{:S(2)}, u32[]{:S(2)}) collective-permute-start(bf16[240,960]{0,1:T(8,128)(2,1)} %bitcast.507), channel_id=1, source_target_pairs={{0,3},{1,2},{2,1},{3,0},{4,7},{5,6},{6,5},{7,4},{8,11},{9,10},{10,... | collective-permute-start | bytes 1382408 | tf_op jit(solution)/shard_map/ppermute | solution.py:69
  224.3 64.0 %collective-permute-start.33 = (bf16[4,128,960]{1,2,0:T(8,128)(2,1)}, bf16[4,128,960]{1,2,0:T(8,128)(2,1)}, u32[]{:S(2)}, u32[]{:S(2)}) collective-permute-start(bf16[4,128,960]{1,2,0:T(8,128)(2,1)} %pad_maximum_fusion.4), channel_id=1, source_target_pairs={{0,4},{4,0},{8,12},{12,8},{16,20},{20,16},{24,28},{28,24},{1,5},{5... | collective-permute-start | bytes 2949128 | tf_op jit(solution)/shard_map/ppermute | solution.py:69
  230.3 39.8 %copy-start.12 = (f32[1,240,960]{1,2,0:T(8,128)S(1)}, f32[1,240,960]{1,2,0:T(8,128)}, u32[]{:S(2)}) copy-start(f32[1,240,960]{1,2,0:T(8,128)} %copy.137) | copy-start | bytes 2764804
  231.5 63.9 %collective-permute-start.22 = (bf16[4,128,960]{1,2,0:T(8,128)(2,1)}, bf16[4,128,960]{1,2,0:T(8,128)(2,1)}, u32[]{:S(2)}, u32[]{:S(2)}) collective-permute-start(bf16[4,128,960]{1,2,0:T(8,128)(2,1)} %pad_maximum_fusion.3), channel_id=1, source_target_pairs={{0,4},{4,0},{8,12},{12,8},{16,20},{20,16},{24,28},{28,24},{1,5},{5... | collective-permute-start | bytes 2949128 | tf_op jit(solution)/shard_map/ppermute | solution.py:69
  273.2 14.2 %collective-permute-start.57 = (f32[120,320]{1,0:T(8,128)S(1)}, f32[120,320]{1,0:T(8,128)S(1)}, u32[]{:S(2)}, u32[]{:S(2)}) collective-permute-start(f32[120,320]{1,0:T(8,128)S(1)} %bitcast.521), channel_id=1, source_target_pairs={{0,0},{8,1},{16,2},{24,3},{4,4},{12,5},{20,6},{28,7},{1,8},{9,9},{... | collective-permute-start | bytes 460808 | tf_op jit(solution)/shard_map/ppermute | solution.py:164
  275.6 11.9 %collective-permute-start.58 = (f32[120,320]{1,0:T(8,128)S(1)}, f32[120,320]{1,0:T(8,128)S(1)}, u32[]{:S(2)}, u32[]{:S(2)}) collective-permute-start(f32[120,320]{1,0:T(8,128)S(1)} %bitcast.522), channel_id=1, source_target_pairs={{4,0},{12,1},{20,2},{28,3},{0,4},{8,5},{16,6},{24,7},{5,8},{13,9},... | collective-permute-start | bytes 460808 | tf_op jit(solution)/shard_map/ppermute | solution.py:164
  290.1 9.9 %collective-permute-start.34 = (bf16[128,960]{0,1:T(8,128)(2,1)S(1)}, bf16[128,960]{0,1:T(8,128)(2,1)S(1)}, u32[]{:S(2)}, u32[]{:S(2)}) collective-permute-start(bf16[128,960]{0,1:T(8,128)(2,1)S(1)} %get-tuple-element.74), channel_id=1, source_target_pairs={{0,8},{4,12},{8,0},{12,4},{16,24},{20,28},{24,16},{28,20},{1,9},{5... | collective-permute-start | bytes 737288 | tf_op jit(solution)/shard_map/ppermute | solution.py:69
  290.2 15.4 %collective-permute-start.35 = (bf16[128,960]{0,1:T(8,128)(2,1)S(1)}, bf16[128,960]{0,1:T(8,128)(2,1)S(1)}, u32[]{:S(2)}, u32[]{:S(2)}) collective-permute-start(bf16[128,960]{0,1:T(8,128)(2,1)S(1)} %get-tuple-element.76), channel_id=1, source_target_pairs={{0,16},{4,20},{8,24},{12,28},{16,0},{20,4},{24,8},{28,12},{1,17},{... | collective-permute-start | bytes 737288 | tf_op jit(solution)/shard_map/ppermute | solution.py:69
  294.0 13.5 %collective-permute-start.36 = (bf16[128,960]{0,1:T(8,128)(2,1)S(1)}, bf16[128,960]{0,1:T(8,128)(2,1)S(1)}, u32[]{:S(2)}, u32[]{:S(2)}) collective-permute-start(bf16[128,960]{0,1:T(8,128)(2,1)S(1)} %get-tuple-element.75), channel_id=1, source_target_pairs={{0,24},{4,28},{8,16},{12,20},{16,8},{20,12},{24,0},{28,4},{1,25},{... | collective-permute-start | bytes 737288 | tf_op jit(solution)/shard_map/ppermute | solution.py:69
  297.9 59.2 %collective-permute-start.23 = (bf16[128,960]{0,1:T(8,128)(2,1)}, bf16[128,960]{0,1:T(8,128)(2,1)}, u32[]{:S(2)}, u32[]{:S(2)}) collective-permute-start(bf16[128,960]{0,1:T(8,128)(2,1)} %get-tuple-element.77), channel_id=1, source_target_pairs={{0,8},{4,12},{8,0},{12,4},{16,24},{20,28},{24,16},{28,20},{1,9},{5... | collective-permute-start | bytes 737288 | tf_op jit(solution)/shard_map/ppermute | solution.py:69
  298.5 61.5 %collective-permute-start.24 = (bf16[128,960]{0,1:T(8,128)(2,1)}, bf16[128,960]{0,1:T(8,128)(2,1)}, u32[]{:S(2)}, u32[]{:S(2)}) collective-permute-start(bf16[128,960]{0,1:T(8,128)(2,1)} %get-tuple-element.79), channel_id=1, source_target_pairs={{0,16},{4,20},{8,24},{12,28},{16,0},{20,4},{24,8},{28,12},{1,17},{... | collective-permute-start | bytes 737288 | tf_op jit(solution)/shard_map/ppermute | solution.py:69
  300.0 60.0 %collective-permute-start.25 = (bf16[128,960]{0,1:T(8,128)(2,1)}, bf16[128,960]{0,1:T(8,128)(2,1)}, u32[]{:S(2)}, u32[]{:S(2)}) collective-permute-start(bf16[128,960]{0,1:T(8,128)(2,1)} %get-tuple-element.78), channel_id=1, source_target_pairs={{0,24},{4,28},{8,16},{12,20},{16,8},{20,12},{24,0},{28,4},{1,25},{... | collective-permute-start | bytes 737288 | tf_op jit(solution)/shard_map/ppermute | solution.py:69
  324.1 26.6 %copy-start.31 = (bf16[8,128,960]{1,2,0:T(8,128)(2,1)S(1)}, bf16[8,128,960]{1,2,0:T(8,128)(2,1)}, u32[]{:S(2)}) copy-start(bf16[8,128,960]{1,2,0:T(8,128)(2,1)} %copy-done.30) | copy-start | bytes 5898244
  324.1 1.5 collective-permute-start.37
  324.2 7.1 %collective-permute-start.38 = (bf16[144,320]{0,1:T(8,128)(2,1)S(1)}, bf16[144,320]{0,1:T(8,128)(2,1)S(1)}, u32[]{:S(2)}, u32[]{:S(2)}) collective-permute-start(bf16[144,320]{0,1:T(8,128)(2,1)S(1)} %get-tuple-element.104), channel_id=1, source_target_pairs={{0,8},{4,12},{8,0},{12,4},{16,24},{20,28},{24,16},{28,20},{1,9},{5... | collective-permute-start | bytes 276488 | tf_op jit(solution)/shard_map/ppermute | solution.py:69
  325.6 8.3 %collective-permute-start.39 = (bf16[144,320]{0,1:T(8,128)(2,1)S(1)}, bf16[144,320]{0,1:T(8,128)(2,1)S(1)}, u32[]{:S(2)}, u32[]{:S(2)}) collective-permute-start(bf16[144,320]{0,1:T(8,128)(2,1)S(1)} %get-tuple-element.103), channel_id=1, source_target_pairs={{0,12},{4,8},{8,4},{12,0},{16,28},{20,24},{24,20},{28,16},{1,13},{... | collective-permute-start | bytes 276488 | tf_op jit(solution)/shard_map/ppermute | solution.py:69
  331.2 5.3 %collective-permute-start.40 = (bf16[144,320]{0,1:T(8,128)(2,1)S(1)}, bf16[144,320]{0,1:T(8,128)(2,1)S(1)}, u32[]{:S(2)}, u32[]{:S(2)}) collective-permute-start(bf16[144,320]{0,1:T(8,128)(2,1)S(1)} %get-tuple-element.102), channel_id=1, source_target_pairs={{0,16},{4,20},{8,24},{12,28},{16,0},{20,4},{24,8},{28,12},{1,17},{... | collective-permute-start | bytes 276488 | tf_op jit(solution)/shard_map/ppermute | solution.py:69
  333.9 9.6 %collective-permute-start.41 = (bf16[144,320]{0,1:T(8,128)(2,1)S(1)}, bf16[144,320]{0,1:T(8,128)(2,1)S(1)}, u32[]{:S(2)}, u32[]{:S(2)}) collective-permute-start(bf16[144,320]{0,1:T(8,128)(2,1)S(1)} %get-tuple-element.101), channel_id=1, source_target_pairs={{0,20},{4,16},{8,28},{12,24},{16,4},{20,0},{24,12},{28,8},{1,21},{... | collective-permute-start | bytes 276488 | tf_op jit(solution)/shard_map/ppermute | solution.py:69
  336.6 8.8 %collective-permute-start.42 = (bf16[144,320]{0,1:T(8,128)(2,1)S(1)}, bf16[144,320]{0,1:T(8,128)(2,1)S(1)}, u32[]{:S(2)}, u32[]{:S(2)}) collective-permute-start(bf16[144,320]{0,1:T(8,128)(2,1)S(1)} %get-tuple-element.100), channel_id=1, source_target_pairs={{0,24},{4,28},{8,16},{12,20},{16,8},{20,12},{24,0},{28,4},{1,25},{... | collective-permute-start | bytes 276488 | tf_op jit(solution)/shard_map/ppermute | solution.py:69
  343.5 7.1 %collective-permute-start.43 = (bf16[144,320]{0,1:T(8,128)(2,1)S(1)}, bf16[144,320]{0,1:T(8,128)(2,1)S(1)}, u32[]{:S(2)}, u32[]{:S(2)}) collective-permute-start(bf16[144,320]{0,1:T(8,128)(2,1)S(1)} %get-tuple-element.99), channel_id=1, source_target_pairs={{0,28},{4,24},{8,20},{12,16},{16,12},{20,8},{24,4},{28,0},{1,29},{... | collective-permute-start | bytes 276488 | tf_op jit(solution)/shard_map/ppermute | solution.py:69
  356.5 7.8 %collective-permute-start.51 = (bf16[256,320]{1,0:T(8,128)(2,1)S(1)}, bf16[256,320]{1,0:T(8,128)(2,1)S(1)}, u32[]{:S(2)}, u32[]{:S(2)}) collective-permute-start(bf16[256,320]{1,0:T(8,128)(2,1)S(1)} %get-tuple-element.96), channel_id=1, source_target_pairs={{0,1},{1,0},{2,3},{3,2},{4,5},{5,4},{6,7},{7,6},{8,9},{9,8},{10,11... | collective-permute-start | bytes 491528 | tf_op jit(solution)/shard_map/ppermute | solution.py:69
  357.1 9.9 %collective-permute-start.52 = (bf16[256,320]{1,0:T(8,128)(2,1)S(1)}, bf16[256,320]{1,0:T(8,128)(2,1)S(1)}, u32[]{:S(2)}, u32[]{:S(2)}) collective-permute-start(bf16[256,320]{1,0:T(8,128)(2,1)S(1)} %get-tuple-element.97), channel_id=1, source_target_pairs={{0,2},{1,3},{2,0},{3,1},{4,6},{5,7},{6,4},{7,5},{8,10},{9,11},{10,... | collective-permute-start | bytes 491528 | tf_op jit(solution)/shard_map/ppermute | solution.py:69
  357.1 20.1 %collective-permute-start.53 = (bf16[256,320]{1,0:T(8,128)(2,1)S(1)}, bf16[256,320]{1,0:T(8,128)(2,1)S(1)}, u32[]{:S(2)}, u32[]{:S(2)}) collective-permute-start(bf16[256,320]{1,0:T(8,128)(2,1)S(1)} %get-tuple-element.98), channel_id=1, source_target_pairs={{0,3},{1,2},{2,1},{3,0},{4,7},{5,6},{6,5},{7,4},{8,11},{9,10},{10,... | collective-permute-start | bytes 491528 | tf_op jit(solution)/shard_map/ppermute | solution.py:69
  (41 other events, 215.1 us)

commit v2 on v1

--- a/solution.py
+++ b/solution.py
@@ -1,6 +1,8 @@
 import jax
 import jax.numpy as jnp
 from jax import lax
+from jax.experimental import pallas as pl
+from jax.experimental.pallas import tpu as pltpu
 from jax.sharding import PartitionSpec as P
 
 HEADS = 15
@@ -390,6 +392,691 @@
     )
 
 
+def vspec():
+    return pl.BlockSpec(memory_space=pltpu.VMEM)
+
+
+def kernel_call(body, outs, args, specs=None, scratch=(), megabytes=8, micros=1.0):
+    if specs is None:
+        specs = [None] * len(args)
+    kinds = {
+        None: pltpu.VMEM,
+        "any": pl.ANY,
+        "smem": pltpu.SMEM,
+    }
+    return pl.pallas_call(
+        body,
+        out_shape=outs,
+        in_specs=[pl.BlockSpec(memory_space=kinds[s]) for s in specs],
+        out_specs=[pl.BlockSpec(memory_space=pltpu.VMEM) for _ in outs],
+        scratch_shapes=list(scratch),
+        compiler_params=pltpu.CompilerParams(vmem_limit_bytes=63 * 2**20),
+        cost_estimate=pl.CostEstimate(
+            flops=0, bytes_accessed=int(micros * 3.0e6), transcendentals=0
+        ),
+    )(*args)
+
+
+def shape(dims, dtype):
+    return jax.ShapeDtypeStruct(dims, dtype)
+
+
+def blocks_of(values, width):
+    return [values[:, i : i + width] for i in range(0, values.shape[1], width)]
+
+
+def turn(values):
+    half = values.shape[-1] // 2
+    return jnp.concatenate([-values[:, half:], values[:, :half]], 1)
+
+
+def pad_lanes(values, before, total):
+    rows, count = values.shape
+    parts = []
+    if before:
+        parts.append(jnp.zeros((rows, before), values.dtype))
+    parts.append(values)
+    if total - before - count:
+        parts.append(jnp.zeros((rows, total - before - count), values.dtype))
+    return jnp.concatenate(parts, 1)
+
+
+def pack_attention(q_ref, k_ref, v_ref, o_ref, out_ref):
+    kv = jnp.concatenate([k_ref[...], v_ref[...]], 0).astype(F32).T.astype(BF16)
+    qkv = jnp.concatenate([q_ref[...], kv], 1)
+    o = o_ref[...]
+    half = o.shape[0] // 2
+    out_ref[...] = jnp.concatenate([qkv[:half], o[:half], o[half:], qkv[half:]], 1)
+
+
+def pack_down(ids, down_ref, _, p0_ref, p1_ref):
+    down = down_ref[...]
+    units = down.shape[1] // 2
+    first = down[:, :units].astype(F32)
+    second = down[:, units:].astype(F32)
+    even = (ids[0] % 2) == 0
+    p0_ref[...] = jnp.where(even, first, second).astype(BF16)
+    p1_ref[...] = jnp.where(even, second, first).astype(BF16)
+
+
+def pack_feed(ids, gate_ref, up_ref, r0_ref, r1_ref, _, out_ref):
+    gate_up = jnp.concatenate([gate_ref[...], up_ref[...]], 0).astype(F32).T
+    even = (ids[0] % 2) == 0
+    r0 = r0_ref[...].astype(F32)
+    r1 = r1_ref[...].astype(F32)
+    joined = jnp.concatenate([jnp.where(even, r0, r1), jnp.where(even, r1, r0)], 1)
+    rows = gate_up.shape[0]
+    out_ref[:rows] = gate_up.astype(BF16)
+    out_ref[rows:] = joined.astype(BF16)
+
+
+def join_first(own_ref, got_ref, ag_ref, fg_ref, out_ref):
+    half = own_ref.shape[0]
+    out_ref[: 2 * half] = jnp.concatenate([own_ref[...], got_ref[...]], 0)
+    gains = jnp.concatenate([ag_ref[...], fg_ref[...]], 1)
+    row = pad_lanes(gains, 0, out_ref.shape[1])
+    out_ref[2 * half :] = jnp.broadcast_to(row, (16, out_ref.shape[1]))
+
+
+def join_second(a_ref, b_ref, _, out_ref):
+    out_ref[...] = jnp.concatenate([a_ref[...], b_ref[...]], 0)
+
+
+def line_blocks(buffer, f, offset):
+    return [
+        jnp.concatenate(
+            [buffer[2 * (f ^ j) + offset][:, :120], buffer[2 * (f ^ (j + 1)) + offset][:, :120]], 1
+        )
+        for j in (0, 2)
+    ]
+
+
+def attention_forward(
+    ids, x_ref, cos_ref, sin_ref, segc_ref, segr_ref, *rest
+):
+    first = rest[:8]
+    second = rest[8:16]
+    (
+        x2_ref, h2_ref, att_ref, qr_ref, kr_ref, vr_ref, lse_ref, gains_ref,
+        hb, tb, gb,
+    ) = rest[16:]
+    d = ids[0]
+    f = ids[1]
+    length = x_ref.shape[0]
+    for s in range(8):
+        gb[d ^ s] = first[s][240:248, :256].astype(F32)
+    gain_one = jnp.concatenate([gb[i][:, :120] for i in range(8)], 1)
+    gain_two = jnp.concatenate([gb[i][:, 120:240] for i in range(8)], 1)
+    gains_ref[0] = gain_one
+    gains_ref[1] = gain_two
+    x = x_ref[...].astype(F32)
+    scale = lax.rsqrt(jnp.mean(x * x, -1, keepdims=True) + EPS)
+    h1 = (x * scale * gain_one[:1]).astype(BF16)
+    for i, block in enumerate(blocks_of(h1, 120)):
+        hb[i, :, :120] = block
+    left = line_blocks(hb, f, 0)
+    right = line_blocks(hb, f, 1)
+    for s in range(8):
+        a = dot(left[0], first[s][:240, 0:256]) + dot(left[1], second[s][:, 0:256])
+        b = dot(right[0], first[s][:240, 384:640]) + dot(right[1], second[s][:, 384:640])
+        tb[d ^ s, :, :200] = a[:, :200] + b[:, 56:256]
+    parts = [tb[i] for i in range(8)]
+    q = jnp.concatenate([p[:, :120] for p in parts], 1)
+    k = jnp.concatenate([p[:, 120:160] for p in parts], 1)
+    v = jnp.concatenate([p[:, 160:200] for p in parts], 1)
+    cosines = cos_ref[...]
+    sines = sin_ref[...]
+    index_q = lax.broadcasted_iota(jnp.int32, (length, length), 0)
+    index_k = lax.broadcasted_iota(jnp.int32, (length, length), 1)
+    allowed = (segc_ref[...] == segr_ref[...]) & (index_q >= index_k)
+    bias = jnp.where(allowed, 0.0, NEGATIVE)
+    bias = jnp.concatenate([bias] * GROUP, 0)
+    heads = []
+    for g in range(KV_HEADS):
+        kg = k[:, g * HD : (g + 1) * HD]
+        kr = (kg * cosines + turn(kg) * sines).astype(BF16)
+        vr = v[:, g * HD : (g + 1) * HD].astype(BF16)
+        rows = []
+        for h in range(g * GROUP, (g + 1) * GROUP):
+            qh = q[:, h * HD : (h + 1) * HD]
+            rows.append((qh * cosines + turn(qh) * sines).astype(BF16))
+        qr = jnp.concatenate(rows, 0)
+        qr_ref[g] = qr
+        kr_ref[g] = kr
+        vr_ref[g] = vr
+        scores = contract_last(qr, kr) * HD ** (-0.5) + bias
+        top = jnp.max(scores, -1, keepdims=True)
+        exps = jnp.exp(scores - top)
+        totals = jnp.sum(exps, -1, keepdims=True)
+        lse_ref[g] = top + jnp.log(totals)
+        probs = (exps / totals).astype(BF16)
+        out = dot(probs, vr).astype(BF16)
+        heads += [out[i * length : (i + 1) * length] for i in range(GROUP)]
+    attended = jnp.concatenate(heads, 1)
+    att_ref[...] = attended
+    for i, block in enumerate(blocks_of(attended, 120)):
+        hb[i, :, :120] = block
+    left = line_blocks(hb, f, 0)
+    right = line_blocks(hb, f, 1)
+    for s in range(8):
+        a = dot(left[0], first[s][:240, 128:384]) + dot(left[1], second[s][:, 128:384])
+        b = dot(right[0], first[s][:240, 256:512]) + dot(right[1], second[s][:, 256:512])
+        tb[d ^ s, :, :120] = a[:, 72:192] + b[:, 64:184]
+    x2 = x + jnp.concatenate([tb[i][:, :120] for i in range(8)], 1)
+    x2_ref[...] = x2
+    scale_two = lax.rsqrt(jnp.mean(x2 * x2, -1, keepdims=True) + EPS)
+    h2_ref[...] = (x2 * scale_two * gain_two[:1]).astype(BF16)
+
+
+def start_stack(refs, buffer, sems):
+    copies = []
+    for s, ref in enumerate(refs):
+        rows = ref.shape[0]
+        copy = pltpu.make_async_copy(ref, buffer.at[pl.ds(s * rows, rows)], sems.at[s])
+        copy.start()
+        copies.append(copy)
+    return copies
+
+
+def place_feed(feed_ref, gu, dt):
+    for j in range(4):
+        gu[240 * j : 240 * (j + 1), :] = feed_ref[360 * j : 360 * j + 240, :]
+        dt[240 * j : 240 * (j + 1), :] = unfold_down(feed_ref[360 * j + 240 : 360 * (j + 1), :])
+
+
+def unfold_down(both):
+    half = both.shape[1] // 2
+    return jnp.concatenate([both[:, :half], both[:, half:]], 0)
+
+
+def feed_critical(*rest):
+    h_refs, c_refs, feed_ref = rest[:8], rest[8:16], rest[16]
+    even_ref, odd_ref, delta_ref, mixed_ref, hs, cs, gu, dt, h_sems, c_sems = rest[17:]
+    c_copies = start_stack(c_refs, cs, c_sems)
+    h_copies = start_stack(h_refs, hs, h_sems)
+    place_feed(feed_ref, gu, dt)
+    for copy in c_copies + h_copies:
+        copy.wait()
+    units = dt.shape[1]
+
+    def step(c, carry):
+        rows = pl.ds(pl.multiple_of(c * 256, 256), 256)
+        both = dot(hs[rows, :], gu[...])
+        mixed_grad = dot(cs[rows, :], dt[...])
+        gate = both[:, :units]
+        up = both[:, units:]
+        sig = 1.0 / (1.0 + jnp.exp(-gate))
+        silu = gate * sig
+        mixed_ref[rows, :] = (silu * up).astype(BF16)
+        gate_delta = (mixed_grad * up * sig * (1.0 + gate * (1.0 - sig))).astype(BF16)
+        up_delta = (mixed_grad * silu).astype(BF16)
+        deltas = jnp.concatenate([gate_delta, up_delta], 1)
+        delta_ref[rows, :] = deltas
+        back = contract_last(deltas, gu[...])
+        even_ref[c] = back[:128]
+        odd_ref[pl.ds(pl.multiple_of(c * 128, 128), 128), :] = back[128:].astype(BF16)
+        return carry
+
+    lax.fori_loop(0, 4, step, 0)
+
+
+def pair_sum(even_ref, odd_ref, *rest):
+    own_ref, a_ref, b_ref, c_ref = rest[-4:]
+    rows = own_ref.shape[0]
+    own_ref[...] = even_ref[0] + odd_ref[:rows].astype(F32)
+    for i, ref in ((1, a_ref), (2, b_ref), (3, c_ref)):
+        ref[...] = (even_ref[i] + odd_ref[rows * i : rows * (i + 1)].astype(F32)).astype(BF16)
+
+
+def feed_rest(*rest):
+    h_refs, c_refs, feed_ref = rest[:8], rest[8:16], rest[16]
+    delta_ref, mixed_ref = rest[17:19]
+    grad_ref, even_ref, odd_ref, hs, cs, h_sems, c_sems = rest[20:]
+    h_copies = start_stack(h_refs, hs, h_sems)
+    c_copies = start_stack(c_refs, cs, c_sems)
+    for copy in h_copies + c_copies:
+        copy.wait()
+    for j in range(4):
+        part = contract_first(hs[:, 240 * j : 240 * (j + 1)], delta_ref[...])
+        grad_ref[360 * j : 360 * j + 240, :] = part.astype(BF16)
+        part = contract_first(cs[:, 240 * j : 240 * (j + 1)], mixed_ref[...])
+        part = jnp.concatenate([part[:120], part[120:]], 1)
+        grad_ref[360 * j + 240 : 360 * (j + 1), :] = part.astype(BF16)
+    turned = [unfold_down(feed_ref[360 * j + 240 : 360 * (j + 1), :]) for j in range(4)]
+    down = jnp.concatenate(turned, 0)
+    for c in range(4):
+        part = contract_last(mixed_ref[256 * c : 256 * (c + 1), :], down)
+        even_ref[c] = part[:128]
+        odd_ref[128 * c : 128 * (c + 1), :] = part[128:].astype(BF16)
+
+
+def spread_line(buffer, parts, f, offset):
+    for j, part in enumerate(parts):
+        buffer[2 * (f ^ (2 * j)) + offset, :, :120] = part[:, :120]
+        buffer[2 * (f ^ (2 * j + 1)) + offset, :, :120] = part[:, 120:240]
+
+
+def attention_backward(ids, *rest):
+    own_ref, a_ref, b_ref, c_ref, cot_ref, x2_ref, x_ref, gains_ref = rest[:8]
+    cos_ref, sin_ref, segc_ref, segr_ref, qr_ref, kr_ref, vr_ref, lse_ref = rest[8:16]
+    first, second = rest[16:24], rest[24:32]
+    outs = rest[32:40]
+    grad_ref, fb, db, eb, gb = rest[40:]
+    d = ids[0]
+    f = ids[1]
+    length = x_ref.shape[0]
+    gain_one = gains_ref[0, :1]
+    gain_two = gains_ref[1, :1]
+    dh2 = (
+        own_ref[...] + a_ref[...].astype(F32) + b_ref[...].astype(F32) + c_ref[...].astype(F32)
+    )
+    x2 = x2_ref[...]
+    scale_two = lax.rsqrt(jnp.mean(x2 * x2, -1, keepdims=True) + EPS)
+    unit = x2 * scale_two
+    feed_gain_grad = jnp.sum(dh2 * unit, 0, keepdims=True)
+    scaled = dh2 * gain_two
+    dx2 = cot_ref[...].astype(F32) + scale_two * (
+        scaled - unit * jnp.mean(scaled * unit, -1, keepdims=True)
+    )
+    rounded = dx2.astype(BF16)
+    for i, block in enumerate(blocks_of(rounded, 120)):
+        db[i, :, :120] = block
+    left = [jnp.zeros((length, 240), F32)] * 2
+    right = [jnp.zeros((length, 240), F32)] * 2
+    for s in range(8):
+        mine = db[d ^ s][:, :120]
+        for_left = pad_lanes(mine, 72, 256)
+        for_right = pad_lanes(mine, 64, 256)
+        left[0] = left[0] + contract_last(for_left, first[s][:240, 128:384])
+        left[1] = left[1] + contract_last(for_left, second[s][:, 128:384])
+        right[0] = right[0] + contract_last(for_right, first[s][:240, 256:512])
+        right[1] = right[1] + contract_last(for_right, second[s][:, 256:512])
+    spread_line(fb, left, f, 0)
+    spread_line(fb, right, f, 1)
+    grad = jnp.concatenate([fb[i][:, :120] for i in range(8)], 1).astype(BF16)
+    cosines = cos_ref[...]
+    sines = sin_ref[...]
+    index_q = lax.broadcasted_iota(jnp.int32, (length, length), 0)
+    index_k = lax.broadcasted_iota(jnp.int32, (length, length), 1)
+    allowed = (segc_ref[...] == segr_ref[...]) & (index_q >= index_k)
+    bias = jnp.where(allowed, 0.0, NEGATIVE)
+    bias = jnp.concatenate([bias] * GROUP, 0)
+    dq, dk, dv = [], [], []
+    for g in range(KV_HEADS):
+        qr = qr_ref[g]
+        kr = kr_ref[g]
+        vr = vr_ref[g]
+        grads = jnp.concatenate(
+            [grad[:, h * HD : (h + 1) * HD] for h in range(g * GROUP, (g + 1) * GROUP)], 0
+        )
+        probs = jnp.exp(contract_last(qr, kr) * HD ** (-0.5) + bias - lse_ref[g])
+        dv.append(contract_first(probs.astype(BF16), grads).astype(BF16))
+        dprob = contract_last(grads, vr)
+        inner = jnp.sum(probs * dprob, -1, keepdims=True)
+        ds = (probs * (dprob - inner) * HD ** (-0.5)).astype(BF16)
+        dqg = dot(ds, kr)
+        dkg = contract_first(ds, qr)
+        dk.append((dkg * cosines - turn(dkg * sines)).astype(BF16))
+        for i in range(GROUP):
+            part = dqg[i * length : (i + 1) * length]
+            dq.append((part * cosines - turn(part * sines)).astype(BF16))
+    dq = blocks_of(jnp.concatenate(dq, 1), 120)
+    dk = blocks_of(jnp.concatenate(dk, 1), 40)
+    dv = blocks_of(jnp.concatenate(dv, 1), 40)
+    for i in range(8):
+        eb[i, :, :200] = jnp.concatenate([dq[i], dk[i], dv[i]], 1)
+    left = [jnp.zeros((length, 240), F32)] * 2
+    right = [jnp.zeros((length, 240), F32)] * 2
+    for s in range(8):
+        mine = eb[d ^ s][:, :200]
+        for_left = pad_lanes(mine, 0, 256)
+        for_right = pad_lanes(mine, 56, 256)
+        left[0] = left[0] + contract_last(for_left, first[s][:240, 0:256])
+        left[1] = left[1] + contract_last(for_left, second[s][:, 0:256])
+        right[0] = right[0] + contract_last(for_right, first[s][:240, 384:640])
+        right[1] = right[1] + contract_last(for_right, second[s][:, 384:640])
+    spread_line(fb, left, f, 0)
+    spread_line(fb, right, f, 1)
+    dh1 = jnp.concatenate([fb[i][:, :120] for i in range(8)], 1)
+    x = x_ref[...].astype(F32)
+    scale_one = lax.rsqrt(jnp.mean(x * x, -1, keepdims=True) + EPS)
+    unit = x * scale_one
+    attention_gain_grad = jnp.sum(dh1 * unit, 0, keepdims=True)
+    scaled = dh1 * gain_one
+    input_grad = dx2 + scale_one * (
+        scaled - unit * jnp.mean(scaled * unit, -1, keepdims=True)
+    )
+    grad_ref[...] = input_grad.T
+    for i in range(8):
+        row = jnp.concatenate(
+            [feed_gain_grad[:, 120 * i : 120 * (i + 1)], attention_gain_grad[:, 120 * i : 120 * (i + 1)]], 1
+        )
+        gb[i] = jnp.broadcast_to(pad_lanes(row, 0, 640), (16, 640))
+    half = length // 2
+    for s in range(8):
+        delta = eb[d ^ s][:, :200]
+        mine = db[d ^ s][:, :120]
+        outs[s][:half] = jnp.concatenate(
+            [delta[:half], mine[:half], mine[half:], delta[half:]], 1
+        )
+        outs[s][half:] = gb[d ^ s].astype(BF16)
+
+
+def attention_weights(ids, *rest):
+    x_refs, att_refs, got, gains_ref = rest[:8], rest[8:16], rest[16:24], rest[24]
+    own_ref, g1_ref, g2_ref, g3_ref, hs, at, dl, acc, x_sems, a_sems = rest[25:]
+    f = ids[1]
+    length = 128
+    half = 64
+    x_copies = start_stack(x_refs, hs, x_sems)
+    a_copies = start_stack(att_refs, at, a_sems)
+    gain_sum = jnp.zeros((8, 640), F32)
+    for s in range(8):
+        block = got[s][:half]
+        dl[s * length : s * length + half, 0:320] = block[:, :320]
+        dl[s * length + half : (s + 1) * length, 0:320] = jnp.concatenate(
+            [block[:, 440:], block[:, 320:440]], 1
+        )
+        gain_sum = gain_sum + got[s][half : half + 8].astype(F32)
+    gain_one = gains_ref[0, :1]
+    for copy in x_copies + a_copies:
+        copy.wait()
+    for s in range(8):
+        x = hs[length * s : length * (s + 1)].astype(F32)
+        scale = lax.rsqrt(jnp.mean(x * x, -1, keepdims=True) + EPS)
+        hs[s * length : (s + 1) * length] = (x * scale * gain_one).astype(BF16)
+    qkv = contract_first(dl[:, :200], hs[...])
+    out = contract_first(dl[:, 200:320], at[...])
+    both = jnp.concatenate([qkv, out], 0)
+    for i in range(4):
+        acc[i, :320, :240] = both[:, 240 * i : 240 * (i + 1)]
+        acc[i, 320:, :240] = jnp.concatenate([gain_sum[:, :240]] * 2, 0)
+    own_ref[...] = acc[f][:, :240]
+    for j, ref in ((1, g1_ref), (2, g2_ref), (3, g3_ref)):
+        ref[...] = acc[f ^ j][:, :240].astype(BF16)
+
+
+def finish_feed(ids, sum_ref, gate_ref, up_ref, a_ref, b_ref):
+    total = sum_ref[:240].astype(F32).T
+    gate_ref[...] = total[:320]
+    up_ref[...] = total[320:]
+    even = (ids[0] % 2) == 0
+    down = sum_ref[240:].astype(F32)
+    left = down[:, :320]
+    right = down[:, 320:]
+    a_ref[...] = jnp.where(even, left, right).astype(BF16)
+    b_ref[...] = jnp.where(even, right, left).astype(BF16)
+
+
+def finish_down(ids, a_ref, b_ref, out_ref):
+    even = (ids[0] % 2) == 0
+    a = a_ref[...].astype(F32)
+    b = b_ref[...].astype(F32)
+    out_ref[...] = jnp.concatenate([jnp.where(even, a, b), jnp.where(even, b, a)], 1)
+
+
+def finish_output(x2_ref, own_ref, a_ref, b_ref, c_ref, out_ref):
+    total = (
+        x2_ref[...]
+        + own_ref[...]
+        + a_ref[...].astype(F32)
+        + b_ref[...].astype(F32)
+        + c_ref[...].astype(F32)
+    )
+    out_ref[...] = total.T.astype(BF16)
+
+
+def finish_attention(own_ref, a_ref, b_ref, c_ref, q_ref, k_ref, v_ref, o_ref, ag_ref, fg_ref):
+    total = (
+        own_ref[...] + a_ref[...].astype(F32) + b_ref[...].astype(F32) + c_ref[...].astype(F32)
+    )
+    q_ref[...] = total[:120].T
+    k_ref[...] = total[120:160]
+    v_ref[...] = total[160:200]
+    o_ref[...] = total[200:320].T
+    fg_ref[...] = total[320:328, :120]
+    ag_ref[...] = total[320:328, 120:240]
+
+
+def fast(
+    hidden_in,
+    segment_ids,
+    positions,
+    query_weight,
+    key_weight,
+    value_weight,
+    output_weight,
+    attention_gain,
+    gate_weight,
+    up_weight,
+    down_weight,
+    feedforward_gain,
+    output_cotangent,
+):
+    hidden = hidden_in[0]
+    cotangent = output_cotangent[0]
+    length, features = hidden.shape
+    d = lax.axis_index("dp")
+    f = lax.axis_index("fsdp")
+    ids = jnp.stack([d, f]).astype(jnp.int32)
+    tokens = 8 * length
+
+    (block,) = kernel_call(
+        pack_attention,
+        [shape((120, 640), BF16)],
+        [query_weight, key_weight.T, value_weight.T, output_weight],
+    )
+    line = [block] + [send(block, "fsdp", j) for j in (1, 2, 3)]
+    (chunk_a,) = kernel_call(
+        join_first,
+        [shape((256, 640), BF16)],
+        [line[0], line[1], attention_gain[None], feedforward_gain[None]],
+    )
+    (chunk_b,) = kernel_call(join_second, [shape((240, 640), BF16)], [line[2], line[3], chunk_a], [None, None, "any"])
+
+    def spread(chunk, near, far):
+        slots = [chunk, send(chunk, "dp", 1)] + [None] * 6
+        slots[near] = send(chunk, "dp", near)
+        slots[far] = send(chunk, "dp", far)
+        slots[6] = send(slots[near], "dp", far)
+        for s in (near, far, 6):
+            slots[s + 1] = send(slots[s], "dp", 1)
+        return slots
+
+    first = spread(chunk_a, 2, 4)
+    second = spread(chunk_b, 4, 2)
+
+    piece_a, piece_b = kernel_call(
+        pack_down,
+        [shape((120, 320), BF16), shape((120, 320), BF16)],
+        [ids, down_weight.T, block],
+        ["smem", None, "any"],
+    )
+    routes = down_routes(8, 4)
+    piece_a = lax.ppermute(piece_a, ("dp", "fsdp"), routes[0])
+    piece_b = lax.ppermute(piece_b, ("dp", "fsdp"), routes[1])
+    (feed_block,) = kernel_call(
+        pack_feed,
+        [shape((360, 640), BF16)],
+        [ids, gate_weight.T, up_weight.T, piece_a, piece_b, chunk_b],
+        ["smem"] + [None] * 4 + ["any"],
+    )
+    feed = lax.all_gather(feed_block, "fsdp", axis=0, tiled=True)
+
+    def gather(values):
+        slots = [values, send(values, "dp", 1)] + [None] * 6
+        for s in (2, 4, 6):
+            slots[s] = send(values, "dp", s)
+            slots[s + 1] = send(slots[s], "dp", 1)
+        return slots
+
+    cotangent_slots = gather(cotangent)
+
+    cosines, sines = rotary_tables(positions[0], HD)
+    seg_column = segment_ids[0][:, None]
+    seg_row = segment_ids
+    x2, h2, attended, qr, kr, vr, lse, gains = kernel_call(
+        attention_forward,
+        [
+            shape((length, features), F32),
+            shape((length, features), BF16),
+            shape((length, features), BF16),
+            shape((KV_HEADS, GROUP * length, HD), BF16),
+            shape((KV_HEADS, length, HD), BF16),
+            shape((KV_HEADS, length, HD), BF16),
+            shape((KV_HEADS, GROUP * length, 1), F32),
+            shape((2, 8, features), F32),
+        ],
+        [ids, hidden, cosines, sines, seg_column, seg_row, *first, *second],
+        ["smem"] + [None] * 21,
+        [
+            pltpu.VMEM((8, length, 128), BF16),
+            pltpu.VMEM((8, length, 256), F32),
+            pltpu.VMEM((8, 8, 256), F32),
+        ],
+        16,
+        8.5,
+    )
+    h2_slots = gather(h2)
+    even, odd, deltas, mixed = kernel_call(
+        feed_critical,
+        [
+            shape((4, length, features), F32),
+            shape((4 * length, features), BF16),
+            shape((tokens, 640), BF16),
+            shape((tokens, 320), BF16),
+        ],
+        [*h2_slots, *cotangent_slots, feed],
+        ["any"] * 16 + [None],
+        [
+            pltpu.VMEM((tokens, features), BF16),
+            pltpu.VMEM((tokens, features), BF16),
+            pltpu.VMEM((features, 640), BF16),
+            pltpu.VMEM((features, 320), BF16),
+            pltpu.SemaphoreType.DMA((8,)),
+            pltpu.SemaphoreType.DMA((8,)),
+        ],
+        24,
+        9.0,
+    )
+
+    def scatter_sum(even, odd, *after):
+        odd = send(odd, "dp", 1)
+        own, a, b, c = kernel_call(
+            pair_sum,
+            [shape((length, features), F32)] + [shape((length, features), BF16)] * 3,
+            [even, odd, *after],
+            [None, None] + ["any"] * len(after),
+            (),
+            12,
+        )
+        return own, send(a, "dp", 2), send(b, "dp", 4), send(c, "dp", 6)
+
+    back_own, back_a, back_b, back_c = scatter_sum(even, odd)
+    feed_grad, f_even, f_odd = kernel_call(
+        feed_rest,
+        [
+            shape((4 * 360, 640), BF16),
+            shape((4, length, features), F32),
+            shape((4 * length, features), BF16),
+        ],
+        [*h2_slots, *cotangent_slots, feed, deltas, mixed, back_own],
+        ["any"] * 16 + [None] * 3 + ["any"],
+        [
+            pltpu.VMEM((tokens, features), BF16),
+            pltpu.VMEM((tokens, features), BF16),
+            pltpu.SemaphoreType.DMA((8,)),
+            pltpu.SemaphoreType.DMA((8,)),
+        ],
+        24,
+        9.0,
+    )
+    feed_sum = lax.psum_scatter(feed_grad, "fsdp", scatter_dimension=0, tiled=True)
+    attended_slots = gather(attended)
+    hidden_slots = gather(hidden)
+    *outgoing, input_grad = kernel_call(
+        attention_backward,
+        [shape((80, 640), BF16)] * 8 + [shape((features, length), F32)],
+        [
+            ids, back_own, back_a, back_b, back_c, cotangent, x2, hidden, gains,
+            cosines, sines, seg_column, seg_row, qr, kr, vr, lse, *first, *second,
+        ],
+        ["smem"] + [None] * 32,
+        [
+            pltpu.VMEM((8, length, 128), F32),
+            pltpu.VMEM((8, length, 128), BF16),
+            pltpu.VMEM((8, length, 256), BF16),
+            pltpu.VMEM((8, 16, 640), F32),
+        ],
+        18,
+        10.5,
+    )
+    arrived = [outgoing[0]] + [send(outgoing[s], "dp", s) for s in range(1, 8)]
+    w0, w1, w2, w3 = kernel_call(
+        attention_weights,
+        [shape((336, 240), F32)] + [shape((336, 240), BF16)] * 3,
+        [ids, *hidden_slots, *attended_slots, *arrived, gains],
+        ["smem"] + ["any"] * 16 + [None] * 9,
+        [
+            pltpu.VMEM((tokens, features), BF16),
+            pltpu.VMEM((tokens, features), BF16),
+            pltpu.VMEM((tokens, 320), BF16),
+            pltpu.VMEM((4, 336, 256), F32),
+            pltpu.SemaphoreType.DMA((8,)),
+            pltpu.SemaphoreType.DMA((8,)),
+        ],
+        20,
+        4.5,
+    )
+
+    gate_out, up_out, piece_a, piece_b = kernel_call(
+        finish_feed,
+        [shape((320, 240), F32)] * 2 + [shape((120, 320), BF16)] * 2,
+        [ids, feed_sum],
+        ["smem", None],
+    )
+    back = [[(t, s) for s, t in pairs] for pairs in routes]
+    piece_a = lax.ppermute(piece_a, ("dp", "fsdp"), back[0])
+    piece_b = lax.ppermute(piece_b, ("dp", "fsdp"), back[1])
+    (down_out,) = kernel_call(
+        finish_down, [shape((120, 640), F32)], [ids, piece_a, piece_b], ["smem", None, None]
+    )
+    sums = scatter_sum(f_even, f_odd, w0)
+    (block_output,) = kernel_call(
+        finish_output, [shape((features, length), BF16)], [x2, *sums]
+    )
+    parts = [send(w, "fsdp", j) for j, w in ((1, w1), (2, w2), (3, w3))]
+    q_out, k_out, v_out, o_out, ag_out, fg_out = kernel_call(
+        finish_attention,
+        [
+            shape((240, 120), F32),
+            shape((40, 240), F32),
+            shape((40, 240), F32),
+            shape((240, 120), F32),
+            shape((8, 120), F32),
+            shape((8, 120), F32),
+        ],
+        [w0, *parts],
+    )
+    return (
+        block_output.T[None],
+        input_grad.T[None],
+        q_out,
+        k_out.T,
+        v_out.T,
+        o_out,
+        ag_out[0],
+        gate_out.T,
+        up_out.T,
+        down_out.T,
+        fg_out[0],
+    )
+
+
+def fits(mesh_shape):
+    return mesh_shape["dp"] == 8 and mesh_shape["fsdp"] == 4
+
+
 def solution(mesh):
     in_specs = (
         P(("dp", "fsdp"), None, None),
@@ -419,4 +1106,5 @@
         P("fsdp", "dp"),
         P("dp"),
     )
-    return jax.shard_map(local, mesh=mesh, in_specs=in_specs, out_specs=out_specs, check_vma=False)
+    body = fast if fits(mesh.shape) else local
+    return jax.shard_map(body, mesh=mesh, in_specs=in_specs, out_specs=out_specs, check_vma=False)

time: 388 us -> 277 us (0.71)
  the two profiles are of different devices: /device:TPU:8 before, /device:TPU:12 now
where the time goes in v2:
time: 277 us; the launch traced here: 276 us
  waiting for transfers between devices  118 us (43%)
  Pallas kernels  74.7 us (27%)
  starting transfers between devices  49.3 us (18%)
  local copies, waits for them, and re-layouts  18 us (6%)
  between operations  14.6 us (5%)
    ppermute x63, waiting for transfers between devices, send(): return lax.ppermute(values, axis, [(i, i ^ distance) for i in range(count)])  117 us
    pallas_call x16, Pallas kernels, kernel_call(): pl.pallas_call(body, out_shape=outs, in_specs=[pl.BlockSpec(memory_space=...  74.7 us
    ppermute x63, starting transfers between devices, send(): return lax.ppermute(values, axis, [(i, i ^ distance) for i in range(count)])  40.4 us
    unnamed x84, local copies, waits for them, and re-layouts  9.08 us
  transfers between devices with their start and end apart: 69, of which 27 were waited for; matrix products, arithmetic and copies ran while one was open for 4% of the time, Pallas kernels for 16%

profile of v2, /device:TPU:12, one launch (start us, length us, event | category | flops | bytes accessed | tf_op | source)
XLA Modules:
  0.0 276.4 jit_solution(544274330089711062)
XLA Ops:
  7.2 1.8 shard_map.212.own_ref._
  9.5 2.6 collective-permute-start.8
  13.2 1.8 shard_map.216
  14.9 4.3 %collective-permute-start.31 = (bf16[120,320]{1,0:T(8,128)(2,1)}, bf16[120,320]{1,0:T(8,128)(2,1)}, u32[]{:S(2)}, u32[]{:S(2)}) collective-permute-start(bf16[120,320]{1,0:T(8,128)(2,1)} %get-tuple-element.61), channel_id=1, source_target_pairs={{0,0},{1,8},{2,16},{3,24},{4,4},{5,12},{6,20},{7,28},{8,1},{9,9},{... | collective-permute-start | bytes 230408 | tf_op jit(solution)/shard_map/ppermute | solution.py:896
  20.0 1.8 shard_map.213._.rest_0_.rest_16_
  21.9 5.3 %collective-permute-done.8.a_ref = bf16[120,640]{1,0:T(8,128)(2,1)S(1)} collective-permute-done((bf16[120,640]{1,0:T(8,128)(2,1)}, bf16[120,640]{1,0:T(8,128)(2,1)S(1)}, u32[]{:S(2)}, u32[]{:S(2)}) %collective-permute-start.8) | collective-permute-done | bytes 153632 | tf_op jit(solution)/shard_map/ppermute | solution.py:71
  27.1 3.3 %collective-permute-done.9.b_ref = bf16[120,640]{1,0:T(8,128)(2,1)S(1)} collective-permute-done((bf16[120,640]{1,0:T(8,128)(2,1)}, bf16[120,640]{1,0:T(8,128)(2,1)S(1)}, u32[]{:S(2)}, u32[]{:S(2)}) %collective-permute-start.9) | collective-permute-done | bytes 153632 | tf_op jit(solution)/shard_map/ppermute | solution.py:71
  31.1 1.7 shard_map.214.rest_8_._.rest_24_
  32.8 1.1 collective-permute-done.31.r0_ref
  34.0 2.1 shard_map.217
  36.6 1.1 copy.30
  37.7 1.5 collective-permute-start.25
  40.1 1.3 collective-permute-start.2
  41.9 5.2 %collective-permute-done.25.rest_10_ = bf16[128,960]{1,0:T(8,128)(2,1)} collective-permute-done((bf16[128,960]{1,0:T(8,128)(2,1)S(1)}, bf16[128,960]{1,0:T(8,128)(2,1)}, u32[]{:S(2)}, u32[]{:S(2)}) %collective-permute-start.25) | collective-permute-done | bytes 245792 | tf_op jit(solution)/shard_map/ppermute | solution.py:71
  47.1 5.2 %collective-permute-done.27.rest_12_ = bf16[128,960]{1,0:T(8,128)(2,1)} collective-permute-done((bf16[128,960]{1,0:T(8,128)(2,1)S(1)}, bf16[128,960]{1,0:T(8,128)(2,1)}, u32[]{:S(2)}, u32[]{:S(2)}) %collective-permute-start.27) | collective-permute-done | bytes 245792 | tf_op jit(solution)/shard_map/ppermute | solution.py:71
  53.1 1.9 copy.28
  55.7 5.5 %collective-permute-done.11.rest_10_.rest_26_ = bf16[240,640]{1,0:T(8,128)(2,1)S(1)} collective-permute-done((bf16[240,640]{1,0:T(8,128)(2,1)S(1)}, bf16[240,640]{1,0:T(8,128)(2,1)S(1)}, u32[]{:S(2)}, u32[]{:S(2)}) %collective-permute-start.11) | collective-permute-done | bytes 307232 | tf_op jit(solution)/shard_map/ppermute | solution.py:71
  62.6 6.8 %collective-permute-done.15.rest_14_.rest_30_ = bf16[240,640]{1,0:T(8,128)(2,1)S(1)} collective-permute-done((bf16[240,640]{1,0:T(8,128)(2,1)S(1)}, bf16[240,640]{1,0:T(8,128)(2,1)S(1)}, u32[]{:S(2)}, u32[]{:S(2)}) %collective-permute-start.15) | collective-permute-done | bytes 307232 | tf_op jit(solution)/shard_map/ppermute | solution.py:71
  70.6 6.8 %collective-permute-done.6.rest_6_.rest_22_ = bf16[256,640]{1,0:T(8,128)(2,1)S(1)} collective-permute-done((bf16[256,640]{1,0:T(8,128)(2,1)S(1)}, bf16[256,640]{1,0:T(8,128)(2,1)S(1)}, u32[]{:S(2)}, u32[]{:S(2)}) %collective-permute-start.6) | collective-permute-done | bytes 327712 | tf_op jit(solution)/shard_map/ppermute | solution.py:71
  80.5 10.1 %shard_map.215 = (f32[128,960]{1,0:T(8,128)}, bf16[128,960]{1,0:T(8,128)(2,1)}, bf16[128,960]{1,0:T(8,128)(2,1)}, bf16[5,384,64]{2,1,0:T(8,128)(2,1)}, bf16[5,12...) custom-call(s32[2]{0:T(128)} %pad_add_fusion.ids, ...), custom_call_target="tpu_custom_call" | custom-call | bytes 25500000 | tf_op jit(solution)/shard_map/pallas_call | solution.py:407
  90.7 1.8 collective-permute-start.18
  93.0 1.3 collective-permute-start.22
  94.8 5.4 %collective-permute-done.18.rest_2_ = bf16[128,960]{1,0:T(8,128)(2,1)S(1)} collective-permute-done((bf16[128,960]{1,0:T(8,128)(2,1)}, bf16[128,960]{1,0:T(8,128)(2,1)S(1)}, u32[]{:S(2)}, u32[]{:S(2)}) %collective-permute-start.18) | collective-permute-done | bytes 245792 | tf_op jit(solution)/shard_map/ppermute | solution.py:71
  100.1 6.1 %collective-permute-done.20.rest_4_ = bf16[128,960]{1,0:T(8,128)(2,1)S(1)} collective-permute-done((bf16[128,960]{1,0:T(8,128)(2,1)}, bf16[128,960]{1,0:T(8,128)(2,1)S(1)}, u32[]{:S(2)}, u32[]{:S(2)}) %collective-permute-start.20) | collective-permute-done | bytes 245792 | tf_op jit(solution)/shard_map/ppermute | solution.py:71
  108.6 11.7 %shard_map.218 = (f32[4,128,960]{2,1,0:T(8,128)}, bf16[512,960]{1,0:T(8,128)(2,1)}, bf16[1024,640]{1,0:T(8,128)(2,1)}, bf16[1024,320]{1,0:T(8,128)(2,1)}) custom-call(bf16[128,960]{1,0:T(8,128)(2,1)} %get-tuple-element.60.rest_0_, bf16[128,960]{1,0:T(8,128)(2,1)} %copy-done.22, bf16[128,960]{1,0:T(8,128)(2,1)} %copy-done.18, bf16[128,960]{1,0:T(8,128)(2,1)} %copy-done.23, ...), custom_call_target="tpu_custom_call" | custom-call | bytes 27000000 | tf_op jit(solution)/shard_map/pallas_call | solution.py:407
  120.3 1.5 copy.31
  121.9 2.4 collective-permute-done.33
  124.4 1.3 copy.32.odd_ref
  125.7 2.9 %shard_map.219 = (f32[128,960]{1,0:T(8,128)}, bf16[128,960]{1,0:T(8,128)(2,1)}, bf16[128,960]{1,0:T(8,128)(2,1)}, bf16[128,960]{1,0:T(8,128)(2,1)}) custom-call(f32[4,128,960]{2,1,0:T(8,128)} %get-tuple-element.65.even_ref, bf16[512,960]{1,0:T(8,128)(2,1)} %copy.32.odd_ref), custom_call_target="tpu_custom_call" | custom-call | bytes 3000000 | tf_op jit(solution)/shard_map/pallas_call | solution.py:407
  128.6 11.3 %shard_map.220 = (bf16[1440,640]{1,0:T(8,128)(2,1)}, f32[4,128,960]{2,1,0:T(8,128)}, bf16[512,960]{1,0:T(8,128)(2,1)}) custom-call(bf16[128,960]{1,0:T(8,128)(2,1)} %get-tuple-element.60.rest_0_, bf16[128,960]{1,0:T(8,128)(2,1)} %copy-done.22, bf16[128,960]{1,0:T(8,128)(2,1)} %copy-done.18, bf16[128,960]{1,0:T(8,128)(2,1)} %copy-done.23, ...), custom_call_target="tpu_custom_call" | custom-call | bytes 27000000 | tf_op jit(solution)/shard_map/pallas_call | solution.py:407
  142.2 2.3 collective-permute-start.40
  144.4 5.7 %collective-permute-done.36.rest_2_ = bf16[128,960]{1,0:T(8,128)(2,1)S(1)} collective-permute-done((bf16[128,960]{1,0:T(8,128)(2,1)S(1)}, bf16[128,960]{1,0:T(8,128)(2,1)S(1)}, u32[]{:S(2)}, u32[]{:S(2)}) %collective-permute-start.36) | collective-permute-done | bytes 245792 | tf_op jit(solution)/shard_map/ppermute | solution.py:71
  150.1 4.9 %collective-permute-done.38.rest_4_ = bf16[128,960]{1,0:T(8,128)(2,1)S(1)} collective-permute-done((bf16[128,960]{1,0:T(8,128)(2,1)S(1)}, bf16[128,960]{1,0:T(8,128)(2,1)S(1)}, u32[]{:S(2)}, u32[]{:S(2)}) %collective-permute-start.38) | collective-permute-done | bytes 245792 | tf_op jit(solution)/shard_map/ppermute | solution.py:71
  155.5 1.7 collective-permute-start.43
  158.8 1.2 collective-permute-start.47
  159.9 1.7 collective-permute-start.49
  161.7 3.3 %collective-permute-done.43.rest_10_ = bf16[128,960]{1,0:T(8,128)(2,1)} collective-permute-done((bf16[128,960]{1,0:T(8,128)(2,1)}, bf16[128,960]{1,0:T(8,128)(2,1)}, u32[]{:S(2)}, u32[]{:S(2)}) %collective-permute-start.43) | collective-permute-done | bytes 245792 | tf_op jit(solution)/shard_map/ppermute | solution.py:71
  165.8 5.8 %collective-permute-done.45.rest_12_ = bf16[128,960]{1,0:T(8,128)(2,1)} collective-permute-done((bf16[128,960]{1,0:T(8,128)(2,1)}, bf16[128,960]{1,0:T(8,128)(2,1)}, u32[]{:S(2)}, u32[]{:S(2)}) %collective-permute-start.45) | collective-permute-done | bytes 245792 | tf_op jit(solution)/shard_map/ppermute | solution.py:71
  171.6 4.6 %collective-permute-done.49.rest_1_ = bf16[128,960]{1,0:T(8,128)(2,1)} collective-permute-done((bf16[128,960]{1,0:T(8,128)(2,1)}, bf16[128,960]{1,0:T(8,128)(2,1)}, u32[]{:S(2)}, u32[]{:S(2)}) %collective-permute-start.49) | collective-permute-done | bytes 245792 | tf_op jit(solution)/shard_map/ppermute | solution.py:71
  176.3 6.1 %collective-permute-done.50.rest_2_ = bf16[128,960]{1,0:T(8,128)(2,1)} collective-permute-done((bf16[128,960]{1,0:T(8,128)(2,1)}, bf16[128,960]{1,0:T(8,128)(2,1)}, u32[]{:S(2)}, u32[]{:S(2)}) %collective-permute-start.50) | collective-permute-done | bytes 245792 | tf_op jit(solution)/shard_map/ppermute | solution.py:71
  182.9 12.1 %shard_map.221 = (bf16[80,640]{1,0:T(8,128)(2,1)}, bf16[80,640]{1,0:T(8,128)(2,1)}, bf16[80,640]{1,0:T(8,128)(2,1)}, bf16[80,640]{1,0:T(8,128)(2,1)}, bf16[80,64...) custom-call(s32[2]{0:T(128)} %pad_add_fusion.ids, ...), custom_call_target="tpu_custom_call" | custom-call | bytes 31500000 | tf_op jit(solution)/shard_map/pallas_call | solution.py:407
  195.6 1.4 collective-permute-start.54
  197.4 1.2 collective-permute-start.56
  198.7 2.5 collective-permute-done.53.rest_18_
  201.2 1.1 collective-permute-start.57
  204.0 3.5 %collective-permute-done.57.rest_22_ = bf16[80,640]{1,0:T(8,128)(2,1)} collective-permute-done((bf16[80,640]{1,0:T(8,128)(2,1)}, bf16[80,640]{1,0:T(8,128)(2,1)}, u32[]{:S(2)}, u32[]{:S(2)}) %collective-permute-start.57) | collective-permute-done | bytes 102432 | tf_op jit(solution)/shard_map/ppermute | solution.py:71
  207.5 1.3 collective-permute-done.58.rest_23_
  208.8 6.2 %shard_map.222 = (f32[336,240]{1,0:T(8,128)}, bf16[336,240]{1,0:T(8,128)(2,1)}, bf16[336,240]{1,0:T(8,128)(2,1)}, bf16[336,240]{1,0:T(8,128)(2,1)}) custom-call(s32[2]{0:T(128)} %pad_add_fusion.ids, bf16[128,960]{1,0:T(8,128)(2,1)} %bitcast.39, bf16[128,960]{1,0:T(8,128)(2,1)} %copy-done.32, bf16[128,960]{1,0:T(8,128)(2,1)} %copy-done.29, ...), custom_call_target="tpu_custom_call" | custom-call | bytes 13500000 | tf_op jit(solution)/shard_map/pallas_call | solution.py:407
  215.1 3.2 %collective-permute-start.63 = (bf16[336,240]{1,0:T(8,128)(2,1)}, bf16[336,240]{1,0:T(8,128)(2,1)}, u32[]{:S(2)}, u32[]{:S(2)}) collective-permute-start(bf16[336,240]{1,0:T(8,128)(2,1)} %get-tuple-element.94), channel_id=1, source_target_pairs={{0,2},{1,3},{2,0},{3,1},{4,6},{5,7},{6,4},{7,5},{8,10},{9,11},{10,... | collective-permute-start | bytes 483848 | tf_op jit(solution)/shard_map/ppermute | solution.py:71
  218.5 4.3 %collective-permute-done.62.a_ref = bf16[336,240]{1,0:T(8,128)(2,1)} collective-permute-done((bf16[336,240]{1,0:T(8,128)(2,1)}, bf16[336,240]{1,0:T(8,128)(2,1)}, u32[]{:S(2)}, u32[]{:S(2)}) %collective-permute-start.62) | collective-permute-done | bytes 161312 | tf_op jit(solution)/shard_map/ppermute | solution.py:71
  222.8 7.9 %collective-permute-done.63.b_ref = bf16[336,240]{1,0:T(8,128)(2,1)} collective-permute-done((bf16[336,240]{1,0:T(8,128)(2,1)}, bf16[336,240]{1,0:T(8,128)(2,1)}, u32[]{:S(2)}, u32[]{:S(2)}) %collective-permute-start.63) | collective-permute-done | bytes 161312 | tf_op jit(solution)/shard_map/ppermute | solution.py:71
  230.7 3.6 %collective-permute-done.64.c_ref = bf16[336,240]{1,0:T(8,128)(2,1)} collective-permute-done((bf16[336,240]{1,0:T(8,128)(2,1)}, bf16[336,240]{1,0:T(8,128)(2,1)}, u32[]{:S(2)}, u32[]{:S(2)}) %collective-permute-start.64) | collective-permute-done | bytes 161312 | tf_op jit(solution)/shard_map/ppermute | solution.py:71
  234.3 2.0 shard_map.225
  236.3 2.3 copy.35.odd_ref
  238.6 3.0 %shard_map.223 = (f32[128,960]{1,0:T(8,128)}, bf16[128,960]{1,0:T(8,128)(2,1)}, bf16[128,960]{1,0:T(8,128)(2,1)}, bf16[128,960]{1,0:T(8,128)(2,1)}) custom-call(f32[4,128,960]{2,1,0:T(8,128)} %get-tuple-element.68.even_ref, bf16[512,960]{1,0:T(8,128)(2,1)} %copy.35.odd_ref, f32[336,240]{1,0:T(8,128)} %get-tuple-element.87.rest_0_.own_ref), custom_call_target="tpu_custom_call" | custom-call | bytes 3000000 | tf_op jit(solution)/shard_map/pallas_call | solution.py:407
  242.5 1.0 collective-permute-start.60
  243.5 1.5 collective-permute-start.61
  245.0 1.2 slice_bitcast_fusion
  246.2 2.1 shard_map.226
  248.3 4.3 %collective-permute-start.65 = (bf16[120,320]{1,0:T(8,128)(2,1)}, bf16[120,320]{1,0:T(8,128)(2,1)S(1)}, u32[]{:S(2)}, u32[]{:S(2)}) collective-permute-start(bf16[120,320]{1,0:T(8,128)(2,1)} %get-tuple-element.104), channel_id=1, source_target_pairs={{0,0},{8,1},{16,2},{24,3},{4,4},{12,5},{20,6},{28,7},{1,8},{9,9},{... | collective-permute-start | bytes 230408 | tf_op jit(solution)/shard_map/ppermute | solution.py:1039
  252.7 1.2 slice_bitcast_fusion.1
  253.9 9.6 %collective-permute-done.61.c_ref = bf16[128,960]{1,0:T(8,128)(2,1)S(1)} collective-permute-done((bf16[128,960]{1,0:T(8,128)(2,1)}, bf16[128,960]{1,0:T(8,128)(2,1)S(1)}, u32[]{:S(2)}, u32[]{:S(2)}) %collective-permute-start.61) | collective-permute-done | bytes 245792 | tf_op jit(solution)/shard_map/ppermute | solution.py:71
  264.2 2.3 shard_map.224
  267.8 1.8 shard_map.227
  (188 shorter events, 27.2 us)
Async XLA Ops:
  7.2 101.4 %all-gather.2.cloned.1.call-start = ((), (), s32[]{:S(2)}) async-start(), calls=%async_computation.1 | async-start | bytes 2304000 | tf_op jit(solution)/shard_map/all_gather | solution.py:904
  9.0 10.3 %collective-permute-start = (bf16[120,640]{1,0:T(8,128)(2,1)}, bf16[120,640]{1,0:T(8,128)(2,1)S(1)}, u32[]{:S(2)}, u32[]{:S(2)}) collective-permute-start(bf16[120,640]{1,0:T(8,128)(2,1)} %shard_map.212.own_ref._), channel_id=1, source_target_pairs={{0,1},{1,0},{2,3},{3,2},{4,5},{5,4},{6,7},{7,6},{8,9},{9,8},{10,11... | collective-permute-start | bytes 460808 | tf_op jit(solution)/shard_map/ppermute | solution.py:71
  9.5 17.7 %collective-permute-start.8 = (bf16[120,640]{1,0:T(8,128)(2,1)}, bf16[120,640]{1,0:T(8,128)(2,1)S(1)}, u32[]{:S(2)}, u32[]{:S(2)}) collective-permute-start(bf16[120,640]{1,0:T(8,128)(2,1)} %shard_map.212.own_ref._), channel_id=1, source_target_pairs={{0,2},{1,3},{2,0},{3,1},{4,6},{5,7},{6,4},{7,5},{8,10},{9,11},{10,... | collective-permute-start | bytes 460808 | tf_op jit(solution)/shard_map/ppermute | solution.py:71
  12.1 18.4 %collective-permute-start.9 = (bf16[120,640]{1,0:T(8,128)(2,1)}, bf16[120,640]{1,0:T(8,128)(2,1)S(1)}, u32[]{:S(2)}, u32[]{:S(2)}) collective-permute-start(bf16[120,640]{1,0:T(8,128)(2,1)} %shard_map.212.own_ref._), channel_id=1, source_target_pairs={{0,3},{1,2},{2,1},{3,0},{4,7},{5,6},{6,5},{7,4},{8,11},{9,10},{10,... | collective-permute-start | bytes 460808 | tf_op jit(solution)/shard_map/ppermute | solution.py:71
  14.9 19.0 %collective-permute-start.31 = (bf16[120,320]{1,0:T(8,128)(2,1)}, bf16[120,320]{1,0:T(8,128)(2,1)}, u32[]{:S(2)}, u32[]{:S(2)}) collective-permute-start(bf16[120,320]{1,0:T(8,128)(2,1)} %get-tuple-element.61), channel_id=1, source_target_pairs={{0,0},{1,8},{2,16},{3,24},{4,4},{5,12},{6,20},{7,28},{8,1},{9,9},{... | collective-permute-start | bytes 230408 | tf_op jit(solution)/shard_map/ppermute | solution.py:896
  19.3 14.7 %collective-permute-start.32 = (bf16[120,320]{1,0:T(8,128)(2,1)}, bf16[120,320]{1,0:T(8,128)(2,1)}, u32[]{:S(2)}, u32[]{:S(2)}) collective-permute-start(bf16[120,320]{1,0:T(8,128)(2,1)} %get-tuple-element.62), channel_id=1, source_target_pairs={{0,4},{1,12},{2,20},{3,28},{4,0},{5,8},{6,16},{7,24},{8,5},{9,13},... | collective-permute-start | bytes 230408 | tf_op jit(solution)/shard_map/ppermute | solution.py:897
  36.1 210.1 %reduce-scatter.4.cloned.1.call-start = ((), (), s32[]{:S(2)}) async-start(), calls=%async_computation.2 | async-start | bytes 2304000
  36.1 17.0 %collective-permute-start.13 = (bf16[240,640]{1,0:T(8,128)(2,1)}, bf16[240,640]{1,0:T(8,128)(2,1)S(1)}, u32[]{:S(2)}, u32[]{:S(2)}) collective-permute-start(bf16[240,640]{1,0:T(8,128)(2,1)} %shard_map.214.rest_8_._.rest_24_), channel_id=1, source_target_pairs={{0,16},{4,20},{8,24},{12,28},{16,0},{20,4},{24,8},{28,12},{1,17},{... | collective-permute-start | bytes 921608 | tf_op jit(solution)/shard_map/ppermute | solution.py:71
  37.7 9.3 %collective-permute-start.25 = (bf16[128,960]{1,0:T(8,128)(2,1)S(1)}, bf16[128,960]{1,0:T(8,128)(2,1)}, u32[]{:S(2)}, u32[]{:S(2)}) collective-permute-start(bf16[128,960]{1,0:T(8,128)(2,1)S(1)} %bitcast.30), channel_id=1, source_target_pairs={{0,8},{4,12},{8,0},{12,4},{16,24},{20,28},{24,16},{28,20},{1,9},{5... | collective-permute-start | bytes 737288 | tf_op jit(solution)/shard_map/ppermute | solution.py:71
  39.3 13.0 %collective-permute-start.27 = (bf16[128,960]{1,0:T(8,128)(2,1)S(1)}, bf16[128,960]{1,0:T(8,128)(2,1)}, u32[]{:S(2)}, u32[]{:S(2)}) collective-permute-start(bf16[128,960]{1,0:T(8,128)(2,1)S(1)} %bitcast.31), channel_id=1, source_target_pairs={{0,16},{4,20},{8,24},{12,28},{16,0},{20,4},{24,8},{28,12},{1,17},{... | collective-permute-start | bytes 737288 | tf_op jit(solution)/shard_map/ppermute | solution.py:71
  40.1 21.4 %collective-permute-start.2 = (bf16[256,640]{1,0:T(8,128)(2,1)S(1)}, bf16[256,640]{1,0:T(8,128)(2,1)S(1)}, u32[]{:S(2)}, u32[]{:S(2)}) collective-permute-start(bf16[256,640]{1,0:T(8,128)(2,1)S(1)} %copy-done), channel_id=1, source_target_pairs={{0,8},{4,12},{8,0},{12,4},{16,24},{20,28},{24,16},{28,20},{1,9},{5... | collective-permute-start | bytes 983048 | tf_op jit(solution)/shard_map/ppermute | solution.py:71
  41.4 20.6 %collective-permute-start.4 = (bf16[256,640]{1,0:T(8,128)(2,1)S(1)}, bf16[256,640]{1,0:T(8,128)(2,1)S(1)}, u32[]{:S(2)}, u32[]{:S(2)}) collective-permute-start(bf16[256,640]{1,0:T(8,128)(2,1)S(1)} %copy-done), channel_id=1, source_target_pairs={{0,16},{4,20},{8,24},{12,28},{16,0},{20,4},{24,8},{28,12},{1,17},{... | collective-permute-start | bytes 983048 | tf_op jit(solution)/shard_map/ppermute | solution.py:71
  47.1 15.5 %collective-permute-start.1 = (bf16[256,640]{1,0:T(8,128)(2,1)S(1)}, bf16[256,640]{1,0:T(8,128)(2,1)S(1)}, u32[]{:S(2)}, u32[]{:S(2)}) collective-permute-start(bf16[256,640]{1,0:T(8,128)(2,1)S(1)} %copy-done), channel_id=1, source_target_pairs={{0,4},{4,0},{8,12},{12,8},{16,20},{20,16},{24,28},{28,24},{1,5},{5... | collective-permute-start | bytes 983048 | tf_op jit(solution)/shard_map/ppermute | solution.py:71
  52.3 9.0 %collective-permute-start.11 = (bf16[240,640]{1,0:T(8,128)(2,1)S(1)}, bf16[240,640]{1,0:T(8,128)(2,1)S(1)}, u32[]{:S(2)}, u32[]{:S(2)}) collective-permute-start(bf16[240,640]{1,0:T(8,128)(2,1)S(1)} %copy-done.1), channel_id=1, source_target_pairs={{0,8},{4,12},{8,0},{12,4},{16,24},{20,28},{24,16},{28,20},{1,9},{5... | collective-permute-start | bytes 921608 | tf_op jit(solution)/shard_map/ppermute | solution.py:71
  53.1 8.4 %collective-permute-start.10 = (bf16[240,640]{1,0:T(8,128)(2,1)S(1)}, bf16[240,640]{1,0:T(8,128)(2,1)S(1)}, u32[]{:S(2)}, u32[]{:S(2)}) collective-permute-start(bf16[240,640]{1,0:T(8,128)(2,1)S(1)} %copy-done.1), channel_id=1, source_target_pairs={{0,4},{4,0},{8,12},{12,8},{16,20},{20,16},{24,28},{28,24},{1,5},{5... | collective-permute-start | bytes 921608 | tf_op jit(solution)/shard_map/ppermute | solution.py:71
  61.2 8.2 %collective-permute-start.15 = (bf16[240,640]{1,0:T(8,128)(2,1)S(1)}, bf16[240,640]{1,0:T(8,128)(2,1)S(1)}, u32[]{:S(2)}, u32[]{:S(2)}) collective-permute-start(bf16[240,640]{1,0:T(8,128)(2,1)S(1)} %collective-permute-done.13.rest_12_.rest_28_), channel_id=1, source_target_pairs={{0,8},{4,12},{8,0},{12,4},{16,24},{20,28},{24,16},{28,20},{1,9},{5... | collective-permute-start | bytes 921608 | tf_op jit(solution)/shard_map/ppermute | solution.py:71
  61.5 8.4 %collective-permute-start.14 = (bf16[240,640]{1,0:T(8,128)(2,1)S(1)}, bf16[240,640]{1,0:T(8,128)(2,1)S(1)}, u32[]{:S(2)}, u32[]{:S(2)}) collective-permute-start(bf16[240,640]{1,0:T(8,128)(2,1)S(1)} %collective-permute-done.13.rest_12_.rest_28_), channel_id=1, source_target_pairs={{0,4},{4,0},{8,12},{12,8},{16,20},{20,16},{24,28},{28,24},{1,5},{5... | collective-permute-start | bytes 921608 | tf_op jit(solution)/shard_map/ppermute | solution.py:71
  61.5 8.5 %collective-permute-start.12 = (bf16[240,640]{1,0:T(8,128)(2,1)S(1)}, bf16[240,640]{1,0:T(8,128)(2,1)S(1)}, u32[]{:S(2)}, u32[]{:S(2)}) collective-permute-start(bf16[240,640]{1,0:T(8,128)(2,1)S(1)} %collective-permute-done.11.rest_10_.rest_26_), channel_id=1, source_target_pairs={{0,4},{4,0},{8,12},{12,8},{16,20},{20,16},{24,28},{28,24},{1,5},{5... | collective-permute-start | bytes 921608 | tf_op jit(solution)/shard_map/ppermute | solution.py:71
  62.0 15.3 %collective-permute-start.6 = (bf16[256,640]{1,0:T(8,128)(2,1)S(1)}, bf16[256,640]{1,0:T(8,128)(2,1)S(1)}, u32[]{:S(2)}, u32[]{:S(2)}) collective-permute-start(bf16[256,640]{1,0:T(8,128)(2,1)S(1)} %collective-permute-done.2.rest_2_.rest_18_), channel_id=1, source_target_pairs={{0,16},{4,20},{8,24},{12,28},{16,0},{20,4},{24,8},{28,12},{1,17},{... | collective-permute-start | bytes 983048 | tf_op jit(solution)/shard_map/ppermute | solution.py:71
  62.5 14.8 %collective-permute-start.3 = (bf16[256,640]{1,0:T(8,128)(2,1)S(1)}, bf16[256,640]{1,0:T(8,128)(2,1)S(1)}, u32[]{:S(2)}, u32[]{:S(2)}) collective-permute-start(bf16[256,640]{1,0:T(8,128)(2,1)S(1)} %collective-permute-done.2.rest_2_.rest_18_), channel_id=1, source_target_pairs={{0,4},{4,0},{8,12},{12,8},{16,20},{20,16},{24,28},{28,24},{1,5},{5... | collective-permute-start | bytes 983048 | tf_op jit(solution)/shard_map/ppermute | solution.py:71
  69.4 23.1 %collective-permute-start.29 = (bf16[128,960]{1,0:T(8,128)(2,1)S(1)}, bf16[128,960]{1,0:T(8,128)(2,1)}, u32[]{:S(2)}, u32[]{:S(2)}) collective-permute-start(bf16[128,960]{1,0:T(8,128)(2,1)S(1)} %bitcast.32), channel_id=1, source_target_pairs={{0,24},{4,28},{8,16},{12,20},{16,8},{20,12},{24,0},{28,4},{1,25},{... | collective-permute-start | bytes 737288 | tf_op jit(solution)/shard_map/ppermute | solution.py:71
  69.9 23.1 %collective-permute-start.24 = (bf16[128,960]{1,0:T(8,128)(2,1)S(1)}, bf16[128,960]{1,0:T(8,128)(2,1)}, u32[]{:S(2)}, u32[]{:S(2)}) collective-permute-start(bf16[128,960]{1,0:T(8,128)(2,1)S(1)} %bitcast.33), channel_id=1, source_target_pairs={{0,4},{4,0},{8,12},{12,8},{16,20},{20,16},{24,28},{28,24},{1,5},{5... | collective-permute-start | bytes 737288 | tf_op jit(solution)/shard_map/ppermute | solution.py:71
  70.1 9.0 %collective-permute-start.5 = (bf16[256,640]{1,0:T(8,128)(2,1)S(1)}, bf16[256,640]{1,0:T(8,128)(2,1)S(1)}, u32[]{:S(2)}, u32[]{:S(2)}) collective-permute-start(bf16[256,640]{1,0:T(8,128)(2,1)S(1)} %collective-permute-done.4.rest_4_.rest_20_), channel_id=1, source_target_pairs={{0,4},{4,0},{8,12},{12,8},{16,20},{20,16},{24,28},{28,24},{1,5},{5... | collective-permute-start | bytes 983048 | tf_op jit(solution)/shard_map/ppermute | solution.py:71
  79.1 15.2 %collective-permute-start.26 = (bf16[128,960]{1,0:T(8,128)(2,1)}, bf16[128,960]{1,0:T(8,128)(2,1)}, u32[]{:S(2)}, u32[]{:S(2)}) collective-permute-start(bf16[128,960]{1,0:T(8,128)(2,1)} %collective-permute-done.25.rest_10_), channel_id=1, source_target_pairs={{0,4},{4,0},{8,12},{12,8},{16,20},{20,16},{24,28},{28,24},{1,5},{5... | collective-permute-start | bytes 737288 | tf_op jit(solution)/shard_map/ppermute | solution.py:71
  79.2 15.1 %collective-permute-start.28 = (bf16[128,960]{1,0:T(8,128)(2,1)}, bf16[128,960]{1,0:T(8,128)(2,1)}, u32[]{:S(2)}, u32[]{:S(2)}) collective-permute-start(bf16[128,960]{1,0:T(8,128)(2,1)} %collective-permute-done.27.rest_12_), channel_id=1, source_target_pairs={{0,4},{4,0},{8,12},{12,8},{16,20},{20,16},{24,28},{28,24},{1,5},{5... | collective-permute-start | bytes 737288 | tf_op jit(solution)/shard_map/ppermute | solution.py:71
  90.7 9.4 %collective-permute-start.18 = (bf16[128,960]{1,0:T(8,128)(2,1)}, bf16[128,960]{1,0:T(8,128)(2,1)S(1)}, u32[]{:S(2)}, u32[]{:S(2)}) collective-permute-start(bf16[128,960]{1,0:T(8,128)(2,1)} %get-tuple-element.60.rest_0_), channel_id=1, source_target_pairs={{0,8},{4,12},{8,0},{12,4},{16,24},{20,28},{24,16},{28,20},{1,9},{5... | collective-permute-start | bytes 737288 | tf_op jit(solution)/shard_map/ppermute | solution.py:71
  92.5 13.8 %collective-permute-start.20 = (bf16[128,960]{1,0:T(8,128)(2,1)}, bf16[128,960]{1,0:T(8,128)(2,1)S(1)}, u32[]{:S(2)}, u32[]{:S(2)}) collective-permute-start(bf16[128,960]{1,0:T(8,128)(2,1)} %get-tuple-element.60.rest_0_), channel_id=1, source_target_pairs={{0,16},{4,20},{8,24},{12,28},{16,0},{20,4},{24,8},{28,12},{1,17},{... | collective-permute-start | bytes 737288 | tf_op jit(solution)/shard_map/ppermute | solution.py:71
  93.0 13.3 %collective-permute-start.22 = (bf16[128,960]{1,0:T(8,128)(2,1)}, bf16[128,960]{1,0:T(8,128)(2,1)S(1)}, u32[]{:S(2)}, u32[]{:S(2)}) collective-permute-start(bf16[128,960]{1,0:T(8,128)(2,1)} %get-tuple-element.60.rest_0_), channel_id=1, source_target_pairs={{0,24},{4,28},{8,16},{12,20},{16,8},{20,12},{24,0},{28,4},{1,25},{... | collective-permute-start | bytes 737288 | tf_op jit(solution)/shard_map/ppermute | solution.py:71
  94.3 12.6 %collective-permute-start.30 = (bf16[128,960]{1,0:T(8,128)(2,1)}, bf16[128,960]{1,0:T(8,128)(2,1)S(1)}, u32[]{:S(2)}, u32[]{:S(2)}) collective-permute-start(bf16[128,960]{1,0:T(8,128)(2,1)} %collective-permute-done.29.rest_14_), channel_id=1, source_target_pairs={{0,4},{4,0},{8,12},{12,8},{16,20},{20,16},{24,28},{28,24},{1,5},{5... | collective-permute-start | bytes 737288 | tf_op jit(solution)/shard_map/ppermute | solution.py:71
  94.3 12.5 %collective-permute-start.17 = (bf16[128,960]{1,0:T(8,128)(2,1)}, bf16[128,960]{1,0:T(8,128)(2,1)S(1)}, u32[]{:S(2)}, u32[]{:S(2)}) collective-permute-start(bf16[128,960]{1,0:T(8,128)(2,1)} %get-tuple-element.60.rest_0_), channel_id=1, source_target_pairs={{0,4},{4,0},{8,12},{12,8},{16,20},{20,16},{24,28},{28,24},{1,5},{5... | collective-permute-start | bytes 737288 | tf_op jit(solution)/shard_map/ppermute | solution.py:71
  100.1 6.7 %collective-permute-start.19 = (bf16[128,960]{1,0:T(8,128)(2,1)S(1)}, bf16[128,960]{1,0:T(8,128)(2,1)S(1)}, u32[]{:S(2)}, u32[]{:S(2)}) collective-permute-start(bf16[128,960]{1,0:T(8,128)(2,1)S(1)} %collective-permute-done.18.rest_2_), channel_id=1, source_target_pairs={{0,4},{4,0},{8,12},{12,8},{16,20},{20,16},{24,28},{28,24},{1,5},{5... | collective-permute-start | bytes 737288 | tf_op jit(solution)/shard_map/ppermute | solution.py:71
  121.7 2.6 collective-permute-start.33
  140.9 9.1 %collective-permute-start.36 = (bf16[128,960]{1,0:T(8,128)(2,1)S(1)}, bf16[128,960]{1,0:T(8,128)(2,1)S(1)}, u32[]{:S(2)}, u32[]{:S(2)}) collective-permute-start(bf16[128,960]{1,0:T(8,128)(2,1)S(1)} %bitcast.40), channel_id=1, source_target_pairs={{0,8},{4,12},{8,0},{12,4},{16,24},{20,28},{24,16},{28,20},{1,9},{5... | collective-permute-start | bytes 737288 | tf_op jit(solution)/shard_map/ppermute | solution.py:71
  141.3 13.7 %collective-permute-start.38 = (bf16[128,960]{1,0:T(8,128)(2,1)S(1)}, bf16[128,960]{1,0:T(8,128)(2,1)S(1)}, u32[]{:S(2)}, u32[]{:S(2)}) collective-permute-start(bf16[128,960]{1,0:T(8,128)(2,1)S(1)} %bitcast.41), channel_id=1, source_target_pairs={{0,16},{4,20},{8,24},{12,28},{16,0},{20,4},{24,8},{28,12},{1,17},{... | collective-permute-start | bytes 737288 | tf_op jit(solution)/shard_map/ppermute | solution.py:71
  142.2 12.8 %collective-permute-start.40 = (bf16[128,960]{1,0:T(8,128)(2,1)S(1)}, bf16[128,960]{1,0:T(8,128)(2,1)S(1)}, u32[]{:S(2)}, u32[]{:S(2)}) collective-permute-start(bf16[128,960]{1,0:T(8,128)(2,1)S(1)} %bitcast.42), channel_id=1, source_target_pairs={{0,24},{4,28},{8,16},{12,20},{16,8},{20,12},{24,0},{28,4},{1,25},{... | collective-permute-start | bytes 737288 | tf_op jit(solution)/shard_map/ppermute | solution.py:71
  144.4 12.7 %collective-permute-start.35 = (bf16[128,960]{1,0:T(8,128)(2,1)S(1)}, bf16[128,960]{1,0:T(8,128)(2,1)S(1)}, u32[]{:S(2)}, u32[]{:S(2)}) collective-permute-start(bf16[128,960]{1,0:T(8,128)(2,1)S(1)} %bitcast.43), channel_id=1, source_target_pairs={{0,4},{4,0},{8,12},{12,8},{16,20},{20,16},{24,28},{28,24},{1,5},{5... | collective-permute-start | bytes 737288 | tf_op jit(solution)/shard_map/ppermute | solution.py:71
  150.1 8.5 %collective-permute-start.37 = (bf16[128,960]{1,0:T(8,128)(2,1)S(1)}, bf16[128,960]{1,0:T(8,128)(2,1)S(1)}, u32[]{:S(2)}, u32[]{:S(2)}) collective-permute-start(bf16[128,960]{1,0:T(8,128)(2,1)S(1)} %collective-permute-done.36.rest_2_), channel_id=1, source_target_pairs={{0,4},{4,0},{8,12},{12,8},{16,20},{20,16},{24,28},{28,24},{1,5},{5... | collective-permute-start | bytes 737288 | tf_op jit(solution)/shard_map/ppermute | solution.py:71
  155.0 3.8 %collective-permute-start.39 = (bf16[128,960]{1,0:T(8,128)(2,1)S(1)}, bf16[128,960]{1,0:T(8,128)(2,1)}, u32[]{:S(2)}, u32[]{:S(2)}) collective-permute-start(bf16[128,960]{1,0:T(8,128)(2,1)S(1)} %collective-permute-done.38.rest_4_), channel_id=1, source_target_pairs={{0,4},{4,0},{8,12},{12,8},{16,20},{20,16},{24,28},{28,24},{1,5},{5... | collective-permute-start | bytes 737288 | tf_op jit(solution)/shard_map/ppermute | solution.py:71
  155.0 4.9 %collective-permute-start.41 = (bf16[128,960]{1,0:T(8,128)(2,1)S(1)}, bf16[128,960]{1,0:T(8,128)(2,1)}, u32[]{:S(2)}, u32[]{:S(2)}) collective-permute-start(bf16[128,960]{1,0:T(8,128)(2,1)S(1)} %collective-permute-done.40.rest_6_), channel_id=1, source_target_pairs={{0,4},{4,0},{8,12},{12,8},{16,20},{20,16},{24,28},{28,24},{1,5},{5... | collective-permute-start | bytes 737288 | tf_op jit(solution)/shard_map/ppermute | solution.py:71
  155.5 9.5 %collective-permute-start.43 = (bf16[128,960]{1,0:T(8,128)(2,1)}, bf16[128,960]{1,0:T(8,128)(2,1)}, u32[]{:S(2)}, u32[]{:S(2)}) collective-permute-start(bf16[128,960]{1,0:T(8,128)(2,1)} %get-tuple-element.70.rest_8_), channel_id=1, source_target_pairs={{0,8},{4,12},{8,0},{12,4},{16,24},{20,28},{24,16},{28,20},{1,9},{5... | collective-permute-start | bytes 737288 | tf_op jit(solution)/shard_map/ppermute | solution.py:71
  157.2 14.4 %collective-permute-start.45 = (bf16[128,960]{1,0:T(8,128)(2,1)}, bf16[128,960]{1,0:T(8,128)(2,1)}, u32[]{:S(2)}, u32[]{:S(2)}) collective-permute-start(bf16[128,960]{1,0:T(8,128)(2,1)} %get-tuple-element.70.rest_8_), channel_id=1, source_target_pairs={{0,16},{4,20},{8,24},{12,28},{16,0},{20,4},{24,8},{28,12},{1,17},{... | collective-permute-start | bytes 737288 | tf_op jit(solution)/shard_map/ppermute | solution.py:71
  158.6 77.6 %collective-permute-start.34 = (bf16[512,960]{0,1:T(8,128)(2,1)S(1)}, bf16[512,960]{0,1:T(8,128)(2,1)}, u32[]{:S(2)}, u32[]{:S(2)}) collective-permute-start(bf16[512,960]{0,1:T(8,128)(2,1)S(1)} %copy.33), channel_id=1, source_target_pairs={{0,4},{4,0},{8,12},{12,8},{16,20},{20,16},{24,28},{28,24},{1,5},{5... | collective-permute-start | bytes 2949128 | tf_op jit(solution)/shard_map/ppermute | solution.py:71
  158.8 12.8 %collective-permute-start.47 = (bf16[128,960]{1,0:T(8,128)(2,1)}, bf16[128,960]{1,0:T(8,128)(2,1)}, u32[]{:S(2)}, u32[]{:S(2)}) collective-permute-start(bf16[128,960]{1,0:T(8,128)(2,1)} %get-tuple-element.70.rest_8_), channel_id=1, source_target_pairs={{0,24},{4,28},{8,16},{12,20},{16,8},{20,12},{24,0},{28,4},{1,25},{... | collective-permute-start | bytes 737288 | tf_op jit(solution)/shard_map/ppermute | solution.py:71
  159.9 16.3 %collective-permute-start.49 = (bf16[128,960]{1,0:T(8,128)(2,1)}, bf16[128,960]{1,0:T(8,128)(2,1)}, u32[]{:S(2)}, u32[]{:S(2)}) collective-permute-start(bf16[128,960]{1,0:T(8,128)(2,1)} %get-tuple-element.71), channel_id=1, source_target_pairs={{0,8},{4,12},{8,0},{12,4},{16,24},{20,28},{24,16},{28,20},{1,9},{5... | collective-permute-start | bytes 737288 | tf_op jit(solution)/shard_map/ppermute | solution.py:71
  165.0 17.4 %collective-permute-start.50 = (bf16[128,960]{1,0:T(8,128)(2,1)}, bf16[128,960]{1,0:T(8,128)(2,1)}, u32[]{:S(2)}, u32[]{:S(2)}) collective-permute-start(bf16[128,960]{1,0:T(8,128)(2,1)} %get-tuple-element.72), channel_id=1, source_target_pairs={{0,16},{4,20},{8,24},{12,28},{16,0},{20,4},{24,8},{28,12},{1,17},{... | collective-permute-start | bytes 737288 | tf_op jit(solution)/shard_map/ppermute | solution.py:71
  171.6 10.8 %collective-permute-start.51 = (bf16[128,960]{1,0:T(8,128)(2,1)}, bf16[128,960]{1,0:T(8,128)(2,1)}, u32[]{:S(2)}, u32[]{:S(2)}) collective-permute-start(bf16[128,960]{1,0:T(8,128)(2,1)} %get-tuple-element.73), channel_id=1, source_target_pairs={{0,24},{4,28},{8,16},{12,20},{16,8},{20,12},{24,0},{28,4},{1,25},{... | collective-permute-start | bytes 737288 | tf_op jit(solution)/shard_map/ppermute | solution.py:71
  171.6 23.4 %collective-permute-start.42 = (bf16[128,960]{1,0:T(8,128)(2,1)}, bf16[128,960]{1,0:T(8,128)(2,1)}, u32[]{:S(2)}, u32[]{:S(2)}) collective-permute-start(bf16[128,960]{1,0:T(8,128)(2,1)} %get-tuple-element.70.rest_8_), channel_id=1, source_target_pairs={{0,4},{4,0},{8,12},{12,8},{16,20},{20,16},{24,28},{28,24},{1,5},{5... | collective-permute-start | bytes 737288 | tf_op jit(solution)/shard_map/ppermute | solution.py:71
  176.3 18.8 %collective-permute-start.44 = (bf16[128,960]{1,0:T(8,128)(2,1)}, bf16[128,960]{1,0:T(8,128)(2,1)}, u32[]{:S(2)}, u32[]{:S(2)}) collective-permute-start(bf16[128,960]{1,0:T(8,128)(2,1)} %collective-permute-done.43.rest_10_), channel_id=1, source_target_pairs={{0,4},{4,0},{8,12},{12,8},{16,20},{20,16},{24,28},{28,24},{1,5},{5... | collective-permute-start | bytes 737288 | tf_op jit(solution)/shard_map/ppermute | solution.py:71
  182.3 13.2 %collective-permute-start.46 = (bf16[128,960]{1,0:T(8,128)(2,1)}, bf16[128,960]{1,0:T(8,128)(2,1)}, u32[]{:S(2)}, u32[]{:S(2)}) collective-permute-start(bf16[128,960]{1,0:T(8,128)(2,1)} %collective-permute-done.45.rest_12_), channel_id=1, source_target_pairs={{0,4},{4,0},{8,12},{12,8},{16,20},{20,16},{24,28},{28,24},{1,5},{5... | collective-permute-start | bytes 737288 | tf_op jit(solution)/shard_map/ppermute | solution.py:71
  182.3 14.6 %collective-permute-start.48 = (bf16[128,960]{1,0:T(8,128)(2,1)}, bf16[128,960]{1,0:T(8,128)(2,1)}, u32[]{:S(2)}, u32[]{:S(2)}) collective-permute-start(bf16[128,960]{1,0:T(8,128)(2,1)} %collective-permute-done.47.rest_14_), channel_id=1, source_target_pairs={{0,4},{4,0},{8,12},{12,8},{16,20},{20,16},{24,28},{28,24},{1,5},{5... | collective-permute-start | bytes 737288 | tf_op jit(solution)/shard_map/ppermute | solution.py:71
  195.1 6.1 %collective-permute-start.53 = (bf16[80,640]{1,0:T(8,128)(2,1)}, bf16[80,640]{1,0:T(8,128)(2,1)}, u32[]{:S(2)}, u32[]{:S(2)}) collective-permute-start(bf16[80,640]{1,0:T(8,128)(2,1)} %get-tuple-element.81), channel_id=1, source_target_pairs={{0,8},{4,12},{8,0},{12,4},{16,24},{20,28},{24,16},{28,20},{1,9},{5... | collective-permute-start | bytes 307208 | tf_op jit(solution)/shard_map/ppermute | solution.py:71
  195.6 6.8 %collective-permute-start.54 = (bf16[80,640]{1,0:T(8,128)(2,1)}, bf16[80,640]{1,0:T(8,128)(2,1)}, u32[]{:S(2)}, u32[]{:S(2)}) collective-permute-start(bf16[80,640]{1,0:T(8,128)(2,1)} %get-tuple-element.82), channel_id=1, source_target_pairs={{0,12},{4,8},{8,4},{12,0},{16,28},{20,24},{24,20},{28,16},{1,13},{... | collective-permute-start | bytes 307208 | tf_op jit(solution)/shard_map/ppermute | solution.py:71
  196.9 6.4 %collective-permute-start.55 = (bf16[80,640]{1,0:T(8,128)(2,1)}, bf16[80,640]{1,0:T(8,128)(2,1)}, u32[]{:S(2)}, u32[]{:S(2)}) collective-permute-start(bf16[80,640]{1,0:T(8,128)(2,1)} %get-tuple-element.83), channel_id=1, source_target_pairs={{0,16},{4,20},{8,24},{12,28},{16,0},{20,4},{24,8},{28,12},{1,17},{... | collective-permute-start | bytes 307208 | tf_op jit(solution)/shard_map/ppermute | solution.py:71
  197.4 6.6 %collective-permute-start.56 = (bf16[80,640]{1,0:T(8,128)(2,1)}, bf16[80,640]{1,0:T(8,128)(2,1)}, u32[]{:S(2)}, u32[]{:S(2)}) collective-permute-start(bf16[80,640]{1,0:T(8,128)(2,1)} %get-tuple-element.84), channel_id=1, source_target_pairs={{0,20},{4,16},{8,28},{12,24},{16,4},{20,0},{24,12},{28,8},{1,21},{... | collective-permute-start | bytes 307208 | tf_op jit(solution)/shard_map/ppermute | solution.py:71
  201.2 6.3 %collective-permute-start.57 = (bf16[80,640]{1,0:T(8,128)(2,1)}, bf16[80,640]{1,0:T(8,128)(2,1)}, u32[]{:S(2)}, u32[]{:S(2)}) collective-permute-start(bf16[80,640]{1,0:T(8,128)(2,1)} %get-tuple-element.85), channel_id=1, source_target_pairs={{0,24},{4,28},{8,16},{12,20},{16,8},{20,12},{24,0},{28,4},{1,25},{... | collective-permute-start | bytes 307208 | tf_op jit(solution)/shard_map/ppermute | solution.py:71
  202.4 6.3 %collective-permute-start.58 = (bf16[80,640]{1,0:T(8,128)(2,1)}, bf16[80,640]{1,0:T(8,128)(2,1)}, u32[]{:S(2)}, u32[]{:S(2)}) collective-permute-start(bf16[80,640]{1,0:T(8,128)(2,1)} %get-tuple-element.86), channel_id=1, source_target_pairs={{0,28},{4,24},{8,20},{12,16},{16,12},{20,8},{24,4},{28,0},{1,29},{... | collective-permute-start | bytes 307208 | tf_op jit(solution)/shard_map/ppermute | solution.py:71
  215.0 7.8 %collective-permute-start.62 = (bf16[336,240]{1,0:T(8,128)(2,1)}, bf16[336,240]{1,0:T(8,128)(2,1)}, u32[]{:S(2)}, u32[]{:S(2)}) collective-permute-start(bf16[336,240]{1,0:T(8,128)(2,1)} %get-tuple-element.93), channel_id=1, source_target_pairs={{0,1},{1,0},{2,3},{3,2},{4,5},{5,4},{6,7},{7,6},{8,9},{9,8},{10,11... | collective-permute-start | bytes 483848 | tf_op jit(solution)/shard_map/ppermute | solution.py:71
  215.1 15.6 %collective-permute-start.63 = (bf16[336,240]{1,0:T(8,128)(2,1)}, bf16[336,240]{1,0:T(8,128)(2,1)}, u32[]{:S(2)}, u32[]{:S(2)}) collective-permute-start(bf16[336,240]{1,0:T(8,128)(2,1)} %get-tuple-element.94), channel_id=1, source_target_pairs={{0,2},{1,3},{2,0},{3,1},{4,6},{5,7},{6,4},{7,5},{8,10},{9,11},{10,... | collective-permute-start | bytes 483848 | tf_op jit(solution)/shard_map/ppermute | solution.py:71
  218.2 16.0 %collective-permute-start.64 = (bf16[336,240]{1,0:T(8,128)(2,1)}, bf16[336,240]{1,0:T(8,128)(2,1)}, u32[]{:S(2)}, u32[]{:S(2)}) collective-permute-start(bf16[336,240]{1,0:T(8,128)(2,1)} %get-tuple-element.95), channel_id=1, source_target_pairs={{0,3},{1,2},{2,1},{3,0},{4,7},{5,6},{6,5},{7,4},{8,11},{9,10},{10,... | collective-permute-start | bytes 483848 | tf_op jit(solution)/shard_map/ppermute | solution.py:71
  241.5 12.4 %collective-permute-start.59 = (bf16[128,960]{1,0:T(8,128)(2,1)}, bf16[128,960]{1,0:T(8,128)(2,1)S(1)}, u32[]{:S(2)}, u32[]{:S(2)}) collective-permute-start(bf16[128,960]{1,0:T(8,128)(2,1)} %get-tuple-element.89), channel_id=1, source_target_pairs={{0,8},{4,12},{8,0},{12,4},{16,24},{20,28},{24,16},{28,20},{1,9},{5... | collective-permute-start | bytes 737288 | tf_op jit(solution)/shard_map/ppermute | solution.py:71
  242.5 11.4 %collective-permute-start.60 = (bf16[128,960]{1,0:T(8,128)(2,1)}, bf16[128,960]{1,0:T(8,128)(2,1)S(1)}, u32[]{:S(2)}, u32[]{:S(2)}) collective-permute-start(bf16[128,960]{1,0:T(8,128)(2,1)} %get-tuple-element.90), channel_id=1, source_target_pairs={{0,16},{4,20},{8,24},{12,28},{16,0},{20,4},{24,8},{28,12},{1,17},{... | collective-permute-start | bytes 737288 | tf_op jit(solution)/shard_map/ppermute | solution.py:71
  243.5 20.0 %collective-permute-start.61 = (bf16[128,960]{1,0:T(8,128)(2,1)}, bf16[128,960]{1,0:T(8,128)(2,1)S(1)}, u32[]{:S(2)}, u32[]{:S(2)}) collective-permute-start(bf16[128,960]{1,0:T(8,128)(2,1)} %get-tuple-element.91), channel_id=1, source_target_pairs={{0,24},{4,28},{8,16},{12,20},{16,8},{20,12},{24,0},{28,4},{1,25},{... | collective-permute-start | bytes 737288 | tf_op jit(solution)/shard_map/ppermute | solution.py:71
  248.3 18.3 %collective-permute-start.65 = (bf16[120,320]{1,0:T(8,128)(2,1)}, bf16[120,320]{1,0:T(8,128)(2,1)S(1)}, u32[]{:S(2)}, u32[]{:S(2)}) collective-permute-start(bf16[120,320]{1,0:T(8,128)(2,1)} %get-tuple-element.104), channel_id=1, source_target_pairs={{0,0},{8,1},{16,2},{24,3},{4,4},{12,5},{20,6},{28,7},{1,8},{9,9},{... | collective-permute-start | bytes 230408 | tf_op jit(solution)/shard_map/ppermute | solution.py:1039
  252.6 14.0 %collective-permute-start.66 = (bf16[120,320]{1,0:T(8,128)(2,1)}, bf16[120,320]{1,0:T(8,128)(2,1)S(1)}, u32[]{:S(2)}, u32[]{:S(2)}) collective-permute-start(bf16[120,320]{1,0:T(8,128)(2,1)} %get-tuple-element.105), channel_id=1, source_target_pairs={{4,0},{12,1},{20,2},{28,3},{0,4},{8,5},{16,6},{24,7},{5,8},{13,9},... | collective-permute-start | bytes 230408 | tf_op jit(solution)/shard_map/ppermute | solution.py:1040
  (46 other events, 378.7 us)
Sparse Core Ops, SparseCore 0:
  36.2 42.0 all-gather.1
  140.1 39.0 reduce-scatter.3

commit v3 on v2

--- a/solution.py
+++ b/solution.py
@@ -412,9 +412,24 @@
         scratch_shapes=list(scratch),
         compiler_params=pltpu.CompilerParams(vmem_limit_bytes=63 * 2**20),
         cost_estimate=pl.CostEstimate(
-            flops=0, bytes_accessed=int(micros * 3.0e6), transcendentals=0
+            flops=int(micros * 1.1e9), bytes_accessed=int(micros * 3.0e6), transcendentals=0
         ),
     )(*args)
+
+
+def after_all(values, *others):
+    count = len(values)
+    return pl.pallas_call(
+        lambda *refs: None,
+        out_shape=[shape(value.shape, value.dtype) for value in values],
+        in_specs=[pl.BlockSpec(memory_space=pl.ANY)] * (count + len(others)),
+        out_specs=[pl.BlockSpec(memory_space=pl.ANY)] * count,
+        input_output_aliases={i: i for i in range(count)},
+    )(*values, *others)
+
+
+def after(value, *others):
+    return after_all([value], *others)[0]
 
 
 def shape(dims, dtype):
@@ -449,28 +464,80 @@
     out_ref[...] = jnp.concatenate([qkv[:half], o[:half], o[half:], qkv[half:]], 1)
 
 
-def pack_down(ids, down_ref, _, p0_ref, p1_ref):
-    down = down_ref[...]
-    units = down.shape[1] // 2
-    first = down[:, :units].astype(F32)
-    second = down[:, units:].astype(F32)
-    even = (ids[0] % 2) == 0
-    p0_ref[...] = jnp.where(even, first, second).astype(BF16)
-    p1_ref[...] = jnp.where(even, second, first).astype(BF16)
-
-
-def pack_feed(ids, gate_ref, up_ref, r0_ref, r1_ref, _, out_ref):
+def pack_feed(gate_ref, up_ref, down_ref, _, out_ref):
     gate_up = jnp.concatenate([gate_ref[...], up_ref[...]], 0).astype(F32).T
-    even = (ids[0] % 2) == 0
-    r0 = r0_ref[...].astype(F32)
-    r1 = r1_ref[...].astype(F32)
-    joined = jnp.concatenate([jnp.where(even, r0, r1), jnp.where(even, r1, r0)], 1)
     rows = gate_up.shape[0]
     out_ref[:rows] = gate_up.astype(BF16)
-    out_ref[rows:] = joined.astype(BF16)
-
-
-def join_first(own_ref, got_ref, ag_ref, fg_ref, out_ref):
+    out_ref[rows:] = down_ref[...]
+
+
+def fold_block(block):
+    tail = jnp.concatenate([block[64:], jnp.zeros((8, 320), F32)], 0)
+    return jnp.concatenate([block[:64], tail], 1).astype(BF16)
+
+
+def unfold_block(both):
+    both = both.astype(F32)
+    return jnp.concatenate([both[:, :320], both[:56, 320:]], 0)
+
+
+def fill_exchange(outs, buffer, d):
+    outs[0][...] = fold_block(buffer[d])
+    outs[1][...] = fold_block(buffer[d ^ 1])
+    for i in (1, 2, 3):
+        outs[i + 1][:64] = fold_block(buffer[d ^ (2 * i)])
+        outs[i + 1][64:] = fold_block(buffer[d ^ (2 * i + 1)])
+
+
+def place_exchanged(refs, passed, d, buffer, convert):
+    buffer[d] = convert(refs[0][...])
+    buffer[d ^ 1] = convert(refs[1][...])
+    for i in (1, 2, 3):
+        buffer[d ^ (2 * i)] = convert(refs[i + 1][:64])
+        buffer[d ^ (2 * i + 1)] = convert(passed[i - 1][64:])
+
+
+def exchange_shapes():
+    return [shape((64, 640), BF16)] * 2 + [shape((128, 640), BF16)] * 3
+
+
+def exchange(blocks):
+    arrived = [blocks[0], send(blocks[1], "dp", 1)]
+    return arrived + [send(blocks[i + 1], "dp", 2 * i) for i in (1, 2, 3)]
+
+
+def split_down(ids, feed_ref, *rest):
+    outs, buffer = rest[-6:-1], rest[-1]
+    for i in range(8):
+        start = 360 * (i // 2) + 240
+        buffer[i] = feed_ref[start : start + 120, 320 * (i % 2) : 320 * (i % 2) + 320].astype(F32)
+    fill_exchange(outs, buffer, ids[0])
+
+
+def flatten_block(block):
+    return jnp.concatenate([block[:40], block[40:80], block[80:]], 1)
+
+
+def restore_block(rows):
+    return jnp.concatenate([rows[:, :320], rows[:, 320:640], rows[:, 640:960]], 0)
+
+
+def join_down(ids, own_ref, pair_ref, *rest):
+    others, passed_ref, out_ref, buffer = rest[:3], rest[3], rest[-2], rest[-1]
+    d = ids[0]
+    buffer[d] = restore_block(own_ref[...].astype(F32)[:40])
+    buffer[d ^ 1] = restore_block(pair_ref[...].astype(F32)[:40])
+    passed = passed_ref[...].astype(F32)
+    for i in (1, 2, 3):
+        buffer[d ^ (2 * i)] = restore_block(others[i - 1][128:].astype(F32)[:40])
+        buffer[d ^ (2 * i + 1)] = restore_block(passed[40 * (i - 1) : 40 * i])
+    for j in range(4):
+        both = jnp.concatenate([buffer[2 * j], buffer[2 * j + 1]], 1)
+        out_ref[120 * j : 120 * (j + 1), :] = both.astype(BF16)
+
+
+def join_lines(own_ref, got_ref, ag_ref, fg_ref, *rest):
+    out_ref = rest[-1]
     half = own_ref.shape[0]
     out_ref[: 2 * half] = jnp.concatenate([own_ref[...], got_ref[...]], 0)
     gains = jnp.concatenate([ag_ref[...], fg_ref[...]], 1)
@@ -478,21 +545,26 @@
     out_ref[2 * half :] = jnp.broadcast_to(row, (16, out_ref.shape[1]))
 
 
-def join_second(a_ref, b_ref, _, out_ref):
-    out_ref[...] = jnp.concatenate([a_ref[...], b_ref[...]], 0)
-
-
 def line_blocks(buffer, f, offset):
     return [
         jnp.concatenate(
-            [buffer[2 * (f ^ j) + offset][:, :120], buffer[2 * (f ^ (j + 1)) + offset][:, :120]], 1
+            [buffer[2 * (f ^ j) + offset][:, :120], buffer[2 * (f ^ j ^ 2) + offset][:, :120]], 1
         )
-        for j in (0, 2)
+        for j in (0, 1)
     ]
 
 
+def mask_bias(seg_ref):
+    length = seg_ref.shape[1]
+    keys = jnp.broadcast_to(seg_ref[...].astype(F32), (length, length))
+    index_q = lax.broadcasted_iota(jnp.int32, (length, length), 0)
+    index_k = lax.broadcasted_iota(jnp.int32, (length, length), 1)
+    allowed = (keys.T == keys) & (index_q >= index_k)
+    return jnp.concatenate([jnp.where(allowed, 0.0, NEGATIVE)] * GROUP, 0)
+
+
 def attention_forward(
-    ids, x_ref, cos_ref, sin_ref, segc_ref, segr_ref, *rest
+    ids, x_ref, cos_ref, sin_ref, seg_ref, *rest
 ):
     first = rest[:8]
     second = rest[8:16]
@@ -502,14 +574,14 @@
     ) = rest[16:]
     d = ids[0]
     f = ids[1]
-    length = x_ref.shape[0]
+    length = x_ref.shape[1]
     for s in range(8):
         gb[d ^ s] = first[s][240:248, :256].astype(F32)
     gain_one = jnp.concatenate([gb[i][:, :120] for i in range(8)], 1)
     gain_two = jnp.concatenate([gb[i][:, 120:240] for i in range(8)], 1)
     gains_ref[0] = gain_one
     gains_ref[1] = gain_two
-    x = x_ref[...].astype(F32)
+    x = x_ref[...].astype(F32).T
     scale = lax.rsqrt(jnp.mean(x * x, -1, keepdims=True) + EPS)
     h1 = (x * scale * gain_one[:1]).astype(BF16)
     for i, block in enumerate(blocks_of(h1, 120)):
@@ -517,8 +589,8 @@
     left = line_blocks(hb, f, 0)
     right = line_blocks(hb, f, 1)
     for s in range(8):
-        a = dot(left[0], first[s][:240, 0:256]) + dot(left[1], second[s][:, 0:256])
-        b = dot(right[0], first[s][:240, 384:640]) + dot(right[1], second[s][:, 384:640])
+        a = dot(left[0], first[s][:240, 0:256]) + dot(left[1], second[s][:240, 0:256])
+        b = dot(right[0], first[s][:240, 384:640]) + dot(right[1], second[s][:240, 384:640])
         tb[d ^ s, :, :200] = a[:, :200] + b[:, 56:256]
     parts = [tb[i] for i in range(8)]
     q = jnp.concatenate([p[:, :120] for p in parts], 1)
@@ -526,11 +598,7 @@
     v = jnp.concatenate([p[:, 160:200] for p in parts], 1)
     cosines = cos_ref[...]
     sines = sin_ref[...]
-    index_q = lax.broadcasted_iota(jnp.int32, (length, length), 0)
-    index_k = lax.broadcasted_iota(jnp.int32, (length, length), 1)
-    allowed = (segc_ref[...] == segr_ref[...]) & (index_q >= index_k)
-    bias = jnp.where(allowed, 0.0, NEGATIVE)
-    bias = jnp.concatenate([bias] * GROUP, 0)
+    bias = mask_bias(seg_ref)
     heads = []
     for g in range(KV_HEADS):
         kg = k[:, g * HD : (g + 1) * HD]
@@ -559,8 +627,8 @@
     left = line_blocks(hb, f, 0)
     right = line_blocks(hb, f, 1)
     for s in range(8):
-        a = dot(left[0], first[s][:240, 128:384]) + dot(left[1], second[s][:, 128:384])
-        b = dot(right[0], first[s][:240, 256:512]) + dot(right[1], second[s][:, 256:512])
+        a = dot(left[0], first[s][:240, 128:384]) + dot(left[1], second[s][:240, 128:384])
+        b = dot(right[0], first[s][:240, 256:512]) + dot(right[1], second[s][:240, 256:512])
         tb[d ^ s, :, :120] = a[:, 72:192] + b[:, 64:184]
     x2 = x + jnp.concatenate([tb[i][:, :120] for i in range(8)], 1)
     x2_ref[...] = x2
@@ -578,23 +646,29 @@
     return copies
 
 
-def place_feed(feed_ref, gu, dt):
+def start_columns(refs, buffer, sems):
+    copies = []
+    for s, ref in enumerate(refs):
+        target = buffer.at[s // 2, :, pl.ds(128 * (s % 2), 128)]
+        copy = pltpu.make_async_copy(ref, target, sems.at[s])
+        copy.start()
+        copies.append(copy)
+    return copies
+
+
+def feed_critical(ids, *rest):
+    h_refs, c_refs, feed_ref, down_refs = rest[:8], rest[8:16], rest[16], rest[17:22]
+    even_ref, odd_ref, delta_ref, mixed_ref, dt, own_ref = rest[25:31]
+    fat_refs = rest[31:34]
+    hs, cs, gu, db, h_sems, c_sems = rest[34:]
+    passed = rest[22:25]
+    c_copies = start_columns(c_refs, cs, c_sems)
+    h_copies = start_stack(h_refs, hs, h_sems)
+    d = ids[0]
     for j in range(4):
         gu[240 * j : 240 * (j + 1), :] = feed_ref[360 * j : 360 * j + 240, :]
-        dt[240 * j : 240 * (j + 1), :] = unfold_down(feed_ref[360 * j + 240 : 360 * (j + 1), :])
-
-
-def unfold_down(both):
-    half = both.shape[1] // 2
-    return jnp.concatenate([both[:, :half], both[:, half:]], 0)
-
-
-def feed_critical(*rest):
-    h_refs, c_refs, feed_ref = rest[:8], rest[8:16], rest[16]
-    even_ref, odd_ref, delta_ref, mixed_ref, hs, cs, gu, dt, h_sems, c_sems = rest[17:]
-    c_copies = start_stack(c_refs, cs, c_sems)
-    h_copies = start_stack(h_refs, hs, h_sems)
-    place_feed(feed_ref, gu, dt)
+    place_exchanged(down_refs, passed, d, db, unfold_block)
+    dt[...] = jnp.concatenate([db[i] for i in range(8)], 0).astype(BF16)
     for copy in c_copies + h_copies:
         copy.wait()
     units = dt.shape[1]
@@ -602,7 +676,7 @@
     def step(c, carry):
         rows = pl.ds(pl.multiple_of(c * 256, 256), 256)
         both = dot(hs[rows, :], gu[...])
-        mixed_grad = dot(cs[rows, :], dt[...])
+        mixed_grad = contract_first(cs[c], dt[...])
         gate = both[:, :units]
         up = both[:, units:]
         sig = 1.0 / (1.0 + jnp.exp(-gate))
@@ -614,68 +688,92 @@
         delta_ref[rows, :] = deltas
         back = contract_last(deltas, gu[...])
         even_ref[c] = back[:128]
-        odd_ref[pl.ds(pl.multiple_of(c * 128, 128), 128), :] = back[128:].astype(BF16)
+        odd_ref[pl.ds(pl.multiple_of(c * 128, 128), 128), :960] = back[128:].astype(BF16)
         return carry
 
     lax.fori_loop(0, 4, step, 0)
+    for j in range(4):
+        part = jnp.zeros((240, 320), F32)
+        for c in range(4):
+            rows = slice(256 * c, 256 * (c + 1))
+            part = part + dot(cs[c, 240 * j : 240 * (j + 1), :], mixed_ref[rows, :])
+        db[2 * j] = part[:120]
+        db[2 * j + 1] = part[120:]
+    filler = jnp.zeros((8, 960), F32)
+    own_ref[...] = jnp.concatenate([flatten_block(db[d]), filler], 0).astype(BF16)
+    pair = jnp.concatenate([flatten_block(db[d ^ 1]), filler], 0)
+    odd_ref[512:, :960] = pair.astype(BF16)
+    for i in (1, 2, 3):
+        both = [flatten_block(db[d ^ (2 * i)]), flatten_block(db[d ^ (2 * i + 1)])]
+        fat_refs[i - 1][...] = jnp.concatenate(both, 0).astype(BF16)
+
+
+def pair_sum_down(even_ref, odd_ref, *rest):
+    fat_refs, own_ref, pair_ref = rest[:3], rest[3], rest[4]
+    rows = own_ref.shape[0]
+    own_ref[...] = even_ref[0] + odd_ref[:rows, :960].astype(F32)
+    pair_ref[...] = odd_ref[4 * rows :, :960]
+    for i, ref in enumerate(rest[5:], 1):
+        total = even_ref[i] + odd_ref[rows * i : rows * (i + 1), :960].astype(F32)
+        ref[:rows] = total.astype(BF16)
+        ref[rows:] = fat_refs[i - 1][...]
 
 
 def pair_sum(even_ref, odd_ref, *rest):
     own_ref, a_ref, b_ref, c_ref = rest[-4:]
     rows = own_ref.shape[0]
-    own_ref[...] = even_ref[0] + odd_ref[:rows].astype(F32)
+    own_ref[...] = even_ref[0] + odd_ref[:rows, :960].astype(F32)
     for i, ref in ((1, a_ref), (2, b_ref), (3, c_ref)):
-        ref[...] = (even_ref[i] + odd_ref[rows * i : rows * (i + 1)].astype(F32)).astype(BF16)
+        ref[...] = (even_ref[i] + odd_ref[rows * i : rows * (i + 1), :960].astype(F32)).astype(BF16)
 
 
 def feed_rest(*rest):
-    h_refs, c_refs, feed_ref = rest[:8], rest[8:16], rest[16]
-    delta_ref, mixed_ref = rest[17:19]
-    grad_ref, even_ref, odd_ref, hs, cs, h_sems, c_sems = rest[20:]
-    h_copies = start_stack(h_refs, hs, h_sems)
-    c_copies = start_stack(c_refs, cs, c_sems)
-    for copy in h_copies + c_copies:
+    h_refs, dt, delta_ref, mixed_ref = rest[:8], rest[8], rest[9], rest[10]
+    grad_ref, even_ref, odd_ref, hs, h_sems = rest[12:]
+    for copy in start_stack(h_refs, hs, h_sems):
         copy.wait()
     for j in range(4):
         part = contract_first(hs[:, 240 * j : 240 * (j + 1)], delta_ref[...])
-        grad_ref[360 * j : 360 * j + 240, :] = part.astype(BF16)
-        part = contract_first(cs[:, 240 * j : 240 * (j + 1)], mixed_ref[...])
-        part = jnp.concatenate([part[:120], part[120:]], 1)
-        grad_ref[360 * j + 240 : 360 * (j + 1), :] = part.astype(BF16)
-    turned = [unfold_down(feed_ref[360 * j + 240 : 360 * (j + 1), :]) for j in range(4)]
-    down = jnp.concatenate(turned, 0)
+        grad_ref[240 * j : 240 * (j + 1), :] = part.astype(BF16)
+    down = dt[...]
     for c in range(4):
         part = contract_last(mixed_ref[256 * c : 256 * (c + 1), :], down)
         even_ref[c] = part[:128]
-        odd_ref[128 * c : 128 * (c + 1), :] = part[128:].astype(BF16)
+        odd_ref[128 * c : 128 * (c + 1), :960] = part[128:].astype(BF16)
 
 
 def spread_line(buffer, parts, f, offset):
     for j, part in enumerate(parts):
-        buffer[2 * (f ^ (2 * j)) + offset, :, :120] = part[:, :120]
-        buffer[2 * (f ^ (2 * j + 1)) + offset, :, :120] = part[:, 120:240]
+        buffer[2 * (f ^ j) + offset, :, :120] = part[:, :120]
+        buffer[2 * (f ^ j ^ 2) + offset, :, :120] = part[:, 120:240]
 
 
 def attention_backward(ids, *rest):
     own_ref, a_ref, b_ref, c_ref, cot_ref, x2_ref, x_ref, gains_ref = rest[:8]
-    cos_ref, sin_ref, segc_ref, segr_ref, qr_ref, kr_ref, vr_ref, lse_ref = rest[8:16]
-    first, second = rest[16:24], rest[24:32]
-    outs = rest[32:40]
-    grad_ref, fb, db, eb, gb = rest[40:]
+    cos_ref, sin_ref, seg_ref, qr_ref, kr_ref, vr_ref, lse_ref = rest[8:15]
+    first, second = rest[15:23], rest[23:31]
+    outs = rest[-14:-6]
+    grad_ref, pass_ref, fb, db, eb, gb = rest[-6:]
     d = ids[0]
     f = ids[1]
-    length = x_ref.shape[0]
+    length = x_ref.shape[1]
     gain_one = gains_ref[0, :1]
     gain_two = gains_ref[1, :1]
     dh2 = (
-        own_ref[...] + a_ref[...].astype(F32) + b_ref[...].astype(F32) + c_ref[...].astype(F32)
-    )
+        own_ref[...]
+        + a_ref[:128].astype(F32)
+        + b_ref[:128].astype(F32)
+        + c_ref[:128].astype(F32)
+    )
+    passed = [ref[128:].astype(F32)[40:] for ref in (a_ref, b_ref, c_ref)]
+    passed = jnp.concatenate([*passed, jnp.zeros((8, 960), F32)], 0)
+    pass_ref[...] = passed.astype(BF16)
     x2 = x2_ref[...]
     scale_two = lax.rsqrt(jnp.mean(x2 * x2, -1, keepdims=True) + EPS)
     unit = x2 * scale_two
     feed_gain_grad = jnp.sum(dh2 * unit, 0, keepdims=True)
     scaled = dh2 * gain_two
-    dx2 = cot_ref[...].astype(F32) + scale_two * (
+    dx2 = cot_ref[...].astype(F32).T + scale_two * (
         scaled - unit * jnp.mean(scaled * unit, -1, keepdims=True)
     )
     rounded = dx2.astype(BF16)
@@ -688,19 +786,15 @@
         for_left = pad_lanes(mine, 72, 256)
         for_right = pad_lanes(mine, 64, 256)
         left[0] = left[0] + contract_last(for_left, first[s][:240, 128:384])
-        left[1] = left[1] + contract_last(for_left, second[s][:, 128:384])
+        left[1] = left[1] + contract_last(for_left, second[s][:240, 128:384])
         right[0] = right[0] + contract_last(for_right, first[s][:240, 256:512])
-        right[1] = right[1] + contract_last(for_right, second[s][:, 256:512])
+        right[1] = right[1] + contract_last(for_right, second[s][:240, 256:512])
     spread_line(fb, left, f, 0)
     spread_line(fb, right, f, 1)
     grad = jnp.concatenate([fb[i][:, :120] for i in range(8)], 1).astype(BF16)
     cosines = cos_ref[...]
     sines = sin_ref[...]
-    index_q = lax.broadcasted_iota(jnp.int32, (length, length), 0)
-    index_k = lax.broadcasted_iota(jnp.int32, (length, length), 1)
-    allowed = (segc_ref[...] == segr_ref[...]) & (index_q >= index_k)
-    bias = jnp.where(allowed, 0.0, NEGATIVE)
-    bias = jnp.concatenate([bias] * GROUP, 0)
+    bias = mask_bias(seg_ref)
     dq, dk, dv = [], [], []
     for g in range(KV_HEADS):
         qr = qr_ref[g]
@@ -732,13 +826,13 @@
         for_left = pad_lanes(mine, 0, 256)
         for_right = pad_lanes(mine, 56, 256)
         left[0] = left[0] + contract_last(for_left, first[s][:240, 0:256])
-        left[1] = left[1] + contract_last(for_left, second[s][:, 0:256])
+        left[1] = left[1] + contract_last(for_left, second[s][:240, 0:256])
         right[0] = right[0] + contract_last(for_right, first[s][:240, 384:640])
-        right[1] = right[1] + contract_last(for_right, second[s][:, 384:640])
+        right[1] = right[1] + contract_last(for_right, second[s][:240, 384:640])
     spread_line(fb, left, f, 0)
     spread_line(fb, right, f, 1)
     dh1 = jnp.concatenate([fb[i][:, :120] for i in range(8)], 1)
-    x = x_ref[...].astype(F32)
+    x = x_ref[...].astype(F32).T
     scale_one = lax.rsqrt(jnp.mean(x * x, -1, keepdims=True) + EPS)
     unit = x * scale_one
     attention_gain_grad = jnp.sum(dh1 * unit, 0, keepdims=True)
@@ -763,30 +857,29 @@
 
 
 def attention_weights(ids, *rest):
-    x_refs, att_refs, got, gains_ref = rest[:8], rest[8:16], rest[16:24], rest[24]
-    own_ref, g1_ref, g2_ref, g3_ref, hs, at, dl, acc, x_sems, a_sems = rest[25:]
+    x_refs, att_ref, got, gains_ref = rest[:8], rest[8], rest[9:17], rest[17]
+    own_ref, g1_ref, g2_ref, g3_ref, hs, dl, acc = rest[21:]
+    d = ids[0]
     f = ids[1]
     length = 128
     half = 64
-    x_copies = start_stack(x_refs, hs, x_sems)
-    a_copies = start_stack(att_refs, at, a_sems)
     gain_sum = jnp.zeros((8, 640), F32)
     for s in range(8):
         block = got[s][:half]
-        dl[s * length : s * length + half, 0:320] = block[:, :320]
-        dl[s * length + half : (s + 1) * length, 0:320] = jnp.concatenate(
+        start = pl.multiple_of(length * (d ^ s), length)
+        dl[pl.ds(start, half), 0:320] = block[:, :320]
+        dl[pl.ds(start + half, half), 0:320] = jnp.concatenate(
             [block[:, 440:], block[:, 320:440]], 1
         )
         gain_sum = gain_sum + got[s][half : half + 8].astype(F32)
-    gain_one = gains_ref[0, :1]
-    for copy in x_copies + a_copies:
-        copy.wait()
+    gain_one = gains_ref[0].T[:, :1]
     for s in range(8):
-        x = hs[length * s : length * (s + 1)].astype(F32)
-        scale = lax.rsqrt(jnp.mean(x * x, -1, keepdims=True) + EPS)
-        hs[s * length : (s + 1) * length] = (x * scale * gain_one).astype(BF16)
-    qkv = contract_first(dl[:, :200], hs[...])
-    out = contract_first(dl[:, 200:320], at[...])
+        x = x_refs[s][...].astype(F32)
+        scale = lax.rsqrt(jnp.mean(x * x, 0, keepdims=True) + EPS)
+        start = pl.multiple_of(length * (d ^ s), length)
+        hs[:, pl.ds(start, length)] = (x * scale * gain_one).astype(BF16)
+    qkv = dot(hs[...], dl[:, :200]).T
+    out = contract_first(dl[:, 200:320], att_ref[...])
     both = jnp.concatenate([qkv, out], 0)
     for i in range(4):
         acc[i, :320, :240] = both[:, 240 * i : 240 * (i + 1)]
@@ -796,23 +889,10 @@
         ref[...] = acc[f ^ j][:, :240].astype(BF16)
 
 
-def finish_feed(ids, sum_ref, gate_ref, up_ref, a_ref, b_ref):
-    total = sum_ref[:240].astype(F32).T
+def finish_feed(sum_ref, _, gate_ref, up_ref):
+    total = sum_ref[...].astype(F32).T
     gate_ref[...] = total[:320]
     up_ref[...] = total[320:]
-    even = (ids[0] % 2) == 0
-    down = sum_ref[240:].astype(F32)
-    left = down[:, :320]
-    right = down[:, 320:]
-    a_ref[...] = jnp.where(even, left, right).astype(BF16)
-    b_ref[...] = jnp.where(even, right, left).astype(BF16)
-
-
-def finish_down(ids, a_ref, b_ref, out_ref):
-    even = (ids[0] % 2) == 0
-    a = a_ref[...].astype(F32)
-    b = b_ref[...].astype(F32)
-    out_ref[...] = jnp.concatenate([jnp.where(even, a, b), jnp.where(even, b, a)], 1)
 
 
 def finish_output(x2_ref, own_ref, a_ref, b_ref, c_ref, out_ref):
@@ -826,7 +906,9 @@
     out_ref[...] = total.T.astype(BF16)
 
 
-def finish_attention(own_ref, a_ref, b_ref, c_ref, q_ref, k_ref, v_ref, o_ref, ag_ref, fg_ref):
+def finish_attention(own_ref, a_ref, b_ref, c_ref, down_ref, *rest):
+    q_ref, k_ref, v_ref, o_ref, ag_ref, fg_ref, down_out = rest[-7:]
+    down_out[...] = down_ref[...].astype(F32)
     total = (
         own_ref[...] + a_ref[...].astype(F32) + b_ref[...].astype(F32) + c_ref[...].astype(F32)
     )
@@ -834,8 +916,8 @@
     k_ref[...] = total[120:160]
     v_ref[...] = total[160:200]
     o_ref[...] = total[200:320].T
-    fg_ref[...] = total[320:328, :120]
-    ag_ref[...] = total[320:328, 120:240]
+    fg_ref[...] = total[320:321, :120]
+    ag_ref[...] = total[320:321, 120:240]
 
 
 def fast(
@@ -853,9 +935,9 @@
     feedforward_gain,
     output_cotangent,
 ):
-    hidden = hidden_in[0]
-    cotangent = output_cotangent[0]
-    length, features = hidden.shape
+    hidden = hidden_in[0].T
+    cotangent = output_cotangent[0].T
+    features, length = hidden.shape
     d = lax.axis_index("dp")
     f = lax.axis_index("fsdp")
     ids = jnp.stack([d, f]).astype(jnp.int32)
@@ -866,55 +948,38 @@
         [shape((120, 640), BF16)],
         [query_weight, key_weight.T, value_weight.T, output_weight],
     )
-    line = [block] + [send(block, "fsdp", j) for j in (1, 2, 3)]
+    far = [send(cotangent, "dp", s) for s in (2, 4, 6)]
+    cotangent_slots = [cotangent, send(cotangent, "dp", 1)]
+    for other in far:
+        cotangent_slots += [other, send(other, "dp", 1)]
+    line = send(block, "fsdp", 2)
     (chunk_a,) = kernel_call(
-        join_first,
+        join_lines,
         [shape((256, 640), BF16)],
-        [line[0], line[1], attention_gain[None], feedforward_gain[None]],
-    )
-    (chunk_b,) = kernel_call(join_second, [shape((240, 640), BF16)], [line[2], line[3], chunk_a], [None, None, "any"])
-
-    def spread(chunk, near, far):
-        slots = [chunk, send(chunk, "dp", 1)] + [None] * 6
-        slots[near] = send(chunk, "dp", near)
-        slots[far] = send(chunk, "dp", far)
-        slots[6] = send(slots[near], "dp", far)
-        for s in (near, far, 6):
-            slots[s + 1] = send(slots[s], "dp", 1)
-        return slots
-
-    first = spread(chunk_a, 2, 4)
-    second = spread(chunk_b, 4, 2)
-
-    piece_a, piece_b = kernel_call(
-        pack_down,
-        [shape((120, 320), BF16), shape((120, 320), BF16)],
-        [ids, down_weight.T, block],
-        ["smem", None, "any"],
-    )
-    routes = down_routes(8, 4)
-    piece_a = lax.ppermute(piece_a, ("dp", "fsdp"), routes[0])
-    piece_b = lax.ppermute(piece_b, ("dp", "fsdp"), routes[1])
-    (feed_block,) = kernel_call(
+        [block, line, attention_gain[None], feedforward_gain[None], *far],
+        [None] * 4 + ["any"] * 3,
+    )
+    chunk_b = send(chunk_a, "fsdp", 1)
+    a_near, a_far = send(chunk_a, "dp", 2), send(chunk_a, "dp", 4)
+    chunk_b = after(chunk_b, a_near, a_far)
+    b_near, b_far = send(chunk_b, "dp", 4), send(chunk_b, "dp", 2)
+    a_near, b_near = after_all([a_near, b_near])
+    a_last, b_last = send(a_near, "dp", 4), send(b_near, "dp", 2)
+    first, second = [], []
+    for value in (chunk_a, a_near, a_far, a_last):
+        first += [value, send(value, "dp", 1)]
+    for value in (chunk_b, b_far, b_near, b_last):
+        second += [value, send(value, "dp", 1)]
+
+    (feed,) = kernel_call(
         pack_feed,
         [shape((360, 640), BF16)],
-        [ids, gate_weight.T, up_weight.T, piece_a, piece_b, chunk_b],
-        ["smem"] + [None] * 4 + ["any"],
-    )
-    feed = lax.all_gather(feed_block, "fsdp", axis=0, tiled=True)
-
-    def gather(values):
-        slots = [values, send(values, "dp", 1)] + [None] * 6
-        for s in (2, 4, 6):
-            slots[s] = send(values, "dp", s)
-            slots[s + 1] = send(slots[s], "dp", 1)
-        return slots
-
-    cotangent_slots = gather(cotangent)
+        [gate_weight.T, up_weight.T, down_weight.T, chunk_b],
+        [None, None, None, "any"],
+    )
+    feed = lax.all_gather(feed, "fsdp", axis=0, tiled=True)
 
     cosines, sines = rotary_tables(positions[0], HD)
-    seg_column = segment_ids[0][:, None]
-    seg_row = segment_ids
     x2, h2, attended, qr, kr, vr, lse, gains = kernel_call(
         attention_forward,
         [
@@ -927,8 +992,8 @@
             shape((KV_HEADS, GROUP * length, 1), F32),
             shape((2, 8, features), F32),
         ],
-        [ids, hidden, cosines, sines, seg_column, seg_row, *first, *second],
-        ["smem"] + [None] * 21,
+        [ids, hidden, cosines, sines, segment_ids, *first, *second],
+        ["smem"] + [None] * 20,
         [
             pltpu.VMEM((8, length, 128), BF16),
             pltpu.VMEM((8, length, 256), F32),
@@ -937,22 +1002,44 @@
         16,
         8.5,
     )
-    h2_slots = gather(h2)
-    even, odd, deltas, mixed = kernel_call(
+    hidden_rows = after(hidden, b_near, b_far)
+    far = [send(hidden_rows, "dp", s) for s in (2, 4, 6)]
+    hidden_slots = [hidden_rows, send(hidden_rows, "dp", 1)]
+    for other in far:
+        hidden_slots += [other, send(other, "dp", 1)]
+    down_blocks = kernel_call(
+        split_down,
+        exchange_shapes(),
+        [ids, feed, h2, *far],
+        ["smem", None] + ["any"] * 4,
+        [pltpu.VMEM((8, 120, 320), F32)],
+    )
+    down_blocks = exchange(down_blocks)
+    others = after_all([send(h2, "dp", s) for s in (2, 4, 6)], *down_blocks[1:])
+    down_passed = [send(value, "dp", 1) for value in down_blocks[2:]]
+    h2_slots = [h2, send(h2, "dp", 1)]
+    for other in others:
+        h2_slots += [other, send(other, "dp", 1)]
+    attended = after(attended, *others, *down_passed)
+    attended = lax.all_gather(attended, "dp", axis=0, tiled=True)
+    even, odd, deltas, mixed, down, own_block, *fats = kernel_call(
         feed_critical,
         [
             shape((4, length, features), F32),
-            shape((4 * length, features), BF16),
+            shape((4 * length + 48, 1024), BF16),
             shape((tokens, 640), BF16),
             shape((tokens, 320), BF16),
-        ],
-        [*h2_slots, *cotangent_slots, feed],
-        ["any"] * 16 + [None],
+            shape((features, 320), BF16),
+            shape((48, 960), BF16),
+        ]
+        + [shape((80, 960), BF16)] * 3,
+        [ids, *h2_slots, *cotangent_slots, feed, *down_blocks, *down_passed],
+        ["smem"] + ["any"] * 16 + [None] * 9,
         [
             pltpu.VMEM((tokens, features), BF16),
-            pltpu.VMEM((tokens, features), BF16),
+            pltpu.VMEM((4, features, 256), BF16),
             pltpu.VMEM((features, 640), BF16),
-            pltpu.VMEM((features, 320), BF16),
+            pltpu.VMEM((8, 120, 320), F32),
             pltpu.SemaphoreType.DMA((8,)),
             pltpu.SemaphoreType.DMA((8,)),
         ],
@@ -960,48 +1047,41 @@
         9.0,
     )
 
-    def scatter_sum(even, odd, *after):
-        odd = send(odd, "dp", 1)
-        own, a, b, c = kernel_call(
-            pair_sum,
-            [shape((length, features), F32)] + [shape((length, features), BF16)] * 3,
-            [even, odd, *after],
-            [None, None] + ["any"] * len(after),
-            (),
-            12,
-        )
-        return own, send(a, "dp", 2), send(b, "dp", 4), send(c, "dp", 6)
-
-    back_own, back_a, back_b, back_c = scatter_sum(even, odd)
+    odd = send(odd, "dp", 1)
+    back_own, pair_block, back_a, back_b, back_c = kernel_call(
+        pair_sum_down,
+        [shape((length, features), F32), shape((48, features), BF16)]
+        + [shape((length + 80, features), BF16)] * 3,
+        [even, odd, *fats],
+    )
+    back_a, back_b, back_c = send(back_a, "dp", 2), send(back_b, "dp", 4), send(back_c, "dp", 6)
     feed_grad, f_even, f_odd = kernel_call(
         feed_rest,
         [
-            shape((4 * 360, 640), BF16),
+            shape((4 * 240, 640), BF16),
             shape((4, length, features), F32),
-            shape((4 * length, features), BF16),
+            shape((4 * length, 1024), BF16),
         ],
-        [*h2_slots, *cotangent_slots, feed, deltas, mixed, back_own],
-        ["any"] * 16 + [None] * 3 + ["any"],
+        [*h2_slots, down, deltas, mixed, back_own],
+        ["any"] * 8 + [None] * 3 + ["any"],
         [
             pltpu.VMEM((tokens, features), BF16),
-            pltpu.VMEM((tokens, features), BF16),
-            pltpu.SemaphoreType.DMA((8,)),
             pltpu.SemaphoreType.DMA((8,)),
         ],
         24,
         9.0,
     )
+    feed_grad = after(feed_grad, back_a, back_b, back_c, attended)
     feed_sum = lax.psum_scatter(feed_grad, "fsdp", scatter_dimension=0, tiled=True)
-    attended_slots = gather(attended)
-    hidden_slots = gather(hidden)
-    *outgoing, input_grad = kernel_call(
+    *outgoing, input_grad, passed = kernel_call(
         attention_backward,
-        [shape((80, 640), BF16)] * 8 + [shape((features, length), F32)],
+        [shape((80, 640), BF16)] * 8
+        + [shape((features, length), F32), shape((length, features), BF16)],
         [
             ids, back_own, back_a, back_b, back_c, cotangent, x2, hidden, gains,
-            cosines, sines, seg_column, seg_row, qr, kr, vr, lse, *first, *second,
+            cosines, sines, segment_ids, qr, kr, vr, lse, *first, *second, feed_grad,
         ],
-        ["smem"] + [None] * 32,
+        ["smem"] + [None] * 31 + ["any"],
         [
             pltpu.VMEM((8, length, 128), F32),
             pltpu.VMEM((8, length, 128), BF16),
@@ -1012,51 +1092,58 @@
         10.5,
     )
     arrived = [outgoing[0]] + [send(outgoing[s], "dp", s) for s in range(1, 8)]
+    passed = send(passed, "dp", 1)
+    (down_grad,) = kernel_call(
+        join_down,
+        [shape((4 * 120, 640), BF16)],
+        [ids, own_block, pair_block, back_a, back_b, back_c, passed],
+        ["smem"] + [None] * 6,
+        [pltpu.VMEM((8, 120, 320), F32)],
+    )
+    f_odd = send(after(f_odd, outgoing[0]), "dp", 1)
+    y_own, *y_parts = kernel_call(
+        pair_sum,
+        [shape((length, features), F32)] + [shape((length, features), BF16)] * 3,
+        [f_even, f_odd, outgoing[0]],
+        [None, None, "any"],
+    )
+    down_sum = lax.psum_scatter(down_grad, "fsdp", scatter_dimension=0, tiled=True)
     w0, w1, w2, w3 = kernel_call(
         attention_weights,
         [shape((336, 240), F32)] + [shape((336, 240), BF16)] * 3,
-        [ids, *hidden_slots, *attended_slots, *arrived, gains],
-        ["smem"] + ["any"] * 16 + [None] * 9,
+        [ids, *hidden_slots, attended, *arrived, gains, y_own, down_grad, feed_sum],
+        ["smem"] + [None] * 18 + ["any"] * 3,
         [
-            pltpu.VMEM((tokens, features), BF16),
-            pltpu.VMEM((tokens, features), BF16),
+            pltpu.VMEM((features, tokens), BF16),
             pltpu.VMEM((tokens, 320), BF16),
             pltpu.VMEM((4, 336, 256), F32),
-            pltpu.SemaphoreType.DMA((8,)),
-            pltpu.SemaphoreType.DMA((8,)),
         ],
         20,
         4.5,
     )
 
-    gate_out, up_out, piece_a, piece_b = kernel_call(
-        finish_feed,
-        [shape((320, 240), F32)] * 2 + [shape((120, 320), BF16)] * 2,
-        [ids, feed_sum],
-        ["smem", None],
-    )
-    back = [[(t, s) for s, t in pairs] for pairs in routes]
-    piece_a = lax.ppermute(piece_a, ("dp", "fsdp"), back[0])
-    piece_b = lax.ppermute(piece_b, ("dp", "fsdp"), back[1])
-    (down_out,) = kernel_call(
-        finish_down, [shape((120, 640), F32)], [ids, piece_a, piece_b], ["smem", None, None]
-    )
-    sums = scatter_sum(f_even, f_odd, w0)
+    y_parts = after_all(y_parts, w0)
+    sums = [y_own] + [send(part, "dp", 2 * i + 2) for i, part in enumerate(y_parts)]
+    parts = [send(w, "fsdp", j) for j, w in ((1, w1), (2, w2), (3, w3))]
+    gate_out, up_out = kernel_call(
+        finish_feed, [shape((320, 240), F32)] * 2, [feed_sum, parts[0]], [None, "any"]
+    )
     (block_output,) = kernel_call(
         finish_output, [shape((features, length), BF16)], [x2, *sums]
     )
-    parts = [send(w, "fsdp", j) for j, w in ((1, w1), (2, w2), (3, w3))]
-    q_out, k_out, v_out, o_out, ag_out, fg_out = kernel_call(
+    q_out, k_out, v_out, o_out, ag_out, fg_out, down_out = kernel_call(
         finish_attention,
         [
             shape((240, 120), F32),
             shape((40, 240), F32),
             shape((40, 240), F32),
             shape((240, 120), F32),
-            shape((8, 120), F32),
-            shape((8, 120), F32),
+            shape((1, 120), F32),
+            shape((1, 120), F32),
+            shape((120, 640), F32),
         ],
-        [w0, *parts],
+        [w0, *parts, down_sum, block_output, gate_out],
+        [None] * 5 + ["any"] * 2,
     )
     return (
         block_output.T[None],

time: 277 us -> 225 us (0.81)
  the two profiles are of different devices: /device:TPU:12 before, /device:TPU:8 now
where the time goes in v3:
time: 225 us; the launch traced here: 222 us
  waiting for transfers between devices  75.9 us (34%)
  Pallas kernels  74.3 us (33%)
  starting transfers between devices  47 us (21%)
  between operations  14.2 us (6%)
  local copies, waits for them, and re-layouts  9.16 us (4%)
    pallas_call x15, Pallas kernels, kernel_call(): pl.pallas_call(body, out_shape=outs, in_specs=[pl.BlockSpec(memory_space=...  74.3 us
    ppermute x63, waiting for transfers between devices, send(): return lax.ppermute(values, axis, [(i, i ^ distance) for i in range(count)])  70.4 us
    ppermute x63, starting transfers between devices, send(): return lax.ppermute(values, axis, [(i, i ^ distance) for i in range(count)])  46.4 us
    unnamed x115, local copies, waits for them, and re-layouts  9.16 us
    all_gather x1, waiting for transfers between devices, fast(): feed = lax.all_gather(feed, 'fsdp', axis=0, tiled=True)  5.41 us
  transfers between devices with their start and end apart: 67, of which 30 were waited for; matrix products, arithmetic and copies ran while one was open for 1% of the time, Pallas kernels for 31%

profile of v3, /device:TPU:8, one launch (start us, length us, event | category | flops | bytes accessed | tf_op | source)
XLA Modules:
  0.0 222.2 jit_solution(7449473105942598446)
XLA Ops:
  7.2 1.6 collective-permute-start.1
  8.8 1.5 collective-permute-start.2
  10.8 1.8 shard_map.212.own_ref
  12.6 2.6 %collective-permute-start = (bf16[120,640]{1,0:T(8,128)(2,1)}, bf16[120,640]{1,0:T(8,128)(2,1)S(1)}, u32[]{:S(2)}, u32[]{:S(2)}) collective-permute-start(bf16[120,640]{1,0:T(8,128)(2,1)} %shard_map.212.own_ref), channel_id=1, source_target_pairs={{0,2},{1,3},{2,0},{3,1},{4,6},{5,7},{6,4},{7,5},{8,10},{9,11},{10,... | collective-permute-start | bytes 460808 | tf_op jit(solution)/shard_map/ppermute | solution.py:71
  15.2 5.9 %collective-permute-done.got_ref = bf16[120,640]{1,0:T(8,128)(2,1)S(1)} collective-permute-done((bf16[120,640]{1,0:T(8,128)(2,1)}, bf16[120,640]{1,0:T(8,128)(2,1)S(1)}, u32[]{:S(2)}, u32[]{:S(2)}) %collective-permute-start) | collective-permute-done | bytes 153632 | tf_op jit(solution)/shard_map/ppermute | solution.py:71
  22.4 1.8 shard_map.213.rest_0_.rest_15_
  24.3 1.2 collective-permute-start.5
  25.4 1.1 collective-permute-start.6
  26.5 1.5 collective-permute-start.7
  28.0 5.3 %collective-permute-done.5.refs_1_.refs_0_ = bf16[256,640]{1,0:T(8,128)(2,1)S(1)} collective-permute-done((bf16[256,640]{1,0:T(8,128)(2,1)}, bf16[256,640]{1,0:T(8,128)(2,1)S(1)}, u32[]{:S(2)}, u32[]{:S(2)}) %collective-permute-start.5) | collective-permute-done | bytes 327712 | tf_op jit(solution)/shard_map/ppermute | solution.py:71
  33.4 1.2 collective-permute-done.6.refs_0_
  35.3 0.7 copy-done.10
  36.1 2.1 shard_map.217
  38.2 1.6 collective-permute-start.8
  41.6 4.8 %collective-permute-done.8.refs_1_ = bf16[256,640]{1,0:T(8,128)(2,1)S(1)} collective-permute-done((bf16[256,640]{1,0:T(8,128)(2,1)S(1)}, bf16[256,640]{1,0:T(8,128)(2,1)S(1)}, u32[]{:S(2)}, u32[]{:S(2)}) %collective-permute-start.8) | collective-permute-done | bytes 327712 | tf_op jit(solution)/shard_map/ppermute | solution.py:71
  46.4 0.7 copy-done.1
  47.1 1.7 collective-permute-start.11
  48.7 0.7 collective-permute-start.17
  50.7 0.9 collective-permute-done.14.rest_10_.refs_2_.rest_25_
  51.6 2.9 %collective-permute-done.11.rest_6_.rest_21_ = bf16[256,640]{1,0:T(8,128)(2,1)S(1)} collective-permute-done((bf16[256,640]{1,0:T(8,128)(2,1)}, bf16[256,640]{1,0:T(8,128)(2,1)S(1)}, u32[]{:S(2)}, u32[]{:S(2)}) %collective-permute-start.11) | collective-permute-done | bytes 327712 | tf_op jit(solution)/shard_map/ppermute | solution.py:71
  54.5 3.3 %collective-permute-done.17.rest_14_.rest_29_ = bf16[256,640]{1,0:T(8,128)(2,1)S(1)} collective-permute-done((bf16[256,640]{1,0:T(8,128)(2,1)}, bf16[256,640]{1,0:T(8,128)(2,1)S(1)}, u32[]{:S(2)}, u32[]{:S(2)}) %collective-permute-start.17) | collective-permute-done | bytes 327712 | tf_op jit(solution)/shard_map/ppermute | solution.py:71
  58.1 0.8 pad_maximum_fusion
  60.0 2.5 %collective-permute-start.25 = (bf16[960,128]{1,0:T(8,128)(2,1)}, bf16[960,128]{1,0:T(8,128)(2,1)}, u32[]{:S(2)}, u32[]{:S(2)}) collective-permute-start(bf16[960,128]{1,0:T(8,128)(2,1)} %shard_map.218.rest_0_), channel_id=1, source_target_pairs={{0,24},{4,28},{8,16},{12,20},{16,8},{20,12},{24,0},{28,4},{1,25},{... | collective-permute-start | bytes 737288 | tf_op jit(solution)/shard_map/ppermute | solution.py:71
  62.6 10.3 %shard_map.216 = (f32[128,960]{1,0:T(8,128)}, bf16[128,960]{1,0:T(8,128)(2,1)}, bf16[128,960]{1,0:T(8,128)(2,1)}, bf16[5,384,64]{2,1,0:T(8,128)(2,1)}, bf16[5,12...) custom-call(s32[2]{0:T(128)} %pad_add_fusion.ids, ...), custom_call_target="tpu_custom_call" | custom-call | flops 9349999616 | bytes 25500000 | tf_op jit(solution)/shard_map/pallas_call | solution.py:407
  74.2 5.4 %all-gather.3.cloned.1.call-done.feed_ref.rest_16_ = bf16[1440,640]{1,0:T(8,128)(2,1)} async-done(((bf16[360,640]{1,0:T(8,128)(2,1)}), bf16[1440,640]{1,0:T(8,128)(2,1)}) %all-gather.3.cloned.1.call-update) | async-done | bytes 1843216 | tf_op jit(solution)/shard_map/all_gather | solution.py:980
  79.6 2.6 %shard_map.219 = (bf16[64,640]{1,0:T(8,128)(2,1)}, bf16[64,640]{1,0:T(8,128)(2,1)}, bf16[128,640]{1,0:T(8,128)(2,1)}, bf16[128,640]{1,0:T(8,128)(2,1)}, bf16[128,640]{1,0:T(8,128)(2,1)}) custom-call(s32[2]{0:T(128)} %pad_add_fusion.ids, bf16[1440,640]{1,0:T(8,128)(2,1)} %all-gather.3.cloned.1.call-done.feed_ref.rest_16_, ...), custom_call_target="tpu_custom_call" | custom-call | flops 1100000000 | bytes 3000000 | tf_op jit(solution)/shard_map/pallas_call | solution.py:407
  82.2 1.5 collective-permute-start.27
  83.7 1.4 collective-permute-start.22
  85.7 2.4 %collective-permute-start.29 = (bf16[128,640]{1,0:T(8,128)(2,1)}, bf16[128,640]{1,0:T(8,128)(2,1)S(1)}, u32[]{:S(2)}, u32[]{:S(2)}) collective-permute-start(bf16[128,640]{1,0:T(8,128)(2,1)} %get-tuple-element.83), channel_id=1, source_target_pairs={{0,24},{4,28},{8,16},{12,20},{16,8},{20,12},{24,0},{28,4},{1,25},{... | collective-permute-start | bytes 491528 | tf_op jit(solution)/shard_map/ppermute | solution.py:71
  88.1 1.4 collective-permute-done.27.refs_4_.rest_19_
  90.1 9.6 %collective-permute-done.28.refs_5_.rest_20_ = bf16[128,640]{1,0:T(8,128)(2,1)S(1)} collective-permute-done((bf16[128,640]{1,0:T(8,128)(2,1)}, bf16[128,640]{1,0:T(8,128)(2,1)S(1)}, u32[]{:S(2)}, u32[]{:S(2)}) %collective-permute-start.28) | collective-permute-done | bytes 163872 | tf_op jit(solution)/shard_map/ppermute | solution.py:71
  105.6 0.7 copy-done.35
  106.3 12.8 %shard_map.221 = (f32[4,128,960]{2,1,0:T(8,128)}, bf16[560,1024]{1,0:T(8,128)(2,1)}, bf16[1024,640]{1,0:T(8,128)(2,1)}, bf16[1024,320]{1,0:T(8,128)(2,1)}, bf16[...) custom-call(s32[2]{0:T(128)} %pad_add_fusion.ids, ...), custom_call_target="tpu_custom_call" | custom-call | flops 9900000256 | bytes 27000000 | tf_op jit(solution)/shard_map/pallas_call | solution.py:407
  119.5 2.8 %collective-permute-done.40.odd_ref = bf16[560,1024]{1,0:T(8,128)(2,1)} collective-permute-done((bf16[560,1024]{1,0:T(8,128)(2,1)}, bf16[560,1024]{1,0:T(8,128)(2,1)}, u32[]{:S(2)}, u32[]{:S(2)}) %collective-permute-start.40) | collective-permute-done | bytes 1146912 | tf_op jit(solution)/shard_map/ppermute | solution.py:71
  122.4 3.3 %shard_map.222 = (f32[128,960]{1,0:T(8,128)}, bf16[48,960]{1,0:T(8,128)(2,1)}, bf16[208,960]{1,0:T(8,128)(2,1)}, bf16[208,960]{1,0:T(8,128)(2,1)}, bf16[208,960]{1,0:T(8,128)(2,1)}) custom-call(f32[4,128,960]{2,1,0:T(8,128)} %get-tuple-element.91.even_ref, bf16[560,1024]{1,0:T(8,128)(2,1)} %collective-permute-done.40.odd_ref, ...), custom_call_target="tpu_custom_call" | custom-call | flops 1100000000 | bytes 3000000 | tf_op jit(solution)/shard_map/pallas_call | solution.py:407
  125.7 1.5 collective-permute-start.41
  127.1 0.7 collective-permute-start.42
  127.8 1.3 collective-permute-start.43
  129.1 8.4 %shard_map.223 = (bf16[960,640]{1,0:T(8,128)(2,1)}, f32[4,128,960]{2,1,0:T(8,128)}, bf16[512,1024]{1,0:T(8,128)(2,1)}) custom-call(bf16[128,960]{1,0:T(8,128)(2,1)} %get-tuple-element.79.rest_0_, bf16[128,960]{1,0:T(8,128)(2,1)} %copy-done.32, bf16[128,960]{1,0:T(8,128)(2,1)} %get-tuple-element.84.rest_2_.refs_1_, bf16[128,960]{1,0:T(8,128)(2,1)} %copy-done.33, ...), custom_call_target="tpu_custom_call" | custom-call | flops 9900000256 | bytes 27000000 | tf_op jit(solution)/shard_map/pallas_call | solution.py:407
  137.6 0.9 collective-permute-done.41.refs_1_.rest_1_.rest_0_
  138.5 9.8 %collective-permute-done.42.refs_2_.rest_2_.rest_1_ = bf16[208,960]{1,0:T(8,128)(2,1)} collective-permute-done((bf16[208,960]{1,0:T(8,128)(2,1)}, bf16[208,960]{1,0:T(8,128)(2,1)}, u32[]{:S(2)}, u32[]{:S(2)}) %collective-permute-start.42) | collective-permute-done | bytes 399392 | tf_op jit(solution)/shard_map/ppermute | solution.py:71
  148.7 12.6 %shard_map.226 = (bf16[80,640]{1,0:T(8,128)(2,1)}, bf16[80,640]{1,0:T(8,128)(2,1)}, bf16[80,640]{1,0:T(8,128)(2,1)}, bf16[80,640]{1,0:T(8,128)(2,1)}, bf16[80,64...) custom-call(s32[2]{0:T(128)} %pad_add_fusion.ids, ...), custom_call_target="tpu_custom_call" | custom-call | flops 11550000128 | bytes 31500000 | tf_op jit(solution)/shard_map/pallas_call | solution.py:407
  161.4 0.8 copy-done.36
  162.8 1.9 collective-permute-done.56.rest_3_
  164.8 0.7 copy-done.40
  165.5 2.7 %shard_map.229.rest_19_ = bf16[480,640]{1,0:T(8,128)(2,1)} custom-call(s32[2]{0:T(128)} %pad_add_fusion.ids, bf16[48,960]{1,0:T(8,128)(2,1)} %get-tuple-element.121.own_ref, bf16[48,960]{1,0:T(8,128)(2,1)} %get-tuple-element.122.pair_ref, bf16[208,960]{1,0:T(8,128)(2,1)} %copy-done.9, bf16[208,960]{1,0:T(8,128)(2,1)} %collective-permute-done.42.refs_2_.rest_2_.rest_1_, ...), custom_call_target="tpu_custom_call" | custom-call | flops 1100000000 | bytes 3000000 | tf_op jit(solution)/shard_map/pallas_call | solution.py:407
  170.7 0.8 collective-permute-start.52
  171.5 1.0 collective-permute-start.53
  172.5 2.4 %collective-permute-done.50.rest_11_ = bf16[80,640]{1,0:T(8,128)(2,1)S(1)} collective-permute-done((bf16[80,640]{1,0:T(8,128)(2,1)}, bf16[80,640]{1,0:T(8,128)(2,1)S(1)}, u32[]{:S(2)}, u32[]{:S(2)}) %collective-permute-start.50) | collective-permute-done | bytes 102432 | tf_op jit(solution)/shard_map/ppermute | solution.py:71
  174.9 1.2 collective-permute-start.54
  176.2 3.0 %shard_map.228 = (f32[128,960]{1,0:T(8,128)}, bf16[128,960]{1,0:T(8,128)(2,1)}, bf16[128,960]{1,0:T(8,128)(2,1)}, bf16[128,960]{1,0:T(8,128)(2,1)}) custom-call(f32[4,128,960]{2,1,0:T(8,128)} %get-tuple-element.97.even_ref, bf16[512,1024]{1,0:T(8,128)(2,1)} %collective-permute-done.44.odd_ref, bf16[80,640]{1,0:T(8,128)(2,1)} %get-tuple-element.109.refs_1_.rest_0_.rest_9_), custom_call_target="tpu_custom_call" | custom-call | flops 1100000000 | bytes 3000000 | tf_op jit(solution)/shard_map/pallas_call | solution.py:407
  179.2 1.9 collective-permute-done.54.rest_15_
  181.2 1.1 collective-permute-done.55.rest_16_
  182.2 6.4 %shard_map.230 = (f32[336,240]{1,0:T(8,128)}, bf16[336,240]{1,0:T(8,128)(2,1)}, bf16[336,240]{1,0:T(8,128)(2,1)}, bf16[336,240]{1,0:T(8,128)(2,1)}) custom-call(s32[2]{0:T(128)} %pad_add_fusion.ids, bf16[960,128]{1,0:T(8,128)(2,1)} %shard_map.218.rest_0_, bf16[960,128]{1,0:T(8,128)(2,1)} %copy-done.45, ...), custom_call_target="tpu_custom_call" | custom-call | flops 4950000128 | bytes 13500000 | tf_op jit(solution)/shard_map/pallas_call | solution.py:407
  188.6 2.1 collective-permute-start.60
  190.7 1.4 collective-permute-start.57
  192.1 0.8 collective-permute-start.58
  192.9 1.3 collective-permute-start.59
  194.2 2.0 collective-permute-start.61
  196.2 7.3 %collective-permute-done.60._.a_ref = bf16[336,240]{1,0:T(8,128)(2,1)S(1)} collective-permute-done((bf16[336,240]{1,0:T(8,128)(2,1)}, bf16[336,240]{1,0:T(8,128)(2,1)S(1)}, u32[]{:S(2)}, u32[]{:S(2)}) %collective-permute-start.60) | collective-permute-done | bytes 161312 | tf_op jit(solution)/shard_map/ppermute | solution.py:71
  204.1 2.0 shard_map.233
  207.5 2.3 %shard_map.232.rest_0_ = bf16[960,128]{1,0:T(8,128)(2,1)} custom-call(f32[128,960]{1,0:T(8,128)} %get-tuple-element.78.rest_5_.x2_ref, f32[128,960]{1,0:T(8,128)} %get-tuple-element.110.rest_18_.own_ref, bf16[128,960]{1,0:T(8,128)(2,1)} %copy-done.37, bf16[128,960]{1,0:T(8,128)(2,1)} %copy-done.38, bf16[128,960]{1,0:T(8,128)(2,1)} %copy-done.39), custom_call_target="tpu_custom_call" | custom-call | flops 1100000000 | bytes 3000000 | tf_op jit(solution)/shard_map/pallas_call | solution.py:407
  210.5 3.0 %collective-permute-done.62.c_ref = bf16[336,240]{1,0:T(8,128)(2,1)} collective-permute-done((bf16[336,240]{1,0:T(8,128)(2,1)}, bf16[336,240]{1,0:T(8,128)(2,1)}, u32[]{:S(2)}, u32[]{:S(2)}) %collective-permute-start.62) | collective-permute-done | bytes 161312 | tf_op jit(solution)/shard_map/ppermute | solution.py:71
  213.5 2.2 shard_map.234
  (217 shorter events, 22.1 us)
Async XLA Ops:
  7.2 72.4 %all-gather.3.cloned.1.call-start = ((), (), s32[]{:S(2)}) async-start(), calls=%async_computation.2 | async-start | bytes 2304000 | tf_op jit(solution)/shard_map/all_gather | solution.py:980
  7.2 13.8 %collective-permute-start.1 = (bf16[960,128]{1,0:T(8,128)(2,1)}, bf16[960,128]{1,0:T(8,128)(2,1)S(1)}, u32[]{:S(2)}, u32[]{:S(2)}) collective-permute-start(bf16[960,128]{1,0:T(8,128)(2,1)} %bitcast.34), channel_id=1, source_target_pairs={{0,8},{4,12},{8,0},{12,4},{16,24},{20,28},{24,16},{28,20},{1,9},{5... | collective-permute-start | bytes 737288 | tf_op jit(solution)/shard_map/ppermute | solution.py:71
  8.8 12.9 %collective-permute-start.2 = (bf16[960,128]{1,0:T(8,128)(2,1)}, bf16[960,128]{1,0:T(8,128)(2,1)S(1)}, u32[]{:S(2)}, u32[]{:S(2)}) collective-permute-start(bf16[960,128]{1,0:T(8,128)(2,1)} %bitcast.35), channel_id=1, source_target_pairs={{0,16},{4,20},{8,24},{12,28},{16,0},{20,4},{24,8},{28,12},{1,17},{... | collective-permute-start | bytes 737288 | tf_op jit(solution)/shard_map/ppermute | solution.py:71
  10.3 11.4 %collective-permute-start.3 = (bf16[960,128]{1,0:T(8,128)(2,1)}, bf16[960,128]{1,0:T(8,128)(2,1)S(1)}, u32[]{:S(2)}, u32[]{:S(2)}) collective-permute-start(bf16[960,128]{1,0:T(8,128)(2,1)} %bitcast.36), channel_id=1, source_target_pairs={{0,24},{4,28},{8,16},{12,20},{16,8},{20,12},{24,0},{28,4},{1,25},{... | collective-permute-start | bytes 737288 | tf_op jit(solution)/shard_map/ppermute | solution.py:71
  12.6 8.5 %collective-permute-start = (bf16[120,640]{1,0:T(8,128)(2,1)}, bf16[120,640]{1,0:T(8,128)(2,1)S(1)}, u32[]{:S(2)}, u32[]{:S(2)}) collective-permute-start(bf16[120,640]{1,0:T(8,128)(2,1)} %shard_map.212.own_ref), channel_id=1, source_target_pairs={{0,2},{1,3},{2,0},{3,1},{4,6},{5,7},{6,4},{7,5},{8,10},{9,11},{10,... | collective-permute-start | bytes 460808 | tf_op jit(solution)/shard_map/ppermute | solution.py:71
  24.3 9.1 %collective-permute-start.5 = (bf16[256,640]{1,0:T(8,128)(2,1)}, bf16[256,640]{1,0:T(8,128)(2,1)S(1)}, u32[]{:S(2)}, u32[]{:S(2)}) collective-permute-start(bf16[256,640]{1,0:T(8,128)(2,1)} %shard_map.213.rest_0_.rest_15_), channel_id=1, source_target_pairs={{0,8},{4,12},{8,0},{12,4},{16,24},{20,28},{24,16},{28,20},{1,9},{5... | collective-permute-start | bytes 983048 | tf_op jit(solution)/shard_map/ppermute | solution.py:71
  25.4 9.2 %collective-permute-start.6 = (bf16[256,640]{1,0:T(8,128)(2,1)}, bf16[256,640]{1,0:T(8,128)(2,1)S(1)}, u32[]{:S(2)}, u32[]{:S(2)}) collective-permute-start(bf16[256,640]{1,0:T(8,128)(2,1)} %shard_map.213.rest_0_.rest_15_), channel_id=1, source_target_pairs={{0,1},{1,0},{2,3},{3,2},{4,5},{5,4},{6,7},{7,6},{8,9},{9,8},{10,11... | collective-permute-start | bytes 983048 | tf_op jit(solution)/shard_map/ppermute | solution.py:71
  26.5 8.2 %collective-permute-start.7 = (bf16[256,640]{1,0:T(8,128)(2,1)}, bf16[256,640]{1,0:T(8,128)(2,1)S(1)}, u32[]{:S(2)}, u32[]{:S(2)}) collective-permute-start(bf16[256,640]{1,0:T(8,128)(2,1)} %shard_map.213.rest_0_.rest_15_), channel_id=1, source_target_pairs={{0,16},{4,20},{8,24},{12,28},{16,0},{20,4},{24,8},{28,12},{1,17},{... | collective-permute-start | bytes 983048 | tf_op jit(solution)/shard_map/ppermute | solution.py:71
  38.2 110.2 %all-gather.5.cloned.1.call-start = ((), (), s32[]{:S(2)}) async-start(), calls=%async_computation.3 | async-start | bytes 2359296 | tf_op jit(solution)/shard_map/all_gather | solution.py:1024
  38.2 8.1 %collective-permute-start.8 = (bf16[256,640]{1,0:T(8,128)(2,1)S(1)}, bf16[256,640]{1,0:T(8,128)(2,1)S(1)}, u32[]{:S(2)}, u32[]{:S(2)}) collective-permute-start(bf16[256,640]{1,0:T(8,128)(2,1)S(1)} %copy-done.13), channel_id=1, source_target_pairs={{0,16},{4,20},{8,24},{12,28},{16,0},{20,4},{24,8},{28,12},{1,17},{... | collective-permute-start | bytes 983048 | tf_op jit(solution)/shard_map/ppermute | solution.py:71
  39.8 8.9 %collective-permute-start.4 = (bf16[256,640]{1,0:T(8,128)(2,1)}, bf16[256,640]{1,0:T(8,128)(2,1)S(1)}, u32[]{:S(2)}, u32[]{:S(2)}) collective-permute-start(bf16[256,640]{1,0:T(8,128)(2,1)} %shard_map.213.rest_0_.rest_15_), channel_id=1, source_target_pairs={{0,4},{4,0},{8,12},{12,8},{16,20},{20,16},{24,28},{28,24},{1,5},{5... | collective-permute-start | bytes 983048 | tf_op jit(solution)/shard_map/ppermute | solution.py:71
  40.5 9.6 %collective-permute-start.13 = (bf16[256,640]{1,0:T(8,128)(2,1)S(1)}, bf16[256,640]{1,0:T(8,128)(2,1)S(1)}, u32[]{:S(2)}, u32[]{:S(2)}) collective-permute-start(bf16[256,640]{1,0:T(8,128)(2,1)S(1)} %copy-done.13), channel_id=1, source_target_pairs={{0,4},{4,0},{8,12},{12,8},{16,20},{20,16},{24,28},{28,24},{1,5},{5... | collective-permute-start | bytes 983048 | tf_op jit(solution)/shard_map/ppermute | solution.py:71
  41.0 10.6 %collective-permute-start.14 = (bf16[256,640]{1,0:T(8,128)(2,1)S(1)}, bf16[256,640]{1,0:T(8,128)(2,1)S(1)}, u32[]{:S(2)}, u32[]{:S(2)}) collective-permute-start(bf16[256,640]{1,0:T(8,128)(2,1)S(1)} %copy-done.13), channel_id=1, source_target_pairs={{0,8},{4,12},{8,0},{12,4},{16,24},{20,28},{24,16},{28,20},{1,9},{5... | collective-permute-start | bytes 983048 | tf_op jit(solution)/shard_map/ppermute | solution.py:71
  41.6 8.5 %collective-permute-start.10 = (bf16[256,640]{1,0:T(8,128)(2,1)S(1)}, bf16[256,640]{1,0:T(8,128)(2,1)S(1)}, u32[]{:S(2)}, u32[]{:S(2)}) collective-permute-start(bf16[256,640]{1,0:T(8,128)(2,1)S(1)} %copy-done.11), channel_id=1, source_target_pairs={{0,4},{4,0},{8,12},{12,8},{16,20},{20,16},{24,28},{28,24},{1,5},{5... | collective-permute-start | bytes 983048 | tf_op jit(solution)/shard_map/ppermute | solution.py:71
  47.1 7.4 %collective-permute-start.11 = (bf16[256,640]{1,0:T(8,128)(2,1)}, bf16[256,640]{1,0:T(8,128)(2,1)S(1)}, u32[]{:S(2)}, u32[]{:S(2)}) collective-permute-start(bf16[256,640]{1,0:T(8,128)(2,1)} %get-tuple-element.76.rest_2_.rest_17_), channel_id=1, source_target_pairs={{0,16},{4,20},{8,24},{12,28},{16,0},{20,4},{24,8},{28,12},{1,17},{... | collective-permute-start | bytes 983048 | tf_op jit(solution)/shard_map/ppermute | solution.py:71
  48.7 9.0 %collective-permute-start.17 = (bf16[256,640]{1,0:T(8,128)(2,1)}, bf16[256,640]{1,0:T(8,128)(2,1)S(1)}, u32[]{:S(2)}, u32[]{:S(2)}) collective-permute-start(bf16[256,640]{1,0:T(8,128)(2,1)} %get-tuple-element.77.rest_12_.refs_1_.rest_27_), channel_id=1, source_target_pairs={{0,8},{4,12},{8,0},{12,4},{16,24},{20,28},{24,16},{28,20},{1,9},{5... | collective-permute-start | bytes 983048 | tf_op jit(solution)/shard_map/ppermute | solution.py:71
  50.1 8.7 %collective-permute-start.9 = (bf16[256,640]{1,0:T(8,128)(2,1)}, bf16[256,640]{1,0:T(8,128)(2,1)S(1)}, u32[]{:S(2)}, u32[]{:S(2)}) collective-permute-start(bf16[256,640]{1,0:T(8,128)(2,1)} %get-tuple-element.76.rest_2_.rest_17_), channel_id=1, source_target_pairs={{0,4},{4,0},{8,12},{12,8},{16,20},{20,16},{24,28},{28,24},{1,5},{5... | collective-permute-start | bytes 983048 | tf_op jit(solution)/shard_map/ppermute | solution.py:71
  50.2 9.8 %collective-permute-start.16 = (bf16[256,640]{1,0:T(8,128)(2,1)}, bf16[256,640]{1,0:T(8,128)(2,1)S(1)}, u32[]{:S(2)}, u32[]{:S(2)}) collective-permute-start(bf16[256,640]{1,0:T(8,128)(2,1)} %get-tuple-element.77.rest_12_.refs_1_.rest_27_), channel_id=1, source_target_pairs={{0,4},{4,0},{8,12},{12,8},{16,20},{20,16},{24,28},{28,24},{1,5},{5... | collective-permute-start | bytes 983048 | tf_op jit(solution)/shard_map/ppermute | solution.py:71
  51.6 7.8 %collective-permute-start.15 = (bf16[256,640]{1,0:T(8,128)(2,1)S(1)}, bf16[256,640]{1,0:T(8,128)(2,1)S(1)}, u32[]{:S(2)}, u32[]{:S(2)}) collective-permute-start(bf16[256,640]{1,0:T(8,128)(2,1)S(1)} %collective-permute-done.14.rest_10_.refs_2_.rest_25_), channel_id=1, source_target_pairs={{0,4},{4,0},{8,12},{12,8},{16,20},{20,16},{24,28},{28,24},{1,5},{5... | collective-permute-start | bytes 983048 | tf_op jit(solution)/shard_map/ppermute | solution.py:71
  54.5 8.1 %collective-permute-start.12 = (bf16[256,640]{1,0:T(8,128)(2,1)S(1)}, bf16[256,640]{1,0:T(8,128)(2,1)}, u32[]{:S(2)}, u32[]{:S(2)}) collective-permute-start(bf16[256,640]{1,0:T(8,128)(2,1)S(1)} %collective-permute-done.11.rest_6_.rest_21_), channel_id=1, source_target_pairs={{0,4},{4,0},{8,12},{12,8},{16,20},{20,16},{24,28},{28,24},{1,5},{5... | collective-permute-start | bytes 983048 | tf_op jit(solution)/shard_map/ppermute | solution.py:71
  57.7 4.8 %collective-permute-start.18 = (bf16[256,640]{1,0:T(8,128)(2,1)S(1)}, bf16[256,640]{1,0:T(8,128)(2,1)}, u32[]{:S(2)}, u32[]{:S(2)}) collective-permute-start(bf16[256,640]{1,0:T(8,128)(2,1)S(1)} %collective-permute-done.17.rest_14_.rest_29_), channel_id=1, source_target_pairs={{0,4},{4,0},{8,12},{12,8},{16,20},{20,16},{24,28},{28,24},{1,5},{5... | collective-permute-start | bytes 983048 | tf_op jit(solution)/shard_map/ppermute | solution.py:71
  58.8 15.3 %collective-permute-start.23 = (bf16[960,128]{1,0:T(8,128)(2,1)}, bf16[960,128]{1,0:T(8,128)(2,1)}, u32[]{:S(2)}, u32[]{:S(2)}) collective-permute-start(bf16[960,128]{1,0:T(8,128)(2,1)} %shard_map.218.rest_0_), channel_id=1, source_target_pairs={{0,8},{4,12},{8,0},{12,4},{16,24},{20,28},{24,16},{28,20},{1,9},{5... | collective-permute-start | bytes 737288 | tf_op jit(solution)/shard_map/ppermute | solution.py:71
  59.4 14.7 %collective-permute-start.24 = (bf16[960,128]{1,0:T(8,128)(2,1)}, bf16[960,128]{1,0:T(8,128)(2,1)}, u32[]{:S(2)}, u32[]{:S(2)}) collective-permute-start(bf16[960,128]{1,0:T(8,128)(2,1)} %shard_map.218.rest_0_), channel_id=1, source_target_pairs={{0,16},{4,20},{8,24},{12,28},{16,0},{20,4},{24,8},{28,12},{1,17},{... | collective-permute-start | bytes 737288 | tf_op jit(solution)/shard_map/ppermute | solution.py:71
  60.0 14.1 %collective-permute-start.25 = (bf16[960,128]{1,0:T(8,128)(2,1)}, bf16[960,128]{1,0:T(8,128)(2,1)}, u32[]{:S(2)}, u32[]{:S(2)}) collective-permute-start(bf16[960,128]{1,0:T(8,128)(2,1)} %shard_map.218.rest_0_), channel_id=1, source_target_pairs={{0,24},{4,28},{8,16},{12,20},{16,8},{20,12},{24,0},{28,4},{1,25},{... | collective-permute-start | bytes 737288 | tf_op jit(solution)/shard_map/ppermute | solution.py:71
  72.9 12.8 %collective-permute-start.20 = (bf16[128,960]{1,0:T(8,128)(2,1)}, bf16[128,960]{1,0:T(8,128)(2,1)S(1)}, u32[]{:S(2)}, u32[]{:S(2)}) collective-permute-start(bf16[128,960]{1,0:T(8,128)(2,1)} %get-tuple-element.79.rest_0_), channel_id=1, source_target_pairs={{0,8},{4,12},{8,0},{12,4},{16,24},{20,28},{24,16},{28,20},{1,9},{5... | collective-permute-start | bytes 737288 | tf_op jit(solution)/shard_map/ppermute | solution.py:71
  73.5 16.0 %collective-permute-start.21 = (bf16[128,960]{1,0:T(8,128)(2,1)}, bf16[128,960]{1,0:T(8,128)(2,1)S(1)}, u32[]{:S(2)}, u32[]{:S(2)}) collective-permute-start(bf16[128,960]{1,0:T(8,128)(2,1)} %get-tuple-element.79.rest_0_), channel_id=1, source_target_pairs={{0,16},{4,20},{8,24},{12,28},{16,0},{20,4},{24,8},{28,12},{1,17},{... | collective-permute-start | bytes 737288 | tf_op jit(solution)/shard_map/ppermute | solution.py:71
  82.2 7.3 %collective-permute-start.27 = (bf16[128,640]{1,0:T(8,128)(2,1)}, bf16[128,640]{1,0:T(8,128)(2,1)S(1)}, u32[]{:S(2)}, u32[]{:S(2)}) collective-permute-start(bf16[128,640]{1,0:T(8,128)(2,1)} %get-tuple-element.81), channel_id=1, source_target_pairs={{0,8},{4,12},{8,0},{12,4},{16,24},{20,28},{24,16},{28,20},{1,9},{5... | collective-permute-start | bytes 491528 | tf_op jit(solution)/shard_map/ppermute | solution.py:71
  83.7 16.5 %collective-permute-start.22 = (bf16[128,960]{1,0:T(8,128)(2,1)S(1)}, bf16[128,960]{1,0:T(8,128)(2,1)S(1)}, u32[]{:S(2)}, u32[]{:S(2)}) collective-permute-start(bf16[128,960]{1,0:T(8,128)(2,1)S(1)} %copy-done.31), channel_id=1, source_target_pairs={{0,24},{4,28},{8,16},{12,20},{16,8},{20,12},{24,0},{28,4},{1,25},{... | collective-permute-start | bytes 737288 | tf_op jit(solution)/shard_map/ppermute | solution.py:71
  85.1 14.5 %collective-permute-start.28 = (bf16[128,640]{1,0:T(8,128)(2,1)}, bf16[128,640]{1,0:T(8,128)(2,1)S(1)}, u32[]{:S(2)}, u32[]{:S(2)}) collective-permute-start(bf16[128,640]{1,0:T(8,128)(2,1)} %get-tuple-element.82), channel_id=1, source_target_pairs={{0,16},{4,20},{8,24},{12,28},{16,0},{20,4},{24,8},{28,12},{1,17},{... | collective-permute-start | bytes 491528 | tf_op jit(solution)/shard_map/ppermute | solution.py:71
  85.7 13.9 %collective-permute-start.29 = (bf16[128,640]{1,0:T(8,128)(2,1)}, bf16[128,640]{1,0:T(8,128)(2,1)S(1)}, u32[]{:S(2)}, u32[]{:S(2)}) collective-permute-start(bf16[128,640]{1,0:T(8,128)(2,1)} %get-tuple-element.83), channel_id=1, source_target_pairs={{0,24},{4,28},{8,16},{12,20},{16,8},{20,12},{24,0},{28,4},{1,25},{... | collective-permute-start | bytes 491528 | tf_op jit(solution)/shard_map/ppermute | solution.py:71
  89.5 11.2 %collective-permute-start.37 = (bf16[128,640]{1,0:T(8,128)(2,1)S(1)}, bf16[128,640]{1,0:T(8,128)(2,1)S(1)}, u32[]{:S(2)}, u32[]{:S(2)}) collective-permute-start(bf16[128,640]{1,0:T(8,128)(2,1)S(1)} %collective-permute-done.27.refs_4_.rest_19_), channel_id=1, source_target_pairs={{0,4},{4,0},{8,12},{12,8},{16,20},{20,16},{24,28},{28,24},{1,5},{5... | collective-permute-start | bytes 491528 | tf_op jit(solution)/shard_map/ppermute | solution.py:71
  89.6 10.7 %collective-permute-start.26 = (bf16[64,640]{1,0:T(8,128)(2,1)}, bf16[64,640]{1,0:T(8,128)(2,1)S(1)}, u32[]{:S(2)}, u32[]{:S(2)}) collective-permute-start(bf16[64,640]{1,0:T(8,128)(2,1)} %get-tuple-element.80), channel_id=1, source_target_pairs={{0,4},{4,0},{8,12},{12,8},{16,20},{20,16},{24,28},{28,24},{1,5},{5... | collective-permute-start | bytes 245768 | tf_op jit(solution)/shard_map/ppermute | solution.py:71
  99.7 1.6 collective-permute-start.39
  100.2 2.6 %collective-permute-start.33 = (bf16[960,128]{1,0:T(8,128)(2,1)}, bf16[960,128]{1,0:T(8,128)(2,1)S(1)}, u32[]{:S(2)}, u32[]{:S(2)}) collective-permute-start(bf16[960,128]{1,0:T(8,128)(2,1)} %bitcast.37), channel_id=1, source_target_pairs={{0,4},{4,0},{8,12},{12,8},{16,20},{20,16},{24,28},{28,24},{1,5},{5... | collective-permute-start | bytes 737288 | tf_op jit(solution)/shard_map/ppermute | solution.py:71
  100.3 2.9 %collective-permute-start.34 = (bf16[960,128]{1,0:T(8,128)(2,1)}, bf16[960,128]{1,0:T(8,128)(2,1)S(1)}, u32[]{:S(2)}, u32[]{:S(2)}) collective-permute-start(bf16[960,128]{1,0:T(8,128)(2,1)} %copy-done.41), channel_id=1, source_target_pairs={{0,4},{4,0},{8,12},{12,8},{16,20},{20,16},{24,28},{28,24},{1,5},{5... | collective-permute-start | bytes 737288 | tf_op jit(solution)/shard_map/ppermute | solution.py:71
  100.7 2.7 %collective-permute-start.35 = (bf16[960,128]{1,0:T(8,128)(2,1)}, bf16[960,128]{1,0:T(8,128)(2,1)}, u32[]{:S(2)}, u32[]{:S(2)}) collective-permute-start(bf16[960,128]{1,0:T(8,128)(2,1)} %copy-done.42), channel_id=1, source_target_pairs={{0,4},{4,0},{8,12},{12,8},{16,20},{20,16},{24,28},{28,24},{1,5},{5... | collective-permute-start | bytes 737288 | tf_op jit(solution)/shard_map/ppermute | solution.py:71
  102.0 80.3 %reduce-scatter.5.cloned.1.call-start = ((), (), s32[]{:S(2)}) async-start(), calls=%async_computation.4 | async-start | bytes 1536000 | tf_op jit(solution)/shard_map/reduce_scatter | solution.py:1075
  102.8 1.7 collective-permute-start.30
  103.1 1.8 collective-permute-start.31
  103.4 1.8 collective-permute-start.32
  119.2 3.2 %collective-permute-start.40 = (bf16[560,1024]{1,0:T(8,128)(2,1)}, bf16[560,1024]{1,0:T(8,128)(2,1)}, u32[]{:S(2)}, u32[]{:S(2)}) collective-permute-start(bf16[560,1024]{1,0:T(8,128)(2,1)} %get-tuple-element.92), channel_id=1, source_target_pairs={{0,4},{4,0},{8,12},{12,8},{16,20},{20,16},{24,28},{28,24},{1,5},{5... | collective-permute-start | bytes 3440648 | tf_op jit(solution)/shard_map/ppermute | solution.py:71
  125.7 12.9 %collective-permute-start.41 = (bf16[208,960]{1,0:T(8,128)(2,1)}, bf16[208,960]{1,0:T(8,128)(2,1)S(1)}, u32[]{:S(2)}, u32[]{:S(2)}) collective-permute-start(bf16[208,960]{1,0:T(8,128)(2,1)} %get-tuple-element.99), channel_id=1, source_target_pairs={{0,8},{4,12},{8,0},{12,4},{16,24},{20,28},{24,16},{28,20},{1,9},{5... | collective-permute-start | bytes 1198088 | tf_op jit(solution)/shard_map/ppermute | solution.py:71
  127.1 21.2 %collective-permute-start.42 = (bf16[208,960]{1,0:T(8,128)(2,1)}, bf16[208,960]{1,0:T(8,128)(2,1)}, u32[]{:S(2)}, u32[]{:S(2)}) collective-permute-start(bf16[208,960]{1,0:T(8,128)(2,1)} %get-tuple-element.100), channel_id=1, source_target_pairs={{0,16},{4,20},{8,24},{12,28},{16,0},{20,4},{24,8},{28,12},{1,17},{... | collective-permute-start | bytes 1198088 | tf_op jit(solution)/shard_map/ppermute | solution.py:71
  127.8 20.5 %collective-permute-start.43 = (bf16[208,960]{1,0:T(8,128)(2,1)}, bf16[208,960]{1,0:T(8,128)(2,1)}, u32[]{:S(2)}, u32[]{:S(2)}) collective-permute-start(bf16[208,960]{1,0:T(8,128)(2,1)} %get-tuple-element.101), channel_id=1, source_target_pairs={{0,24},{4,28},{8,16},{12,20},{16,8},{20,12},{24,0},{28,4},{1,25},{... | collective-permute-start | bytes 1198088 | tf_op jit(solution)/shard_map/ppermute | solution.py:71
  148.4 61.5 %reduce-scatter.7.cloned.1.call-start = ((), (), s32[]{:S(2)}) async-start(), calls=%async_computation.5 | async-start | bytes 768000
  161.3 14.7 %collective-permute-start.44 = (bf16[512,1024]{1,0:T(8,128)(2,1)}, bf16[512,1024]{1,0:T(8,128)(2,1)}, u32[]{:S(2)}, u32[]{:S(2)}) collective-permute-start(bf16[512,1024]{1,0:T(8,128)(2,1)} %shard_map.227), channel_id=1, source_target_pairs={{0,4},{4,0},{8,12},{12,8},{16,20},{20,16},{24,28},{28,24},{1,5},{5... | collective-permute-start | bytes 3145736 | tf_op jit(solution)/shard_map/ppermute | solution.py:71
  162.2 2.5 %collective-permute-start.56 = (bf16[128,960]{1,0:T(8,128)(2,1)S(1)}, bf16[128,960]{1,0:T(8,128)(2,1)S(1)}, u32[]{:S(2)}, u32[]{:S(2)}) collective-permute-start(bf16[128,960]{1,0:T(8,128)(2,1)S(1)} %copy-done.36), channel_id=1, source_target_pairs={{0,4},{4,0},{8,12},{12,8},{16,20},{20,16},{24,28},{28,24},{1,5},{5... | collective-permute-start | bytes 737288 | tf_op jit(solution)/shard_map/ppermute | solution.py:71
  162.3 6.5 %collective-permute-start.45 = (bf16[960,128]{1,0:T(8,128)(2,1)S(1)}, bf16[960,128]{1,0:T(8,128)(2,1)S(1)}, u32[]{:S(2)}, u32[]{:S(2)}) collective-permute-start(bf16[960,128]{1,0:T(8,128)(2,1)S(1)} %copy-done.8), channel_id=1, source_target_pairs={{0,4},{4,0},{8,12},{12,8},{16,20},{20,16},{24,28},{28,24},{1,5},{5... | collective-permute-start | bytes 737288 | tf_op jit(solution)/shard_map/ppermute | solution.py:71
  162.8 6.2 %collective-permute-start.46 = (bf16[960,128]{1,0:T(8,128)(2,1)}, bf16[960,128]{1,0:T(8,128)(2,1)}, u32[]{:S(2)}, u32[]{:S(2)}) collective-permute-start(bf16[960,128]{1,0:T(8,128)(2,1)} %collective-permute-done.23.rest_1_.rest_2_), channel_id=1, source_target_pairs={{0,4},{4,0},{8,12},{12,8},{16,20},{20,16},{24,28},{28,24},{1,5},{5... | collective-permute-start | bytes 737288 | tf_op jit(solution)/shard_map/ppermute | solution.py:71
  168.2 1.8 collective-permute-start.47
  168.4 2.2 %collective-permute-start.48 = (bf16[960,128]{1,0:T(8,128)(2,1)}, bf16[960,128]{1,0:T(8,128)(2,1)}, u32[]{:S(2)}, u32[]{:S(2)}) collective-permute-start(bf16[960,128]{1,0:T(8,128)(2,1)} %collective-permute-done.25.rest_3_.rest_6_), channel_id=1, source_target_pairs={{0,4},{4,0},{8,12},{12,8},{16,20},{20,16},{24,28},{28,24},{1,5},{5... | collective-permute-start | bytes 737288 | tf_op jit(solution)/shard_map/ppermute | solution.py:71
  168.8 2.7 %collective-permute-start.49 = (bf16[80,640]{1,0:T(8,128)(2,1)}, bf16[80,640]{1,0:T(8,128)(2,1)S(1)}, u32[]{:S(2)}, u32[]{:S(2)}) collective-permute-start(bf16[80,640]{1,0:T(8,128)(2,1)} %get-tuple-element.114), channel_id=1, source_target_pairs={{0,4},{4,0},{8,12},{12,8},{16,20},{20,16},{24,28},{28,24},{1,5},{5... | collective-permute-start | bytes 307208 | tf_op jit(solution)/shard_map/ppermute | solution.py:71
  168.9 5.9 %collective-permute-start.50 = (bf16[80,640]{1,0:T(8,128)(2,1)}, bf16[80,640]{1,0:T(8,128)(2,1)S(1)}, u32[]{:S(2)}, u32[]{:S(2)}) collective-permute-start(bf16[80,640]{1,0:T(8,128)(2,1)} %get-tuple-element.115), channel_id=1, source_target_pairs={{0,8},{4,12},{8,0},{12,4},{16,24},{20,28},{24,16},{28,20},{1,9},{5... | collective-permute-start | bytes 307208 | tf_op jit(solution)/shard_map/ppermute | solution.py:71
  170.0 9.2 %collective-permute-start.51 = (bf16[80,640]{1,0:T(8,128)(2,1)}, bf16[80,640]{1,0:T(8,128)(2,1)}, u32[]{:S(2)}, u32[]{:S(2)}) collective-permute-start(bf16[80,640]{1,0:T(8,128)(2,1)} %get-tuple-element.116), channel_id=1, source_target_pairs={{0,12},{4,8},{8,4},{12,0},{16,28},{20,24},{24,20},{28,16},{1,13},{... | collective-permute-start | bytes 307208 | tf_op jit(solution)/shard_map/ppermute | solution.py:71
  170.7 8.6 %collective-permute-start.52 = (bf16[80,640]{1,0:T(8,128)(2,1)}, bf16[80,640]{1,0:T(8,128)(2,1)}, u32[]{:S(2)}, u32[]{:S(2)}) collective-permute-start(bf16[80,640]{1,0:T(8,128)(2,1)} %get-tuple-element.117), channel_id=1, source_target_pairs={{0,16},{4,20},{8,24},{12,28},{16,0},{20,4},{24,8},{28,12},{1,17},{... | collective-permute-start | bytes 307208 | tf_op jit(solution)/shard_map/ppermute | solution.py:71
  171.5 7.7 %collective-permute-start.53 = (bf16[80,640]{1,0:T(8,128)(2,1)}, bf16[80,640]{1,0:T(8,128)(2,1)}, u32[]{:S(2)}, u32[]{:S(2)}) collective-permute-start(bf16[80,640]{1,0:T(8,128)(2,1)} %get-tuple-element.118), channel_id=1, source_target_pairs={{0,20},{4,16},{8,28},{12,24},{16,4},{20,0},{24,12},{28,8},{1,21},{... | collective-permute-start | bytes 307208 | tf_op jit(solution)/shard_map/ppermute | solution.py:71
  174.9 6.3 %collective-permute-start.54 = (bf16[80,640]{1,0:T(8,128)(2,1)S(1)}, bf16[80,640]{1,0:T(8,128)(2,1)}, u32[]{:S(2)}, u32[]{:S(2)}) collective-permute-start(bf16[80,640]{1,0:T(8,128)(2,1)S(1)} %copy-done.53), channel_id=1, source_target_pairs={{0,24},{4,28},{8,16},{12,20},{16,8},{20,12},{24,0},{28,4},{1,25},{... | collective-permute-start | bytes 307208 | tf_op jit(solution)/shard_map/ppermute | solution.py:71
  176.0 6.2 %collective-permute-start.55 = (bf16[80,640]{1,0:T(8,128)(2,1)S(1)}, bf16[80,640]{1,0:T(8,128)(2,1)}, u32[]{:S(2)}, u32[]{:S(2)}) collective-permute-start(bf16[80,640]{1,0:T(8,128)(2,1)S(1)} %copy-done.52), channel_id=1, source_target_pairs={{0,28},{4,24},{8,20},{12,16},{16,12},{20,8},{24,4},{28,0},{1,29},{... | collective-permute-start | bytes 307208 | tf_op jit(solution)/shard_map/ppermute | solution.py:71
  188.6 14.8 %collective-permute-start.60 = (bf16[336,240]{1,0:T(8,128)(2,1)}, bf16[336,240]{1,0:T(8,128)(2,1)S(1)}, u32[]{:S(2)}, u32[]{:S(2)}) collective-permute-start(bf16[336,240]{1,0:T(8,128)(2,1)} %get-tuple-element.129), channel_id=1, source_target_pairs={{0,1},{1,0},{2,3},{3,2},{4,5},{5,4},{6,7},{7,6},{8,9},{9,8},{10,11... | collective-permute-start | bytes 483848 | tf_op jit(solution)/shard_map/ppermute | solution.py:71
  190.7 15.4 %collective-permute-start.57 = (bf16[128,960]{1,0:T(8,128)(2,1)}, bf16[128,960]{1,0:T(8,128)(2,1)S(1)}, u32[]{:S(2)}, u32[]{:S(2)}) collective-permute-start(bf16[128,960]{1,0:T(8,128)(2,1)} %get-tuple-element.125), channel_id=1, source_target_pairs={{0,8},{4,12},{8,0},{12,4},{16,24},{20,28},{24,16},{28,20},{1,9},{5... | collective-permute-start | bytes 737288 | tf_op jit(solution)/shard_map/ppermute | solution.py:71
  192.1 13.9 %collective-permute-start.58 = (bf16[128,960]{1,0:T(8,128)(2,1)}, bf16[128,960]{1,0:T(8,128)(2,1)S(1)}, u32[]{:S(2)}, u32[]{:S(2)}) collective-permute-start(bf16[128,960]{1,0:T(8,128)(2,1)} %get-tuple-element.126), channel_id=1, source_target_pairs={{0,16},{4,20},{8,24},{12,28},{16,0},{20,4},{24,8},{28,12},{1,17},{... | collective-permute-start | bytes 737288 | tf_op jit(solution)/shard_map/ppermute | solution.py:71
  192.9 13.2 %collective-permute-start.59 = (bf16[128,960]{1,0:T(8,128)(2,1)}, bf16[128,960]{1,0:T(8,128)(2,1)S(1)}, u32[]{:S(2)}, u32[]{:S(2)}) collective-permute-start(bf16[128,960]{1,0:T(8,128)(2,1)} %get-tuple-element.127), channel_id=1, source_target_pairs={{0,24},{4,28},{8,16},{12,20},{16,8},{20,12},{24,0},{28,4},{1,25},{... | collective-permute-start | bytes 737288 | tf_op jit(solution)/shard_map/ppermute | solution.py:71
  194.2 16.3 %collective-permute-start.61 = (bf16[336,240]{1,0:T(8,128)(2,1)}, bf16[336,240]{1,0:T(8,128)(2,1)}, u32[]{:S(2)}, u32[]{:S(2)}) collective-permute-start(bf16[336,240]{1,0:T(8,128)(2,1)} %get-tuple-element.130), channel_id=1, source_target_pairs={{0,2},{1,3},{2,0},{3,1},{4,6},{5,7},{6,4},{7,5},{8,10},{9,11},{10,... | collective-permute-start | bytes 483848 | tf_op jit(solution)/shard_map/ppermute | solution.py:71
  203.5 10.0 %collective-permute-start.62 = (bf16[336,240]{1,0:T(8,128)(2,1)}, bf16[336,240]{1,0:T(8,128)(2,1)}, u32[]{:S(2)}, u32[]{:S(2)}) collective-permute-start(bf16[336,240]{1,0:T(8,128)(2,1)} %get-tuple-element.131), channel_id=1, source_target_pairs={{0,3},{1,2},{2,1},{3,0},{4,7},{5,6},{6,5},{7,4},{8,11},{9,10},{10,... | collective-permute-start | bytes 483848 | tf_op jit(solution)/shard_map/ppermute | solution.py:71
  (60 other events, 234.7 us)
Sparse Core Ops, SparseCore 0:
  38.3 41.2 all-gather.2
  102.1 27.4 all-gather.4
  148.5 28.0 reduce-scatter.4
  178.8 26.2 reduce-scatter.6

commit v4 on v3

--- a/solution.py
+++ b/solution.py
@@ -522,20 +522,6 @@
     return jnp.concatenate([rows[:, :320], rows[:, 320:640], rows[:, 640:960]], 0)
 
 
-def join_down(ids, own_ref, pair_ref, *rest):
-    others, passed_ref, out_ref, buffer = rest[:3], rest[3], rest[-2], rest[-1]
-    d = ids[0]
-    buffer[d] = restore_block(own_ref[...].astype(F32)[:40])
-    buffer[d ^ 1] = restore_block(pair_ref[...].astype(F32)[:40])
-    passed = passed_ref[...].astype(F32)
-    for i in (1, 2, 3):
-        buffer[d ^ (2 * i)] = restore_block(others[i - 1][128:].astype(F32)[:40])
-        buffer[d ^ (2 * i + 1)] = restore_block(passed[40 * (i - 1) : 40 * i])
-    for j in range(4):
-        both = jnp.concatenate([buffer[2 * j], buffer[2 * j + 1]], 1)
-        out_ref[120 * j : 120 * (j + 1), :] = both.astype(BF16)
-
-
 def join_lines(own_ref, got_ref, ag_ref, fg_ref, *rest):
     out_ref = rest[-1]
     half = own_ref.shape[0]
@@ -569,7 +555,7 @@
     first = rest[:8]
     second = rest[8:16]
     (
-        x2_ref, h2_ref, att_ref, qr_ref, kr_ref, vr_ref, lse_ref, gains_ref,
+        x2_ref, h2_ref, att_ref, qr_ref, kr_ref, vr_ref, probs_ref, gains_ref,
         hb, tb, gb,
     ) = rest[16:]
     d = ids[0]
@@ -616,8 +602,9 @@
         top = jnp.max(scores, -1, keepdims=True)
         exps = jnp.exp(scores - top)
         totals = jnp.sum(exps, -1, keepdims=True)
-        lse_ref[g] = top + jnp.log(totals)
-        probs = (exps / totals).astype(BF16)
+        probs = exps / totals
+        probs_ref[g] = probs
+        probs = probs.astype(BF16)
         out = dot(probs, vr).astype(BF16)
         heads += [out[i * length : (i + 1) * length] for i in range(GROUP)]
     attended = jnp.concatenate(heads, 1)
@@ -669,12 +656,12 @@
         gu[240 * j : 240 * (j + 1), :] = feed_ref[360 * j : 360 * j + 240, :]
     place_exchanged(down_refs, passed, d, db, unfold_block)
     dt[...] = jnp.concatenate([db[i] for i in range(8)], 0).astype(BF16)
-    for copy in c_copies + h_copies:
-        copy.wait()
     units = dt.shape[1]
 
-    def step(c, carry):
-        rows = pl.ds(pl.multiple_of(c * 256, 256), 256)
+    for c in range(4):
+        for copy in h_copies[2 * c : 2 * c + 2] + c_copies[2 * c : 2 * c + 2]:
+            copy.wait()
+        rows = slice(256 * c, 256 * (c + 1))
         both = dot(hs[rows, :], gu[...])
         mixed_grad = contract_first(cs[c], dt[...])
         gate = both[:, :units]
@@ -688,10 +675,7 @@
         delta_ref[rows, :] = deltas
         back = contract_last(deltas, gu[...])
         even_ref[c] = back[:128]
-        odd_ref[pl.ds(pl.multiple_of(c * 128, 128), 128), :960] = back[128:].astype(BF16)
-        return carry
-
-    lax.fori_loop(0, 4, step, 0)
+        odd_ref[128 * c : 128 * (c + 1), :960] = back[128:].astype(BF16)
     for j in range(4):
         part = jnp.zeros((240, 320), F32)
         for c in range(4):
@@ -701,22 +685,25 @@
         db[2 * j + 1] = part[120:]
     filler = jnp.zeros((8, 960), F32)
     own_ref[...] = jnp.concatenate([flatten_block(db[d]), filler], 0).astype(BF16)
-    pair = jnp.concatenate([flatten_block(db[d ^ 1]), filler], 0)
-    odd_ref[512:, :960] = pair.astype(BF16)
+    for i in range(4):
+        block = jnp.concatenate([flatten_block(db[d ^ (2 * i + 1)]), filler], 0)
+        odd_ref[512 + 48 * i : 560 + 48 * i, :960] = block.astype(BF16)
     for i in (1, 2, 3):
-        both = [flatten_block(db[d ^ (2 * i)]), flatten_block(db[d ^ (2 * i + 1)])]
-        fat_refs[i - 1][...] = jnp.concatenate(both, 0).astype(BF16)
+        block = jnp.concatenate([flatten_block(db[d ^ (2 * i)]), filler], 0)
+        fat_refs[i - 1][...] = block.astype(BF16)
 
 
 def pair_sum_down(even_ref, odd_ref, *rest):
     fat_refs, own_ref, pair_ref = rest[:3], rest[3], rest[4]
     rows = own_ref.shape[0]
     own_ref[...] = even_ref[0] + odd_ref[:rows, :960].astype(F32)
-    pair_ref[...] = odd_ref[4 * rows :, :960]
+    pair_ref[...] = odd_ref[4 * rows : 4 * rows + 48, :960]
     for i, ref in enumerate(rest[5:], 1):
         total = even_ref[i] + odd_ref[rows * i : rows * (i + 1), :960].astype(F32)
         ref[:rows] = total.astype(BF16)
-        ref[rows:] = fat_refs[i - 1][...]
+        start = 4 * rows + 48 * i
+        blocks = [fat_refs[i - 1][...].astype(F32)[:40], odd_ref[start : start + 48, :960].astype(F32)[:40]]
+        ref[rows:] = jnp.concatenate(blocks, 0).astype(BF16)
 
 
 def pair_sum(even_ref, odd_ref, *rest):
@@ -750,10 +737,11 @@
 
 def attention_backward(ids, *rest):
     own_ref, a_ref, b_ref, c_ref, cot_ref, x2_ref, x_ref, gains_ref = rest[:8]
-    cos_ref, sin_ref, seg_ref, qr_ref, kr_ref, vr_ref, lse_ref = rest[8:15]
-    first, second = rest[15:23], rest[23:31]
-    outs = rest[-14:-6]
-    grad_ref, pass_ref, fb, db, eb, gb = rest[-6:]
+    cos_ref, sin_ref, qr_ref, kr_ref, vr_ref, probs_ref = rest[8:14]
+    first, second = rest[14:22], rest[22:30]
+    block_ref, pair_ref = rest[30:32]
+    outs = rest[-15:-7]
+    grad_ref, down_ref, fb, db, eb, gb, jb = rest[-7:]
     d = ids[0]
     f = ids[1]
     length = x_ref.shape[1]
@@ -765,9 +753,15 @@
         + b_ref[:128].astype(F32)
         + c_ref[:128].astype(F32)
     )
-    passed = [ref[128:].astype(F32)[40:] for ref in (a_ref, b_ref, c_ref)]
-    passed = jnp.concatenate([*passed, jnp.zeros((8, 960), F32)], 0)
-    pass_ref[...] = passed.astype(BF16)
+    jb[d] = restore_block(block_ref[...].astype(F32)[:40])
+    jb[d ^ 1] = restore_block(pair_ref[...].astype(F32)[:40])
+    for i, ref in ((1, a_ref), (2, b_ref), (3, c_ref)):
+        both = ref[128:].astype(F32)
+        jb[d ^ (2 * i)] = restore_block(both[:40])
+        jb[d ^ (2 * i + 1)] = restore_block(both[40:])
+    for j in range(4):
+        both = jnp.concatenate([jb[2 * j], jb[2 * j + 1]], 1)
+        down_ref[120 * j : 120 * (j + 1), :] = both.astype(BF16)
     x2 = x2_ref[...]
     scale_two = lax.rsqrt(jnp.mean(x2 * x2, -1, keepdims=True) + EPS)
     unit = x2 * scale_two
@@ -794,7 +788,6 @@
     grad = jnp.concatenate([fb[i][:, :120] for i in range(8)], 1).astype(BF16)
     cosines = cos_ref[...]
     sines = sin_ref[...]
-    bias = mask_bias(seg_ref)
     dq, dk, dv = [], [], []
     for g in range(KV_HEADS):
         qr = qr_ref[g]
@@ -803,7 +796,7 @@
         grads = jnp.concatenate(
             [grad[:, h * HD : (h + 1) * HD] for h in range(g * GROUP, (g + 1) * GROUP)], 0
         )
-        probs = jnp.exp(contract_last(qr, kr) * HD ** (-0.5) + bias - lse_ref[g])
+        probs = probs_ref[g]
         dv.append(contract_first(probs.astype(BF16), grads).astype(BF16))
         dprob = contract_last(grads, vr)
         inner = jnp.sum(probs * dprob, -1, keepdims=True)
@@ -980,7 +973,7 @@
     feed = lax.all_gather(feed, "fsdp", axis=0, tiled=True)
 
     cosines, sines = rotary_tables(positions[0], HD)
-    x2, h2, attended, qr, kr, vr, lse, gains = kernel_call(
+    x2, h2, attended, qr, kr, vr, probs, gains = kernel_call(
         attention_forward,
         [
             shape((length, features), F32),
@@ -989,7 +982,7 @@
             shape((KV_HEADS, GROUP * length, HD), BF16),
             shape((KV_HEADS, length, HD), BF16),
             shape((KV_HEADS, length, HD), BF16),
-            shape((KV_HEADS, GROUP * length, 1), F32),
+            shape((KV_HEADS, GROUP * length, length), F32),
             shape((2, 8, features), F32),
         ],
         [ids, hidden, cosines, sines, segment_ids, *first, *second],
@@ -1000,7 +993,7 @@
             pltpu.VMEM((8, 8, 256), F32),
         ],
         16,
-        8.5,
+        10.0,
     )
     hidden_rows = after(hidden, b_near, b_far)
     far = [send(hidden_rows, "dp", s) for s in (2, 4, 6)]
@@ -1026,13 +1019,13 @@
         feed_critical,
         [
             shape((4, length, features), F32),
-            shape((4 * length + 48, 1024), BF16),
+            shape((4 * length + 192, 1024), BF16),
             shape((tokens, 640), BF16),
             shape((tokens, 320), BF16),
             shape((features, 320), BF16),
             shape((48, 960), BF16),
         ]
-        + [shape((80, 960), BF16)] * 3,
+        + [shape((48, 960), BF16)] * 3,
         [ids, *h2_slots, *cotangent_slots, feed, *down_blocks, *down_passed],
         ["smem"] + ["any"] * 16 + [None] * 9,
         [
@@ -1044,7 +1037,7 @@
             pltpu.SemaphoreType.DMA((8,)),
         ],
         24,
-        9.0,
+        11.0,
     )
 
     odd = send(odd, "dp", 1)
@@ -1069,38 +1062,32 @@
             pltpu.SemaphoreType.DMA((8,)),
         ],
         24,
-        9.0,
+        4.0,
     )
     feed_grad = after(feed_grad, back_a, back_b, back_c, attended)
     feed_sum = lax.psum_scatter(feed_grad, "fsdp", scatter_dimension=0, tiled=True)
-    *outgoing, input_grad, passed = kernel_call(
+    *outgoing, input_grad, down_grad = kernel_call(
         attention_backward,
         [shape((80, 640), BF16)] * 8
-        + [shape((features, length), F32), shape((length, features), BF16)],
+        + [shape((features, length), F32), shape((4 * 120, 640), BF16)],
         [
             ids, back_own, back_a, back_b, back_c, cotangent, x2, hidden, gains,
-            cosines, sines, segment_ids, qr, kr, vr, lse, *first, *second, feed_grad,
+            cosines, sines, qr, kr, vr, probs, *first, *second, own_block,
+            pair_block, feed_grad,
         ],
-        ["smem"] + [None] * 31 + ["any"],
+        ["smem"] + [None] * 32 + ["any"],
         [
             pltpu.VMEM((8, length, 128), F32),
             pltpu.VMEM((8, length, 128), BF16),
             pltpu.VMEM((8, length, 256), BF16),
             pltpu.VMEM((8, 16, 640), F32),
+            pltpu.VMEM((8, 120, 320), F32),
         ],
         18,
-        10.5,
+        12.0,
     )
     arrived = [outgoing[0]] + [send(outgoing[s], "dp", s) for s in range(1, 8)]
-    passed = send(passed, "dp", 1)
-    (down_grad,) = kernel_call(
-        join_down,
-        [shape((4 * 120, 640), BF16)],
-        [ids, own_block, pair_block, back_a, back_b, back_c, passed],
-        ["smem"] + [None] * 6,
-        [pltpu.VMEM((8, 120, 320), F32)],
-    )
-    f_odd = send(after(f_odd, outgoing[0]), "dp", 1)
+    f_odd = send(f_odd, "dp", 1)
     y_own, *y_parts = kernel_call(
         pair_sum,
         [shape((length, features), F32)] + [shape((length, features), BF16)] * 3,
@@ -1119,7 +1106,7 @@
             pltpu.VMEM((4, 336, 256), F32),
         ],
         20,
-        4.5,
+        6.5,
     )
 
     y_parts = after_all(y_parts, w0)

time: 225 us -> 222 us (0.987)
  waiting for transfers between devices: 75.9 us -> 79.7 us
  Pallas kernels: 74.3 us -> 70.7 us
    unnamed x5, waiting for transfers between devices: 0.07 us -> 5.62 us
    pallas_call x15 -> x14, Pallas kernels: 74.3 us -> 70.7 us  [kernel_call(): pl.pallas_call(body, out_shape=outs, in_specs=[pl.BlockSpec(memory_space=...]
    ppermute x63 -> x62, waiting for transfers between devices: 70.4 us -> 68.7 us  [send(): return lax.ppermute(values, axis, [(i, i ^ distance) for i in range(count)])]
    unnamed x115 -> x109, local copies, waits for them, and re-layouts: 9.16 us -> 8.15 us
    ppermute x63 -> x62, starting transfers between devices: 46.4 us -> 46.4 us  [send(): return lax.ppermute(values, axis, [(i, i ^ distance) for i in range(count)])]
  transfers between devices with their start and end apart: 67 -> 66, of which waited for: 30 -> 28; matrix products, arithmetic and copies ran while one was open for 1% -> 1% of each run, Pallas kernels for 31% -> 29%
where the time goes in v4:
time: 222 us; the launch traced here: 221 us
  waiting for transfers between devices  79.7 us (36%)
  Pallas kernels  70.7 us (32%)
  starting transfers between devices  47 us (21%)
  between operations  14.2 us (6%)
  local copies, waits for them, and re-layouts  8.15 us (4%)
    pallas_call x14, Pallas kernels, kernel_call(): pl.pallas_call(body, out_shape=outs, in_specs=[pl.BlockSpec(memory_space=...  70.7 us
    ppermute x62, waiting for transfers between devices, send(): return lax.ppermute(values, axis, [(i, i ^ distance) for i in range(count)])  68.7 us
    ppermute x62, starting transfers between devices, send(): return lax.ppermute(values, axis, [(i, i ^ distance) for i in range(count)])  46.4 us
    unnamed x109, local copies, waits for them, and re-layouts  8.15 us
    unnamed x5, waiting for transfers between devices  5.62 us
    all_gather x1, waiting for transfers between devices, fast(): feed = lax.all_gather(feed, 'fsdp', axis=0, tiled=True)  5.44 us
  transfers between devices with their start and end apart: 66, of which 28 were waited for; matrix products, arithmetic and copies ran while one was open for 1% of the time, Pallas kernels for 29%

profile of v4, /device:TPU:8, one launch (start us, length us, event | category | flops | bytes accessed | tf_op | source)
XLA Modules:
  0.0 221.4 jit_solution(13936233270305117318)
XLA Ops:
  7.2 1.6 collective-permute-start.1
  8.8 1.5 collective-permute-start.2
  10.8 1.8 shard_map.212.own_ref
  12.6 2.6 %collective-permute-start = (bf16[120,640]{1,0:T(8,128)(2,1)}, bf16[120,640]{1,0:T(8,128)(2,1)S(1)}, u32[]{:S(2)}, u32[]{:S(2)}) collective-permute-start(bf16[120,640]{1,0:T(8,128)(2,1)} %shard_map.212.own_ref), channel_id=1, source_target_pairs={{0,2},{1,3},{2,0},{3,1},{4,6},{5,7},{6,4},{7,5},{8,10},{9,11},{10,... | collective-permute-start | bytes 460808 | tf_op jit(solution)/shard_map/ppermute | solution.py:71
  15.2 5.9 %collective-permute-done.got_ref = bf16[120,640]{1,0:T(8,128)(2,1)S(1)} collective-permute-done((bf16[120,640]{1,0:T(8,128)(2,1)}, bf16[120,640]{1,0:T(8,128)(2,1)S(1)}, u32[]{:S(2)}, u32[]{:S(2)}) %collective-permute-start) | collective-permute-done | bytes 153632 | tf_op jit(solution)/shard_map/ppermute | solution.py:71
  22.4 1.8 shard_map.213.rest_0_.rest_14_
  24.3 1.2 collective-permute-start.5
  25.4 1.1 collective-permute-start.6
  26.5 1.5 collective-permute-start.7
  28.0 5.3 %collective-permute-done.5.refs_1_.refs_0_ = bf16[256,640]{1,0:T(8,128)(2,1)S(1)} collective-permute-done((bf16[256,640]{1,0:T(8,128)(2,1)}, bf16[256,640]{1,0:T(8,128)(2,1)S(1)}, u32[]{:S(2)}, u32[]{:S(2)}) %collective-permute-start.5) | collective-permute-done | bytes 327712 | tf_op jit(solution)/shard_map/ppermute | solution.py:71
  33.4 1.2 collective-permute-done.6.refs_0_
  35.3 0.7 copy-done.10
  36.0 2.1 shard_map.217
  38.2 1.6 collective-permute-start.8
  39.8 0.7 copy.39.refs_0_
  41.6 4.8 %collective-permute-done.8.refs_1_ = bf16[256,640]{1,0:T(8,128)(2,1)S(1)} collective-permute-done((bf16[256,640]{1,0:T(8,128)(2,1)S(1)}, bf16[256,640]{1,0:T(8,128)(2,1)S(1)}, u32[]{:S(2)}, u32[]{:S(2)}) %collective-permute-start.8) | collective-permute-done | bytes 327712 | tf_op jit(solution)/shard_map/ppermute | solution.py:71
  46.3 0.7 copy-done.1
  47.1 1.7 collective-permute-start.11
  48.7 0.8 collective-permute-start.17
  50.7 0.9 collective-permute-done.14.rest_10_.refs_2_.rest_24_
  51.6 2.9 %collective-permute-done.11.rest_6_.rest_20_ = bf16[256,640]{1,0:T(8,128)(2,1)S(1)} collective-permute-done((bf16[256,640]{1,0:T(8,128)(2,1)}, bf16[256,640]{1,0:T(8,128)(2,1)S(1)}, u32[]{:S(2)}, u32[]{:S(2)}) %collective-permute-start.11) | collective-permute-done | bytes 327712 | tf_op jit(solution)/shard_map/ppermute | solution.py:71
  54.5 3.2 %collective-permute-done.17.rest_14_.rest_28_ = bf16[256,640]{1,0:T(8,128)(2,1)S(1)} collective-permute-done((bf16[256,640]{1,0:T(8,128)(2,1)}, bf16[256,640]{1,0:T(8,128)(2,1)S(1)}, u32[]{:S(2)}, u32[]{:S(2)}) %collective-permute-start.17) | collective-permute-done | bytes 327712 | tf_op jit(solution)/shard_map/ppermute | solution.py:71
  58.1 0.7 pad_maximum_fusion
  60.0 2.5 %collective-permute-start.25 = (bf16[960,128]{1,0:T(8,128)(2,1)}, bf16[960,128]{1,0:T(8,128)(2,1)}, u32[]{:S(2)}, u32[]{:S(2)}) collective-permute-start(bf16[960,128]{1,0:T(8,128)(2,1)} %shard_map.218.rest_0_), channel_id=1, source_target_pairs={{0,24},{4,28},{8,16},{12,20},{16,8},{20,12},{24,0},{28,4},{1,25},{... | collective-permute-start | bytes 737288 | tf_op jit(solution)/shard_map/ppermute | solution.py:71
  62.6 10.3 %shard_map.216 = (f32[128,960]{1,0:T(8,128)}, bf16[128,960]{1,0:T(8,128)(2,1)}, bf16[128,960]{1,0:T(8,128)(2,1)}, bf16[5,384,64]{2,1,0:T(8,128)(2,1)}, bf16[5,12...) custom-call(s32[2]{0:T(128)} %pad_add_fusion.ids, ...), custom_call_target="tpu_custom_call" | custom-call | flops 11000000512 | bytes 30000000 | tf_op jit(solution)/shard_map/pallas_call | solution.py:407
  72.9 0.6 collective-permute-start.20
  74.1 5.4 %all-gather.3.cloned.1.call-done.feed_ref.rest_16_ = bf16[1440,640]{1,0:T(8,128)(2,1)} async-done(((bf16[360,640]{1,0:T(8,128)(2,1)}), bf16[1440,640]{1,0:T(8,128)(2,1)}) %all-gather.3.cloned.1.call-update) | async-done | bytes 1843216 | tf_op jit(solution)/shard_map/all_gather | solution.py:973
  79.6 2.6 %shard_map.219 = (bf16[64,640]{1,0:T(8,128)(2,1)}, bf16[64,640]{1,0:T(8,128)(2,1)}, bf16[128,640]{1,0:T(8,128)(2,1)}, bf16[128,640]{1,0:T(8,128)(2,1)}, bf16[128,640]{1,0:T(8,128)(2,1)}) custom-call(s32[2]{0:T(128)} %pad_add_fusion.ids, bf16[1440,640]{1,0:T(8,128)(2,1)} %all-gather.3.cloned.1.call-done.feed_ref.rest_16_, ...), custom_call_target="tpu_custom_call" | custom-call | flops 1100000000 | bytes 3000000 | tf_op jit(solution)/shard_map/pallas_call | solution.py:407
  82.2 1.5 collective-permute-start.27
  83.7 1.5 collective-permute-start.22
  85.7 2.4 %collective-permute-start.29 = (bf16[128,640]{1,0:T(8,128)(2,1)}, bf16[128,640]{1,0:T(8,128)(2,1)S(1)}, u32[]{:S(2)}, u32[]{:S(2)}) collective-permute-start(bf16[128,640]{1,0:T(8,128)(2,1)} %get-tuple-element.83), channel_id=1, source_target_pairs={{0,24},{4,28},{8,16},{12,20},{16,8},{20,12},{24,0},{28,4},{1,25},{... | collective-permute-start | bytes 491528 | tf_op jit(solution)/shard_map/ppermute | solution.py:71
  88.1 1.4 collective-permute-done.27.refs_4_.rest_19_
  90.1 9.6 %collective-permute-done.28.refs_5_.rest_20_ = bf16[128,640]{1,0:T(8,128)(2,1)S(1)} collective-permute-done((bf16[128,640]{1,0:T(8,128)(2,1)}, bf16[128,640]{1,0:T(8,128)(2,1)S(1)}, u32[]{:S(2)}, u32[]{:S(2)}) %collective-permute-start.28) | collective-permute-done | bytes 163872 | tf_op jit(solution)/shard_map/ppermute | solution.py:71
  105.6 0.7 copy-done.35
  106.3 11.7 %shard_map.221 = (f32[4,128,960]{2,1,0:T(8,128)}, bf16[704,1024]{1,0:T(8,128)(2,1)}, bf16[1024,640]{1,0:T(8,128)(2,1)}, bf16[1024,320]{1,0:T(8,128)(2,1)}, bf16[...) custom-call(s32[2]{0:T(128)} %pad_add_fusion.ids, ...), custom_call_target="tpu_custom_call" | custom-call | flops 12099999744 | bytes 33000000 | tf_op jit(solution)/shard_map/pallas_call | solution.py:407
  118.3 3.3 %collective-permute-done.40.odd_ref = bf16[704,1024]{1,0:T(8,128)(2,1)} collective-permute-done((bf16[704,1024]{1,0:T(8,128)(2,1)}, bf16[704,1024]{1,0:T(8,128)(2,1)}, u32[]{:S(2)}, u32[]{:S(2)}) %collective-permute-start.40) | collective-permute-done | bytes 1441824 | tf_op jit(solution)/shard_map/ppermute | solution.py:71
  121.6 3.4 %shard_map.222 = (f32[128,960]{1,0:T(8,128)}, bf16[48,960]{1,0:T(8,128)(2,1)}, bf16[208,960]{1,0:T(8,128)(2,1)}, bf16[208,960]{1,0:T(8,128)(2,1)}, bf16[208,960]{1,0:T(8,128)(2,1)}) custom-call(f32[4,128,960]{2,1,0:T(8,128)} %get-tuple-element.91.even_ref, bf16[704,1024]{1,0:T(8,128)(2,1)} %collective-permute-done.40.odd_ref, ...), custom_call_target="tpu_custom_call" | custom-call | flops 1100000000 | bytes 3000000 | tf_op jit(solution)/shard_map/pallas_call | solution.py:407
  125.0 1.5 collective-permute-start.42
  127.0 1.5 collective-permute-start.44
  128.5 8.4 %shard_map.223 = (bf16[960,640]{1,0:T(8,128)(2,1)}, f32[4,128,960]{2,1,0:T(8,128)}, bf16[512,1024]{1,0:T(8,128)(2,1)}) custom-call(bf16[128,960]{1,0:T(8,128)(2,1)} %get-tuple-element.79.rest_0_, bf16[128,960]{1,0:T(8,128)(2,1)} %copy-done.32, bf16[128,960]{1,0:T(8,128)(2,1)} %get-tuple-element.84.rest_2_.refs_1_, bf16[128,960]{1,0:T(8,128)(2,1)} %copy-done.33, ...), custom_call_target="tpu_custom_call" | custom-call | flops 4400000000 | bytes 12000000 | tf_op jit(solution)/shard_map/pallas_call | solution.py:407
  136.9 0.9 collective-permute-done.42.refs_1_.rest_1_
  137.8 9.8 %collective-permute-done.43.refs_2_.rest_2_ = bf16[208,960]{1,0:T(8,128)(2,1)} collective-permute-done((bf16[208,960]{1,0:T(8,128)(2,1)}, bf16[208,960]{1,0:T(8,128)(2,1)}, u32[]{:S(2)}, u32[]{:S(2)}) %collective-permute-start.43) | collective-permute-done | bytes 399392 | tf_op jit(solution)/shard_map/ppermute | solution.py:71
  148.0 0.6 copy-done.8
  149.6 12.7 %shard_map.226 = (bf16[80,640]{1,0:T(8,128)(2,1)}, bf16[80,640]{1,0:T(8,128)(2,1)}, bf16[80,640]{1,0:T(8,128)(2,1)}, bf16[80,640]{1,0:T(8,128)(2,1)}, bf16[80,64...) custom-call(s32[2]{0:T(128)} %pad_add_fusion.ids, ...), custom_call_target="tpu_custom_call" | custom-call | flops 13200000000 | bytes 36000000 | tf_op jit(solution)/shard_map/pallas_call | solution.py:407
  162.3 0.7 collective-permute-start.49
  163.4 1.2 collective-permute-start.51
  164.9 1.7 collective-permute-start.53
  166.6 1.0 collective-permute-start.54
  167.6 1.4 collective-permute-done.50.rest_11_
  169.0 3.0 %shard_map.227 = (f32[128,960]{1,0:T(8,128)}, bf16[128,960]{1,0:T(8,128)(2,1)}, bf16[128,960]{1,0:T(8,128)(2,1)}, bf16[128,960]{1,0:T(8,128)(2,1)}) custom-call(f32[4,128,960]{2,1,0:T(8,128)} %get-tuple-element.97.even_ref, bf16[512,1024]{1,0:T(8,128)(2,1)} %collective-permute-done.41.odd_ref, bf16[80,640]{1,0:T(8,128)(2,1)} %get-tuple-element.111.rest_0_.rest_9_), custom_call_target="tpu_custom_call" | custom-call | flops 1100000000 | bytes 3000000 | tf_op jit(solution)/shard_map/pallas_call | solution.py:407
  172.0 3.0 %collective-permute-done.52.rest_13_ = bf16[80,640]{1,0:T(8,128)(2,1)} collective-permute-done((bf16[80,640]{1,0:T(8,128)(2,1)}, bf16[80,640]{1,0:T(8,128)(2,1)}, u32[]{:S(2)}, u32[]{:S(2)}) %collective-permute-start.52) | collective-permute-done | bytes 102432 | tf_op jit(solution)/shard_map/ppermute | solution.py:71
  175.0 1.6 collective-permute-done.53.rest_14_
  176.7 6.5 %shard_map.228 = (f32[336,240]{1,0:T(8,128)}, bf16[336,240]{1,0:T(8,128)(2,1)}, bf16[336,240]{1,0:T(8,128)(2,1)}, bf16[336,240]{1,0:T(8,128)(2,1)}) custom-call(s32[2]{0:T(128)} %pad_add_fusion.ids, bf16[960,128]{1,0:T(8,128)(2,1)} %shard_map.218.rest_0_, bf16[960,128]{1,0:T(8,128)(2,1)} %copy-done.43, ...), custom_call_target="tpu_custom_call" | custom-call | flops 7150000128 | bytes 19500000 | tf_op jit(solution)/shard_map/pallas_call | solution.py:407
  183.2 2.7 %collective-permute-start.59 = (bf16[336,240]{1,0:T(8,128)(2,1)}, bf16[336,240]{1,0:T(8,128)(2,1)S(1)}, u32[]{:S(2)}, u32[]{:S(2)}) collective-permute-start(bf16[336,240]{1,0:T(8,128)(2,1)} %get-tuple-element.129), channel_id=1, source_target_pairs={{0,1},{1,0},{2,3},{3,2},{4,5},{5,4},{6,7},{7,6},{8,9},{9,8},{10,11... | collective-permute-start | bytes 483848 | tf_op jit(solution)/shard_map/ppermute | solution.py:71
  186.0 1.8 collective-permute-start.57
  187.7 1.7 collective-permute-start.58
  190.0 8.4 %collective-permute-done.59._.a_ref = bf16[336,240]{1,0:T(8,128)(2,1)S(1)} collective-permute-done((bf16[336,240]{1,0:T(8,128)(2,1)}, bf16[336,240]{1,0:T(8,128)(2,1)S(1)}, u32[]{:S(2)}, u32[]{:S(2)}) %collective-permute-start.59) | collective-permute-done | bytes 161312 | tf_op jit(solution)/shard_map/ppermute | solution.py:71
  199.1 2.0 shard_map.231
  201.1 0.7 copy-done.36
  201.9 0.7 copy-done.38
  202.6 2.3 %shard_map.230.rest_0_ = bf16[960,128]{1,0:T(8,128)(2,1)} custom-call(f32[128,960]{1,0:T(8,128)} %get-tuple-element.78.rest_5_.x2_ref, f32[128,960]{1,0:T(8,128)} %get-tuple-element.112.rest_18_.own_ref, bf16[128,960]{1,0:T(8,128)(2,1)} %copy-done.36, bf16[128,960]{1,0:T(8,128)(2,1)} %copy-done.37, bf16[128,960]{1,0:T(8,128)(2,1)} %copy-done.38), custom_call_target="tpu_custom_call" | custom-call | flops 1100000000 | bytes 3000000 | tf_op jit(solution)/shard_map/pallas_call | solution.py:407
  204.9 5.6 %reduce-scatter.7.cloned.1.call-done.down_ref = bf16[120,640]{1,0:T(8,128)(2,1)} async-done(((bf16[480,640]{1,0:T(8,128)(2,1)}), bf16[120,640]{1,0:T(8,128)(2,1)}) %reduce-scatter.7.cloned.1.call-update) | async-done | bytes 153616
  210.5 2.2 collective-permute-done.61.c_ref
  212.7 2.2 shard_map.232
  (207 shorter events, 18.3 us)
Async XLA Ops:
  7.2 72.4 %all-gather.3.cloned.1.call-start = ((), (), s32[]{:S(2)}) async-start(), calls=%async_computation.2 | async-start | bytes 2304000 | tf_op jit(solution)/shard_map/all_gather | solution.py:973
  7.2 13.8 %collective-permute-start.1 = (bf16[960,128]{1,0:T(8,128)(2,1)}, bf16[960,128]{1,0:T(8,128)(2,1)S(1)}, u32[]{:S(2)}, u32[]{:S(2)}) collective-permute-start(bf16[960,128]{1,0:T(8,128)(2,1)} %bitcast.34), channel_id=1, source_target_pairs={{0,8},{4,12},{8,0},{12,4},{16,24},{20,28},{24,16},{28,20},{1,9},{5... | collective-permute-start | bytes 737288 | tf_op jit(solution)/shard_map/ppermute | solution.py:71
  8.8 12.9 %collective-permute-start.2 = (bf16[960,128]{1,0:T(8,128)(2,1)}, bf16[960,128]{1,0:T(8,128)(2,1)S(1)}, u32[]{:S(2)}, u32[]{:S(2)}) collective-permute-start(bf16[960,128]{1,0:T(8,128)(2,1)} %bitcast.35), channel_id=1, source_target_pairs={{0,16},{4,20},{8,24},{12,28},{16,0},{20,4},{24,8},{28,12},{1,17},{... | collective-permute-start | bytes 737288 | tf_op jit(solution)/shard_map/ppermute | solution.py:71
  10.3 11.4 %collective-permute-start.3 = (bf16[960,128]{1,0:T(8,128)(2,1)}, bf16[960,128]{1,0:T(8,128)(2,1)S(1)}, u32[]{:S(2)}, u32[]{:S(2)}) collective-permute-start(bf16[960,128]{1,0:T(8,128)(2,1)} %bitcast.36), channel_id=1, source_target_pairs={{0,24},{4,28},{8,16},{12,20},{16,8},{20,12},{24,0},{28,4},{1,25},{... | collective-permute-start | bytes 737288 | tf_op jit(solution)/shard_map/ppermute | solution.py:71
  12.6 8.5 %collective-permute-start = (bf16[120,640]{1,0:T(8,128)(2,1)}, bf16[120,640]{1,0:T(8,128)(2,1)S(1)}, u32[]{:S(2)}, u32[]{:S(2)}) collective-permute-start(bf16[120,640]{1,0:T(8,128)(2,1)} %shard_map.212.own_ref), channel_id=1, source_target_pairs={{0,2},{1,3},{2,0},{3,1},{4,6},{5,7},{6,4},{7,5},{8,10},{9,11},{10,... | collective-permute-start | bytes 460808 | tf_op jit(solution)/shard_map/ppermute | solution.py:71
  24.3 9.1 %collective-permute-start.5 = (bf16[256,640]{1,0:T(8,128)(2,1)}, bf16[256,640]{1,0:T(8,128)(2,1)S(1)}, u32[]{:S(2)}, u32[]{:S(2)}) collective-permute-start(bf16[256,640]{1,0:T(8,128)(2,1)} %shard_map.213.rest_0_.rest_14_), channel_id=1, source_target_pairs={{0,8},{4,12},{8,0},{12,4},{16,24},{20,28},{24,16},{28,20},{1,9},{5... | collective-permute-start | bytes 983048 | tf_op jit(solution)/shard_map/ppermute | solution.py:71
  25.4 9.2 %collective-permute-start.6 = (bf16[256,640]{1,0:T(8,128)(2,1)}, bf16[256,640]{1,0:T(8,128)(2,1)S(1)}, u32[]{:S(2)}, u32[]{:S(2)}) collective-permute-start(bf16[256,640]{1,0:T(8,128)(2,1)} %shard_map.213.rest_0_.rest_14_), channel_id=1, source_target_pairs={{0,1},{1,0},{2,3},{3,2},{4,5},{5,4},{6,7},{7,6},{8,9},{9,8},{10,11... | collective-permute-start | bytes 983048 | tf_op jit(solution)/shard_map/ppermute | solution.py:71
  26.5 8.2 %collective-permute-start.7 = (bf16[256,640]{1,0:T(8,128)(2,1)}, bf16[256,640]{1,0:T(8,128)(2,1)S(1)}, u32[]{:S(2)}, u32[]{:S(2)}) collective-permute-start(bf16[256,640]{1,0:T(8,128)(2,1)} %shard_map.213.rest_0_.rest_14_), channel_id=1, source_target_pairs={{0,16},{4,20},{8,24},{12,28},{16,0},{20,4},{24,8},{28,12},{1,17},{... | collective-permute-start | bytes 983048 | tf_op jit(solution)/shard_map/ppermute | solution.py:71
  38.2 109.5 %all-gather.5.cloned.1.call-start = ((), (), s32[]{:S(2)}) async-start(), calls=%async_computation.3 | async-start | bytes 2359296 | tf_op jit(solution)/shard_map/all_gather | solution.py:1017
  38.2 8.1 %collective-permute-start.8 = (bf16[256,640]{1,0:T(8,128)(2,1)S(1)}, bf16[256,640]{1,0:T(8,128)(2,1)S(1)}, u32[]{:S(2)}, u32[]{:S(2)}) collective-permute-start(bf16[256,640]{1,0:T(8,128)(2,1)S(1)} %copy-done.13), channel_id=1, source_target_pairs={{0,16},{4,20},{8,24},{12,28},{16,0},{20,4},{24,8},{28,12},{1,17},{... | collective-permute-start | bytes 983048 | tf_op jit(solution)/shard_map/ppermute | solution.py:71
  39.8 8.9 %collective-permute-start.4 = (bf16[256,640]{1,0:T(8,128)(2,1)}, bf16[256,640]{1,0:T(8,128)(2,1)S(1)}, u32[]{:S(2)}, u32[]{:S(2)}) collective-permute-start(bf16[256,640]{1,0:T(8,128)(2,1)} %shard_map.213.rest_0_.rest_14_), channel_id=1, source_target_pairs={{0,4},{4,0},{8,12},{12,8},{16,20},{20,16},{24,28},{28,24},{1,5},{5... | collective-permute-start | bytes 983048 | tf_op jit(solution)/shard_map/ppermute | solution.py:71
  40.5 9.7 %collective-permute-start.13 = (bf16[256,640]{1,0:T(8,128)(2,1)S(1)}, bf16[256,640]{1,0:T(8,128)(2,1)S(1)}, u32[]{:S(2)}, u32[]{:S(2)}) collective-permute-start(bf16[256,640]{1,0:T(8,128)(2,1)S(1)} %copy-done.13), channel_id=1, source_target_pairs={{0,4},{4,0},{8,12},{12,8},{16,20},{20,16},{24,28},{28,24},{1,5},{5... | collective-permute-start | bytes 983048 | tf_op jit(solution)/shard_map/ppermute | solution.py:71
  41.0 10.6 %collective-permute-start.14 = (bf16[256,640]{1,0:T(8,128)(2,1)S(1)}, bf16[256,640]{1,0:T(8,128)(2,1)S(1)}, u32[]{:S(2)}, u32[]{:S(2)}) collective-permute-start(bf16[256,640]{1,0:T(8,128)(2,1)S(1)} %copy-done.13), channel_id=1, source_target_pairs={{0,8},{4,12},{8,0},{12,4},{16,24},{20,28},{24,16},{28,20},{1,9},{5... | collective-permute-start | bytes 983048 | tf_op jit(solution)/shard_map/ppermute | solution.py:71
  41.6 8.5 %collective-permute-start.10 = (bf16[256,640]{1,0:T(8,128)(2,1)S(1)}, bf16[256,640]{1,0:T(8,128)(2,1)S(1)}, u32[]{:S(2)}, u32[]{:S(2)}) collective-permute-start(bf16[256,640]{1,0:T(8,128)(2,1)S(1)} %copy-done.11), channel_id=1, source_target_pairs={{0,4},{4,0},{8,12},{12,8},{16,20},{20,16},{24,28},{28,24},{1,5},{5... | collective-permute-start | bytes 983048 | tf_op jit(solution)/shard_map/ppermute | solution.py:71
  47.1 7.4 %collective-permute-start.11 = (bf16[256,640]{1,0:T(8,128)(2,1)}, bf16[256,640]{1,0:T(8,128)(2,1)S(1)}, u32[]{:S(2)}, u32[]{:S(2)}) collective-permute-start(bf16[256,640]{1,0:T(8,128)(2,1)} %get-tuple-element.76.rest_2_.rest_16_), channel_id=1, source_target_pairs={{0,16},{4,20},{8,24},{12,28},{16,0},{20,4},{24,8},{28,12},{1,17},{... | collective-permute-start | bytes 983048 | tf_op jit(solution)/shard_map/ppermute | solution.py:71
  48.7 9.0 %collective-permute-start.17 = (bf16[256,640]{1,0:T(8,128)(2,1)}, bf16[256,640]{1,0:T(8,128)(2,1)S(1)}, u32[]{:S(2)}, u32[]{:S(2)}) collective-permute-start(bf16[256,640]{1,0:T(8,128)(2,1)} %get-tuple-element.77.rest_12_.refs_1_.rest_26_), channel_id=1, source_target_pairs={{0,8},{4,12},{8,0},{12,4},{16,24},{20,28},{24,16},{28,20},{1,9},{5... | collective-permute-start | bytes 983048 | tf_op jit(solution)/shard_map/ppermute | solution.py:71
  50.1 8.7 %collective-permute-start.9 = (bf16[256,640]{1,0:T(8,128)(2,1)}, bf16[256,640]{1,0:T(8,128)(2,1)S(1)}, u32[]{:S(2)}, u32[]{:S(2)}) collective-permute-start(bf16[256,640]{1,0:T(8,128)(2,1)} %get-tuple-element.76.rest_2_.rest_16_), channel_id=1, source_target_pairs={{0,4},{4,0},{8,12},{12,8},{16,20},{20,16},{24,28},{28,24},{1,5},{5... | collective-permute-start | bytes 983048 | tf_op jit(solution)/shard_map/ppermute | solution.py:71
  50.2 9.8 %collective-permute-start.16 = (bf16[256,640]{1,0:T(8,128)(2,1)}, bf16[256,640]{1,0:T(8,128)(2,1)S(1)}, u32[]{:S(2)}, u32[]{:S(2)}) collective-permute-start(bf16[256,640]{1,0:T(8,128)(2,1)} %get-tuple-element.77.rest_12_.refs_1_.rest_26_), channel_id=1, source_target_pairs={{0,4},{4,0},{8,12},{12,8},{16,20},{20,16},{24,28},{28,24},{1,5},{5... | collective-permute-start | bytes 983048 | tf_op jit(solution)/shard_map/ppermute | solution.py:71
  51.6 7.8 %collective-permute-start.15 = (bf16[256,640]{1,0:T(8,128)(2,1)S(1)}, bf16[256,640]{1,0:T(8,128)(2,1)S(1)}, u32[]{:S(2)}, u32[]{:S(2)}) collective-permute-start(bf16[256,640]{1,0:T(8,128)(2,1)S(1)} %collective-permute-done.14.rest_10_.refs_2_.rest_24_), channel_id=1, source_target_pairs={{0,4},{4,0},{8,12},{12,8},{16,20},{20,16},{24,28},{28,24},{1,5},{5... | collective-permute-start | bytes 983048 | tf_op jit(solution)/shard_map/ppermute | solution.py:71
  54.5 8.0 %collective-permute-start.12 = (bf16[256,640]{1,0:T(8,128)(2,1)S(1)}, bf16[256,640]{1,0:T(8,128)(2,1)}, u32[]{:S(2)}, u32[]{:S(2)}) collective-permute-start(bf16[256,640]{1,0:T(8,128)(2,1)S(1)} %collective-permute-done.11.rest_6_.rest_20_), channel_id=1, source_target_pairs={{0,4},{4,0},{8,12},{12,8},{16,20},{20,16},{24,28},{28,24},{1,5},{5... | collective-permute-start | bytes 983048 | tf_op jit(solution)/shard_map/ppermute | solution.py:71
  57.7 4.8 %collective-permute-start.18 = (bf16[256,640]{1,0:T(8,128)(2,1)S(1)}, bf16[256,640]{1,0:T(8,128)(2,1)}, u32[]{:S(2)}, u32[]{:S(2)}) collective-permute-start(bf16[256,640]{1,0:T(8,128)(2,1)S(1)} %collective-permute-done.17.rest_14_.rest_28_), channel_id=1, source_target_pairs={{0,4},{4,0},{8,12},{12,8},{16,20},{20,16},{24,28},{28,24},{1,5},{5... | collective-permute-start | bytes 983048 | tf_op jit(solution)/shard_map/ppermute | solution.py:71
  58.8 15.3 %collective-permute-start.23 = (bf16[960,128]{1,0:T(8,128)(2,1)}, bf16[960,128]{1,0:T(8,128)(2,1)}, u32[]{:S(2)}, u32[]{:S(2)}) collective-permute-start(bf16[960,128]{1,0:T(8,128)(2,1)} %shard_map.218.rest_0_), channel_id=1, source_target_pairs={{0,8},{4,12},{8,0},{12,4},{16,24},{20,28},{24,16},{28,20},{1,9},{5... | collective-permute-start | bytes 737288 | tf_op jit(solution)/shard_map/ppermute | solution.py:71
  59.4 14.7 %collective-permute-start.24 = (bf16[960,128]{1,0:T(8,128)(2,1)}, bf16[960,128]{1,0:T(8,128)(2,1)}, u32[]{:S(2)}, u32[]{:S(2)}) collective-permute-start(bf16[960,128]{1,0:T(8,128)(2,1)} %shard_map.218.rest_0_), channel_id=1, source_target_pairs={{0,16},{4,20},{8,24},{12,28},{16,0},{20,4},{24,8},{28,12},{1,17},{... | collective-permute-start | bytes 737288 | tf_op jit(solution)/shard_map/ppermute | solution.py:71
  60.0 14.1 %collective-permute-start.25 = (bf16[960,128]{1,0:T(8,128)(2,1)}, bf16[960,128]{1,0:T(8,128)(2,1)}, u32[]{:S(2)}, u32[]{:S(2)}) collective-permute-start(bf16[960,128]{1,0:T(8,128)(2,1)} %shard_map.218.rest_0_), channel_id=1, source_target_pairs={{0,24},{4,28},{8,16},{12,20},{16,8},{20,12},{24,0},{28,4},{1,25},{... | collective-permute-start | bytes 737288 | tf_op jit(solution)/shard_map/ppermute | solution.py:71
  72.9 12.8 %collective-permute-start.20 = (bf16[128,960]{1,0:T(8,128)(2,1)}, bf16[128,960]{1,0:T(8,128)(2,1)S(1)}, u32[]{:S(2)}, u32[]{:S(2)}) collective-permute-start(bf16[128,960]{1,0:T(8,128)(2,1)} %get-tuple-element.79.rest_0_), channel_id=1, source_target_pairs={{0,8},{4,12},{8,0},{12,4},{16,24},{20,28},{24,16},{28,20},{1,9},{5... | collective-permute-start | bytes 737288 | tf_op jit(solution)/shard_map/ppermute | solution.py:71
  73.5 16.0 %collective-permute-start.21 = (bf16[128,960]{1,0:T(8,128)(2,1)}, bf16[128,960]{1,0:T(8,128)(2,1)S(1)}, u32[]{:S(2)}, u32[]{:S(2)}) collective-permute-start(bf16[128,960]{1,0:T(8,128)(2,1)} %get-tuple-element.79.rest_0_), channel_id=1, source_target_pairs={{0,16},{4,20},{8,24},{12,28},{16,0},{20,4},{24,8},{28,12},{1,17},{... | collective-permute-start | bytes 737288 | tf_op jit(solution)/shard_map/ppermute | solution.py:71
  82.2 7.3 %collective-permute-start.27 = (bf16[128,640]{1,0:T(8,128)(2,1)}, bf16[128,640]{1,0:T(8,128)(2,1)S(1)}, u32[]{:S(2)}, u32[]{:S(2)}) collective-permute-start(bf16[128,640]{1,0:T(8,128)(2,1)} %get-tuple-element.81), channel_id=1, source_target_pairs={{0,8},{4,12},{8,0},{12,4},{16,24},{20,28},{24,16},{28,20},{1,9},{5... | collective-permute-start | bytes 491528 | tf_op jit(solution)/shard_map/ppermute | solution.py:71
  83.7 16.5 %collective-permute-start.22 = (bf16[128,960]{1,0:T(8,128)(2,1)S(1)}, bf16[128,960]{1,0:T(8,128)(2,1)S(1)}, u32[]{:S(2)}, u32[]{:S(2)}) collective-permute-start(bf16[128,960]{1,0:T(8,128)(2,1)S(1)} %copy-done.31), channel_id=1, source_target_pairs={{0,24},{4,28},{8,16},{12,20},{16,8},{20,12},{24,0},{28,4},{1,25},{... | collective-permute-start | bytes 737288 | tf_op jit(solution)/shard_map/ppermute | solution.py:71
  85.1 14.5 %collective-permute-start.28 = (bf16[128,640]{1,0:T(8,128)(2,1)}, bf16[128,640]{1,0:T(8,128)(2,1)S(1)}, u32[]{:S(2)}, u32[]{:S(2)}) collective-permute-start(bf16[128,640]{1,0:T(8,128)(2,1)} %get-tuple-element.82), channel_id=1, source_target_pairs={{0,16},{4,20},{8,24},{12,28},{16,0},{20,4},{24,8},{28,12},{1,17},{... | collective-permute-start | bytes 491528 | tf_op jit(solution)/shard_map/ppermute | solution.py:71
  85.7 13.9 %collective-permute-start.29 = (bf16[128,640]{1,0:T(8,128)(2,1)}, bf16[128,640]{1,0:T(8,128)(2,1)S(1)}, u32[]{:S(2)}, u32[]{:S(2)}) collective-permute-start(bf16[128,640]{1,0:T(8,128)(2,1)} %get-tuple-element.83), channel_id=1, source_target_pairs={{0,24},{4,28},{8,16},{12,20},{16,8},{20,12},{24,0},{28,4},{1,25},{... | collective-permute-start | bytes 491528 | tf_op jit(solution)/shard_map/ppermute | solution.py:71
  89.5 11.2 %collective-permute-start.37 = (bf16[128,640]{1,0:T(8,128)(2,1)S(1)}, bf16[128,640]{1,0:T(8,128)(2,1)S(1)}, u32[]{:S(2)}, u32[]{:S(2)}) collective-permute-start(bf16[128,640]{1,0:T(8,128)(2,1)S(1)} %collective-permute-done.27.refs_4_.rest_19_), channel_id=1, source_target_pairs={{0,4},{4,0},{8,12},{12,8},{16,20},{20,16},{24,28},{28,24},{1,5},{5... | collective-permute-start | bytes 491528 | tf_op jit(solution)/shard_map/ppermute | solution.py:71
  89.6 10.7 %collective-permute-start.26 = (bf16[64,640]{1,0:T(8,128)(2,1)}, bf16[64,640]{1,0:T(8,128)(2,1)S(1)}, u32[]{:S(2)}, u32[]{:S(2)}) collective-permute-start(bf16[64,640]{1,0:T(8,128)(2,1)} %get-tuple-element.80), channel_id=1, source_target_pairs={{0,4},{4,0},{8,12},{12,8},{16,20},{20,16},{24,28},{28,24},{1,5},{5... | collective-permute-start | bytes 245768 | tf_op jit(solution)/shard_map/ppermute | solution.py:71
  99.7 1.6 collective-permute-start.39
  100.2 2.6 %collective-permute-start.33 = (bf16[960,128]{1,0:T(8,128)(2,1)}, bf16[960,128]{1,0:T(8,128)(2,1)S(1)}, u32[]{:S(2)}, u32[]{:S(2)}) collective-permute-start(bf16[960,128]{1,0:T(8,128)(2,1)} %bitcast.37), channel_id=1, source_target_pairs={{0,4},{4,0},{8,12},{12,8},{16,20},{20,16},{24,28},{28,24},{1,5},{5... | collective-permute-start | bytes 737288 | tf_op jit(solution)/shard_map/ppermute | solution.py:71
  100.3 2.9 %collective-permute-start.34 = (bf16[960,128]{1,0:T(8,128)(2,1)}, bf16[960,128]{1,0:T(8,128)(2,1)S(1)}, u32[]{:S(2)}, u32[]{:S(2)}) collective-permute-start(bf16[960,128]{1,0:T(8,128)(2,1)} %copy-done.39), channel_id=1, source_target_pairs={{0,4},{4,0},{8,12},{12,8},{16,20},{20,16},{24,28},{28,24},{1,5},{5... | collective-permute-start | bytes 737288 | tf_op jit(solution)/shard_map/ppermute | solution.py:71
  100.7 2.7 %collective-permute-start.35 = (bf16[960,128]{1,0:T(8,128)(2,1)}, bf16[960,128]{1,0:T(8,128)(2,1)}, u32[]{:S(2)}, u32[]{:S(2)}) collective-permute-start(bf16[960,128]{1,0:T(8,128)(2,1)} %copy-done.40), channel_id=1, source_target_pairs={{0,4},{4,0},{8,12},{12,8},{16,20},{20,16},{24,28},{28,24},{1,5},{5... | collective-permute-start | bytes 737288 | tf_op jit(solution)/shard_map/ppermute | solution.py:71
  102.0 74.7 %reduce-scatter.5.cloned.1.call-start = ((), (), s32[]{:S(2)}) async-start(), calls=%async_computation.4 | async-start | bytes 1536000 | tf_op jit(solution)/shard_map/reduce_scatter | solution.py:1068
  102.6 1.6 collective-permute-start.19
  102.8 1.7 collective-permute-start.30
  103.1 1.8 collective-permute-start.31
  103.4 1.8 collective-permute-start.32
  118.0 3.6 %collective-permute-start.40 = (bf16[704,1024]{1,0:T(8,128)(2,1)}, bf16[704,1024]{1,0:T(8,128)(2,1)}, u32[]{:S(2)}, u32[]{:S(2)}) collective-permute-start(bf16[704,1024]{1,0:T(8,128)(2,1)} %get-tuple-element.92), channel_id=1, source_target_pairs={{0,4},{4,0},{8,12},{12,8},{16,20},{20,16},{24,28},{28,24},{1,5},{5... | collective-permute-start | bytes 4325384 | tf_op jit(solution)/shard_map/ppermute | solution.py:71
  125.0 12.8 %collective-permute-start.42 = (bf16[208,960]{1,0:T(8,128)(2,1)}, bf16[208,960]{1,0:T(8,128)(2,1)S(1)}, u32[]{:S(2)}, u32[]{:S(2)}) collective-permute-start(bf16[208,960]{1,0:T(8,128)(2,1)} %get-tuple-element.99), channel_id=1, source_target_pairs={{0,8},{4,12},{8,0},{12,4},{16,24},{20,28},{24,16},{28,20},{1,9},{5... | collective-permute-start | bytes 1198088 | tf_op jit(solution)/shard_map/ppermute | solution.py:71
  126.5 21.2 %collective-permute-start.43 = (bf16[208,960]{1,0:T(8,128)(2,1)}, bf16[208,960]{1,0:T(8,128)(2,1)}, u32[]{:S(2)}, u32[]{:S(2)}) collective-permute-start(bf16[208,960]{1,0:T(8,128)(2,1)} %get-tuple-element.100), channel_id=1, source_target_pairs={{0,16},{4,20},{8,24},{12,28},{16,0},{20,4},{24,8},{28,12},{1,17},{... | collective-permute-start | bytes 1198088 | tf_op jit(solution)/shard_map/ppermute | solution.py:71
  127.0 20.6 %collective-permute-start.44 = (bf16[208,960]{1,0:T(8,128)(2,1)}, bf16[208,960]{1,0:T(8,128)(2,1)}, u32[]{:S(2)}, u32[]{:S(2)}) collective-permute-start(bf16[208,960]{1,0:T(8,128)(2,1)} %get-tuple-element.101), channel_id=1, source_target_pairs={{0,24},{4,28},{8,16},{12,20},{16,8},{20,12},{24,0},{28,4},{1,25},{... | collective-permute-start | bytes 1198088 | tf_op jit(solution)/shard_map/ppermute | solution.py:71
  147.7 62.8 %reduce-scatter.7.cloned.1.call-start = ((), (), s32[]{:S(2)}) async-start(), calls=%async_computation.5 | async-start | bytes 768000
  148.6 13.7 %collective-permute-start.45 = (bf16[960,128]{1,0:T(8,128)(2,1)S(1)}, bf16[960,128]{1,0:T(8,128)(2,1)S(1)}, u32[]{:S(2)}, u32[]{:S(2)}) collective-permute-start(bf16[960,128]{1,0:T(8,128)(2,1)S(1)} %copy-done.8), channel_id=1, source_target_pairs={{0,4},{4,0},{8,12},{12,8},{16,20},{20,16},{24,28},{28,24},{1,5},{5... | collective-permute-start | bytes 737288 | tf_op jit(solution)/shard_map/ppermute | solution.py:71
  148.6 14.4 %collective-permute-start.46 = (bf16[960,128]{1,0:T(8,128)(2,1)}, bf16[960,128]{1,0:T(8,128)(2,1)S(1)}, u32[]{:S(2)}, u32[]{:S(2)}) collective-permute-start(bf16[960,128]{1,0:T(8,128)(2,1)} %collective-permute-done.23.rest_1_.rest_2_), channel_id=1, source_target_pairs={{0,4},{4,0},{8,12},{12,8},{16,20},{20,16},{24,28},{28,24},{1,5},{5... | collective-permute-start | bytes 737288 | tf_op jit(solution)/shard_map/ppermute | solution.py:71
  149.1 14.3 %collective-permute-start.47 = (bf16[960,128]{1,0:T(8,128)(2,1)}, bf16[960,128]{1,0:T(8,128)(2,1)S(1)}, u32[]{:S(2)}, u32[]{:S(2)}) collective-permute-start(bf16[960,128]{1,0:T(8,128)(2,1)} %collective-permute-done.24.rest_2_.rest_4_), channel_id=1, source_target_pairs={{0,4},{4,0},{8,12},{12,8},{16,20},{20,16},{24,28},{28,24},{1,5},{5... | collective-permute-start | bytes 737288 | tf_op jit(solution)/shard_map/ppermute | solution.py:71
  149.1 15.5 %collective-permute-start.48 = (bf16[960,128]{1,0:T(8,128)(2,1)}, bf16[960,128]{1,0:T(8,128)(2,1)}, u32[]{:S(2)}, u32[]{:S(2)}) collective-permute-start(bf16[960,128]{1,0:T(8,128)(2,1)} %collective-permute-done.25.rest_3_.rest_6_), channel_id=1, source_target_pairs={{0,4},{4,0},{8,12},{12,8},{16,20},{20,16},{24,28},{28,24},{1,5},{5... | collective-permute-start | bytes 737288 | tf_op jit(solution)/shard_map/ppermute | solution.py:71
  149.6 15.3 %collective-permute-start.41 = (bf16[512,1024]{1,0:T(8,128)(2,1)}, bf16[512,1024]{1,0:T(8,128)(2,1)}, u32[]{:S(2)}, u32[]{:S(2)}) collective-permute-start(bf16[512,1024]{1,0:T(8,128)(2,1)} %get-tuple-element.98), channel_id=1, source_target_pairs={{0,4},{4,0},{8,12},{12,8},{16,20},{20,16},{24,28},{28,24},{1,5},{5... | collective-permute-start | bytes 3145736 | tf_op jit(solution)/shard_map/ppermute | solution.py:71
  162.3 4.3 %collective-permute-start.49 = (bf16[80,640]{1,0:T(8,128)(2,1)}, bf16[80,640]{1,0:T(8,128)(2,1)S(1)}, u32[]{:S(2)}, u32[]{:S(2)}) collective-permute-start(bf16[80,640]{1,0:T(8,128)(2,1)} %get-tuple-element.116), channel_id=1, source_target_pairs={{0,4},{4,0},{8,12},{12,8},{16,20},{20,16},{24,28},{28,24},{1,5},{5... | collective-permute-start | bytes 307208 | tf_op jit(solution)/shard_map/ppermute | solution.py:71
  163.0 5.9 %collective-permute-start.50 = (bf16[80,640]{1,0:T(8,128)(2,1)}, bf16[80,640]{1,0:T(8,128)(2,1)S(1)}, u32[]{:S(2)}, u32[]{:S(2)}) collective-permute-start(bf16[80,640]{1,0:T(8,128)(2,1)} %get-tuple-element.117), channel_id=1, source_target_pairs={{0,8},{4,12},{8,0},{12,4},{16,24},{20,28},{24,16},{28,20},{1,9},{5... | collective-permute-start | bytes 307208 | tf_op jit(solution)/shard_map/ppermute | solution.py:71
  163.4 8.6 %collective-permute-start.51 = (bf16[80,640]{1,0:T(8,128)(2,1)}, bf16[80,640]{1,0:T(8,128)(2,1)}, u32[]{:S(2)}, u32[]{:S(2)}) collective-permute-start(bf16[80,640]{1,0:T(8,128)(2,1)} %get-tuple-element.118), channel_id=1, source_target_pairs={{0,12},{4,8},{8,4},{12,0},{16,28},{20,24},{24,20},{28,16},{1,13},{... | collective-permute-start | bytes 307208 | tf_op jit(solution)/shard_map/ppermute | solution.py:71
  164.6 10.5 %collective-permute-start.52 = (bf16[80,640]{1,0:T(8,128)(2,1)}, bf16[80,640]{1,0:T(8,128)(2,1)}, u32[]{:S(2)}, u32[]{:S(2)}) collective-permute-start(bf16[80,640]{1,0:T(8,128)(2,1)} %get-tuple-element.119), channel_id=1, source_target_pairs={{0,16},{4,20},{8,24},{12,28},{16,0},{20,4},{24,8},{28,12},{1,17},{... | collective-permute-start | bytes 307208 | tf_op jit(solution)/shard_map/ppermute | solution.py:71
  164.9 11.8 %collective-permute-start.53 = (bf16[80,640]{1,0:T(8,128)(2,1)}, bf16[80,640]{1,0:T(8,128)(2,1)}, u32[]{:S(2)}, u32[]{:S(2)}) collective-permute-start(bf16[80,640]{1,0:T(8,128)(2,1)} %get-tuple-element.120), channel_id=1, source_target_pairs={{0,20},{4,16},{8,28},{12,24},{16,4},{20,0},{24,12},{28,8},{1,21},{... | collective-permute-start | bytes 307208 | tf_op jit(solution)/shard_map/ppermute | solution.py:71
  166.6 10.0 %collective-permute-start.54 = (bf16[80,640]{1,0:T(8,128)(2,1)}, bf16[80,640]{1,0:T(8,128)(2,1)}, u32[]{:S(2)}, u32[]{:S(2)}) collective-permute-start(bf16[80,640]{1,0:T(8,128)(2,1)} %get-tuple-element.121), channel_id=1, source_target_pairs={{0,24},{4,28},{8,16},{12,20},{16,8},{20,12},{24,0},{28,4},{1,25},{... | collective-permute-start | bytes 307208 | tf_op jit(solution)/shard_map/ppermute | solution.py:71
  169.0 7.7 %collective-permute-start.55 = (bf16[80,640]{1,0:T(8,128)(2,1)}, bf16[80,640]{1,0:T(8,128)(2,1)}, u32[]{:S(2)}, u32[]{:S(2)}) collective-permute-start(bf16[80,640]{1,0:T(8,128)(2,1)} %get-tuple-element.122), channel_id=1, source_target_pairs={{0,28},{4,24},{8,20},{12,16},{16,12},{20,8},{24,4},{28,0},{1,29},{... | collective-permute-start | bytes 307208 | tf_op jit(solution)/shard_map/ppermute | solution.py:71
  183.2 15.2 %collective-permute-start.59 = (bf16[336,240]{1,0:T(8,128)(2,1)}, bf16[336,240]{1,0:T(8,128)(2,1)S(1)}, u32[]{:S(2)}, u32[]{:S(2)}) collective-permute-start(bf16[336,240]{1,0:T(8,128)(2,1)} %get-tuple-element.129), channel_id=1, source_target_pairs={{0,1},{1,0},{2,3},{3,2},{4,5},{5,4},{6,7},{7,6},{8,9},{9,8},{10,11... | collective-permute-start | bytes 483848 | tf_op jit(solution)/shard_map/ppermute | solution.py:71
  186.0 15.1 %collective-permute-start.56 = (bf16[128,960]{1,0:T(8,128)(2,1)}, bf16[128,960]{1,0:T(8,128)(2,1)S(1)}, u32[]{:S(2)}, u32[]{:S(2)}) collective-permute-start(bf16[128,960]{1,0:T(8,128)(2,1)} %get-tuple-element.125), channel_id=1, source_target_pairs={{0,8},{4,12},{8,0},{12,4},{16,24},{20,28},{24,16},{28,20},{1,9},{5... | collective-permute-start | bytes 737288 | tf_op jit(solution)/shard_map/ppermute | solution.py:71
  186.0 15.1 %collective-permute-start.57 = (bf16[128,960]{1,0:T(8,128)(2,1)}, bf16[128,960]{1,0:T(8,128)(2,1)S(1)}, u32[]{:S(2)}, u32[]{:S(2)}) collective-permute-start(bf16[128,960]{1,0:T(8,128)(2,1)} %get-tuple-element.126), channel_id=1, source_target_pairs={{0,16},{4,20},{8,24},{12,28},{16,0},{20,4},{24,8},{28,12},{1,17},{... | collective-permute-start | bytes 737288 | tf_op jit(solution)/shard_map/ppermute | solution.py:71
  187.7 13.4 %collective-permute-start.58 = (bf16[128,960]{1,0:T(8,128)(2,1)}, bf16[128,960]{1,0:T(8,128)(2,1)S(1)}, u32[]{:S(2)}, u32[]{:S(2)}) collective-permute-start(bf16[128,960]{1,0:T(8,128)(2,1)} %get-tuple-element.127), channel_id=1, source_target_pairs={{0,24},{4,28},{8,16},{12,20},{16,8},{20,12},{24,0},{28,4},{1,25},{... | collective-permute-start | bytes 737288 | tf_op jit(solution)/shard_map/ppermute | solution.py:71
  189.5 21.0 %collective-permute-start.60 = (bf16[336,240]{1,0:T(8,128)(2,1)}, bf16[336,240]{1,0:T(8,128)(2,1)}, u32[]{:S(2)}, u32[]{:S(2)}) collective-permute-start(bf16[336,240]{1,0:T(8,128)(2,1)} %get-tuple-element.130), channel_id=1, source_target_pairs={{0,2},{1,3},{2,0},{3,1},{4,6},{5,7},{6,4},{7,5},{8,10},{9,11},{10,... | collective-permute-start | bytes 483848 | tf_op jit(solution)/shard_map/ppermute | solution.py:71
  198.5 14.2 %collective-permute-start.61 = (bf16[336,240]{1,0:T(8,128)(2,1)}, bf16[336,240]{1,0:T(8,128)(2,1)}, u32[]{:S(2)}, u32[]{:S(2)}) collective-permute-start(bf16[336,240]{1,0:T(8,128)(2,1)} %get-tuple-element.131), channel_id=1, source_target_pairs={{0,3},{1,2},{2,1},{3,0},{4,7},{5,6},{6,5},{7,4},{8,11},{9,10},{10,... | collective-permute-start | bytes 483848 | tf_op jit(solution)/shard_map/ppermute | solution.py:71
  (56 other events, 226.5 us)
Sparse Core Ops, SparseCore 0:
  38.3 41.2 all-gather.2
  102.1 27.3 all-gather.4
  147.8 27.3 reduce-scatter.4
  177.4 32.9 reduce-scatter.6

commit v5 on v4

--- a/solution.py
+++ b/solution.py
@@ -1008,7 +1008,8 @@
         [pltpu.VMEM((8, 120, 320), F32)],
     )
     down_blocks = exchange(down_blocks)
-    others = after_all([send(h2, "dp", s) for s in (2, 4, 6)], *down_blocks[1:])
+    near = send(h2, "dp", 2)
+    others = after_all([near, send(h2, "dp", 4), send(near, "dp", 4)], *down_blocks[1:])
     down_passed = [send(value, "dp", 1) for value in down_blocks[2:]]
     h2_slots = [h2, send(h2, "dp", 1)]
     for other in others:

time: 222 us -> 221 us (level)
    ppermute x62, waiting for transfers between devices: 68.7 us -> 66.4 us  [send(): return lax.ppermute(values, axis, [(i, i ^ distance) for i in range(count)])]
  transfers between devices with their start and end apart: 66 -> 66, of which waited for: 28 -> 27; matrix products, arithmetic and copies ran while one was open for 1% -> 1% of each run, Pallas kernels for 29% -> 29%
where the time goes in v5:
time: 221 us; the launch traced here: 220 us
  waiting for transfers between devices  77.7 us (35%)
  Pallas kernels  70.6 us (32%)
  starting transfers between devices  48.3 us (22%)
  between operations  14.2 us (6%)
  local copies, waits for them, and re-layouts  7.61 us (3%)
    pallas_call x14, Pallas kernels, kernel_call(): pl.pallas_call(body, out_shape=outs, in_specs=[pl.BlockSpec(memory_space=...  70.6 us
    ppermute x62, waiting for transfers between devices, send(): return lax.ppermute(values, axis, [(i, i ^ distance) for i in range(count)])  66.4 us
    ppermute x62, starting transfers between devices, send(): return lax.ppermute(values, axis, [(i, i ^ distance) for i in range(count)])  47.8 us
    unnamed x109, local copies, waits for them, and re-layouts  7.61 us
    unnamed x5, waiting for transfers between devices  5.91 us
    all_gather x1, waiting for transfers between devices, fast(): feed = lax.all_gather(feed, 'fsdp', axis=0, tiled=True)  5.45 us
  transfers between devices with their start and end apart: 66, of which 27 were waited for; matrix products, arithmetic and copies ran while one was open for 1% of the time, Pallas kernels for 29%

profile of v5, /device:TPU:8, one launch (start us, length us, event | category | flops | bytes accessed | tf_op | source)
XLA Modules:
  0.0 220.1 jit_solution(628111432580393219)
XLA Ops:
  7.2 1.6 collective-permute-start.1
  8.8 1.5 collective-permute-start.2
  10.8 1.8 shard_map.212.own_ref
  12.6 2.6 %collective-permute-start = (bf16[120,640]{1,0:T(8,128)(2,1)}, bf16[120,640]{1,0:T(8,128)(2,1)S(1)}, u32[]{:S(2)}, u32[]{:S(2)}) collective-permute-start(bf16[120,640]{1,0:T(8,128)(2,1)} %shard_map.212.own_ref), channel_id=1, source_target_pairs={{0,2},{1,3},{2,0},{3,1},{4,6},{5,7},{6,4},{7,5},{8,10},{9,11},{10,... | collective-permute-start | bytes 460808 | tf_op jit(solution)/shard_map/ppermute | solution.py:71
  15.2 5.9 %collective-permute-done.got_ref = bf16[120,640]{1,0:T(8,128)(2,1)S(1)} collective-permute-done((bf16[120,640]{1,0:T(8,128)(2,1)}, bf16[120,640]{1,0:T(8,128)(2,1)S(1)}, u32[]{:S(2)}, u32[]{:S(2)}) %collective-permute-start) | collective-permute-done | bytes 153632 | tf_op jit(solution)/shard_map/ppermute | solution.py:71
  22.4 1.8 shard_map.213.rest_0_.rest_14_
  24.3 1.2 collective-permute-start.5
  25.4 1.1 collective-permute-start.6
  26.5 1.5 collective-permute-start.7
  28.0 5.3 %collective-permute-done.5.refs_1_.refs_0_ = bf16[256,640]{1,0:T(8,128)(2,1)S(1)} collective-permute-done((bf16[256,640]{1,0:T(8,128)(2,1)}, bf16[256,640]{1,0:T(8,128)(2,1)S(1)}, u32[]{:S(2)}, u32[]{:S(2)}) %collective-permute-start.5) | collective-permute-done | bytes 327712 | tf_op jit(solution)/shard_map/ppermute | solution.py:71
  33.4 1.2 collective-permute-done.6.refs_0_
  35.3 0.7 copy-done.10
  36.0 2.1 shard_map.217
  38.2 1.6 collective-permute-start.8
  39.8 0.7 copy.39.refs_0_
  41.6 4.8 %collective-permute-done.8.refs_1_ = bf16[256,640]{1,0:T(8,128)(2,1)S(1)} collective-permute-done((bf16[256,640]{1,0:T(8,128)(2,1)S(1)}, bf16[256,640]{1,0:T(8,128)(2,1)S(1)}, u32[]{:S(2)}, u32[]{:S(2)}) %collective-permute-start.8) | collective-permute-done | bytes 327712 | tf_op jit(solution)/shard_map/ppermute | solution.py:71
  46.3 0.7 copy-done.1
  47.1 1.7 collective-permute-start.11
  48.7 0.8 collective-permute-start.17
  50.7 0.9 collective-permute-done.14.rest_10_.refs_2_.rest_24_
  51.6 2.9 %collective-permute-done.11.rest_6_.rest_20_ = bf16[256,640]{1,0:T(8,128)(2,1)S(1)} collective-permute-done((bf16[256,640]{1,0:T(8,128)(2,1)}, bf16[256,640]{1,0:T(8,128)(2,1)S(1)}, u32[]{:S(2)}, u32[]{:S(2)}) %collective-permute-start.11) | collective-permute-done | bytes 327712 | tf_op jit(solution)/shard_map/ppermute | solution.py:71
  54.5 3.2 %collective-permute-done.17.rest_14_.rest_28_ = bf16[256,640]{1,0:T(8,128)(2,1)S(1)} collective-permute-done((bf16[256,640]{1,0:T(8,128)(2,1)}, bf16[256,640]{1,0:T(8,128)(2,1)S(1)}, u32[]{:S(2)}, u32[]{:S(2)}) %collective-permute-start.17) | collective-permute-done | bytes 327712 | tf_op jit(solution)/shard_map/ppermute | solution.py:71
  58.1 0.7 pad_maximum_fusion
  60.0 2.5 %collective-permute-start.25 = (bf16[960,128]{1,0:T(8,128)(2,1)}, bf16[960,128]{1,0:T(8,128)(2,1)}, u32[]{:S(2)}, u32[]{:S(2)}) collective-permute-start(bf16[960,128]{1,0:T(8,128)(2,1)} %shard_map.218.rest_0_), channel_id=1, source_target_pairs={{0,24},{4,28},{8,16},{12,20},{16,8},{20,12},{24,0},{28,4},{1,25},{... | collective-permute-start | bytes 737288 | tf_op jit(solution)/shard_map/ppermute | solution.py:71
  62.6 10.3 %shard_map.216 = (f32[128,960]{1,0:T(8,128)}, bf16[128,960]{1,0:T(8,128)(2,1)}, bf16[128,960]{1,0:T(8,128)(2,1)}, bf16[5,384,64]{2,1,0:T(8,128)(2,1)}, bf16[5,12...) custom-call(s32[2]{0:T(128)} %pad_add_fusion.ids, ...), custom_call_target="tpu_custom_call" | custom-call | flops 11000000512 | bytes 30000000 | tf_op jit(solution)/shard_map/pallas_call | solution.py:407
  72.9 0.6 collective-permute-start.20
  74.1 5.5 %all-gather.3.cloned.1.call-done.feed_ref.rest_16_ = bf16[1440,640]{1,0:T(8,128)(2,1)} async-done(((bf16[360,640]{1,0:T(8,128)(2,1)}), bf16[1440,640]{1,0:T(8,128)(2,1)}) %all-gather.3.cloned.1.call-update) | async-done | bytes 1843216 | tf_op jit(solution)/shard_map/all_gather | solution.py:973
  79.6 2.6 %shard_map.219 = (bf16[64,640]{1,0:T(8,128)(2,1)}, bf16[64,640]{1,0:T(8,128)(2,1)}, bf16[128,640]{1,0:T(8,128)(2,1)}, bf16[128,640]{1,0:T(8,128)(2,1)}, bf16[128,640]{1,0:T(8,128)(2,1)}) custom-call(s32[2]{0:T(128)} %pad_add_fusion.ids, bf16[1440,640]{1,0:T(8,128)(2,1)} %all-gather.3.cloned.1.call-done.feed_ref.rest_16_, ...), custom_call_target="tpu_custom_call" | custom-call | flops 1100000000 | bytes 3000000 | tf_op jit(solution)/shard_map/pallas_call | solution.py:407
  82.2 1.5 collective-permute-start.27
  83.7 1.5 collective-permute-start.22
  85.7 1.5 collective-permute-start.29
  87.2 1.0 collective-permute-done.27.refs_4_.rest_19_
  88.7 9.5 %collective-permute-done.28.refs_5_.rest_20_ = bf16[128,640]{1,0:T(8,128)(2,1)S(1)} collective-permute-done((bf16[128,640]{1,0:T(8,128)(2,1)}, bf16[128,640]{1,0:T(8,128)(2,1)S(1)}, u32[]{:S(2)}, u32[]{:S(2)}) %collective-permute-start.28) | collective-permute-done | bytes 163872 | tf_op jit(solution)/shard_map/ppermute | solution.py:71
  104.2 0.7 copy-done.35
  104.9 11.7 %shard_map.221 = (f32[4,128,960]{2,1,0:T(8,128)}, bf16[704,1024]{1,0:T(8,128)(2,1)}, bf16[1024,640]{1,0:T(8,128)(2,1)}, bf16[1024,320]{1,0:T(8,128)(2,1)}, bf16[...) custom-call(s32[2]{0:T(128)} %pad_add_fusion.ids, ...), custom_call_target="tpu_custom_call" | custom-call | flops 12099999744 | bytes 33000000 | tf_op jit(solution)/shard_map/pallas_call | solution.py:407
  116.9 3.3 %collective-permute-done.40.odd_ref = bf16[704,1024]{1,0:T(8,128)(2,1)} collective-permute-done((bf16[704,1024]{1,0:T(8,128)(2,1)}, bf16[704,1024]{1,0:T(8,128)(2,1)}, u32[]{:S(2)}, u32[]{:S(2)}) %collective-permute-start.40) | collective-permute-done | bytes 1441824 | tf_op jit(solution)/shard_map/ppermute | solution.py:71
  120.2 3.4 %shard_map.222 = (f32[128,960]{1,0:T(8,128)}, bf16[48,960]{1,0:T(8,128)(2,1)}, bf16[208,960]{1,0:T(8,128)(2,1)}, bf16[208,960]{1,0:T(8,128)(2,1)}, bf16[208,960]{1,0:T(8,128)(2,1)}) custom-call(f32[4,128,960]{2,1,0:T(8,128)} %get-tuple-element.91.even_ref, bf16[704,1024]{1,0:T(8,128)(2,1)} %collective-permute-done.40.odd_ref, ...), custom_call_target="tpu_custom_call" | custom-call | flops 1100000000 | bytes 3000000 | tf_op jit(solution)/shard_map/pallas_call | solution.py:407
  124.1 1.5 collective-permute-start.43
  125.6 1.5 collective-permute-start.44
  127.1 8.4 %shard_map.223 = (bf16[960,640]{1,0:T(8,128)(2,1)}, f32[4,128,960]{2,1,0:T(8,128)}, bf16[512,1024]{1,0:T(8,128)(2,1)}) custom-call(bf16[128,960]{1,0:T(8,128)(2,1)} %get-tuple-element.79.rest_0_, bf16[128,960]{1,0:T(8,128)(2,1)} %copy-done.32, bf16[128,960]{1,0:T(8,128)(2,1)} %get-tuple-element.84.rest_2_.refs_1_, bf16[128,960]{1,0:T(8,128)(2,1)} %copy-done.33, ...), custom_call_target="tpu_custom_call" | custom-call | flops 4400000000 | bytes 12000000 | tf_op jit(solution)/shard_map/pallas_call | solution.py:407
  135.5 0.9 collective-permute-done.42.refs_1_.rest_1_
  136.5 9.5 %collective-permute-done.44.refs_3_.rest_3_ = bf16[208,960]{1,0:T(8,128)(2,1)} collective-permute-done((bf16[208,960]{1,0:T(8,128)(2,1)}, bf16[208,960]{1,0:T(8,128)(2,1)}, u32[]{:S(2)}, u32[]{:S(2)}) %collective-permute-start.44) | collective-permute-done | bytes 399392 | tf_op jit(solution)/shard_map/ppermute | solution.py:71
  146.3 0.6 copy-done.8
  148.0 12.6 %shard_map.226 = (bf16[80,640]{1,0:T(8,128)(2,1)}, bf16[80,640]{1,0:T(8,128)(2,1)}, bf16[80,640]{1,0:T(8,128)(2,1)}, bf16[80,640]{1,0:T(8,128)(2,1)}, bf16[80,64...) custom-call(s32[2]{0:T(128)} %pad_add_fusion.ids, ...), custom_call_target="tpu_custom_call" | custom-call | flops 13200000000 | bytes 36000000 | tf_op jit(solution)/shard_map/pallas_call | solution.py:407
  161.1 0.8 collective-permute-start.50
  162.0 0.7 collective-permute-start.51
  162.7 0.9 collective-permute-start.52
  163.7 1.1 collective-permute-start.53
  164.8 1.7 collective-permute-start.54
  167.1 3.0 %shard_map.227 = (f32[128,960]{1,0:T(8,128)}, bf16[128,960]{1,0:T(8,128)(2,1)}, bf16[128,960]{1,0:T(8,128)(2,1)}, bf16[128,960]{1,0:T(8,128)(2,1)}) custom-call(f32[4,128,960]{2,1,0:T(8,128)} %get-tuple-element.97.even_ref, bf16[512,1024]{1,0:T(8,128)(2,1)} %collective-permute-done.41.odd_ref, bf16[80,640]{1,0:T(8,128)(2,1)} %get-tuple-element.111.rest_0_.rest_9_), custom_call_target="tpu_custom_call" | custom-call | flops 1100000000 | bytes 3000000 | tf_op jit(solution)/shard_map/pallas_call | solution.py:407
  170.2 4.7 %collective-permute-done.53.rest_14_ = bf16[80,640]{1,0:T(8,128)(2,1)} collective-permute-done((bf16[80,640]{1,0:T(8,128)(2,1)}, bf16[80,640]{1,0:T(8,128)(2,1)}, u32[]{:S(2)}, u32[]{:S(2)}) %collective-permute-start.53) | collective-permute-done | bytes 102432 | tf_op jit(solution)/shard_map/ppermute | solution.py:71
  174.8 6.5 %shard_map.228 = (f32[336,240]{1,0:T(8,128)}, bf16[336,240]{1,0:T(8,128)(2,1)}, bf16[336,240]{1,0:T(8,128)(2,1)}, bf16[336,240]{1,0:T(8,128)(2,1)}) custom-call(s32[2]{0:T(128)} %pad_add_fusion.ids, bf16[960,128]{1,0:T(8,128)(2,1)} %shard_map.218.rest_0_, bf16[960,128]{1,0:T(8,128)(2,1)} %copy-done.43, ...), custom_call_target="tpu_custom_call" | custom-call | flops 7150000128 | bytes 19500000 | tf_op jit(solution)/shard_map/pallas_call | solution.py:407
  181.4 3.0 %collective-permute-start.59 = (bf16[336,240]{1,0:T(8,128)(2,1)}, bf16[336,240]{1,0:T(8,128)(2,1)S(1)}, u32[]{:S(2)}, u32[]{:S(2)}) collective-permute-start(bf16[336,240]{1,0:T(8,128)(2,1)} %get-tuple-element.129), channel_id=1, source_target_pairs={{0,1},{1,0},{2,3},{3,2},{4,5},{5,4},{6,7},{7,6},{8,9},{9,8},{10,11... | collective-permute-start | bytes 483848 | tf_op jit(solution)/shard_map/ppermute | solution.py:71
  184.9 1.7 collective-permute-start.57
  186.6 1.2 collective-permute-start.58
  188.3 7.9 %collective-permute-done.59._.a_ref = bf16[336,240]{1,0:T(8,128)(2,1)S(1)} collective-permute-done((bf16[336,240]{1,0:T(8,128)(2,1)}, bf16[336,240]{1,0:T(8,128)(2,1)S(1)}, u32[]{:S(2)}, u32[]{:S(2)}) %collective-permute-start.59) | collective-permute-done | bytes 161312 | tf_op jit(solution)/shard_map/ppermute | solution.py:71
  196.2 1.5 collective-permute-start.61
  197.7 2.0 shard_map.231
  199.7 0.7 copy-done.36
  200.5 0.7 copy-done.38
  201.2 2.3 %shard_map.230.rest_0_ = bf16[960,128]{1,0:T(8,128)(2,1)} custom-call(f32[128,960]{1,0:T(8,128)} %get-tuple-element.78.rest_5_.x2_ref, f32[128,960]{1,0:T(8,128)} %get-tuple-element.112.rest_18_.own_ref, bf16[128,960]{1,0:T(8,128)(2,1)} %copy-done.36, bf16[128,960]{1,0:T(8,128)(2,1)} %copy-done.37, bf16[128,960]{1,0:T(8,128)(2,1)} %copy-done.38), custom_call_target="tpu_custom_call" | custom-call | flops 1100000000 | bytes 3000000 | tf_op jit(solution)/shard_map/pallas_call | solution.py:407
  203.5 5.8 %reduce-scatter.7.cloned.1.call-done.down_ref = bf16[120,640]{1,0:T(8,128)(2,1)} async-done(((bf16[480,640]{1,0:T(8,128)(2,1)}), bf16[120,640]{1,0:T(8,128)(2,1)}) %reduce-scatter.7.cloned.1.call-update) | async-done | bytes 153616
  209.4 2.0 collective-permute-done.61.c_ref
  211.4 2.2 shard_map.232
  (207 shorter events, 18.7 us)
Async XLA Ops:
  7.2 72.4 %all-gather.3.cloned.1.call-start = ((), (), s32[]{:S(2)}) async-start(), calls=%async_computation.2 | async-start | bytes 2304000 | tf_op jit(solution)/shard_map/all_gather | solution.py:973
  7.2 13.8 %collective-permute-start.1 = (bf16[960,128]{1,0:T(8,128)(2,1)}, bf16[960,128]{1,0:T(8,128)(2,1)S(1)}, u32[]{:S(2)}, u32[]{:S(2)}) collective-permute-start(bf16[960,128]{1,0:T(8,128)(2,1)} %bitcast.34), channel_id=1, source_target_pairs={{0,8},{4,12},{8,0},{12,4},{16,24},{20,28},{24,16},{28,20},{1,9},{5... | collective-permute-start | bytes 737288 | tf_op jit(solution)/shard_map/ppermute | solution.py:71
  8.8 12.9 %collective-permute-start.2 = (bf16[960,128]{1,0:T(8,128)(2,1)}, bf16[960,128]{1,0:T(8,128)(2,1)S(1)}, u32[]{:S(2)}, u32[]{:S(2)}) collective-permute-start(bf16[960,128]{1,0:T(8,128)(2,1)} %bitcast.35), channel_id=1, source_target_pairs={{0,16},{4,20},{8,24},{12,28},{16,0},{20,4},{24,8},{28,12},{1,17},{... | collective-permute-start | bytes 737288 | tf_op jit(solution)/shard_map/ppermute | solution.py:71
  10.3 11.4 %collective-permute-start.3 = (bf16[960,128]{1,0:T(8,128)(2,1)}, bf16[960,128]{1,0:T(8,128)(2,1)S(1)}, u32[]{:S(2)}, u32[]{:S(2)}) collective-permute-start(bf16[960,128]{1,0:T(8,128)(2,1)} %bitcast.36), channel_id=1, source_target_pairs={{0,24},{4,28},{8,16},{12,20},{16,8},{20,12},{24,0},{28,4},{1,25},{... | collective-permute-start | bytes 737288 | tf_op jit(solution)/shard_map/ppermute | solution.py:71
  12.6 8.5 %collective-permute-start = (bf16[120,640]{1,0:T(8,128)(2,1)}, bf16[120,640]{1,0:T(8,128)(2,1)S(1)}, u32[]{:S(2)}, u32[]{:S(2)}) collective-permute-start(bf16[120,640]{1,0:T(8,128)(2,1)} %shard_map.212.own_ref), channel_id=1, source_target_pairs={{0,2},{1,3},{2,0},{3,1},{4,6},{5,7},{6,4},{7,5},{8,10},{9,11},{10,... | collective-permute-start | bytes 460808 | tf_op jit(solution)/shard_map/ppermute | solution.py:71
  24.3 9.1 %collective-permute-start.5 = (bf16[256,640]{1,0:T(8,128)(2,1)}, bf16[256,640]{1,0:T(8,128)(2,1)S(1)}, u32[]{:S(2)}, u32[]{:S(2)}) collective-permute-start(bf16[256,640]{1,0:T(8,128)(2,1)} %shard_map.213.rest_0_.rest_14_), channel_id=1, source_target_pairs={{0,8},{4,12},{8,0},{12,4},{16,24},{20,28},{24,16},{28,20},{1,9},{5... | collective-permute-start | bytes 983048 | tf_op jit(solution)/shard_map/ppermute | solution.py:71
  25.4 9.2 %collective-permute-start.6 = (bf16[256,640]{1,0:T(8,128)(2,1)}, bf16[256,640]{1,0:T(8,128)(2,1)S(1)}, u32[]{:S(2)}, u32[]{:S(2)}) collective-permute-start(bf16[256,640]{1,0:T(8,128)(2,1)} %shard_map.213.rest_0_.rest_14_), channel_id=1, source_target_pairs={{0,1},{1,0},{2,3},{3,2},{4,5},{5,4},{6,7},{7,6},{8,9},{9,8},{10,11... | collective-permute-start | bytes 983048 | tf_op jit(solution)/shard_map/ppermute | solution.py:71
  26.5 8.2 %collective-permute-start.7 = (bf16[256,640]{1,0:T(8,128)(2,1)}, bf16[256,640]{1,0:T(8,128)(2,1)S(1)}, u32[]{:S(2)}, u32[]{:S(2)}) collective-permute-start(bf16[256,640]{1,0:T(8,128)(2,1)} %shard_map.213.rest_0_.rest_14_), channel_id=1, source_target_pairs={{0,16},{4,20},{8,24},{12,28},{16,0},{20,4},{24,8},{28,12},{1,17},{... | collective-permute-start | bytes 983048 | tf_op jit(solution)/shard_map/ppermute | solution.py:71
  38.2 107.8 %all-gather.5.cloned.1.call-start = ((), (), s32[]{:S(2)}) async-start(), calls=%async_computation.3 | async-start | bytes 2359296 | tf_op jit(solution)/shard_map/all_gather | solution.py:1018
  38.2 8.1 %collective-permute-start.8 = (bf16[256,640]{1,0:T(8,128)(2,1)S(1)}, bf16[256,640]{1,0:T(8,128)(2,1)S(1)}, u32[]{:S(2)}, u32[]{:S(2)}) collective-permute-start(bf16[256,640]{1,0:T(8,128)(2,1)S(1)} %copy-done.13), channel_id=1, source_target_pairs={{0,16},{4,20},{8,24},{12,28},{16,0},{20,4},{24,8},{28,12},{1,17},{... | collective-permute-start | bytes 983048 | tf_op jit(solution)/shard_map/ppermute | solution.py:71
  39.8 8.9 %collective-permute-start.4 = (bf16[256,640]{1,0:T(8,128)(2,1)}, bf16[256,640]{1,0:T(8,128)(2,1)S(1)}, u32[]{:S(2)}, u32[]{:S(2)}) collective-permute-start(bf16[256,640]{1,0:T(8,128)(2,1)} %shard_map.213.rest_0_.rest_14_), channel_id=1, source_target_pairs={{0,4},{4,0},{8,12},{12,8},{16,20},{20,16},{24,28},{28,24},{1,5},{5... | collective-permute-start | bytes 983048 | tf_op jit(solution)/shard_map/ppermute | solution.py:71
  40.5 9.7 %collective-permute-start.13 = (bf16[256,640]{1,0:T(8,128)(2,1)S(1)}, bf16[256,640]{1,0:T(8,128)(2,1)S(1)}, u32[]{:S(2)}, u32[]{:S(2)}) collective-permute-start(bf16[256,640]{1,0:T(8,128)(2,1)S(1)} %copy-done.13), channel_id=1, source_target_pairs={{0,4},{4,0},{8,12},{12,8},{16,20},{20,16},{24,28},{28,24},{1,5},{5... | collective-permute-start | bytes 983048 | tf_op jit(solution)/shard_map/ppermute | solution.py:71
  41.0 10.6 %collective-permute-start.14 = (bf16[256,640]{1,0:T(8,128)(2,1)S(1)}, bf16[256,640]{1,0:T(8,128)(2,1)S(1)}, u32[]{:S(2)}, u32[]{:S(2)}) collective-permute-start(bf16[256,640]{1,0:T(8,128)(2,1)S(1)} %copy-done.13), channel_id=1, source_target_pairs={{0,8},{4,12},{8,0},{12,4},{16,24},{20,28},{24,16},{28,20},{1,9},{5... | collective-permute-start | bytes 983048 | tf_op jit(solution)/shard_map/ppermute | solution.py:71
  41.6 8.5 %collective-permute-start.10 = (bf16[256,640]{1,0:T(8,128)(2,1)S(1)}, bf16[256,640]{1,0:T(8,128)(2,1)S(1)}, u32[]{:S(2)}, u32[]{:S(2)}) collective-permute-start(bf16[256,640]{1,0:T(8,128)(2,1)S(1)} %copy-done.11), channel_id=1, source_target_pairs={{0,4},{4,0},{8,12},{12,8},{16,20},{20,16},{24,28},{28,24},{1,5},{5... | collective-permute-start | bytes 983048 | tf_op jit(solution)/shard_map/ppermute | solution.py:71
  47.1 7.4 %collective-permute-start.11 = (bf16[256,640]{1,0:T(8,128)(2,1)}, bf16[256,640]{1,0:T(8,128)(2,1)S(1)}, u32[]{:S(2)}, u32[]{:S(2)}) collective-permute-start(bf16[256,640]{1,0:T(8,128)(2,1)} %get-tuple-element.76.rest_2_.rest_16_), channel_id=1, source_target_pairs={{0,16},{4,20},{8,24},{12,28},{16,0},{20,4},{24,8},{28,12},{1,17},{... | collective-permute-start | bytes 983048 | tf_op jit(solution)/shard_map/ppermute | solution.py:71
  48.7 9.0 %collective-permute-start.17 = (bf16[256,640]{1,0:T(8,128)(2,1)}, bf16[256,640]{1,0:T(8,128)(2,1)S(1)}, u32[]{:S(2)}, u32[]{:S(2)}) collective-permute-start(bf16[256,640]{1,0:T(8,128)(2,1)} %get-tuple-element.77.rest_12_.refs_1_.rest_26_), channel_id=1, source_target_pairs={{0,8},{4,12},{8,0},{12,4},{16,24},{20,28},{24,16},{28,20},{1,9},{5... | collective-permute-start | bytes 983048 | tf_op jit(solution)/shard_map/ppermute | solution.py:71
  50.1 8.7 %collective-permute-start.9 = (bf16[256,640]{1,0:T(8,128)(2,1)}, bf16[256,640]{1,0:T(8,128)(2,1)S(1)}, u32[]{:S(2)}, u32[]{:S(2)}) collective-permute-start(bf16[256,640]{1,0:T(8,128)(2,1)} %get-tuple-element.76.rest_2_.rest_16_), channel_id=1, source_target_pairs={{0,4},{4,0},{8,12},{12,8},{16,20},{20,16},{24,28},{28,24},{1,5},{5... | collective-permute-start | bytes 983048 | tf_op jit(solution)/shard_map/ppermute | solution.py:71
  50.2 9.8 %collective-permute-start.16 = (bf16[256,640]{1,0:T(8,128)(2,1)}, bf16[256,640]{1,0:T(8,128)(2,1)S(1)}, u32[]{:S(2)}, u32[]{:S(2)}) collective-permute-start(bf16[256,640]{1,0:T(8,128)(2,1)} %get-tuple-element.77.rest_12_.refs_1_.rest_26_), channel_id=1, source_target_pairs={{0,4},{4,0},{8,12},{12,8},{16,20},{20,16},{24,28},{28,24},{1,5},{5... | collective-permute-start | bytes 983048 | tf_op jit(solution)/shard_map/ppermute | solution.py:71
  51.6 7.8 %collective-permute-start.15 = (bf16[256,640]{1,0:T(8,128)(2,1)S(1)}, bf16[256,640]{1,0:T(8,128)(2,1)S(1)}, u32[]{:S(2)}, u32[]{:S(2)}) collective-permute-start(bf16[256,640]{1,0:T(8,128)(2,1)S(1)} %collective-permute-done.14.rest_10_.refs_2_.rest_24_), channel_id=1, source_target_pairs={{0,4},{4,0},{8,12},{12,8},{16,20},{20,16},{24,28},{28,24},{1,5},{5... | collective-permute-start | bytes 983048 | tf_op jit(solution)/shard_map/ppermute | solution.py:71
  54.5 8.0 %collective-permute-start.12 = (bf16[256,640]{1,0:T(8,128)(2,1)S(1)}, bf16[256,640]{1,0:T(8,128)(2,1)}, u32[]{:S(2)}, u32[]{:S(2)}) collective-permute-start(bf16[256,640]{1,0:T(8,128)(2,1)S(1)} %collective-permute-done.11.rest_6_.rest_20_), channel_id=1, source_target_pairs={{0,4},{4,0},{8,12},{12,8},{16,20},{20,16},{24,28},{28,24},{1,5},{5... | collective-permute-start | bytes 983048 | tf_op jit(solution)/shard_map/ppermute | solution.py:71
  57.7 4.8 %collective-permute-start.18 = (bf16[256,640]{1,0:T(8,128)(2,1)S(1)}, bf16[256,640]{1,0:T(8,128)(2,1)}, u32[]{:S(2)}, u32[]{:S(2)}) collective-permute-start(bf16[256,640]{1,0:T(8,128)(2,1)S(1)} %collective-permute-done.17.rest_14_.rest_28_), channel_id=1, source_target_pairs={{0,4},{4,0},{8,12},{12,8},{16,20},{20,16},{24,28},{28,24},{1,5},{5... | collective-permute-start | bytes 983048 | tf_op jit(solution)/shard_map/ppermute | solution.py:71
  58.8 15.3 %collective-permute-start.23 = (bf16[960,128]{1,0:T(8,128)(2,1)}, bf16[960,128]{1,0:T(8,128)(2,1)}, u32[]{:S(2)}, u32[]{:S(2)}) collective-permute-start(bf16[960,128]{1,0:T(8,128)(2,1)} %shard_map.218.rest_0_), channel_id=1, source_target_pairs={{0,8},{4,12},{8,0},{12,4},{16,24},{20,28},{24,16},{28,20},{1,9},{5... | collective-permute-start | bytes 737288 | tf_op jit(solution)/shard_map/ppermute | solution.py:71
  59.4 14.7 %collective-permute-start.24 = (bf16[960,128]{1,0:T(8,128)(2,1)}, bf16[960,128]{1,0:T(8,128)(2,1)}, u32[]{:S(2)}, u32[]{:S(2)}) collective-permute-start(bf16[960,128]{1,0:T(8,128)(2,1)} %shard_map.218.rest_0_), channel_id=1, source_target_pairs={{0,16},{4,20},{8,24},{12,28},{16,0},{20,4},{24,8},{28,12},{1,17},{... | collective-permute-start | bytes 737288 | tf_op jit(solution)/shard_map/ppermute | solution.py:71
  60.0 14.1 %collective-permute-start.25 = (bf16[960,128]{1,0:T(8,128)(2,1)}, bf16[960,128]{1,0:T(8,128)(2,1)}, u32[]{:S(2)}, u32[]{:S(2)}) collective-permute-start(bf16[960,128]{1,0:T(8,128)(2,1)} %shard_map.218.rest_0_), channel_id=1, source_target_pairs={{0,24},{4,28},{8,16},{12,20},{16,8},{20,12},{24,0},{28,4},{1,25},{... | collective-permute-start | bytes 737288 | tf_op jit(solution)/shard_map/ppermute | solution.py:71
  72.9 10.8 %collective-permute-start.20 = (bf16[128,960]{1,0:T(8,128)(2,1)}, bf16[128,960]{1,0:T(8,128)(2,1)S(1)}, u32[]{:S(2)}, u32[]{:S(2)}) collective-permute-start(bf16[128,960]{1,0:T(8,128)(2,1)} %get-tuple-element.79.rest_0_), channel_id=1, source_target_pairs={{0,8},{4,12},{8,0},{12,4},{16,24},{20,28},{24,16},{28,20},{1,9},{5... | collective-permute-start | bytes 737288 | tf_op jit(solution)/shard_map/ppermute | solution.py:71
  73.5 14.6 %collective-permute-start.21 = (bf16[128,960]{1,0:T(8,128)(2,1)}, bf16[128,960]{1,0:T(8,128)(2,1)S(1)}, u32[]{:S(2)}, u32[]{:S(2)}) collective-permute-start(bf16[128,960]{1,0:T(8,128)(2,1)} %get-tuple-element.79.rest_0_), channel_id=1, source_target_pairs={{0,16},{4,20},{8,24},{12,28},{16,0},{20,4},{24,8},{28,12},{1,17},{... | collective-permute-start | bytes 737288 | tf_op jit(solution)/shard_map/ppermute | solution.py:71
  82.2 5.9 %collective-permute-start.27 = (bf16[128,640]{1,0:T(8,128)(2,1)}, bf16[128,640]{1,0:T(8,128)(2,1)S(1)}, u32[]{:S(2)}, u32[]{:S(2)}) collective-permute-start(bf16[128,640]{1,0:T(8,128)(2,1)} %get-tuple-element.81), channel_id=1, source_target_pairs={{0,8},{4,12},{8,0},{12,4},{16,24},{20,28},{24,16},{28,20},{1,9},{5... | collective-permute-start | bytes 491528 | tf_op jit(solution)/shard_map/ppermute | solution.py:71
  83.7 15.1 %collective-permute-start.22 = (bf16[128,960]{1,0:T(8,128)(2,1)S(1)}, bf16[128,960]{1,0:T(8,128)(2,1)S(1)}, u32[]{:S(2)}, u32[]{:S(2)}) collective-permute-start(bf16[128,960]{1,0:T(8,128)(2,1)S(1)} %collective-permute-done.20.refs_0_), channel_id=1, source_target_pairs={{0,16},{4,20},{8,24},{12,28},{16,0},{20,4},{24,8},{28,12},{1,17},{... | collective-permute-start | bytes 737288 | tf_op jit(solution)/shard_map/ppermute | solution.py:71
  85.2 13.1 %collective-permute-start.28 = (bf16[128,640]{1,0:T(8,128)(2,1)}, bf16[128,640]{1,0:T(8,128)(2,1)S(1)}, u32[]{:S(2)}, u32[]{:S(2)}) collective-permute-start(bf16[128,640]{1,0:T(8,128)(2,1)} %get-tuple-element.82), channel_id=1, source_target_pairs={{0,16},{4,20},{8,24},{12,28},{16,0},{20,4},{24,8},{28,12},{1,17},{... | collective-permute-start | bytes 491528 | tf_op jit(solution)/shard_map/ppermute | solution.py:71
  85.7 12.6 %collective-permute-start.29 = (bf16[128,640]{1,0:T(8,128)(2,1)}, bf16[128,640]{1,0:T(8,128)(2,1)S(1)}, u32[]{:S(2)}, u32[]{:S(2)}) collective-permute-start(bf16[128,640]{1,0:T(8,128)(2,1)} %get-tuple-element.83), channel_id=1, source_target_pairs={{0,24},{4,28},{8,16},{12,20},{16,8},{20,12},{24,0},{28,4},{1,25},{... | collective-permute-start | bytes 491528 | tf_op jit(solution)/shard_map/ppermute | solution.py:71
  88.1 11.2 %collective-permute-start.37 = (bf16[128,640]{1,0:T(8,128)(2,1)S(1)}, bf16[128,640]{1,0:T(8,128)(2,1)S(1)}, u32[]{:S(2)}, u32[]{:S(2)}) collective-permute-start(bf16[128,640]{1,0:T(8,128)(2,1)S(1)} %collective-permute-done.27.refs_4_.rest_19_), channel_id=1, source_target_pairs={{0,4},{4,0},{8,12},{12,8},{16,20},{20,16},{24,28},{28,24},{1,5},{5... | collective-permute-start | bytes 491528 | tf_op jit(solution)/shard_map/ppermute | solution.py:71
  88.2 10.7 %collective-permute-start.26 = (bf16[64,640]{1,0:T(8,128)(2,1)}, bf16[64,640]{1,0:T(8,128)(2,1)S(1)}, u32[]{:S(2)}, u32[]{:S(2)}) collective-permute-start(bf16[64,640]{1,0:T(8,128)(2,1)} %get-tuple-element.80), channel_id=1, source_target_pairs={{0,4},{4,0},{8,12},{12,8},{16,20},{20,16},{24,28},{28,24},{1,5},{5... | collective-permute-start | bytes 245768 | tf_op jit(solution)/shard_map/ppermute | solution.py:71
  98.3 1.6 collective-permute-start.39
  98.8 2.6 %collective-permute-start.33 = (bf16[960,128]{1,0:T(8,128)(2,1)}, bf16[960,128]{1,0:T(8,128)(2,1)S(1)}, u32[]{:S(2)}, u32[]{:S(2)}) collective-permute-start(bf16[960,128]{1,0:T(8,128)(2,1)} %bitcast.37), channel_id=1, source_target_pairs={{0,4},{4,0},{8,12},{12,8},{16,20},{20,16},{24,28},{28,24},{1,5},{5... | collective-permute-start | bytes 737288 | tf_op jit(solution)/shard_map/ppermute | solution.py:71
  98.9 2.9 %collective-permute-start.34 = (bf16[960,128]{1,0:T(8,128)(2,1)}, bf16[960,128]{1,0:T(8,128)(2,1)S(1)}, u32[]{:S(2)}, u32[]{:S(2)}) collective-permute-start(bf16[960,128]{1,0:T(8,128)(2,1)} %copy-done.39), channel_id=1, source_target_pairs={{0,4},{4,0},{8,12},{12,8},{16,20},{20,16},{24,28},{28,24},{1,5},{5... | collective-permute-start | bytes 737288 | tf_op jit(solution)/shard_map/ppermute | solution.py:71
  99.3 2.7 %collective-permute-start.35 = (bf16[960,128]{1,0:T(8,128)(2,1)}, bf16[960,128]{1,0:T(8,128)(2,1)}, u32[]{:S(2)}, u32[]{:S(2)}) collective-permute-start(bf16[960,128]{1,0:T(8,128)(2,1)} %copy-done.40), channel_id=1, source_target_pairs={{0,4},{4,0},{8,12},{12,8},{16,20},{20,16},{24,28},{28,24},{1,5},{5... | collective-permute-start | bytes 737288 | tf_op jit(solution)/shard_map/ppermute | solution.py:71
  100.6 74.3 %reduce-scatter.5.cloned.1.call-start = ((), (), s32[]{:S(2)}) async-start(), calls=%async_computation.4 | async-start | bytes 1536000 | tf_op jit(solution)/shard_map/reduce_scatter | solution.py:1069
  101.2 1.6 collective-permute-start.19
  101.4 1.7 collective-permute-start.30
  101.7 1.8 collective-permute-start.31
  102.0 1.8 collective-permute-start.32
  116.6 3.6 %collective-permute-start.40 = (bf16[704,1024]{1,0:T(8,128)(2,1)}, bf16[704,1024]{1,0:T(8,128)(2,1)}, u32[]{:S(2)}, u32[]{:S(2)}) collective-permute-start(bf16[704,1024]{1,0:T(8,128)(2,1)} %get-tuple-element.92), channel_id=1, source_target_pairs={{0,4},{4,0},{8,12},{12,8},{16,20},{20,16},{24,28},{28,24},{1,5},{5... | collective-permute-start | bytes 4325384 | tf_op jit(solution)/shard_map/ppermute | solution.py:71
  123.6 12.9 %collective-permute-start.42 = (bf16[208,960]{1,0:T(8,128)(2,1)}, bf16[208,960]{1,0:T(8,128)(2,1)S(1)}, u32[]{:S(2)}, u32[]{:S(2)}) collective-permute-start(bf16[208,960]{1,0:T(8,128)(2,1)} %get-tuple-element.99), channel_id=1, source_target_pairs={{0,8},{4,12},{8,0},{12,4},{16,24},{20,28},{24,16},{28,20},{1,9},{5... | collective-permute-start | bytes 1198088 | tf_op jit(solution)/shard_map/ppermute | solution.py:71
  124.1 12.3 %collective-permute-start.43 = (bf16[208,960]{1,0:T(8,128)(2,1)}, bf16[208,960]{1,0:T(8,128)(2,1)}, u32[]{:S(2)}, u32[]{:S(2)}) collective-permute-start(bf16[208,960]{1,0:T(8,128)(2,1)} %get-tuple-element.100), channel_id=1, source_target_pairs={{0,16},{4,20},{8,24},{12,28},{16,0},{20,4},{24,8},{28,12},{1,17},{... | collective-permute-start | bytes 1198088 | tf_op jit(solution)/shard_map/ppermute | solution.py:71
  125.6 20.4 %collective-permute-start.44 = (bf16[208,960]{1,0:T(8,128)(2,1)}, bf16[208,960]{1,0:T(8,128)(2,1)}, u32[]{:S(2)}, u32[]{:S(2)}) collective-permute-start(bf16[208,960]{1,0:T(8,128)(2,1)} %get-tuple-element.101), channel_id=1, source_target_pairs={{0,24},{4,28},{8,16},{12,20},{16,8},{20,12},{24,0},{28,4},{1,25},{... | collective-permute-start | bytes 1198088 | tf_op jit(solution)/shard_map/ppermute | solution.py:71
  146.0 63.3 %reduce-scatter.7.cloned.1.call-start = ((), (), s32[]{:S(2)}) async-start(), calls=%async_computation.5 | async-start | bytes 768000
  146.9 13.6 %collective-permute-start.45 = (bf16[960,128]{1,0:T(8,128)(2,1)S(1)}, bf16[960,128]{1,0:T(8,128)(2,1)S(1)}, u32[]{:S(2)}, u32[]{:S(2)}) collective-permute-start(bf16[960,128]{1,0:T(8,128)(2,1)S(1)} %copy-done.8), channel_id=1, source_target_pairs={{0,4},{4,0},{8,12},{12,8},{16,20},{20,16},{24,28},{28,24},{1,5},{5... | collective-permute-start | bytes 737288 | tf_op jit(solution)/shard_map/ppermute | solution.py:71
  146.9 14.2 %collective-permute-start.46 = (bf16[960,128]{1,0:T(8,128)(2,1)}, bf16[960,128]{1,0:T(8,128)(2,1)S(1)}, u32[]{:S(2)}, u32[]{:S(2)}) collective-permute-start(bf16[960,128]{1,0:T(8,128)(2,1)} %collective-permute-done.23.rest_1_.rest_2_), channel_id=1, source_target_pairs={{0,4},{4,0},{8,12},{12,8},{16,20},{20,16},{24,28},{28,24},{1,5},{5... | collective-permute-start | bytes 737288 | tf_op jit(solution)/shard_map/ppermute | solution.py:71
  147.4 14.5 %collective-permute-start.47 = (bf16[960,128]{1,0:T(8,128)(2,1)}, bf16[960,128]{1,0:T(8,128)(2,1)S(1)}, u32[]{:S(2)}, u32[]{:S(2)}) collective-permute-start(bf16[960,128]{1,0:T(8,128)(2,1)} %collective-permute-done.24.rest_2_.rest_4_), channel_id=1, source_target_pairs={{0,4},{4,0},{8,12},{12,8},{16,20},{20,16},{24,28},{28,24},{1,5},{5... | collective-permute-start | bytes 737288 | tf_op jit(solution)/shard_map/ppermute | solution.py:71
  147.4 15.3 %collective-permute-start.48 = (bf16[960,128]{1,0:T(8,128)(2,1)}, bf16[960,128]{1,0:T(8,128)(2,1)}, u32[]{:S(2)}, u32[]{:S(2)}) collective-permute-start(bf16[960,128]{1,0:T(8,128)(2,1)} %collective-permute-done.25.rest_3_.rest_6_), channel_id=1, source_target_pairs={{0,4},{4,0},{8,12},{12,8},{16,20},{20,16},{24,28},{28,24},{1,5},{5... | collective-permute-start | bytes 737288 | tf_op jit(solution)/shard_map/ppermute | solution.py:71
  148.0 15.7 %collective-permute-start.41 = (bf16[512,1024]{1,0:T(8,128)(2,1)}, bf16[512,1024]{1,0:T(8,128)(2,1)}, u32[]{:S(2)}, u32[]{:S(2)}) collective-permute-start(bf16[512,1024]{1,0:T(8,128)(2,1)} %get-tuple-element.98), channel_id=1, source_target_pairs={{0,4},{4,0},{8,12},{12,8},{16,20},{20,16},{24,28},{28,24},{1,5},{5... | collective-permute-start | bytes 3145736 | tf_op jit(solution)/shard_map/ppermute | solution.py:71
  160.5 4.2 %collective-permute-start.49 = (bf16[80,640]{1,0:T(8,128)(2,1)}, bf16[80,640]{1,0:T(8,128)(2,1)S(1)}, u32[]{:S(2)}, u32[]{:S(2)}) collective-permute-start(bf16[80,640]{1,0:T(8,128)(2,1)} %get-tuple-element.116), channel_id=1, source_target_pairs={{0,4},{4,0},{8,12},{12,8},{16,20},{20,16},{24,28},{28,24},{1,5},{5... | collective-permute-start | bytes 307208 | tf_op jit(solution)/shard_map/ppermute | solution.py:71
  161.1 5.9 %collective-permute-start.50 = (bf16[80,640]{1,0:T(8,128)(2,1)}, bf16[80,640]{1,0:T(8,128)(2,1)S(1)}, u32[]{:S(2)}, u32[]{:S(2)}) collective-permute-start(bf16[80,640]{1,0:T(8,128)(2,1)} %get-tuple-element.117), channel_id=1, source_target_pairs={{0,8},{4,12},{8,0},{12,4},{16,24},{20,28},{24,16},{28,20},{1,9},{5... | collective-permute-start | bytes 307208 | tf_op jit(solution)/shard_map/ppermute | solution.py:71
  162.0 8.1 %collective-permute-start.51 = (bf16[80,640]{1,0:T(8,128)(2,1)}, bf16[80,640]{1,0:T(8,128)(2,1)}, u32[]{:S(2)}, u32[]{:S(2)}) collective-permute-start(bf16[80,640]{1,0:T(8,128)(2,1)} %get-tuple-element.118), channel_id=1, source_target_pairs={{0,12},{4,8},{8,4},{12,0},{16,28},{20,24},{24,20},{28,16},{1,13},{... | collective-permute-start | bytes 307208 | tf_op jit(solution)/shard_map/ppermute | solution.py:71
  162.7 7.4 %collective-permute-start.52 = (bf16[80,640]{1,0:T(8,128)(2,1)}, bf16[80,640]{1,0:T(8,128)(2,1)}, u32[]{:S(2)}, u32[]{:S(2)}) collective-permute-start(bf16[80,640]{1,0:T(8,128)(2,1)} %get-tuple-element.119), channel_id=1, source_target_pairs={{0,16},{4,20},{8,24},{12,28},{16,0},{20,4},{24,8},{28,12},{1,17},{... | collective-permute-start | bytes 307208 | tf_op jit(solution)/shard_map/ppermute | solution.py:71
  163.7 11.2 %collective-permute-start.53 = (bf16[80,640]{1,0:T(8,128)(2,1)}, bf16[80,640]{1,0:T(8,128)(2,1)}, u32[]{:S(2)}, u32[]{:S(2)}) collective-permute-start(bf16[80,640]{1,0:T(8,128)(2,1)} %get-tuple-element.120), channel_id=1, source_target_pairs={{0,20},{4,16},{8,28},{12,24},{16,4},{20,0},{24,12},{28,8},{1,21},{... | collective-permute-start | bytes 307208 | tf_op jit(solution)/shard_map/ppermute | solution.py:71
  164.8 10.0 %collective-permute-start.54 = (bf16[80,640]{1,0:T(8,128)(2,1)}, bf16[80,640]{1,0:T(8,128)(2,1)}, u32[]{:S(2)}, u32[]{:S(2)}) collective-permute-start(bf16[80,640]{1,0:T(8,128)(2,1)} %get-tuple-element.121), channel_id=1, source_target_pairs={{0,24},{4,28},{8,16},{12,20},{16,8},{20,12},{24,0},{28,4},{1,25},{... | collective-permute-start | bytes 307208 | tf_op jit(solution)/shard_map/ppermute | solution.py:71
  167.1 7.7 %collective-permute-start.55 = (bf16[80,640]{1,0:T(8,128)(2,1)}, bf16[80,640]{1,0:T(8,128)(2,1)}, u32[]{:S(2)}, u32[]{:S(2)}) collective-permute-start(bf16[80,640]{1,0:T(8,128)(2,1)} %get-tuple-element.122), channel_id=1, source_target_pairs={{0,28},{4,24},{8,20},{12,16},{16,12},{20,8},{24,4},{28,0},{1,29},{... | collective-permute-start | bytes 307208 | tf_op jit(solution)/shard_map/ppermute | solution.py:71
  181.4 14.8 %collective-permute-start.59 = (bf16[336,240]{1,0:T(8,128)(2,1)}, bf16[336,240]{1,0:T(8,128)(2,1)S(1)}, u32[]{:S(2)}, u32[]{:S(2)}) collective-permute-start(bf16[336,240]{1,0:T(8,128)(2,1)} %get-tuple-element.129), channel_id=1, source_target_pairs={{0,1},{1,0},{2,3},{3,2},{4,5},{5,4},{6,7},{7,6},{8,9},{9,8},{10,11... | collective-permute-start | bytes 483848 | tf_op jit(solution)/shard_map/ppermute | solution.py:71
  184.3 15.4 %collective-permute-start.56 = (bf16[128,960]{1,0:T(8,128)(2,1)}, bf16[128,960]{1,0:T(8,128)(2,1)S(1)}, u32[]{:S(2)}, u32[]{:S(2)}) collective-permute-start(bf16[128,960]{1,0:T(8,128)(2,1)} %get-tuple-element.125), channel_id=1, source_target_pairs={{0,8},{4,12},{8,0},{12,4},{16,24},{20,28},{24,16},{28,20},{1,9},{5... | collective-permute-start | bytes 737288 | tf_op jit(solution)/shard_map/ppermute | solution.py:71
  184.9 14.8 %collective-permute-start.57 = (bf16[128,960]{1,0:T(8,128)(2,1)}, bf16[128,960]{1,0:T(8,128)(2,1)S(1)}, u32[]{:S(2)}, u32[]{:S(2)}) collective-permute-start(bf16[128,960]{1,0:T(8,128)(2,1)} %get-tuple-element.126), channel_id=1, source_target_pairs={{0,16},{4,20},{8,24},{12,28},{16,0},{20,4},{24,8},{28,12},{1,17},{... | collective-permute-start | bytes 737288 | tf_op jit(solution)/shard_map/ppermute | solution.py:71
  186.6 13.1 %collective-permute-start.58 = (bf16[128,960]{1,0:T(8,128)(2,1)}, bf16[128,960]{1,0:T(8,128)(2,1)S(1)}, u32[]{:S(2)}, u32[]{:S(2)}) collective-permute-start(bf16[128,960]{1,0:T(8,128)(2,1)} %get-tuple-element.127), channel_id=1, source_target_pairs={{0,24},{4,28},{8,16},{12,20},{16,8},{20,12},{24,0},{28,4},{1,25},{... | collective-permute-start | bytes 737288 | tf_op jit(solution)/shard_map/ppermute | solution.py:71
  187.8 21.5 %collective-permute-start.60 = (bf16[336,240]{1,0:T(8,128)(2,1)}, bf16[336,240]{1,0:T(8,128)(2,1)}, u32[]{:S(2)}, u32[]{:S(2)}) collective-permute-start(bf16[336,240]{1,0:T(8,128)(2,1)} %get-tuple-element.130), channel_id=1, source_target_pairs={{0,2},{1,3},{2,0},{3,1},{4,6},{5,7},{6,4},{7,5},{8,10},{9,11},{10,... | collective-permute-start | bytes 483848 | tf_op jit(solution)/shard_map/ppermute | solution.py:71
  196.2 15.2 %collective-permute-start.61 = (bf16[336,240]{1,0:T(8,128)(2,1)}, bf16[336,240]{1,0:T(8,128)(2,1)}, u32[]{:S(2)}, u32[]{:S(2)}) collective-permute-start(bf16[336,240]{1,0:T(8,128)(2,1)} %get-tuple-element.131), channel_id=1, source_target_pairs={{0,3},{1,2},{2,1},{3,0},{4,7},{5,6},{6,5},{7,4},{8,11},{9,10},{10,... | collective-permute-start | bytes 483848 | tf_op jit(solution)/shard_map/ppermute | solution.py:71
  (56 other events, 229.4 us)
Sparse Core Ops, SparseCore 0:
  38.3 41.2 all-gather.2
  100.7 27.3 all-gather.4
  146.1 27.9 reduce-scatter.4
  176.4 32.9 reduce-scatter.6
